TPU v7x, 128 devices: a whole 4x4x4 slice. The times are simulated.
128 devices in a mesh: head: 2 (over z_hi), blk: 64 (over z_lo, x, y, core).
Axes of the slice: x: 4, y: 4, z: 4 (z_hi: 2, z_lo: 2; z = z_hi * 2 + z_lo), core: 2. Of those that a mesh axis runs over, the one named last changes fastest.
Arguments:
- hidden_in: bfloat16 [16384, 2048], P(('head', 'blk')), may hold values from -6 to 6
- gain_attn: float32 [2048], replicated, may hold values from 0.1 to 1.9
- gain_ffn: float32 [2048], replicated, may hold values from 0.1 to 1.9
- w_query: bfloat16 [2048, 2048], P(('head', 'blk')), may hold values from -0.125 to 0.125
- w_key: bfloat16 [2048, 1024], P(('head', 'blk')), may hold values from -0.125 to 0.125
- w_value: bfloat16 [2048, 1024], P(('head', 'blk')), may hold values from -0.125 to 0.125
- w_out: bfloat16 [2048, 2048], P(('head', 'blk')), may hold values from -0.375 to 0.375
- w_gate: bfloat16 [2048, 8192], P(('head', 'blk')), may hold values from -0.125 to 0.125
- w_up: bfloat16 [2048, 8192], P(('head', 'blk')), may hold values from -0.125 to 0.125
- w_down: bfloat16 [8192, 2048], P(('head', 'blk')), may hold values from -0.0625 to 0.0625
- qkv_shrink: bfloat16 [2048, 384], replicated, may hold values from -0.125 to 0.125
- query_expand: bfloat16 [128, 2048], replicated, may hold values from -1.5 to 1.5
- key_expand: bfloat16 [128, 1024], replicated, may hold values from -1.5 to 1.5
- value_expand: bfloat16 [128, 1024], replicated, may hold values from -1.5 to 1.5
- out_shrink: bfloat16 [2048, 128], replicated, may hold values from -0.125 to 0.125
- out_expand: bfloat16 [128, 2048], replicated, may hold values from -1.5 to 1.5
- gateup_shrink: bfloat16 [2048, 256], replicated, may hold values from -0.125 to 0.125
- gate_expand: bfloat16 [128, 8192], replicated, may hold values from -1.5 to 1.5
- up_expand: bfloat16 [128, 8192], replicated, may hold values from -1.5 to 1.5
- down_shrink: bfloat16 [8192, 128], replicated, may hold values from -0.0625 to 0.0625
- down_expand: bfloat16 [128, 2048], replicated, may hold values from -1.5 to 1.5
- lengths: int32 [16], replicated, may hold values from 1 to 4096, 16384 in all
- adapter: int32 [16], replicated, may hold values from 0 to 7
- packed_pos: int32 [16384], replicated, may hold values from 0 to 16383, as said below
- cotangent: bfloat16 [16384, 2048], P(('head', 'blk')), may hold values from -6 to 6
Outputs:
- output: bfloat16 [16384, 2048], P(('head', 'blk'))
- grad_input: bfloat16 [16384, 2048], P(('head', 'blk'))
- grad_qkv_shrink: float32 [2048, 384], replicated
- grad_query_expand: float32 [128, 2048], replicated
- grad_key_expand: float32 [128, 1024], replicated
- grad_value_expand: float32 [128, 1024], replicated
- grad_out_shrink: float32 [2048, 128], replicated
- grad_out_expand: float32 [128, 2048], replicated
- grad_gateup_shrink: float32 [2048, 256], replicated
- grad_gate_expand: float32 [128, 8192], replicated
- grad_up_expand: float32 [128, 8192], replicated
- grad_down_shrink: float32 [8192, 128], replicated
- grad_down_expand: float32 [128, 2048], replicated
Inputs may be any that keep to these rules, and one draw needn't show every extreme that they name: The lengths sum to 16384; sequence s takes the packed positions after those of sequences 0 to s - 1; the longest is exactly 4096. packed_pos is a permutation of 0 to 16383. Each half of an aligned block of 128 rows holds one aligned run of 64 packed positions, in shuffled order; the block of 128 rows held by the device at head index i and blk index j (rows (i * 64 + j) * 128 onward) holds runs number (2 i) * 64 + (j + r) % 64 and (2 i + 1) * 64 + (j + r) % 64, for one r per draw.
All inputs are finite; a program needn't handle non-finite values.
Results may differ from a plain program's by a relative error of at most 0.028.
Values may be sent and summed in bfloat16 or wider, within the bound.
No kernel may reach another device: no remote copies, remote signals or barrier semaphores. Data moves between devices by JAX's collectives and lax.ppermute only.
A program may use at most 448 MiB of HBM per device.

v0:
```python
from functools import partial

import jax
import jax.numpy as jnp
from jax import lax
from jax.experimental import pallas as pl
from jax.experimental.pallas import tpu as pltpu
from jax.sharding import Mesh, PartitionSpec as P

HEAD_SIZE = 256
RANK = 16
HALF = 64
GROUP = 512

ALL = ("zh", "zl", "x", "y", "c")

norm_eps = 1e-06
rope_theta = 1000042.0
neg_big = -1e30
far = 1 << 30

f32 = jnp.float32
bf16 = jnp.bfloat16


def product(left, right):
    return jnp.dot(left, right, preferred_element_type=f32)


def times_transposed(left, right):
    return lax.dot_general(left, right, (((1,), (1,)), ((), ())), preferred_element_type=f32)


def inner_rows(left, right):
    return lax.dot_general(left, right, (((0,), (0,)), ((), ())), preferred_element_type=f32)


def row_scale(value_matrix):
    return lax.rsqrt(jnp.mean(value_matrix * value_matrix, axis=-1, keepdims=True) + norm_eps)


def norm_back(value_matrix, scale, gain, grad):
    scaled = gain * grad
    return scale * scaled - value_matrix * (scale * scale * scale) * jnp.mean(
        value_matrix * scaled, axis=-1, keepdims=True
    )


def rotate(value_matrix):
    middle = value_matrix.shape[-1] // 2
    return jnp.concatenate([-value_matrix[..., middle:], value_matrix[..., :middle]], axis=-1)


def rope_tables(positions, width):
    middle = width // 2
    inverse = rope_theta ** (-(jnp.arange(middle, dtype=f32) * 2.0) / width)
    angles = positions.astype(f32)[:, None] * inverse[None, :]
    cos_half, sin_half = jnp.cos(angles), jnp.sin(angles)
    cos_table = jnp.concatenate([cos_half, cos_half], axis=-1)[:, None, :]
    sin_table = jnp.concatenate([sin_half, sin_half], axis=-1)[:, None, :]
    return (cos_table, sin_table)


OVER_X = ("zh", "zl", "y", "c")
RING = {"x": ("x",), "y": ("y",), "z": ("zh", "zl")}


def swap_cores(value):
    return lax.ppermute(value, "c", [(0, 1), (1, 0)])


def shift(value, ring, step):
    return lax.ppermute(value, RING[ring], [(i, (i + step) % 4) for i in range(4)])


def place_in(ring):
    return lax.axis_index(RING[ring])


def gather_near(value, ring, axis=0):
    return jnp.concatenate([value] + [shift(value, ring, -step) for step in (1, 2, 3)], axis=axis)


def gather_ring(value, ring):
    at = place_in(ring)
    whole_ring = jnp.zeros((4,) + value.shape, value.dtype)
    whole_ring = lax.dynamic_update_index_in_dim(whole_ring, value, at, 0)
    for step in (1, 2, 3):
        got = shift(value, ring, -step)
        whole_ring = lax.dynamic_update_index_in_dim(whole_ring, got, (at + step) % 4, 0)
    return whole_ring


def sum_near(blocks, ring):
    got = [shift(blocks[step], ring, step) for step in (2, 1, 3)]
    total = blocks[0].astype(f32)
    for term in got:
        total = total + term.astype(f32)
    return total


def sum_ring(terms, ring):
    at = place_in(ring)
    got = [
        shift(lax.dynamic_index_in_dim(terms, (at + step) % 4, 0, keepdims=False).astype(bf16), ring, step)
        for step in (1, 2, 3)
    ]
    total = lax.dynamic_index_in_dim(terms, at, 0, keepdims=False)
    for term in got:
        total = total + term.astype(f32)
    return total


CORNER = ("zh", "zl", "c")
PARTNER = [(4 * zh + 2 * zl + c, 4 * zh + 2 * (1 - zl) + c) for zh in (0, 1) for zl in (0, 1) for c in (0, 1)]
LATER = [[(2 * zl + 1, 4 + 2 * (zl ^ flip)) for zl in (0, 1)] for flip in (0, 1)]
EARLIER = [[(to, came) for came, to in pairs] for pairs in LATER]
def after(value, *others):
    return lax.optimization_barrier((value,) + others)[0]


def zero_of(value):
    return value[(slice(0, 1),) * value.ndim].reshape(()).astype(f32) * 0.0


def gather_row(key_value):
    line = jnp.stack([key_value] + [shift(key_value, "x", -step) for step in (1, 2, 3)])
    ahead = [lax.ppermute(line, CORNER, pairs) for pairs in LATER]
    partner = lax.ppermute(line, CORNER, PARTNER)
    beside = [lax.ppermute(value, "c", [(0, 1)]) for value in (line, partner)]
    return line, partner, ahead[0], ahead[1], beside[0], beside[1]


def sum_row(own, own_partner, prev, prev_partner):
    got = [lax.ppermute(value, "c", [(1, 0)]) for value in (prev_partner, prev)]
    terms = [lax.ppermute(value, CORNER, pairs) for value, pairs in zip((prev, prev_partner), EARLIER)]
    sent = (own_partner.astype(f32) + got[0].astype(f32)).astype(bf16)
    terms = [got[1], lax.ppermute(sent, CORNER, PARTNER)] + terms
    line = own.astype(f32)
    for term in terms:
        line = line + term.astype(f32)
    sent = line.astype(bf16)
    total = line[0]
    for step in (2, 1, 3):
        total = total + shift(sent[step], "x", step).astype(f32)
    return total


def allowed_mask(own_pos, own_start, key_pos):
    return (key_pos <= own_pos) & (key_pos >= own_start)


def load_tile(tile, tile_buf, own_ref, partner_ref, ahead_ref, ahead_partner_ref, beside_ref, beside_partner_ref):
    @pl.when(tile == 0)
    def _():
        tile_buf[...] = ahead_ref[0] + beside_ref[0]

    @pl.when(tile == 1)
    def _():
        tile_buf[...] = ahead_partner_ref[0] + beside_partner_ref[0]

    @pl.when(tile == 2)
    def _():
        tile_buf[...] = own_ref[0]

    @pl.when(tile == 3)
    def _():
        tile_buf[...] = partner_ref[0]


def attend_kernel(active, q_ref, pos_ref, start_ref, kpos_ref, *refs):
    mixed_ref, lse_ref, tile_buf, top, total, accum = refs[6:]
    step = pl.program_id(0)

    @pl.when(step == 0)
    def _():
        top[...] = jnp.full(top.shape, neg_big, f32)
        total[...] = jnp.zeros(total.shape, f32)
        accum[...] = jnp.zeros(accum.shape, f32)

    @pl.when(active[step] != 0)
    def _():
        load_tile(step // 4, tile_buf, *refs[:6])
        allowed = allowed_mask(pos_ref[...], start_ref[...], kpos_ref[0])
        for head in range(2):
            scores = times_transposed(q_ref[:, head * HEAD_SIZE : (head + 1) * HEAD_SIZE], tile_buf[:, :HEAD_SIZE])
            scores = jnp.where(allowed, scores, neg_big)
            top_old = top[head]
            top_new = jnp.maximum(top_old, jnp.max(scores, axis=-1, keepdims=True))
            weights_p = jnp.where(allowed, jnp.exp(scores - top_new), 0.0)
            damping = jnp.exp(top_old - top_new)
            total[head] = total[head] * damping + jnp.sum(weights_p, axis=-1, keepdims=True)
            accum[head] = accum[head] * damping + product(weights_p.astype(bf16), tile_buf[:, HEAD_SIZE:])
            top[head] = top_new

    @pl.when(step == 15)
    def _():
        for head in range(2):
            mixed_ref[:, head * HEAD_SIZE : (head + 1) * HEAD_SIZE] = accum[head] / total[head]
            lse_ref[head] = top[head] + jnp.log(total[head])


def attend_back_kernel(active, q_ref, pos_ref, start_ref, kpos_ref, *refs):
    mixed_ref, lse_ref, dout_ref, dq_ref, down_ref, dpartner_ref, dprev_ref, dprev_partner_ref = refs[6:14]
    tile_buf, delta, sums = refs[14:]
    step = pl.program_id(0)
    tile = step // 4

    @pl.when(step == 0)
    def _():
        dq_ref[...] = jnp.zeros(dq_ref.shape, f32)
        for head in range(2):
            cols = slice(head * HEAD_SIZE, (head + 1) * HEAD_SIZE)
            delta[head] = jnp.sum(dout_ref[:, cols].astype(f32) * mixed_ref[:, cols], axis=-1, keepdims=True)

    @pl.when(active[step] == 0)
    def _():
        sums[...] = jnp.zeros(sums.shape, bf16)

    @pl.when(active[step] != 0)
    def _():
        load_tile(tile, tile_buf, *refs[:6])
        allowed = allowed_mask(pos_ref[...], start_ref[...], kpos_ref[0])
        dk = jnp.zeros((GROUP, HEAD_SIZE), f32)
        dv = jnp.zeros((GROUP, HEAD_SIZE), f32)
        for head in range(2):
            cols = slice(head * HEAD_SIZE, (head + 1) * HEAD_SIZE)
            query, dout = q_ref[:, cols], dout_ref[:, cols]
            scores = times_transposed(query, tile_buf[:, :HEAD_SIZE])
            weights_p = jnp.where(allowed, jnp.exp(scores - lse_ref[head]), 0.0)
            dprobs = times_transposed(dout, tile_buf[:, HEAD_SIZE:])
            dscores = (weights_p * (dprobs - delta[head])).astype(bf16)
            dq_ref[:, cols] += product(dscores, tile_buf[:, :HEAD_SIZE])
            dk = dk + inner_rows(dscores, query)
            dv = dv + inner_rows(weights_p.astype(bf16), dout)
        sums[:, :HEAD_SIZE] = dk.astype(bf16)
        sums[:, HEAD_SIZE:] = dv.astype(bf16)

    for at, out_ref in enumerate((dprev_ref, dprev_partner_ref, down_ref, dpartner_ref)):

        @pl.when(tile == at)
        def _():
            out_ref[0] = sums[...]


def whole(shape):
    return pl.BlockSpec(shape, lambda *grid_and_refs: (0,) * len(shape))


def line_spec(tile):
    return pl.BlockSpec((1, GROUP, GROUP), lambda i, active: (jnp.clip(i - 4 * tile, 0, 3), 0, 0))


def common_specs():
    return [
        whole((GROUP, GROUP)),
        whole((GROUP, 1)),
        whole((GROUP, 1)),
        pl.BlockSpec((1, 1, GROUP), lambda i, active: (i, 0, 0)),
    ] + [line_spec(tile) for tile in (2, 3, 0, 1, 0, 1)]


def attend(active, *operands):
    return pl.pallas_call(
        attend_kernel,
        grid_spec=pltpu.PrefetchScalarGridSpec(
            num_scalar_prefetch=1,
            grid=(16,),
            in_specs=common_specs(),
            out_specs=[whole((GROUP, GROUP)), whole((2, GROUP, 1))],
            scratch_shapes=[
                pltpu.VMEM((GROUP, GROUP), bf16),
                pltpu.VMEM((2, GROUP, 1), f32),
                pltpu.VMEM((2, GROUP, 1), f32),
                pltpu.VMEM((2, GROUP, HEAD_SIZE), f32),
            ],
        ),
        out_shape=[
            jax.ShapeDtypeStruct((GROUP, GROUP), f32),
            jax.ShapeDtypeStruct((2, GROUP, 1), f32),
        ],
        compiler_params=pltpu.CompilerParams(vmem_limit_bytes=48 << 20),
        cost_estimate=pl.CostEstimate(flops=6 << 30, bytes_accessed=10 << 20, transcendentals=8 << 20),
        name="attend",
    )(active, *operands)


def attend_back(active, *operands):
    return pl.pallas_call(
        attend_back_kernel,
        grid_spec=pltpu.PrefetchScalarGridSpec(
            num_scalar_prefetch=1,
            grid=(16,),
            in_specs=common_specs() + [whole((GROUP, GROUP)), whole((2, GROUP, 1)), whole((GROUP, GROUP))],
            out_specs=[whole((GROUP, GROUP))] + [line_spec(tile) for tile in (2, 3, 0, 1)],
            scratch_shapes=[
                pltpu.VMEM((GROUP, GROUP), bf16),
                pltpu.VMEM((2, GROUP, 1), f32),
                pltpu.VMEM((GROUP, GROUP), bf16),
            ],
        ),
        out_shape=[jax.ShapeDtypeStruct((GROUP, GROUP), f32)]
        + [jax.ShapeDtypeStruct((4, GROUP, GROUP), bf16)] * 4,
        compiler_params=pltpu.CompilerParams(vmem_limit_bytes=48 << 20),
        cost_estimate=pl.CostEstimate(flops=12 << 30, bytes_accessed=20 << 20, transcendentals=8 << 20),
        name="attend_back",
    )(active, *operands)


UNITS = 1024
CHUNK = 256


def ffn_kernel(last, nm_ref, cot_ref, lgu_ref, gld_ref, wg_ref, wu_ref, wd_ref, ge_ref, ue_ref, ds_ref, perm_ref, *refs):
    if last:
        result_in, grad_in, low_in, glow_in = refs[:4]
        refs = refs[4:]
    result_ref, grad_ref, low_ref, glow_ref, gge_ref, gue_ref, gds_ref, nmp, result, grad = refs
    step = pl.program_id(0)
    rank = ds_ref.shape[1]

    @pl.when(step == 0)
    def _():
        for zone in range(4):
            cols = slice(zone * GROUP, (zone + 1) * GROUP)
            nmp[:, cols] = product(nm_ref[:, cols], perm_ref[...]).astype(bf16)
        if last:
            result[...] = result_in[...]
            grad[...] = grad_in[...]
            low_ref[...] = low_in[...]
            glow_ref[...] = glow_in[...]
        else:
            result[...] = jnp.zeros(result.shape, f32)
            grad[...] = jnp.zeros(grad.shape, f32)
            low_ref[...] = jnp.zeros(low_ref.shape, f32)
            glow_ref[...] = jnp.zeros(glow_ref.shape, f32)

    wg, wu = wg_ref[...].reshape(2048, CHUNK), wu_ref[...].reshape(2048, CHUNK)
    wd = wd_ref[...].reshape(CHUNK, 2048)
    low_gate, low_up = lgu_ref[:, :rank], lgu_ref[:, rank:]
    gate_pre = product(nmp[...], wg) + product(low_gate, ge_ref[...])
    up_pre = product(nmp[...], wu) + product(low_up, ue_ref[...])
    sigmoid_g = jax.nn.sigmoid(gate_pre)
    silu_gate = gate_pre * sigmoid_g
    active_units = (silu_gate * up_pre).astype(bf16)
    grad_active = times_transposed(cot_ref[...], wd) + times_transposed(gld_ref[...], ds_ref[...])
    grad_gate = (grad_active * up_pre * sigmoid_g * (1.0 + gate_pre * (1.0 - sigmoid_g))).astype(bf16)
    grad_up = (grad_active * silu_gate).astype(bf16)
    result[...] += product(active_units, wd)
    low_ref[...] += product(active_units, ds_ref[...])
    grad[...] += times_transposed(grad_gate, wg) + times_transposed(grad_up, wu)
    glow_ref[:, :rank] += times_transposed(grad_gate, ge_ref[...])
    glow_ref[:, rank:] += times_transposed(grad_up, ue_ref[...])
    gge_ref[...] = inner_rows(grad_gate, low_gate)
    gue_ref[...] = inner_rows(grad_up, low_up)
    gds_ref[...] = inner_rows(active_units, gld_ref[...])

    @pl.when(step == UNITS // CHUNK - 1)
    def _():
        if last:
            result_ref[...] = result[...].astype(bf16)
            for zone in range(4):
                cols = slice(zone * GROUP, (zone + 1) * GROUP)
                grad_ref[:, cols] = product(grad[:, cols].astype(bf16), perm_ref[...]).astype(bf16)
            grad_ref[:, 2048 : 2048 + 2 * rank] = glow_ref[...].astype(bf16)
            grad_ref[:, 2048 + 2 * rank :] = low_ref[...].astype(bf16)
        else:
            result_ref[...] = result[...]
            grad_ref[...] = grad[...]


def ffn_part(normed_mid, cot, low_gu, grad_low_down, weights, expands, perm, sums=None):
    last = sums is not None
    rank = low_gu.shape[1] // 2
    wide = bf16 if last else f32
    grad_width = 2048 + 3 * rank if last else 2048
    weight_specs = [
        pl.BlockSpec((16, 128, CHUNK), lambda u: (0, 0, u)),
        pl.BlockSpec((16, 128, CHUNK), lambda u: (0, 0, UNITS // CHUNK + u)),
        pl.BlockSpec((4, 64, 2048), lambda u: (u, 2, 0)),
        pl.BlockSpec((rank, CHUNK), lambda u: (0, u)),
        pl.BlockSpec((rank, CHUNK), lambda u: (0, u)),
        pl.BlockSpec((CHUNK, rank), lambda u: (u, 0)),
    ]
    sum_specs = [whole((GROUP, 2048)), whole((GROUP, 2048)), whole((GROUP, rank)), whole((GROUP, 2 * rank))]
    return pl.pallas_call(
        partial(ffn_kernel, last),
        grid=(UNITS // CHUNK,),
        in_specs=[whole((GROUP, 2048)), whole((GROUP, 2048)), whole((GROUP, 2 * rank)), whole((GROUP, rank))]
        + weight_specs
        + [whole((GROUP, GROUP))]
        + (sum_specs if last else []),
        out_specs=[whole((GROUP, 2048)), whole((GROUP, grad_width))]
        + sum_specs[2:]
        + [pl.BlockSpec((CHUNK, rank), lambda u: (u, 0))] * 3,
        out_shape=[
            jax.ShapeDtypeStruct((GROUP, 2048), wide),
            jax.ShapeDtypeStruct((GROUP, grad_width), wide),
            jax.ShapeDtypeStruct((GROUP, rank), f32),
            jax.ShapeDtypeStruct((GROUP, 2 * rank), f32),
        ]
        + [jax.ShapeDtypeStruct((UNITS, rank), f32)] * 3,
        scratch_shapes=[
            pltpu.VMEM((GROUP, 2048), bf16),
            pltpu.VMEM((GROUP, 2048), f32),
            pltpu.VMEM((GROUP, 2048), f32),
        ],
        compiler_params=pltpu.CompilerParams(vmem_limit_bytes=60 << 20),
        cost_estimate=pl.CostEstimate(flops=14 << 30, bytes_accessed=30 << 20, transcendentals=1 << 20),
        name="feed_forward",
    )(normed_mid, cot, low_gu, grad_low_down, weights, weights, weights, *expands, perm, *(sums or ()))


EARLY = (64, 64, 64, 16, 16, 16, 16, 16)
LATE = (16, 8, 8, 16, 16, 16)


def cut(array, sizes):
    found, at = [], 0
    for size in sizes:
        found.append(array[..., at : at + size, :])
        at += size
    return found


def early_kernel(all_ref, gate_ref, up_ref, down_ref, oshrink_ref, oexpand_ref, dexpand_ref, gateup_ref):
    pieces = [piece.astype(f32).reshape(-1, 128) for piece in cut(all_ref[...], EARLY)]
    gate_ref[...] = pieces[0].T
    up_ref[...] = pieces[1].T
    down_ref[...] = pieces[2]
    oshrink_ref[...] = pieces[3]
    oexpand_ref[...] = pieces[4].T
    dexpand_ref[...] = pieces[5].T
    gateup_ref[:, :128] = pieces[6]
    gateup_ref[:, 128:] = pieces[7]


def unpack_early(everyone):
    def rows_at(i):
        return (i % 4) * 4 + i // 4

    return pl.pallas_call(
        early_kernel,
        grid=(16,),
        in_specs=[pl.BlockSpec((8, sum(EARLY), 128), lambda i: (i, 0, 0))],
        out_specs=[
            pl.BlockSpec((128, 512), lambda i: (0, i)),
            pl.BlockSpec((128, 512), lambda i: (0, i)),
            pl.BlockSpec((512, 128), lambda i: (i, 0)),
            pl.BlockSpec((128, 128), lambda i: (rows_at(i), 0)),
            pl.BlockSpec((128, 128), lambda i: (0, rows_at(i))),
            pl.BlockSpec((128, 128), lambda i: (0, rows_at(i))),
            pl.BlockSpec((128, 256), lambda i: (rows_at(i), 0)),
        ],
        out_shape=[
            jax.ShapeDtypeStruct(shape, f32)
            for shape in ((128, 8192), (128, 8192), (8192, 128), (2048, 128), (128, 2048), (128, 2048), (2048, 256))
        ],
        cost_estimate=pl.CostEstimate(flops=1 << 20, bytes_accessed=27 << 20, transcendentals=0),
        name="unpack_early",
    )(everyone)


def late_kernel(core, mine_ref, other_ref, q_ref, k_ref, v_ref, low_ref):
    mine, other = mine_ref[0].astype(f32), other_ref[0].astype(f32)
    first, second = jnp.where(core[0] == 0, mine, other), jnp.where(core[0] == 0, other, mine)
    pieces = [
        jnp.stack(pair, axis=1).reshape(-1, 128) for pair in zip(cut(first, LATE), cut(second, LATE))
    ]
    q_ref[...] = pieces[0].T
    k_ref[...] = pieces[1].T
    v_ref[...] = pieces[2].T
    for at in range(3):
        low_ref[:, at * 128 : (at + 1) * 128] = pieces[3 + at]


def unpack_late(core, mine, other):
    half = pl.BlockSpec((1, 8, sum(LATE), 128), lambda i, core: (i // 2, i % 2, 0, 0))
    return pl.pallas_call(
        late_kernel,
        grid_spec=pltpu.PrefetchScalarGridSpec(
            num_scalar_prefetch=1,
            grid=(8,),
            in_specs=[half, half],
            out_specs=[
                pl.BlockSpec((128, 256), lambda i, core: (0, i)),
                pl.BlockSpec((128, 128), lambda i, core: (0, i)),
                pl.BlockSpec((128, 128), lambda i, core: (0, i)),
                pl.BlockSpec((256, 384), lambda i, core: (i, 0)),
            ],
        ),
        out_shape=[
            jax.ShapeDtypeStruct(shape, f32) for shape in ((128, 2048), (128, 1024), (128, 1024), (2048, 384))
        ],
        cost_estimate=pl.CostEstimate(flops=1 << 20, bytes_accessed=8 << 20, transcendentals=0),
        name="unpack_late",
    )(core, mine, other)


def local(
    hidden_in,
    gain_attn,
    gain_ffn,
    w_query,
    w_key,
    w_value,
    w_out,
    w_gate,
    w_up,
    w_down,
    qkv_shrink,
    query_expand,
    key_expand,
    value_expand,
    out_shrink,
    out_expand,
    gateup_shrink,
    gate_expand,
    up_expand,
    down_shrink,
    down_expand,
    lengths,
    adapter,
    packed_pos,
    cotangent,
):
    zh, zl, x, y, c = (lax.axis_index(name) for name in ALL)
    row = 2 * zh + c
    factor = HEAD_SIZE ** (-0.5)
    rank = out_shrink.shape[1]

    def to_rows(value):
        own = lax.dynamic_slice_in_dim(value, c * HALF, HALF, 0)
        sent = lax.dynamic_slice_in_dim(value, (1 - c) * HALF, HALF, 0)
        return jnp.concatenate([own, swap_cores(sent)], axis=0)

    def from_rows(value):
        own, got = value[:HALF], swap_cores(value[HALF:])
        return jnp.where(c == 0, jnp.concatenate([own, got], 0), jnp.concatenate([got, own], 0))

    hidden = to_rows(hidden_in)
    cot = to_rows(cotangent)

    def roll(array, by, axis):
        return lax.dynamic_slice_in_dim(jnp.concatenate([array, array], axis), by, array.shape[axis], axis)

    spread = packed_pos.reshape(2, 2, 4, 4, 2, 2, HALF)
    spread = jnp.transpose(spread, (0, 5, 1, 2, 3, 4, 6))
    rows_pos = jnp.stack([spread[:, 0], spread[:, 1, :, :, :, ::-1]], axis=1).reshape(4, 2, 4, 4, 128)
    rows_pos = roll(roll(roll(rows_pos, zl, 1), x, 2), y, 3).reshape(4, 8, GROUP)
    own_row = lax.dynamic_index_in_dim(rows_pos, row, 0, keepdims=False)
    prev_row = lax.dynamic_index_in_dim(rows_pos, jnp.maximum(row - 1, 0), 0, keepdims=False)
    prev_row = jnp.where(row == 0, far, prev_row)
    tiles_pos = jnp.concatenate([prev_row, own_row])
    group_pos = own_row[0]
    seq_ends = jnp.cumsum(lengths)
    starts = seq_ends - lengths
    member = (group_pos[:, None] >= starts[None, :]) & (group_pos[:, None] < seq_ends[None, :])
    member_int = member.astype(jnp.int32)
    group_start = jnp.sum(member_int * starts[None, :], axis=1)

    def selected(pos):
        inside = (pos[:, None] >= starts[None, :]) & (pos[:, None] < seq_ends[None, :])
        owner = jnp.sum(inside.astype(jnp.int32) * adapter[None, :], axis=1)
        return (owner[:, None] == (jnp.arange(rank, dtype=jnp.int32) // RANK)[None, :]).astype(f32)

    tile_low, tile_high = jnp.min(tiles_pos, axis=1), jnp.max(tiles_pos, axis=1)
    active = (tile_low <= jnp.max(group_pos)) & (tile_high >= jnp.min(group_start))
    active = active.astype(jnp.int32)
    select_y = selected(group_pos)
    select_x = selected(own_row.reshape(2, 4, 4, 128)[0, :, 0].reshape(GROUP))
    select = select_y[:128]
    cos_table, sin_table = rope_tables(group_pos - group_start, HEAD_SIZE)

    def column_slices(weight):
        parts = weight.reshape(16, 4, 4, 4, 2, 64)
        return jnp.transpose(parts, (2, 4, 0, 1, 3, 5)).reshape(8, 16, 1024)

    def units_at(array, axis, core):
        shape = array.shape
        array = array.reshape(shape[:axis] + (4, 4, 4, 2, 64) + shape[axis + 1 :])
        array = lax.dynamic_slice_in_dim(array, x, 1, axis + 1)
        array = lax.dynamic_slice_in_dim(array, core, 1, axis + 3)
        return array.reshape(shape[:axis] + (1024,) + shape[axis + 1 :])

    heads_q = w_query.reshape(16, 4, 512)
    heads_kv = jnp.concatenate([w_key.reshape(16, 4, 256), w_value.reshape(16, 4, 256)], axis=2)
    qkv_parts = jnp.transpose(jnp.stack([heads_q, heads_kv], axis=2), (1, 2, 0, 3)).reshape(8, 16, 512)
    qkv_parts = lax.all_to_all(qkv_parts, ("y", "c"), split_axis=0, concat_axis=0, tiled=True).reshape(128, 512)
    gate_up = jnp.concatenate([column_slices(w_gate), column_slices(w_up)], axis=2)
    gate_up = lax.all_to_all(after(gate_up, qkv_parts), ("x", "c"), split_axis=0, concat_axis=0, tiled=True).reshape(128, 2048)
    expands = [
        (units_at(gate_expand, 1, core), units_at(up_expand, 1, core), units_at(down_shrink, 0, core))
        for core in (c, 1 - c)
    ]

    def columns_of(array, width):
        return lax.dynamic_slice_in_dim(array, y * width, width, 1)

    inputs = hidden.astype(f32)
    scale_in = row_scale(inputs)
    normed = (inputs * scale_in * gain_attn).astype(bf16)
    normed, cot, qkv_parts, gate_up = lax.optimization_barrier((normed, cot, qkv_parts, gate_up))
    normed_g = gather_near(normed, "y")
    cot_g = gather_near(cot, "x")
    qkv_parts = after(qkv_parts, normed_g, cot_g, expands)
    wo = lax.all_gather(after(w_out, normed_g, cot_g), ALL, axis=0, tiled=True)
    qkv_mine = gather_ring(gather_ring(qkv_parts, "x"), "z").reshape(2048, 512)
    qkv_other = swap_cores(qkv_mine)
    ffn = after(jnp.concatenate([gate_up, w_down], axis=0), normed_g, cot_g)
    ffn_mine = lax.all_gather(ffn, ("zh", "zl", "y"), axis=0, tiled=False)
    q_expand = columns_of(query_expand, 512)
    k_expand = columns_of(key_expand, 256)
    v_expand = columns_of(value_expand, 256)
    low_qkv = (product(normed_g, qkv_shrink) * jnp.tile(select_y, (1, 3))).astype(bf16)
    lin_mine, lin_other = product(normed_g, qkv_mine), product(normed_g, qkv_other)
    query_lin = jnp.where(c == 0, lin_mine, lin_other) + product(low_qkv[:, :rank], q_expand)
    kv_lin = jnp.where(c == 0, lin_other, lin_mine)
    key_lin = kv_lin[:, :256] + product(low_qkv[:, rank : 2 * rank], k_expand)
    value_lin = kv_lin[:, 256:] + product(low_qkv[:, 2 * rank :], v_expand)
    query_heads = query_lin.reshape(GROUP, 2, HEAD_SIZE)
    key_heads = key_lin.reshape(GROUP, 1, HEAD_SIZE)
    query = (query_heads * cos_table + rotate(query_heads) * sin_table).astype(bf16)
    query = (query * bf16(factor)).reshape(GROUP, 512)
    key = (key_heads * cos_table + rotate(key_heads) * sin_table).astype(bf16).reshape(GROUP, 256)

    lines = gather_row(jnp.concatenate([key, value_lin.astype(bf16)], axis=1))
    attended = (query, group_pos[:, None], group_start[:, None], tiles_pos.reshape(16, 1, GROUP)) + lines
    mixed_f, lse = attend(active, *attended)
    mixed = mixed_f.astype(bf16)

    heads = jnp.zeros((4, 128, 512), bf16)
    heads = lax.dynamic_update_index_in_dim(heads, mixed[:128], y, 0)
    for step in (1, 2, 3):
        got = shift(mixed[step * 128 : (step + 1) * 128], "y", step)
        heads = lax.dynamic_update_index_in_dim(heads, got, (y - step) % 4, 0)
    mixed_tok = jnp.transpose(heads, (1, 0, 2)).reshape(128, 2048)
    low_out = (product(mixed_tok, out_shrink) * select).astype(bf16)
    middle = inputs + product(mixed_tok, wo) + product(low_out, out_expand)
    scale_mid = row_scale(middle)
    normed_mid = (middle * scale_mid * gain_ffn).astype(bf16)
    normed_mid_g = gather_near(normed_mid, "x")
    ffn_other = swap_cores(after(ffn_mine, normed_mid))

    select_two = jnp.tile(select_x, (1, 2))
    low_gu = (product(normed_mid_g, gateup_shrink) * select_two).astype(bf16)
    grad_low_down = (times_transposed(cot_g, down_expand) * select_x).astype(bf16)
    place = jnp.arange(GROUP, dtype=jnp.int32)
    turned = (place // 32 % 4) * 128 + (place // 128) * 32 + place % 32
    perm = (turned[:, None] == place[None, :]).astype(bf16)
    given = (normed_mid_g, cot_g, low_gu, grad_low_down)
    sums = ffn_part(*given, ffn_mine, expands[0], perm)
    units_mine, sums = sums[4:], sums[:4]
    sums = ffn_part(*given, ffn_other, expands[1], perm, sums)
    units_other = sums[4:]
    result, back_part = sums[:2]
    unit_grads = (units_mine, units_other)

    def reduce_units(unit_grads):
        def by_halves(pair_at):
            own, others = unit_grads[0][pair_at], unit_grads[1][pair_at]
            own, others = own.reshape(16, 1, 64, rank), others.reshape(16, 1, 64, rank)
            ordered = jnp.where(c == 0, jnp.concatenate([own, others], 1), jnp.concatenate([others, own], 1))
            return ordered.reshape(32, 64, rank)

        unit_terms = jnp.concatenate([by_halves(0), by_halves(1), by_halves(2)], axis=1)
        return lax.psum_scatter(unit_terms, OVER_X, scatter_dimension=0, tiled=False)

    def sum_tokens(part, ring):
        sent = part.astype(bf16)
        return sum_near([sent[i * 128 : (i + 1) * 128] for i in range(4)], ring)

    back = sum_tokens(back_part, "x")
    back, back_low, low_down_sum = back[:, :2048], back[:, 2048 : 2048 + 2 * rank], back[:, 2048 + 2 * rank :]

    low_down = (low_down_sum * select).astype(bf16)
    grad_low_gu = (back_low * jnp.tile(select, (1, 2))).astype(bf16)
    grad_normed_mid = back + times_transposed(grad_low_gu, gateup_shrink)
    cot_f = cot.astype(f32)
    grad_middle = cot_f + norm_back(middle, scale_mid, gain_ffn, grad_normed_mid)
    grad_attn_out = grad_middle.astype(bf16)
    grad_low_out = (times_transposed(grad_attn_out, out_expand) * select).astype(bf16)
    grad_mixed = (times_transposed(grad_attn_out, wo) + times_transposed(grad_low_out, out_shrink)).astype(bf16)

    def slices_near(array):
        def columns_at(step):
            return lax.dynamic_slice_in_dim(array, ((y + step) % 4) * 512, 512, 1)

        return jnp.concatenate([columns_at(0)] + [shift(columns_at(4 - step), "y", -step) for step in (1, 2, 3)])

    unit_sum = reduce_units(unit_grads)
    dout = slices_near(grad_mixed)
    dout = dout + zero_of(unit_sum).astype(bf16)
    dq, *terms = attend_back(active, *attended, mixed_f, lse, dout)
    dkv = sum_row(*terms)
    dk, dv = dkv[:, :HEAD_SIZE], dkv[:, HEAD_SIZE:]
    query_back = (dq * factor).astype(bf16).astype(f32).reshape(GROUP, 2, HEAD_SIZE)
    key_back = dk.astype(bf16).astype(f32).reshape(GROUP, 1, HEAD_SIZE)
    grad_value = dv.astype(bf16)
    grad_query = (query_back * cos_table - rotate(query_back * sin_table)).astype(bf16).reshape(GROUP, 512)
    grad_key = (key_back * cos_table - rotate(key_back * sin_table)).astype(bf16).reshape(GROUP, 256)
    grad_kv = jnp.concatenate([grad_key, grad_value], axis=1)

    grad_low_part = jnp.concatenate(
        [
            times_transposed(grad_query, q_expand),
            times_transposed(grad_key, k_expand),
            times_transposed(grad_value, v_expand),
        ],
        axis=1,
    )
    grad_low_qkv = (sum_tokens(grad_low_part, "y") * jnp.tile(select, (1, 3))).astype(bf16)
    for_mine = jnp.where(c == 0, grad_query, grad_kv)
    for_other = jnp.where(c == 0, grad_kv, grad_query)
    grad_normed_part = times_transposed(for_mine, qkv_mine) + times_transposed(for_other, qkv_other)
    grad_normed = sum_tokens(grad_normed_part, "y") + times_transposed(grad_low_qkv, qkv_shrink)
    ahead = sum_tokens(after(result, grad_normed), "x")
    output = (middle + ahead + product(low_down, down_expand)).astype(bf16)
    grad_input = (grad_middle + norm_back(inputs, scale_in, gain_attn, grad_normed)).astype(bf16)

    def features(array, at):
        return lax.dynamic_slice_in_dim(array, at * 512, 512, 1)

    def by_rows(array):
        return array.reshape(32, array.shape[0] // 32, rank)

    low_near = gather_near(after(jnp.concatenate([low_down, grad_low_gu], axis=1), dout), "x")
    grad_gateup = inner_rows(features(normed_mid_g, x), low_near[:, rank:])
    out_terms = jnp.concatenate([inner_rows(mixed_tok, grad_low_out), inner_rows(grad_attn_out, low_out)], axis=1)
    out_terms = after(out_terms.astype(bf16).reshape(4, 512, 2 * rank), dout)
    out_terms = sum_near(
        [lax.dynamic_index_in_dim(out_terms, (x + step) % 4, 0, keepdims=False) for step in range(4)], "x"
    )
    row_terms = [
        by_rows(out_terms[:, :rank]),
        by_rows(out_terms[:, rank:]),
        by_rows(inner_rows(features(cot_g, x), low_near[:, :rank])),
        by_rows(grad_gateup[:, :rank]),
        by_rows(grad_gateup[:, rank:]),
    ]
    row_sum = lax.psum_scatter(jnp.concatenate(row_terms, axis=1) + zero_of(unit_sum), OVER_X, scatter_dimension=0, tiled=False)
    early_sum = jnp.concatenate([unit_sum, row_sum], axis=0)
    early_sum = after(early_sum.astype(bf16), dkv)
    early_all = lax.all_gather(early_sum, ALL, axis=0, tiled=False)

    grad_qkv = inner_rows(features(normed_g, y), gather_near(grad_low_qkv, "y"))
    late = [
        by_rows(inner_rows(grad_query, low_qkv[:, :rank])),
        by_rows(inner_rows(grad_key, low_qkv[:, rank : 2 * rank])),
        by_rows(inner_rows(grad_value, low_qkv[:, 2 * rank :])),
        by_rows(grad_qkv[:, :rank]),
        by_rows(grad_qkv[:, rank : 2 * rank]),
        by_rows(grad_qkv[:, 2 * rank :]),
    ]
    terms = jnp.concatenate(late, axis=1)
    terms = terms.reshape(16, 2, terms.shape[1], rank)
    kept = lax.dynamic_index_in_dim(terms, c, 1, keepdims=False)
    given = lax.dynamic_index_in_dim(terms, 1 - c, 1, keepdims=False).astype(bf16)
    terms = (kept + swap_cores(given).astype(f32)).reshape(4, 4, -1, rank)
    late_sum = sum_ring(sum_ring(terms, "z"), "x").astype(bf16)
    late_all = gather_ring(gather_ring(gather_ring(late_sum, "x"), "z"), "y")
    late_all = late_all.reshape(4, 16, -1, rank)
    g_gate, g_up, g_down_shrink, g_out_shrink, g_out_expand, g_down_expand, g_gateup = unpack_early(early_all)
    late_other = swap_cores(late_all)
    late_all = after(late_all, g_gate, g_gateup)
    g_q, g_k, g_v, g_qkv = unpack_late(c.reshape(1).astype(jnp.int32), late_all, late_other)
    return (
        from_rows(output),
        from_rows(grad_input),
        g_qkv,
        g_q,
        g_k,
        g_v,
        g_out_shrink,
        g_out_expand,
        g_gateup,
        g_gate,
        g_up,
        g_down_shrink,
        g_down_expand,
    )


def solution(mesh):
    fine = Mesh(mesh.devices.reshape(2, 2, 4, 4, 2), ALL)
    split = P(ALL, None)
    placed = (split, P(), P()) + (split,) * 7 + (P(),) * 14 + (split,)
    return jax.shard_map(
        local,
        mesh=fine,
        in_specs=placed,
        out_specs=(split, split) + (P(),) * 11,
        check_vma=False,
    )
```

profile of v0, /device:TPU:1, one launch (start us, length us, event | category | flops | bytes accessed | tf_op | source)
XLA Modules:
  0.0 886.5 jit_solution(17461914079614984986)
XLA Ops:
  13.4 5.0 all-to-all-start
  23.8 4.9 all-to-all-start.1
  31.5 6.7 all-to-all-done.1
  45.1 5.7 collective-permute-done.5
  53.0 12.7 %collective-permute-done.7 = bf16[128,2048]{1,0:T(8,128)(2,1)S(1)} collective-permute-done((bf16[128,2048]{1,0:T(8,128)(2,1)S(1)}, bf16[128,2048]{1,0:T(8,128)(2,1)S(1)}, u32[]{:S(2)}, u32[]{:S(2)}) %collective-permute-start.7) | collective-permute-done | bytes 524320 | tf_op jit(solution)/shard_map/ppermute | solution.py:73
  67.5 3.4 collective-permute-done.4
  72.9 4.1 copy.145
  77.0 4.1 copy.146
  85.9 2.9 collective-permute-start.8
  89.4 5.2 collective-permute-done.8
  94.8 2.8 collective-permute-done.10
  97.6 3.6 collective-permute-start.11
  104.6 8.2 collective-permute-done.11
  116.7 13.8 %collective-permute-done.13 = bf16[4,128,512]{2,1,0:T(8,128)(2,1)S(1)} collective-permute-done((bf16[4,128,512]{2,1,0:T(8,128)(2,1)S(1)}, bf16[4,128,512]{2,1,0:T(8,128)(2,1)S(1)}, u32[]{:S(2)}, u32[]{:S(2)}) %collective-permute-start.13) | collective-permute-done | bytes 524320 | tf_op jit(solution)/shard_map/ppermute | solution.py:73
  136.3 3.0 fusion.2
  140.5 3.7 fusion.147
  144.2 4.9 broadcast_select_fusion
  152.8 11.4 %collective-permute-done.15 = bf16[512,512]{1,0:T(8,128)(2,1)S(1)} collective-permute-done((bf16[512,512]{1,0:T(8,128)(2,1)S(1)}, bf16[512,512]{1,0:T(8,128)(2,1)S(1)}, u32[]{:S(2)}, u32[]{:S(2)}) %collective-permute-start.15) | collective-permute-done | bytes 524320 | tf_op jit(solution)/shard_map/ppermute | solution.py:73
  164.2 3.1 collective-permute-done.16
  167.3 10.9 %collective-permute-done.17 = bf16[512,512]{1,0:T(8,128)(2,1)S(1)} collective-permute-done((bf16[512,512]{1,0:T(8,128)(2,1)S(1)}, bf16[512,512]{1,0:T(8,128)(2,1)S(1)}, u32[]{:S(2)}, u32[]{:S(2)}) %collective-permute-start.17) | collective-permute-done | bytes 524320 | tf_op jit(solution)/shard_map/ppermute | solution.py:73
  179.8 6.4 collective-permute-start.19
  186.2 2.6 collective-permute-start.20
  190.1 68.9 %collective-permute-done.18.refs_1_ = bf16[4,512,512]{2,1,0:T(8,128)(2,1)} collective-permute-done((bf16[4,512,512]{2,1,0:T(8,128)(2,1)}, bf16[4,512,512]{2,1,0:T(8,128)(2,1)}, u32[]{:S(2)}, u32[]{:S(2)}) %collective-permute-start.18) | collective-permute-done | bytes 2097184 | tf_op jit(solution)/shard_map/ppermute | solution.py:129
  266.4 2.8 reshape.472
  272.7 37.1 %collective-permute-done.19.refs_2_ = bf16[4,512,512]{2,1,0:T(8,128)(2,1)} collective-permute-done((bf16[4,512,512]{2,1,0:T(8,128)(2,1)}, bf16[4,512,512]{2,1,0:T(8,128)(2,1)}, u32[]{:S(2)}, u32[]{:S(2)}) %collective-permute-start.19) | collective-permute-done | bytes 2097184 | tf_op jit(solution)/shard_map/ppermute | solution.py:128
  309.8 17.8 %attend.1 = (f32[512,512]{1,0:T(8,128)S(1)}, f32[2,512,1]{2,1,0:T(8,128)S(1)}) custom-call(s32[16]{0:T(128)S(1)} %and_convert_fusion.active, bf16[512,512]{1,0:T(8,128)(2,1)S(1)} %fusion.23.q_ref, s32[512,1]{1,0:T(8,128)S(1)} %copy.158.pos_ref, s32[512,1]{1,0:T(8,128)S(1)} %copy.159.start_ref, s32[16,1,512]{2,1,0:T(1,128)S(1)} %reshape.473.kpos_ref, ...), custom_call_target="tpu_custom_call" | custom-call | flops 6442450944 | bytes 10485760 | tf_op jit(solution)/shard_map/attend/pallas_call | solution.py:264
  343.3 5.3 multiply_reduce_fusion.1
  356.8 12.8 %collective-permute-start.26 = (bf16[128,2048]{1,0:T(8,128)(2,1)}, bf16[128,2048]{1,0:T(8,128)(2,1)S(1)}, u32[]{:S(2)}, u32[]{:S(2)}) collective-permute-start(bf16[128,2048]{1,0:T(8,128)(2,1)} %multiply_convert_fusion.1), channel_id=1, source_target_pairs={{0,24},{8,0},{16,8},{24,16},{1,25},{9,1},{17,9},{25,17},{2,26},{10... | collective-permute-start | bytes 1572872 | tf_op jit(solution)/shard_map/ppermute | solution.py:73
  371.3 3.0 fusion.4.gld_ref
  374.3 17.9 %collective-permute-done.26 = bf16[128,2048]{1,0:T(8,128)(2,1)S(1)} collective-permute-done((bf16[128,2048]{1,0:T(8,128)(2,1)}, bf16[128,2048]{1,0:T(8,128)(2,1)S(1)}, u32[]{:S(2)}, u32[]{:S(2)}) %collective-permute-start.26) | collective-permute-done | bytes 524320 | tf_op jit(solution)/shard_map/ppermute | solution.py:73
  392.3 3.6 collective-permute-done.28
  399.1 26.3 %feed_forward.2 = (f32[512,2048]{1,0:T(8,128)}, f32[512,2048]{1,0:T(8,128)}, f32[512,128]{1,0:T(8,128)}, f32[512,256]{1,0:T(8,128)}, f32[1024,128]{1,0:T(8,128)}...) custom-call(bf16[512,2048]{1,0:T(8,128)(2,1)} %pad_maximum_fusion.2.nm_ref, bf16[512,2048]{1,0:T(8,128)(2,1)} %copy-done.56, ...), custom_call_target="tpu_custom_call" | custom-call | flops 15032385536 | bytes 31457280 | tf_op jit(solution)/shard_map/feed_forward/pallas_call | solution.py:386
  425.4 28.8 %feed_forward.3 = (bf16[512,2048]{1,0:T(8,128)(2,1)}, bf16[512,2432]{1,0:T(8,128)(2,1)}, f32[512,128]{1,0:T(8,128)}, f32[512,256]{1,0:T(8,128)}, f32[1024,128]{1...) custom-call(bf16[512,2048]{1,0:T(8,128)(2,1)} %pad_maximum_fusion.2.nm_ref, bf16[512,2048]{1,0:T(8,128)(2,1)} %copy-done.56, ...), custom_call_target="tpu_custom_call" | custom-call | flops 15032385536 | bytes 31457280 | tf_op jit(solution)/shard_map/feed_forward/pallas_call | solution.py:386
  459.2 2.7 fusion.135
  462.6 2.7 collective-permute-start.32
  465.2 13.3 %collective-permute-done.30 = bf16[128,2432]{1,0:T(8,128)(2,1)} collective-permute-done((bf16[128,2432]{1,0:T(8,128)(2,1)}, bf16[128,2432]{1,0:T(8,128)(2,1)}, u32[]{:S(2)}, u32[]{:S(2)}) %collective-permute-start.30) | collective-permute-done | bytes 622624 | tf_op jit(solution)/shard_map/ppermute | solution.py:73
  478.5 14.5 %collective-permute-done.31 = bf16[128,2432]{1,0:T(8,128)(2,1)} collective-permute-done((bf16[128,2432]{1,0:T(8,128)(2,1)}, bf16[128,2432]{1,0:T(8,128)(2,1)}, u32[]{:S(2)}, u32[]{:S(2)}) %collective-permute-start.31) | collective-permute-done | bytes 622624 | tf_op jit(solution)/shard_map/ppermute | solution.py:73
  499.2 2.9 fusion.125
  504.6 38.5 %reduce-scatter.3.cloned.1.call-done = f32[1,192,128]{2,1,0:T(8,128)} async-done(((f32[32,192,128]{2,1,0:T(8,128)}), f32[1,192,128]{2,1,0:T(8,128)}) %reduce-scatter.3.cloned.1.call-update) | async-done | bytes 98320 | tf_op jit(solution)/shard_map/reduce_scatter | solution.py:667
  548.4 21.3 %attend_back.1 = (f32[512,512]{1,0:T(8,128)S(1)}, bf16[4,512,512]{2,1,0:T(8,128)(2,1)}, bf16[4,512,512]{2,1,0:T(8,128)(2,1)}, bf16[4,512,512]{2,1,0:T(8,128)(2,1)}, bf16[4,512,512]{2,1,0:T(8,128)(2,1)}) custom-call(s32[16]{0:T(128)S(1)} %and_convert_fusion.active, bf16[512,512]{1,0:T(8,128)(2,1)S(1)} %fusion.23.q_ref, s32[512,1]{1,0:T(8,128)S(1)} %copy-done.4, ...), custom_call_target="tpu_custom_call" | custom-call | flops 12884901888 | bytes 20971520 | tf_op jit(solution)/shard_map/attend_back/pallas_call | solution.py:289
  569.7 4.5 collective-permute-start.37
  580.1 9.7 %collective-permute-start.77 = (bf16[128,384]{1,0:T(8,128)(2,1)S(1)}, bf16[128,384]{1,0:T(8,128)(2,1)S(1)}, u32[]{:S(2)}, u32[]{:S(2)}) collective-permute-start(bf16[128,384]{1,0:T(8,128)(2,1)S(1)} %pad_maximum_fusion.16), channel_id=1, source_target_pairs={{0,24},{8,0},{16,8},{24,16},{1,25},{9,1},{17,9},{25,17},{2,26},{10... | collective-permute-start | bytes 294920 | tf_op jit(solution)/shard_map/ppermute | solution.py:73
  590.5 2.6 collective-permute-start.36
  603.9 3.5 add_convert_fusion.1
  614.5 14.1 %collective-permute-done.39 = bf16[4,512,512]{2,1,0:T(8,128)(2,1)} collective-permute-done((bf16[4,512,512]{2,1,0:T(8,128)(2,1)}, bf16[4,512,512]{2,1,0:T(8,128)(2,1)}, u32[]{:S(2)}, u32[]{:S(2)}) %collective-permute-start.39) | collective-permute-done | bytes 2097184 | tf_op jit(solution)/shard_map/ppermute | solution.py:136
  628.6 17.0 %collective-permute-done.40 = bf16[4,512,512]{2,1,0:T(8,128)(2,1)} collective-permute-done((bf16[4,512,512]{2,1,0:T(8,128)(2,1)}, bf16[4,512,512]{2,1,0:T(8,128)(2,1)}, u32[]{:S(2)}, u32[]{:S(2)}) %collective-permute-start.40) | collective-permute-done | bytes 2097184 | tf_op jit(solution)/shard_map/ppermute | solution.py:136
  645.6 11.0 %collective-permute-done.38 = bf16[4,512,512]{2,1,0:T(8,128)(2,1)} collective-permute-done((bf16[4,512,512]{2,1,0:T(8,128)(2,1)}, bf16[4,512,512]{2,1,0:T(8,128)(2,1)}, u32[]{:S(2)}, u32[]{:S(2)}) %collective-permute-start.38) | collective-permute-done | bytes 2097184 | tf_op jit(solution)/shard_map/ppermute | solution.py:138
  656.6 7.7 fusion.133
  668.9 25.7 %reduce-scatter.5.cloned.1.call-done = f32[1,80,128]{2,1,0:T(8,128)} async-done(((f32[32,80,128]{2,1,0:T(8,128)}), f32[1,80,128]{2,1,0:T(8,128)}) %reduce-scatter.5.cloned.1.call-update) | async-done | bytes 40976 | tf_op jit(solution)/shard_map/reduce_scatter | solution.py:741
  700.5 2.8 reshape.483
  720.9 2.9 fusion.37
  723.9 3.0 add_convert_fusion
  730.9 3.4 collective-permute-done.55
  739.0 4.1 collective-permute-start.58
  750.6 13.8 %collective-permute-done.44 = bf16[128,2048]{1,0:T(8,128)(2,1)} collective-permute-done((bf16[128,2048]{1,0:T(8,128)(2,1)}, bf16[128,2048]{1,0:T(8,128)(2,1)}, u32[]{:S(2)}, u32[]{:S(2)}) %collective-permute-start.44) | collective-permute-done | bytes 524320 | tf_op jit(solution)/shard_map/ppermute | solution.py:73
  764.4 17.7 %collective-permute-done.45 = bf16[128,2048]{1,0:T(8,128)(2,1)} collective-permute-done((bf16[128,2048]{1,0:T(8,128)(2,1)S(1)}, bf16[128,2048]{1,0:T(8,128)(2,1)}, u32[]{:S(2)}, u32[]{:S(2)}) %collective-permute-start.45) | collective-permute-done | bytes 524320 | tf_op jit(solution)/shard_map/ppermute | solution.py:73
  797.8 19.3 %collective-permute-done.66 = bf16[80,128]{1,0:T(8,128)(2,1)S(1)} collective-permute-done((bf16[80,128]{1,0:T(8,128)(2,1)S(1)}, bf16[80,128]{1,0:T(8,128)(2,1)S(1)}, u32[]{:S(2)}, u32[]{:S(2)}) %collective-permute-start.66) | collective-permute-done | bytes 20512 | tf_op jit(solution)/shard_map/ppermute | solution.py:73
  817.2 2.8 collective-permute-done.67
  825.0 3.0 collective-permute-done.70
  831.9 3.4 collective-permute-done.71
  837.9 7.0 collective-permute-done.73
  845.0 8.7 collective-permute-start.80
  858.4 14.6 %unpack_early.1 = (f32[128,8192]{1,0:T(8,128)}, f32[128,8192]{1,0:T(8,128)}, f32[8192,128]{1,0:T(8,128)}, f32[2048,128]{1,0:T(8,128)}, f32[128,2048]{1,0:T(8,128...) custom-call(bf16[128,272,128]{2,1,0:T(8,128)(2,1)} %bitcast.269), custom_call_target="tpu_custom_call" | custom-call | flops 1048576 | bytes 28311552 | tf_op jit(solution)/shard_map/unpack_early/pallas_call | solution.py:442
  873.0 6.8 unpack_late.1
  (506 shorter events, 211.1 us)
Async XLA Ops:
  9.1 19.6 %collective-permute-start = (bf16[64,2048]{1,0:T(8,128)(2,1)}, bf16[64,2048]{1,0:T(8,128)(2,1)S(1)}, u32[]{:S(2)}, u32[]{:S(2)}) collective-permute-start(bf16[64,2048]{1,0:T(8,128)(2,1)} %get-tuple-element.169), channel_id=1, source_target_pairs={{0,1},{1,0},{2,3},{3,2},{4,5},{5,4},{6,7},{7,6},{8,9},{9,8},{10,11... | collective-permute-start | bytes 786440 | tf_op jit(solution)/shard_map/ppermute | solution.py:69
  12.3 17.2 %collective-permute-start.1 = (bf16[64,2048]{1,0:T(8,128)(2,1)}, bf16[64,2048]{1,0:T(8,128)(2,1)}, u32[]{:S(2)}, u32[]{:S(2)}) collective-permute-start(bf16[64,2048]{1,0:T(8,128)(2,1)} %get-tuple-element.167), channel_id=1, source_target_pairs={{0,1},{1,0},{2,3},{3,2},{4,5},{5,4},{6,7},{7,6},{8,9},{9,8},{10,11... | collective-permute-start | bytes 786440 | tf_op jit(solution)/shard_map/ppermute | solution.py:69
  13.4 10.5 %all-to-all-start = ((bf16[8,16,512]{2,1,0:T(8,128)(2,1)}), bf16[8,16,512]{2,1,0:T(8,128)(2,1)S(1)}, u32[]{:S(2)}, u32[]{:S(2)}) async-start(bf16[8,16,512]{2,1,0:T(8,128)(2,1)} %bitcast.7), calls=%async_computation | async-start | bytes 262144 | tf_op jit(solution)/shard_map/all_to_all | solution.py:589
  23.8 14.4 %all-to-all-start.1 = ((bf16[8,16,2048]{2,1,0:T(8,128)(2,1)}), bf16[8,16,2048]{2,1,0:T(8,128)(2,1)S(1)}, u32[]{:S(2)}, u32[]{:S(2)}) async-start(bf16[8,16,2048]{2,1,0:T(8,128)(2,1)} %pad_maximum_fusion.8), calls=%async_computation.1 | async-start | bytes 1048576 | tf_op jit(solution)/shard_map/all_to_all | solution.py:591
  28.8 314.5 %all-gather.6.cloned.1.call-start = ((), (), s32[]{:S(2)}) async-start(), calls=%async_computation.4 | async-start | bytes 8454144 | tf_op jit(solution)/shard_map/all_gather | solution.py:607
  38.3 12.6 %collective-permute-start.5 = (bf16[128,2048]{1,0:T(8,128)(2,1)S(1)}, bf16[128,2048]{1,0:T(8,128)(2,1)S(1)}, u32[]{:S(2)}, u32[]{:S(2)}) collective-permute-start(bf16[128,2048]{1,0:T(8,128)(2,1)S(1)} %pad_maximum_fusion.7), channel_id=1, source_target_pairs={{0,24},{8,0},{16,8},{24,16},{1,25},{9,1},{17,9},{25,17},{2,26},{10... | collective-permute-start | bytes 1572872 | tf_op jit(solution)/shard_map/ppermute | solution.py:73
  39.1 13.8 %collective-permute-start.6 = (bf16[128,2048]{1,0:T(8,128)(2,1)S(1)}, bf16[128,2048]{1,0:T(8,128)(2,1)S(1)}, u32[]{:S(2)}, u32[]{:S(2)}) collective-permute-start(bf16[128,2048]{1,0:T(8,128)(2,1)S(1)} %pad_maximum_fusion.7), channel_id=1, source_target_pairs={{0,16},{8,24},{16,0},{24,8},{1,17},{9,25},{17,1},{25,9},{2,18},{10... | collective-permute-start | bytes 1572872 | tf_op jit(solution)/shard_map/ppermute | solution.py:73
  40.3 25.4 %collective-permute-start.7 = (bf16[128,2048]{1,0:T(8,128)(2,1)S(1)}, bf16[128,2048]{1,0:T(8,128)(2,1)S(1)}, u32[]{:S(2)}, u32[]{:S(2)}) collective-permute-start(bf16[128,2048]{1,0:T(8,128)(2,1)S(1)} %pad_maximum_fusion.7), channel_id=1, source_target_pairs={{0,8},{8,16},{16,24},{24,0},{1,9},{9,17},{17,25},{25,1},{2,10},{10... | collective-permute-start | bytes 1572872 | tf_op jit(solution)/shard_map/ppermute | solution.py:73
  42.2 23.6 %collective-permute-start.2 = (bf16[128,2048]{1,0:T(8,128)(2,1)S(1)}, bf16[128,2048]{1,0:T(8,128)(2,1)S(1)}, u32[]{:S(2)}, u32[]{:S(2)}) collective-permute-start(bf16[128,2048]{1,0:T(8,128)(2,1)S(1)} %copy-done.34), channel_id=1, source_target_pairs={{0,6},{2,0},{4,2},{6,4},{1,7},{3,1},{5,3},{7,5},{8,14},{10,8},{12,... | collective-permute-start | bytes 1572872 | tf_op jit(solution)/shard_map/ppermute | solution.py:73
  44.6 22.2 %collective-permute-start.3 = (bf16[128,2048]{1,0:T(8,128)(2,1)S(1)}, bf16[128,2048]{1,0:T(8,128)(2,1)S(1)}, u32[]{:S(2)}, u32[]{:S(2)}) collective-permute-start(bf16[128,2048]{1,0:T(8,128)(2,1)S(1)} %copy-done.34), channel_id=1, source_target_pairs={{0,4},{2,6},{4,0},{6,2},{1,5},{3,7},{5,1},{7,3},{8,12},{10,14},{12... | collective-permute-start | bytes 1572872 | tf_op jit(solution)/shard_map/ppermute | solution.py:73
  50.8 20.1 %collective-permute-start.4 = (bf16[128,2048]{1,0:T(8,128)(2,1)S(1)}, bf16[128,2048]{1,0:T(8,128)(2,1)S(1)}, u32[]{:S(2)}, u32[]{:S(2)}) collective-permute-start(bf16[128,2048]{1,0:T(8,128)(2,1)S(1)} %copy-done.34), channel_id=1, source_target_pairs={{0,2},{2,4},{4,6},{6,0},{1,3},{3,5},{5,7},{7,1},{8,10},{10,12},{12... | collective-permute-start | bytes 1572872 | tf_op jit(solution)/shard_map/ppermute | solution.py:73
  71.8 277.9 %all-gather.8.cloned.1.call-start = ((), (), s32[]{:S(2)}) async-start(), calls=%async_computation.7 | async-start | bytes 13369344 | tf_op jit(solution)/shard_map/all_gather | solution.py:611
  72.8 470.3 %reduce-scatter.3.cloned.1.call-start = ((), (), s32[]{:S(2)}) async-start(), calls=%async_computation.5 | async-start | bytes 3244032 | tf_op jit(solution)/shard_map/reduce_scatter | solution.py:667
  97.6 15.2 %collective-permute-start.11 = (bf16[4,128,512]{2,1,0:T(8,128)(2,1)S(1)}, bf16[4,128,512]{2,1,0:T(8,128)(2,1)S(1)}, u32[]{:S(2)}, u32[]{:S(2)}) collective-permute-start(bf16[4,128,512]{2,1,0:T(8,128)(2,1)S(1)} %bitcast_dynamic-update-slice_fusion.11), channel_id=1, source_target_pairs={{0,96},{32,0},{64,32},{96,64},{1,97},{33,1},{65,33},{97,65},{2,98}... | collective-permute-start | bytes 1572872 | tf_op jit(solution)/shard_map/ppermute | solution.py:73
  101.3 14.5 %collective-permute-start.12 = (bf16[4,128,512]{2,1,0:T(8,128)(2,1)S(1)}, bf16[4,128,512]{2,1,0:T(8,128)(2,1)S(1)}, u32[]{:S(2)}, u32[]{:S(2)}) collective-permute-start(bf16[4,128,512]{2,1,0:T(8,128)(2,1)S(1)} %bitcast_dynamic-update-slice_fusion.11), channel_id=1, source_target_pairs={{0,64},{32,96},{64,0},{96,32},{1,65},{33,97},{65,1},{97,33},{2,66}... | collective-permute-start | bytes 1572872 | tf_op jit(solution)/shard_map/ppermute | solution.py:73
  101.5 29.0 %collective-permute-start.13 = (bf16[4,128,512]{2,1,0:T(8,128)(2,1)S(1)}, bf16[4,128,512]{2,1,0:T(8,128)(2,1)S(1)}, u32[]{:S(2)}, u32[]{:S(2)}) collective-permute-start(bf16[4,128,512]{2,1,0:T(8,128)(2,1)S(1)} %bitcast_dynamic-update-slice_fusion.11), channel_id=1, source_target_pairs={{0,32},{32,64},{64,96},{96,0},{1,33},{33,65},{65,97},{97,1},{2,34}... | collective-permute-start | bytes 1572872 | tf_op jit(solution)/shard_map/ppermute | solution.py:73
  131.3 12.9 %collective-permute-start.14 = (bf16[2048,512]{1,0:T(8,128)(2,1)}, bf16[2048,512]{1,0:T(8,128)(2,1)}, u32[]{:S(2)}, u32[]{:S(2)}) collective-permute-start(bf16[2048,512]{1,0:T(8,128)(2,1)} %bitcast.29), channel_id=1, source_target_pairs={{0,1},{1,0},{2,3},{3,2},{4,5},{5,4},{6,7},{7,6},{8,9},{9,8},{10,11... | collective-permute-start | bytes 6291464 | tf_op jit(solution)/shard_map/ppermute | solution.py:69
  150.6 13.6 %collective-permute-start.15 = (bf16[512,512]{1,0:T(8,128)(2,1)S(1)}, bf16[512,512]{1,0:T(8,128)(2,1)S(1)}, u32[]{:S(2)}, u32[]{:S(2)}) collective-permute-start(bf16[512,512]{1,0:T(8,128)(2,1)S(1)} %get-tuple-element.163), channel_id=1, source_target_pairs={{0,24},{8,0},{16,8},{24,16},{1,25},{9,1},{17,9},{25,17},{2,26},{10... | collective-permute-start | bytes 1572872 | tf_op jit(solution)/shard_map/ppermute | solution.py:73
  152.1 15.2 %collective-permute-start.16 = (bf16[512,512]{1,0:T(8,128)(2,1)S(1)}, bf16[512,512]{1,0:T(8,128)(2,1)S(1)}, u32[]{:S(2)}, u32[]{:S(2)}) collective-permute-start(bf16[512,512]{1,0:T(8,128)(2,1)S(1)} %get-tuple-element.163), channel_id=1, source_target_pairs={{0,16},{8,24},{16,0},{24,8},{1,17},{9,25},{17,1},{25,9},{2,18},{10... | collective-permute-start | bytes 1572872 | tf_op jit(solution)/shard_map/ppermute | solution.py:73
  152.1 26.1 %collective-permute-start.17 = (bf16[512,512]{1,0:T(8,128)(2,1)S(1)}, bf16[512,512]{1,0:T(8,128)(2,1)S(1)}, u32[]{:S(2)}, u32[]{:S(2)}) collective-permute-start(bf16[512,512]{1,0:T(8,128)(2,1)S(1)} %get-tuple-element.163), channel_id=1, source_target_pairs={{0,8},{8,16},{16,24},{24,0},{1,9},{9,17},{17,25},{25,1},{2,10},{10... | collective-permute-start | bytes 1572872 | tf_op jit(solution)/shard_map/ppermute | solution.py:73
  179.8 79.1 %collective-permute-start.18 = (bf16[4,512,512]{2,1,0:T(8,128)(2,1)}, bf16[4,512,512]{2,1,0:T(8,128)(2,1)}, u32[]{:S(2)}, u32[]{:S(2)}) collective-permute-start(bf16[4,512,512]{2,1,0:T(8,128)(2,1)} %pad_maximum_fusion.1.refs_0_), channel_id=1, source_target_pairs={{0,32},{1,33},{32,0},{33,1},{64,96},{65,97},{96,64},{97,65},{2,34}... | collective-permute-start | bytes 6291464 | tf_op jit(solution)/shard_map/ppermute | solution.py:129
  179.8 129.9 %collective-permute-start.19 = (bf16[4,512,512]{2,1,0:T(8,128)(2,1)}, bf16[4,512,512]{2,1,0:T(8,128)(2,1)}, u32[]{:S(2)}, u32[]{:S(2)}) collective-permute-start(bf16[4,512,512]{2,1,0:T(8,128)(2,1)} %pad_maximum_fusion.1.refs_0_), channel_id=1, source_target_pairs={{1,64},{33,96},{3,66},{35,98},{5,68},{37,100},{7,70},{39,102},{9,7... | collective-permute-start | bytes 6291464 | tf_op jit(solution)/shard_map/ppermute | solution.py:128
  186.2 123.6 %collective-permute-start.20 = (bf16[4,512,512]{2,1,0:T(8,128)(2,1)}, bf16[4,512,512]{2,1,0:T(8,128)(2,1)}, u32[]{:S(2)}, u32[]{:S(2)}) collective-permute-start(bf16[4,512,512]{2,1,0:T(8,128)(2,1)} %pad_maximum_fusion.1.refs_0_), channel_id=1, source_target_pairs={{1,96},{33,64},{3,98},{35,66},{5,100},{37,68},{7,102},{39,70},{9,1... | collective-permute-start | bytes 6291464 | tf_op jit(solution)/shard_map/ppermute | solution.py:128
  188.8 121.0 %collective-permute-start.21 = (bf16[4,512,512]{2,1,0:T(8,128)(2,1)}, bf16[4,512,512]{2,1,0:T(8,128)(2,1)}, u32[]{:S(2)}, u32[]{:S(2)}) collective-permute-start(bf16[4,512,512]{2,1,0:T(8,128)(2,1)} %pad_maximum_fusion.1.refs_0_), channel_id=1, source_target_pairs={{0,1},{2,3},{4,5},{6,7},{8,9},{10,11},{12,13},{14,15},{16,17},{18,... | collective-permute-start | bytes 6291464 | tf_op jit(solution)/shard_map/ppermute | solution.py:130
  259.0 50.8 %collective-permute-start.22 = (bf16[4,512,512]{2,1,0:T(8,128)(2,1)}, bf16[4,512,512]{2,1,0:T(8,128)(2,1)}, u32[]{:S(2)}, u32[]{:S(2)}) collective-permute-start(bf16[4,512,512]{2,1,0:T(8,128)(2,1)} %collective-permute-done.18.refs_1_), channel_id=1, source_target_pairs={{0,1},{2,3},{4,5},{6,7},{8,9},{10,11},{12,13},{14,15},{16,17},{18,... | collective-permute-start | bytes 6291464 | tf_op jit(solution)/shard_map/ppermute | solution.py:130
  349.7 75.7 %collective-permute-start.29 = (bf16[16,192,2048]{2,1,0:T(8,128)(2,1)}, bf16[16,192,2048]{2,1,0:T(8,128)(2,1)}, u32[]{:S(2)}, u32[]{:S(2)}) collective-permute-start(bf16[16,192,2048]{2,1,0:T(8,128)(2,1)} %bitcast.332), channel_id=1, source_target_pairs={{0,1},{1,0},{2,3},{3,2},{4,5},{5,4},{6,7},{7,6},{8,9},{9,8},{10,11... | collective-permute-start | bytes 37748744 | tf_op jit(solution)/shard_map/ppermute | solution.py:69
  356.8 35.4 %collective-permute-start.26 = (bf16[128,2048]{1,0:T(8,128)(2,1)}, bf16[128,2048]{1,0:T(8,128)(2,1)S(1)}, u32[]{:S(2)}, u32[]{:S(2)}) collective-permute-start(bf16[128,2048]{1,0:T(8,128)(2,1)} %multiply_convert_fusion.1), channel_id=1, source_target_pairs={{0,24},{8,0},{16,8},{24,16},{1,25},{9,1},{17,9},{25,17},{2,26},{10... | collective-permute-start | bytes 1572872 | tf_op jit(solution)/shard_map/ppermute | solution.py:73
  369.7 22.6 %collective-permute-start.27 = (bf16[128,2048]{1,0:T(8,128)(2,1)}, bf16[128,2048]{1,0:T(8,128)(2,1)S(1)}, u32[]{:S(2)}, u32[]{:S(2)}) collective-permute-start(bf16[128,2048]{1,0:T(8,128)(2,1)} %multiply_convert_fusion.1), channel_id=1, source_target_pairs={{0,16},{8,24},{16,0},{24,8},{1,17},{9,25},{17,1},{25,9},{2,18},{10... | collective-permute-start | bytes 1572872 | tf_op jit(solution)/shard_map/ppermute | solution.py:73
  369.7 26.2 %collective-permute-start.28 = (bf16[128,2048]{1,0:T(8,128)(2,1)}, bf16[128,2048]{1,0:T(8,128)(2,1)S(1)}, u32[]{:S(2)}, u32[]{:S(2)}) collective-permute-start(bf16[128,2048]{1,0:T(8,128)(2,1)} %multiply_convert_fusion.1), channel_id=1, source_target_pairs={{0,8},{8,16},{16,24},{24,0},{1,9},{9,17},{17,25},{25,1},{2,10},{10... | collective-permute-start | bytes 1572872 | tf_op jit(solution)/shard_map/ppermute | solution.py:73
  459.1 235.5 %reduce-scatter.5.cloned.1.call-start = ((), (), s32[]{:S(2)}) async-start(), calls=%async_computation.6 | async-start | bytes 1351680 | tf_op jit(solution)/shard_map/reduce_scatter | solution.py:741
  461.9 16.6 %collective-permute-start.30 = (bf16[128,2432]{1,0:T(8,128)(2,1)}, bf16[128,2432]{1,0:T(8,128)(2,1)}, u32[]{:S(2)}, u32[]{:S(2)}) collective-permute-start(bf16[128,2432]{1,0:T(8,128)(2,1)} %get-tuple-element.114), channel_id=1, source_target_pairs={{0,16},{8,24},{16,0},{24,8},{1,17},{9,25},{17,1},{25,9},{2,18},{10... | collective-permute-start | bytes 1867784 | tf_op jit(solution)/shard_map/ppermute | solution.py:73
  462.6 30.5 %collective-permute-start.31 = (bf16[128,2432]{1,0:T(8,128)(2,1)}, bf16[128,2432]{1,0:T(8,128)(2,1)}, u32[]{:S(2)}, u32[]{:S(2)}) collective-permute-start(bf16[128,2432]{1,0:T(8,128)(2,1)} %get-tuple-element.116), channel_id=1, source_target_pairs={{0,8},{8,16},{16,24},{24,0},{1,9},{9,17},{17,25},{25,1},{2,10},{10... | collective-permute-start | bytes 1867784 | tf_op jit(solution)/shard_map/ppermute | solution.py:73
  462.6 30.5 %collective-permute-start.32 = (bf16[128,2432]{1,0:T(8,128)(2,1)}, bf16[128,2432]{1,0:T(8,128)(2,1)}, u32[]{:S(2)}, u32[]{:S(2)}) collective-permute-start(bf16[128,2432]{1,0:T(8,128)(2,1)} %get-tuple-element.115), channel_id=1, source_target_pairs={{0,24},{8,0},{16,8},{24,16},{1,25},{9,1},{17,9},{25,17},{2,26},{10... | collective-permute-start | bytes 1867784 | tf_op jit(solution)/shard_map/ppermute | solution.py:73
  502.5 42.5 %collective-permute-start.33 = (bf16[128,512]{1,0:T(8,128)(2,1)S(1)}, bf16[128,512]{1,0:T(8,128)(2,1)S(1)}, u32[]{:S(2)}, u32[]{:S(2)}) collective-permute-start(bf16[128,512]{1,0:T(8,128)(2,1)S(1)} %get-tuple-element.158), channel_id=1, source_target_pairs={{0,6},{2,0},{4,2},{6,4},{1,7},{3,1},{5,3},{7,5},{8,14},{10,8},{12,... | collective-permute-start | bytes 393224 | tf_op jit(solution)/shard_map/ppermute | solution.py:73
  503.9 41.1 %collective-permute-start.34 = (bf16[128,512]{1,0:T(8,128)(2,1)S(1)}, bf16[128,512]{1,0:T(8,128)(2,1)S(1)}, u32[]{:S(2)}, u32[]{:S(2)}) collective-permute-start(bf16[128,512]{1,0:T(8,128)(2,1)S(1)} %get-tuple-element.157), channel_id=1, source_target_pairs={{0,4},{2,6},{4,0},{6,2},{1,5},{3,7},{5,1},{7,3},{8,12},{10,14},{12... | collective-permute-start | bytes 393224 | tf_op jit(solution)/shard_map/ppermute | solution.py:73
  504.0 41.1 %collective-permute-start.35 = (bf16[128,512]{1,0:T(8,128)(2,1)S(1)}, bf16[128,512]{1,0:T(8,128)(2,1)S(1)}, u32[]{:S(2)}, u32[]{:S(2)}) collective-permute-start(bf16[128,512]{1,0:T(8,128)(2,1)S(1)} %get-tuple-element.156), channel_id=1, source_target_pairs={{0,2},{2,4},{4,6},{6,0},{1,3},{3,5},{5,7},{7,1},{8,10},{10,12},{12... | collective-permute-start | bytes 393224 | tf_op jit(solution)/shard_map/ppermute | solution.py:73
  569.7 32.1 %collective-permute-start.37 = (bf16[4,512,512]{2,1,0:T(8,128)(2,1)}, bf16[4,512,512]{2,1,0:T(8,128)(2,1)}, u32[]{:S(2)}, u32[]{:S(2)}) collective-permute-start(bf16[4,512,512]{2,1,0:T(8,128)(2,1)} %get-tuple-element.84), channel_id=1, source_target_pairs={{1,0},{3,2},{5,4},{7,6},{9,8},{11,10},{13,12},{15,14},{17,16},{19,... | collective-permute-start | bytes 6291464 | tf_op jit(solution)/shard_map/ppermute | solution.py:135
  580.1 13.2 %collective-permute-start.77 = (bf16[128,384]{1,0:T(8,128)(2,1)S(1)}, bf16[128,384]{1,0:T(8,128)(2,1)S(1)}, u32[]{:S(2)}, u32[]{:S(2)}) collective-permute-start(bf16[128,384]{1,0:T(8,128)(2,1)S(1)} %pad_maximum_fusion.16), channel_id=1, source_target_pairs={{0,24},{8,0},{16,8},{24,16},{1,25},{9,1},{17,9},{25,17},{2,26},{10... | collective-permute-start | bytes 294920 | tf_op jit(solution)/shard_map/ppermute | solution.py:73
  590.5 24.0 %collective-permute-start.36 = (bf16[4,512,512]{2,1,0:T(8,128)(2,1)}, bf16[4,512,512]{2,1,0:T(8,128)(2,1)}, u32[]{:S(2)}, u32[]{:S(2)}) collective-permute-start(bf16[4,512,512]{2,1,0:T(8,128)(2,1)} %get-tuple-element.82), channel_id=1, source_target_pairs={{1,0},{3,2},{5,4},{7,6},{9,8},{11,10},{13,12},{15,14},{17,16},{19,... | collective-permute-start | bytes 6291464 | tf_op jit(solution)/shard_map/ppermute | solution.py:135
  593.3 35.3 %collective-permute-start.39 = (bf16[4,512,512]{2,1,0:T(8,128)(2,1)}, bf16[4,512,512]{2,1,0:T(8,128)(2,1)}, u32[]{:S(2)}, u32[]{:S(2)}) collective-permute-start(bf16[4,512,512]{2,1,0:T(8,128)(2,1)} %get-tuple-element.82), channel_id=1, source_target_pairs={{64,1},{96,33},{66,3},{98,35},{68,5},{100,37},{70,7},{102,39},{72,... | collective-permute-start | bytes 6291464 | tf_op jit(solution)/shard_map/ppermute | solution.py:136
  595.1 12.4 %collective-permute-start.74 = (bf16[512,256]{0,1:T(8,128)(2,1)S(1)}, bf16[512,256]{0,1:T(8,128)(2,1)S(1)}, u32[]{:S(2)}, u32[]{:S(2)}) collective-permute-start(bf16[512,256]{0,1:T(8,128)(2,1)S(1)} %get-tuple-element.132), channel_id=1, source_target_pairs={{0,16},{8,24},{16,0},{24,8},{1,17},{9,25},{17,1},{25,9},{2,18},{10... | collective-permute-start | bytes 786440 | tf_op jit(solution)/shard_map/ppermute | solution.py:73
  597.2 12.3 %collective-permute-start.75 = (bf16[512,256]{0,1:T(8,128)(2,1)S(1)}, bf16[512,256]{0,1:T(8,128)(2,1)S(1)}, u32[]{:S(2)}, u32[]{:S(2)}) collective-permute-start(bf16[512,256]{0,1:T(8,128)(2,1)S(1)} %get-tuple-element.134), channel_id=1, source_target_pairs={{0,8},{8,16},{16,24},{24,0},{1,9},{9,17},{17,25},{25,1},{2,10},{10... | collective-permute-start | bytes 786440 | tf_op jit(solution)/shard_map/ppermute | solution.py:73
  607.5 38.1 %collective-permute-start.40 = (bf16[4,512,512]{2,1,0:T(8,128)(2,1)}, bf16[4,512,512]{2,1,0:T(8,128)(2,1)}, u32[]{:S(2)}, u32[]{:S(2)}) collective-permute-start(bf16[4,512,512]{2,1,0:T(8,128)(2,1)} %get-tuple-element.84), channel_id=1, source_target_pairs={{96,1},{64,33},{98,3},{66,35},{100,5},{68,37},{102,7},{70,39},{104... | collective-permute-start | bytes 6291464 | tf_op jit(solution)/shard_map/ppermute | solution.py:136
  609.5 47.1 %collective-permute-start.38 = (bf16[4,512,512]{2,1,0:T(8,128)(2,1)}, bf16[4,512,512]{2,1,0:T(8,128)(2,1)}, u32[]{:S(2)}, u32[]{:S(2)}) collective-permute-start(bf16[4,512,512]{2,1,0:T(8,128)(2,1)} %add_convert_fusion.1), channel_id=1, source_target_pairs={{0,32},{1,33},{32,0},{33,1},{64,96},{65,97},{96,64},{97,65},{2,34}... | collective-permute-start | bytes 6291464 | tf_op jit(solution)/shard_map/ppermute | solution.py:138
  614.4 244.0 %all-gather.10.cloned.1.call-start = ((), (), s32[]{:S(2)}) async-start(), calls=%async_computation.8 | async-start | bytes 8982528 | tf_op jit(solution)/shard_map/all_gather | solution.py:744
  665.5 30.6 %collective-permute-start.41 = (bf16[512,512]{1,0:T(8,128)(2,1)}, bf16[512,512]{1,0:T(8,128)(2,1)S(1)}, u32[]{:S(2)}, u32[]{:S(2)}) collective-permute-start(bf16[512,512]{1,0:T(8,128)(2,1)} %get-tuple-element.123), channel_id=1, source_target_pairs={{0,16},{8,24},{16,0},{24,8},{1,17},{9,25},{17,1},{25,9},{2,18},{10... | collective-permute-start | bytes 1572872 | tf_op jit(solution)/shard_map/ppermute | solution.py:73
  666.3 29.8 %collective-permute-start.42 = (bf16[512,512]{1,0:T(8,128)(2,1)}, bf16[512,512]{1,0:T(8,128)(2,1)}, u32[]{:S(2)}, u32[]{:S(2)}) collective-permute-start(bf16[512,512]{1,0:T(8,128)(2,1)} %get-tuple-element.125), channel_id=1, source_target_pairs={{0,8},{8,16},{16,24},{24,0},{1,9},{9,17},{17,25},{25,1},{2,10},{10... | collective-permute-start | bytes 1572872 | tf_op jit(solution)/shard_map/ppermute | solution.py:73
  667.2 28.9 %collective-permute-start.43 = (bf16[512,512]{1,0:T(8,128)(2,1)}, bf16[512,512]{1,0:T(8,128)(2,1)}, u32[]{:S(2)}, u32[]{:S(2)}) collective-permute-start(bf16[512,512]{1,0:T(8,128)(2,1)} %get-tuple-element.124), channel_id=1, source_target_pairs={{0,24},{8,0},{16,8},{24,16},{1,25},{9,1},{17,9},{25,17},{2,26},{10... | collective-permute-start | bytes 1572872 | tf_op jit(solution)/shard_map/ppermute | solution.py:73
  713.8 14.4 %collective-permute-start.47 = (bf16[128,384]{0,1:T(8,128)(2,1)}, bf16[128,384]{0,1:T(8,128)(2,1)}, u32[]{:S(2)}, u32[]{:S(2)}) collective-permute-start(bf16[128,384]{0,1:T(8,128)(2,1)} %get-tuple-element.170), channel_id=1, source_target_pairs={{0,4},{2,6},{4,0},{6,2},{1,5},{3,7},{5,1},{7,3},{8,12},{10,14},{12... | collective-permute-start | bytes 294920 | tf_op jit(solution)/shard_map/ppermute | solution.py:73
  716.1 12.1 %collective-permute-start.48 = (bf16[128,384]{0,1:T(8,128)(2,1)}, bf16[128,384]{0,1:T(8,128)(2,1)}, u32[]{:S(2)}, u32[]{:S(2)}) collective-permute-start(bf16[128,384]{0,1:T(8,128)(2,1)} %get-tuple-element.172), channel_id=1, source_target_pairs={{0,2},{2,4},{4,6},{6,0},{1,3},{3,5},{5,7},{7,1},{8,10},{10,12},{12... | collective-permute-start | bytes 294920 | tf_op jit(solution)/shard_map/ppermute | solution.py:73
  716.4 11.8 %collective-permute-start.49 = (bf16[128,384]{0,1:T(8,128)(2,1)}, bf16[128,384]{0,1:T(8,128)(2,1)}, u32[]{:S(2)}, u32[]{:S(2)}) collective-permute-start(bf16[128,384]{0,1:T(8,128)(2,1)} %get-tuple-element.171), channel_id=1, source_target_pairs={{0,6},{2,0},{4,2},{6,4},{1,7},{3,1},{5,3},{7,5},{8,14},{10,8},{12,... | collective-permute-start | bytes 294920 | tf_op jit(solution)/shard_map/ppermute | solution.py:73
  744.1 20.3 %collective-permute-start.44 = (bf16[128,2048]{1,0:T(8,128)(2,1)}, bf16[128,2048]{1,0:T(8,128)(2,1)}, u32[]{:S(2)}, u32[]{:S(2)}) collective-permute-start(bf16[128,2048]{1,0:T(8,128)(2,1)} %get-tuple-element.120), channel_id=1, source_target_pairs={{0,4},{2,6},{4,0},{6,2},{1,5},{3,7},{5,1},{7,3},{8,12},{10,14},{12... | collective-permute-start | bytes 1572872 | tf_op jit(solution)/shard_map/ppermute | solution.py:73
  745.1 37.0 %collective-permute-start.45 = (bf16[128,2048]{1,0:T(8,128)(2,1)S(1)}, bf16[128,2048]{1,0:T(8,128)(2,1)}, u32[]{:S(2)}, u32[]{:S(2)}) collective-permute-start(bf16[128,2048]{1,0:T(8,128)(2,1)S(1)} %get-tuple-element.122), channel_id=1, source_target_pairs={{0,2},{2,4},{4,6},{6,0},{1,3},{3,5},{5,7},{7,1},{8,10},{10,12},{12... | collective-permute-start | bytes 1572872 | tf_op jit(solution)/shard_map/ppermute | solution.py:73
  745.7 36.5 %collective-permute-start.46 = (bf16[128,2048]{1,0:T(8,128)(2,1)S(1)}, bf16[128,2048]{1,0:T(8,128)(2,1)}, u32[]{:S(2)}, u32[]{:S(2)}) collective-permute-start(bf16[128,2048]{1,0:T(8,128)(2,1)S(1)} %get-tuple-element.121), channel_id=1, source_target_pairs={{0,6},{2,0},{4,2},{6,4},{1,7},{3,1},{5,3},{7,5},{8,14},{10,8},{12,... | collective-permute-start | bytes 1572872 | tf_op jit(solution)/shard_map/ppermute | solution.py:73
  749.1 35.3 %collective-permute-start.59 = (bf16[4,80,128]{2,1,0:T(8,128)(2,1)S(1)}, bf16[4,80,128]{2,1,0:T(8,128)(2,1)S(1)}, u32[]{:S(2)}, u32[]{:S(2)}) collective-permute-start(bf16[4,80,128]{2,1,0:T(8,128)(2,1)S(1)} %get-tuple-element.142), channel_id=1, source_target_pairs={{0,32},{32,64},{64,96},{96,0},{1,33},{33,65},{65,97},{97,1},{2,34}... | collective-permute-start | bytes 245768 | tf_op jit(solution)/shard_map/ppermute | solution.py:73
  749.2 35.3 %collective-permute-start.60 = (bf16[4,80,128]{2,1,0:T(8,128)(2,1)S(1)}, bf16[4,80,128]{2,1,0:T(8,128)(2,1)S(1)}, u32[]{:S(2)}, u32[]{:S(2)}) collective-permute-start(bf16[4,80,128]{2,1,0:T(8,128)(2,1)S(1)} %get-tuple-element.144), channel_id=1, source_target_pairs={{0,64},{32,96},{64,0},{96,32},{1,65},{33,97},{65,1},{97,33},{2,66}... | collective-permute-start | bytes 245768 | tf_op jit(solution)/shard_map/ppermute | solution.py:73
  764.4 20.0 %collective-permute-start.61 = (bf16[4,80,128]{2,1,0:T(8,128)(2,1)S(1)}, bf16[4,80,128]{2,1,0:T(8,128)(2,1)S(1)}, u32[]{:S(2)}, u32[]{:S(2)}) collective-permute-start(bf16[4,80,128]{2,1,0:T(8,128)(2,1)S(1)} %get-tuple-element.143), channel_id=1, source_target_pairs={{0,96},{32,0},{64,32},{96,64},{1,97},{33,1},{65,33},{97,65},{2,98}... | collective-permute-start | bytes 245768 | tf_op jit(solution)/shard_map/ppermute | solution.py:73
  793.4 60.4 %collective-permute-start.50 = (bf16[128,2048]{1,0:T(8,128)(2,1)S(1)}, bf16[128,2048]{1,0:T(8,128)(2,1)S(1)}, u32[]{:S(2)}, u32[]{:S(2)}) collective-permute-start(bf16[128,2048]{1,0:T(8,128)(2,1)S(1)} %get-tuple-element.117), channel_id=1, source_target_pairs={{0,16},{8,24},{16,0},{24,8},{1,17},{9,25},{17,1},{25,9},{2,18},{10... | collective-permute-start | bytes 1572872 | tf_op jit(solution)/shard_map/ppermute | solution.py:73
  793.4 60.4 %collective-permute-start.51 = (bf16[128,2048]{1,0:T(8,128)(2,1)S(1)}, bf16[128,2048]{1,0:T(8,128)(2,1)S(1)}, u32[]{:S(2)}, u32[]{:S(2)}) collective-permute-start(bf16[128,2048]{1,0:T(8,128)(2,1)S(1)} %get-tuple-element.119), channel_id=1, source_target_pairs={{0,8},{8,16},{16,24},{24,0},{1,9},{9,17},{17,25},{25,1},{2,10},{10... | collective-permute-start | bytes 1572872 | tf_op jit(solution)/shard_map/ppermute | solution.py:73
  794.0 59.7 %collective-permute-start.52 = (bf16[128,2048]{1,0:T(8,128)(2,1)S(1)}, bf16[128,2048]{1,0:T(8,128)(2,1)S(1)}, u32[]{:S(2)}, u32[]{:S(2)}) collective-permute-start(bf16[128,2048]{1,0:T(8,128)(2,1)S(1)} %get-tuple-element.118), channel_id=1, source_target_pairs={{0,24},{8,0},{16,8},{24,16},{1,25},{9,1},{17,9},{25,17},{2,26},{10... | collective-permute-start | bytes 1572872 | tf_op jit(solution)/shard_map/ppermute | solution.py:73
  796.1 21.1 %collective-permute-start.66 = (bf16[80,128]{1,0:T(8,128)(2,1)S(1)}, bf16[80,128]{1,0:T(8,128)(2,1)S(1)}, u32[]{:S(2)}, u32[]{:S(2)}) collective-permute-start(bf16[80,128]{1,0:T(8,128)(2,1)S(1)} %get-tuple-element.107), channel_id=1, source_target_pairs={{0,16},{8,24},{16,0},{24,8},{1,17},{9,25},{17,1},{25,9},{2,18},{10... | collective-permute-start | bytes 61448 | tf_op jit(solution)/shard_map/ppermute | solution.py:73
  797.8 22.2 %collective-permute-start.67 = (bf16[80,128]{1,0:T(8,128)(2,1)S(1)}, bf16[80,128]{1,0:T(8,128)(2,1)S(1)}, u32[]{:S(2)}, u32[]{:S(2)}) collective-permute-start(bf16[80,128]{1,0:T(8,128)(2,1)S(1)} %get-tuple-element.107), channel_id=1, source_target_pairs={{0,8},{8,16},{16,24},{24,0},{1,9},{9,17},{17,25},{25,1},{2,10},{10... | collective-permute-start | bytes 61448 | tf_op jit(solution)/shard_map/ppermute | solution.py:73
  835.3 9.6 %collective-permute-start.73 = (bf16[4,4,80,128]{3,2,1,0:T(8,128)(2,1)S(1)}, bf16[4,4,80,128]{3,2,1,0:T(8,128)(2,1)S(1)}, u32[]{:S(2)}, u32[]{:S(2)}) collective-permute-start(bf16[4,4,80,128]{3,2,1,0:T(8,128)(2,1)S(1)} %bitcast_dynamic-update-slice_fusion.15), channel_id=1, source_target_pairs={{0,2},{2,4},{4,6},{6,0},{1,3},{3,5},{5,7},{7,1},{8,10},{10,12},{12... | collective-permute-start | bytes 983048 | tf_op jit(solution)/shard_map/ppermute | solution.py:73
  845.0 28.0 %collective-permute-start.80 = (bf16[4,16,80,128]{3,2,1,0:T(8,128)(2,1)S(1)}, bf16[4,16,80,128]{3,2,1,0:T(8,128)(2,1)}, u32[]{:S(2)}, u32[]{:S(2)}) collective-permute-start(bf16[4,16,80,128]{3,2,1,0:T(8,128)(2,1)S(1)} %bitcast.271), channel_id=1, source_target_pairs={{0,1},{1,0},{2,3},{3,2},{4,5},{5,4},{6,7},{7,6},{8,9},{9,8},{10,11... | collective-permute-start | bytes 3932168 | tf_op jit(solution)/shard_map/ppermute | solution.py:69
  (102 other events, 1686.7 us)
Sparse Core Ops, SparseCore 0:
  71.9 83.2 all-gather.5
  157.9 147.3 all-gather.7
  459.2 83.8 reduce-scatter.2
  614.6 80.0 reduce-scatter.4
  698.8 85.5 all-gather.9
where the time goes:
time: 898 us; the launch traced here: 886 us
  waiting for transfers between devices  433 us (48%)
  starting transfers between devices  134 us (15%)
  Pallas kernels  116 us (13%)
  local copies, waits for them, and re-layouts  77.2 us (9%)
  matrix products  57 us (6%)
  other arithmetic  52.7 us (6%)
  between operations  16.8 us (2%)
    ppermute x63, waiting for transfers between devices, shift(): lax.ppermute(value, RING[ring], [(i, (i + step) % 4) for i in range(4)])  212 us
    ppermute x63, starting transfers between devices, shift(): lax.ppermute(value, RING[ring], [(i, (i + step) % 4) for i in range(4)])  86.4 us
    ppermute x1, waiting for transfers between devices, gather_row(): partner = lax.ppermute(line, CORNER, PARTNER)  68.9 us
    pallas_call x2, Pallas kernels, ffn_part(): pl.pallas_call(partial(ffn_kernel, last), grid=(UNITS // CHUNK,), in_spec...  55 us
    reduce_scatter x1, waiting for transfers between devices, reduce_units(): lax.psum_scatter(unit_terms, OVER_X, scatter_dimension=0, tiled=False)  38.5 us
    ppermute x2, waiting for transfers between devices, gather_row(): ahead = [lax.ppermute(line, CORNER, pairs) for pairs in LATER]  37.1 us
    ppermute x2, waiting for transfers between devices, sum_row(): lax.ppermute(value, CORNER, pairs)  31.1 us
    dot_general x11, matrix products, product(): return jnp.dot(left, right, preferred_element_type=f32)  27 us
  transfers between devices with their start and end apart: 88, of which 45 were waited for; matrix products, arithmetic and copies ran while one was open for 19% of the time, Pallas kernels for 7%

commit v1 on v0

--- a/solution.py
+++ b/solution.py
@@ -251,13 +251,29 @@
     return pl.BlockSpec((1, GROUP, GROUP), lambda i, active: (jnp.clip(i - 4 * tile, 0, 3), 0, 0))
 
 
+def active_spec(tile, table):
+    return pl.BlockSpec(
+        (1, GROUP, GROUP), lambda i, active: (active[16 * table + 4 * tile + jnp.clip(i - 4 * tile, 0, 3)], 0, 0)
+    )
+
+
+def step_tables(active, c):
+    marks = active.reshape(4, 4)
+    at = jnp.arange(4, dtype=jnp.int32)
+    seen = jnp.where((marks[:, None, :] != 0) & (at[None, None, :] <= at[None, :, None]), at[None, None, :], -1)
+    last = jnp.max(seen, axis=2)
+    first = jnp.min(jnp.where(marks != 0, at[None, :], 3), axis=1, keepdims=True)
+    blocks = jnp.where(last >= 0, last, first).reshape(16).astype(jnp.int32)
+    return jnp.concatenate([active, blocks, jnp.where(c == 0, blocks, 0), jnp.where(c == 0, 0, blocks)])
+
+
 def common_specs():
     return [
         whole((GROUP, GROUP)),
         whole((GROUP, 1)),
         whole((GROUP, 1)),
         pl.BlockSpec((1, 1, GROUP), lambda i, active: (i, 0, 0)),
-    ] + [line_spec(tile) for tile in (2, 3, 0, 1, 0, 1)]
+    ] + [active_spec(tile, table) for tile, table in ((2, 1), (3, 1), (0, 2), (1, 2), (0, 3), (1, 3))]
 
 
 def attend(active, *operands):
@@ -311,11 +327,30 @@
 CHUNK = 256
 
 
-def ffn_kernel(last, nm_ref, cot_ref, lgu_ref, gld_ref, wg_ref, wu_ref, wd_ref, ge_ref, ue_ref, ds_ref, perm_ref, *refs):
-    if last:
-        result_in, grad_in, low_in, glow_in = refs[:4]
-        refs = refs[4:]
-    result_ref, grad_ref, low_ref, glow_ref, gge_ref, gue_ref, gds_ref, nmp, result, grad = refs
+def ffn_kernel(
+    at,
+    nm_ref,
+    cot_ref,
+    lgu_ref,
+    gld_ref,
+    wg_ref,
+    wu_ref,
+    wd_ref,
+    ge_ref,
+    ue_ref,
+    ds_ref,
+    perm_ref,
+    pick_ref,
+    result_ref,
+    back_ref,
+    gge_ref,
+    gue_ref,
+    gds_ref,
+    nmp,
+    result,
+    grad,
+    low,
+):
     step = pl.program_id(0)
     rank = ds_ref.shape[1]
 
@@ -324,91 +359,81 @@
         for zone in range(4):
             cols = slice(zone * GROUP, (zone + 1) * GROUP)
             nmp[:, cols] = product(nm_ref[:, cols], perm_ref[...]).astype(bf16)
-        if last:
-            result[...] = result_in[...]
-            grad[...] = grad_in[...]
-            low_ref[...] = low_in[...]
-            glow_ref[...] = glow_in[...]
-        else:
-            result[...] = jnp.zeros(result.shape, f32)
-            grad[...] = jnp.zeros(grad.shape, f32)
-            low_ref[...] = jnp.zeros(low_ref.shape, f32)
-            glow_ref[...] = jnp.zeros(glow_ref.shape, f32)
+        result[...] = jnp.zeros(result.shape, f32)
+        grad[...] = jnp.zeros(grad.shape, f32)
+        low[...] = jnp.zeros(low.shape, f32)
 
     wg, wu = wg_ref[...].reshape(2048, CHUNK), wu_ref[...].reshape(2048, CHUNK)
     wd = wd_ref[...].reshape(CHUNK, 2048)
+    ge, ue = product(ge_ref[...], pick_ref[0]).astype(bf16), product(ue_ref[...], pick_ref[0]).astype(bf16)
+    ds = inner_rows(pick_ref[0], ds_ref[...]).astype(bf16)
     low_gate, low_up = lgu_ref[:, :rank], lgu_ref[:, rank:]
-    gate_pre = product(nmp[...], wg) + product(low_gate, ge_ref[...])
-    up_pre = product(nmp[...], wu) + product(low_up, ue_ref[...])
+    gate_pre = product(nmp[...], wg) + product(low_gate, ge)
+    up_pre = product(nmp[...], wu) + product(low_up, ue)
     sigmoid_g = jax.nn.sigmoid(gate_pre)
     silu_gate = gate_pre * sigmoid_g
     active_units = (silu_gate * up_pre).astype(bf16)
-    grad_active = times_transposed(cot_ref[...], wd) + times_transposed(gld_ref[...], ds_ref[...])
+    grad_active = times_transposed(cot_ref[...], wd) + times_transposed(gld_ref[...], ds)
     grad_gate = (grad_active * up_pre * sigmoid_g * (1.0 + gate_pre * (1.0 - sigmoid_g))).astype(bf16)
     grad_up = (grad_active * silu_gate).astype(bf16)
     result[...] += product(active_units, wd)
-    low_ref[...] += product(active_units, ds_ref[...])
     grad[...] += times_transposed(grad_gate, wg) + times_transposed(grad_up, wu)
-    glow_ref[:, :rank] += times_transposed(grad_gate, ge_ref[...])
-    glow_ref[:, rank:] += times_transposed(grad_up, ue_ref[...])
-    gge_ref[...] = inner_rows(grad_gate, low_gate)
-    gue_ref[...] = inner_rows(grad_up, low_up)
-    gds_ref[...] = inner_rows(active_units, gld_ref[...])
-
-    @pl.when(step == UNITS // CHUNK - 1)
-    def _():
-        if last:
-            result_ref[...] = result[...].astype(bf16)
-            for zone in range(4):
-                cols = slice(zone * GROUP, (zone + 1) * GROUP)
-                grad_ref[:, cols] = product(grad[:, cols].astype(bf16), perm_ref[...]).astype(bf16)
-            grad_ref[:, 2048 : 2048 + 2 * rank] = glow_ref[...].astype(bf16)
-            grad_ref[:, 2048 + 2 * rank :] = low_ref[...].astype(bf16)
-        else:
-            result_ref[...] = result[...]
-            grad_ref[...] = grad[...]
-
-
-def ffn_part(normed_mid, cot, low_gu, grad_low_down, weights, expands, perm, sums=None):
-    last = sums is not None
+    low[:, :rank] += times_transposed(grad_gate, ge)
+    low[:, rank : 2 * rank] += times_transposed(grad_up, ue)
+    low[:, 2 * rank :] += product(active_units, ds)
+    gge_ref[0] = inner_rows(grad_gate, low_gate)
+    gue_ref[0] = inner_rows(grad_up, low_up)
+    gds_ref[0] = inner_rows(active_units, gld_ref[...])
+
+    @pl.when(step == 2 * UNITS // CHUNK - 1)
+    def _():
+        result_ref[...] = result[...].astype(bf16)
+        for zone in range(4):
+            cols = slice(zone * GROUP, (zone + 1) * GROUP)
+            back_ref[:, cols] = product(grad[:, cols].astype(bf16), perm_ref[...]).astype(bf16)
+        back_ref[:, 2048:] = low[...].astype(bf16)
+
+
+def feed_forward(at, normed_mid, cot, low_gu, grad_low_down, weights, expands, perm, picks):
     rank = low_gu.shape[1] // 2
-    wide = bf16 if last else f32
-    grad_width = 2048 + 3 * rank if last else 2048
-    weight_specs = [
-        pl.BlockSpec((16, 128, CHUNK), lambda u: (0, 0, u)),
-        pl.BlockSpec((16, 128, CHUNK), lambda u: (0, 0, UNITS // CHUNK + u)),
-        pl.BlockSpec((4, 64, 2048), lambda u: (u, 2, 0)),
-        pl.BlockSpec((rank, CHUNK), lambda u: (0, u)),
-        pl.BlockSpec((rank, CHUNK), lambda u: (0, u)),
-        pl.BlockSpec((CHUNK, rank), lambda u: (u, 0)),
-    ]
-    sum_specs = [whole((GROUP, 2048)), whole((GROUP, 2048)), whole((GROUP, rank)), whole((GROUP, 2 * rank))]
+    steps = UNITS // CHUNK
+    unit_spec = pl.BlockSpec((1, CHUNK, rank), lambda i, at: (i // steps, i % steps, 0))
     return pl.pallas_call(
-        partial(ffn_kernel, last),
-        grid=(UNITS // CHUNK,),
-        in_specs=[whole((GROUP, 2048)), whole((GROUP, 2048)), whole((GROUP, 2 * rank)), whole((GROUP, rank))]
-        + weight_specs
-        + [whole((GROUP, GROUP))]
-        + (sum_specs if last else []),
-        out_specs=[whole((GROUP, 2048)), whole((GROUP, grad_width))]
-        + sum_specs[2:]
-        + [pl.BlockSpec((CHUNK, rank), lambda u: (u, 0))] * 3,
+        ffn_kernel,
+        grid_spec=pltpu.PrefetchScalarGridSpec(
+            num_scalar_prefetch=1,
+            grid=(2 * steps,),
+            in_specs=[
+                whole((GROUP, 2048)),
+                whole((GROUP, 2048)),
+                whole((GROUP, 2 * rank)),
+                whole((GROUP, rank)),
+                pl.BlockSpec((16, 1, 128, CHUNK), lambda i, at: (0, i // steps, 0, i % steps)),
+                pl.BlockSpec((16, 1, 128, CHUNK), lambda i, at: (0, i // steps, 0, steps + i % steps)),
+                pl.BlockSpec((4, 1, 64, 2048), lambda i, at: (i % steps, i // steps, 2, 0)),
+                pl.BlockSpec((rank, 2 * CHUNK), lambda i, at: (0, 4 * (i % steps) + at[0])),
+                pl.BlockSpec((rank, 2 * CHUNK), lambda i, at: (0, 4 * (i % steps) + at[0])),
+                pl.BlockSpec((2 * CHUNK, rank), lambda i, at: (4 * (i % steps) + at[0], 0)),
+                whole((GROUP, GROUP)),
+                pl.BlockSpec((1, 2 * CHUNK, CHUNK), lambda i, at: (i // steps, 0, 0)),
+            ],
+            out_specs=[whole((GROUP, 2048)), whole((GROUP, 2048 + 3 * rank)), unit_spec, unit_spec, unit_spec],
+            scratch_shapes=[
+                pltpu.VMEM((GROUP, 2048), bf16),
+                pltpu.VMEM((GROUP, 2048), f32),
+                pltpu.VMEM((GROUP, 2048), f32),
+                pltpu.VMEM((GROUP, 3 * rank), f32),
+            ],
+        ),
         out_shape=[
-            jax.ShapeDtypeStruct((GROUP, 2048), wide),
-            jax.ShapeDtypeStruct((GROUP, grad_width), wide),
-            jax.ShapeDtypeStruct((GROUP, rank), f32),
-            jax.ShapeDtypeStruct((GROUP, 2 * rank), f32),
+            jax.ShapeDtypeStruct((GROUP, 2048), bf16),
+            jax.ShapeDtypeStruct((GROUP, 2048 + 3 * rank), bf16),
         ]
-        + [jax.ShapeDtypeStruct((UNITS, rank), f32)] * 3,
-        scratch_shapes=[
-            pltpu.VMEM((GROUP, 2048), bf16),
-            pltpu.VMEM((GROUP, 2048), f32),
-            pltpu.VMEM((GROUP, 2048), f32),
-        ],
+        + [jax.ShapeDtypeStruct((2, UNITS, rank), f32)] * 3,
         compiler_params=pltpu.CompilerParams(vmem_limit_bytes=60 << 20),
-        cost_estimate=pl.CostEstimate(flops=14 << 30, bytes_accessed=30 << 20, transcendentals=1 << 20),
+        cost_estimate=pl.CostEstimate(flops=28 << 30, bytes_accessed=40 << 20, transcendentals=2 << 20),
         name="feed_forward",
-    )(normed_mid, cot, low_gu, grad_low_down, weights, weights, weights, *expands, perm, *(sums or ()))
+    )(at, normed_mid, cot, low_gu, grad_low_down, weights, weights, weights, *expands, perm, picks)
 
 
 EARLY = (64, 64, 64, 16, 16, 16, 16, 16)
@@ -566,7 +591,7 @@
 
     tile_low, tile_high = jnp.min(tiles_pos, axis=1), jnp.max(tiles_pos, axis=1)
     active = (tile_low <= jnp.max(group_pos)) & (tile_high >= jnp.min(group_start))
-    active = active.astype(jnp.int32)
+    active = step_tables(active.astype(jnp.int32), c)
     select_y = selected(group_pos)
     select_x = selected(own_row.reshape(2, 4, 4, 128)[0, :, 0].reshape(GROUP))
     select = select_y[:128]
@@ -575,13 +600,6 @@
     def column_slices(weight):
         parts = weight.reshape(16, 4, 4, 4, 2, 64)
         return jnp.transpose(parts, (2, 4, 0, 1, 3, 5)).reshape(8, 16, 1024)
-
-    def units_at(array, axis, core):
-        shape = array.shape
-        array = array.reshape(shape[:axis] + (4, 4, 4, 2, 64) + shape[axis + 1 :])
-        array = lax.dynamic_slice_in_dim(array, x, 1, axis + 1)
-        array = lax.dynamic_slice_in_dim(array, core, 1, axis + 3)
-        return array.reshape(shape[:axis] + (1024,) + shape[axis + 1 :])
 
     heads_q = w_query.reshape(16, 4, 512)
     heads_kv = jnp.concatenate([w_key.reshape(16, 4, 256), w_value.reshape(16, 4, 256)], axis=2)
@@ -589,11 +607,6 @@
     qkv_parts = lax.all_to_all(qkv_parts, ("y", "c"), split_axis=0, concat_axis=0, tiled=True).reshape(128, 512)
     gate_up = jnp.concatenate([column_slices(w_gate), column_slices(w_up)], axis=2)
     gate_up = lax.all_to_all(after(gate_up, qkv_parts), ("x", "c"), split_axis=0, concat_axis=0, tiled=True).reshape(128, 2048)
-    expands = [
-        (units_at(gate_expand, 1, core), units_at(up_expand, 1, core), units_at(down_shrink, 0, core))
-        for core in (c, 1 - c)
-    ]
-
     def columns_of(array, width):
         return lax.dynamic_slice_in_dim(array, y * width, width, 1)
 
@@ -603,12 +616,10 @@
     normed, cot, qkv_parts, gate_up = lax.optimization_barrier((normed, cot, qkv_parts, gate_up))
     normed_g = gather_near(normed, "y")
     cot_g = gather_near(cot, "x")
-    qkv_parts = after(qkv_parts, normed_g, cot_g, expands)
-    wo = lax.all_gather(after(w_out, normed_g, cot_g), ALL, axis=0, tiled=True)
+    qkv_parts = after(qkv_parts, normed_g, cot_g)
+    wo = lax.all_gather(w_out, ALL, axis=0, tiled=True)
     qkv_mine = gather_ring(gather_ring(qkv_parts, "x"), "z").reshape(2048, 512)
     qkv_other = swap_cores(qkv_mine)
-    ffn = after(jnp.concatenate([gate_up, w_down], axis=0), normed_g, cot_g)
-    ffn_mine = lax.all_gather(ffn, ("zh", "zl", "y"), axis=0, tiled=False)
     q_expand = columns_of(query_expand, 512)
     k_expand = columns_of(key_expand, 256)
     v_expand = columns_of(value_expand, 256)
@@ -625,6 +636,9 @@
     key = (key_heads * cos_table + rotate(key_heads) * sin_table).astype(bf16).reshape(GROUP, 256)
 
     lines = gather_row(jnp.concatenate([key, value_lin.astype(bf16)], axis=1))
+    waited = zero_of(lines[1]) + zero_of(lines[2]) + zero_of(lines[3]) + zero_of(wo)
+    ffn = jnp.concatenate([gate_up, w_down], axis=0) + waited.astype(bf16)
+    ffn = lax.all_gather(ffn, OVER_X, axis=0, tiled=False).reshape(16, 2, 192, 2048)
     attended = (query, group_pos[:, None], group_start[:, None], tiles_pos.reshape(16, 1, GROUP)) + lines
     mixed_f, lse = attend(active, *attended)
     mixed = mixed_f.astype(bf16)
@@ -640,7 +654,6 @@
     scale_mid = row_scale(middle)
     normed_mid = (middle * scale_mid * gain_ffn).astype(bf16)
     normed_mid_g = gather_near(normed_mid, "x")
-    ffn_other = swap_cores(after(ffn_mine, normed_mid))
 
     select_two = jnp.tile(select_x, (1, 2))
     low_gu = (product(normed_mid_g, gateup_shrink) * select_two).astype(bf16)
@@ -648,23 +661,21 @@
     place = jnp.arange(GROUP, dtype=jnp.int32)
     turned = (place // 32 % 4) * 128 + (place // 128) * 32 + place % 32
     perm = (turned[:, None] == place[None, :]).astype(bf16)
-    given = (normed_mid_g, cot_g, low_gu, grad_low_down)
-    sums = ffn_part(*given, ffn_mine, expands[0], perm)
-    units_mine, sums = sums[4:], sums[:4]
-    sums = ffn_part(*given, ffn_other, expands[1], perm, sums)
-    units_other = sums[4:]
-    result, back_part = sums[:2]
-    unit_grads = (units_mine, units_other)
-
-    def reduce_units(unit_grads):
-        def by_halves(pair_at):
-            own, others = unit_grads[0][pair_at], unit_grads[1][pair_at]
-            own, others = own.reshape(16, 1, 64, rank), others.reshape(16, 1, 64, rank)
-            ordered = jnp.where(c == 0, jnp.concatenate([own, others], 1), jnp.concatenate([others, own], 1))
-            return ordered.reshape(32, 64, rank)
-
-        unit_terms = jnp.concatenate([by_halves(0), by_halves(1), by_halves(2)], axis=1)
-        return lax.psum_scatter(unit_terms, OVER_X, scatter_dimension=0, tiled=False)
+    wide, narrow = jnp.arange(2 * CHUNK, dtype=jnp.int32), jnp.arange(CHUNK, dtype=jnp.int32)
+    picks = jnp.stack(
+        [(wide[:, None] == (narrow // 64 * 128 + core * 64 + narrow % 64)[None, :]).astype(bf16) for core in (0, 1)]
+    )
+    result, back_part, *unit_grads = feed_forward(
+        x.reshape(1).astype(jnp.int32),
+        normed_mid_g,
+        cot_g,
+        low_gu,
+        grad_low_down,
+        ffn,
+        (gate_expand, up_expand, down_shrink),
+        perm,
+        picks,
+    )
 
     def sum_tokens(part, ring):
         sent = part.astype(bf16)
@@ -688,9 +699,7 @@
 
         return jnp.concatenate([columns_at(0)] + [shift(columns_at(4 - step), "y", -step) for step in (1, 2, 3)])
 
-    unit_sum = reduce_units(unit_grads)
     dout = slices_near(grad_mixed)
-    dout = dout + zero_of(unit_sum).astype(bf16)
     dq, *terms = attend_back(active, *attended, mixed_f, lse, dout)
     dkv = sum_row(*terms)
     dk, dv = dkv[:, :HEAD_SIZE], dkv[:, HEAD_SIZE:]
@@ -721,48 +730,55 @@
     def features(array, at):
         return lax.dynamic_slice_in_dim(array, at * 512, 512, 1)
 
-    def by_rows(array):
-        return array.reshape(32, array.shape[0] // 32, rank)
-
-    low_near = gather_near(after(jnp.concatenate([low_down, grad_low_gu], axis=1), dout), "x")
+    def by_cores(arrays):
+        parts = jnp.concatenate([array.reshape(16, 2, array.shape[0] // 32, rank) for array in arrays], axis=2)
+        kept = lax.dynamic_index_in_dim(parts, c, 1, keepdims=False)
+        return kept, lax.dynamic_index_in_dim(parts, 1 - c, 1, keepdims=False)
+
+    def sum_plane(kept, given, ring):
+        terms = kept + swap_cores(given.astype(bf16)).astype(f32)
+        return sum_ring(sum_ring(terms.reshape(4, 4, -1, rank), "z"), ring)
+
+    attended_back = zero_of(dq)
+    low_near = jnp.concatenate([low_down, grad_low_gu], axis=1) + attended_back.astype(bf16)
+    low_near = gather_near(low_near, "x")
     grad_gateup = inner_rows(features(normed_mid_g, x), low_near[:, rank:])
     out_terms = jnp.concatenate([inner_rows(mixed_tok, grad_low_out), inner_rows(grad_attn_out, low_out)], axis=1)
-    out_terms = after(out_terms.astype(bf16).reshape(4, 512, 2 * rank), dout)
+    out_terms = (out_terms + attended_back).astype(bf16).reshape(4, 512, 2 * rank)
     out_terms = sum_near(
         [lax.dynamic_index_in_dim(out_terms, (x + step) % 4, 0, keepdims=False) for step in range(4)], "x"
     )
-    row_terms = [
-        by_rows(out_terms[:, :rank]),
-        by_rows(out_terms[:, rank:]),
-        by_rows(inner_rows(features(cot_g, x), low_near[:, :rank])),
-        by_rows(grad_gateup[:, :rank]),
-        by_rows(grad_gateup[:, rank:]),
-    ]
-    row_sum = lax.psum_scatter(jnp.concatenate(row_terms, axis=1) + zero_of(unit_sum), OVER_X, scatter_dimension=0, tiled=False)
-    early_sum = jnp.concatenate([unit_sum, row_sum], axis=0)
-    early_sum = after(early_sum.astype(bf16), dkv)
+    kept, other = by_cores(
+        [
+            out_terms[:, :rank],
+            out_terms[:, rank:],
+            inner_rows(features(cot_g, x), low_near[:, :rank]),
+            grad_gateup[:, :rank],
+            grad_gateup[:, rank:],
+        ]
+    )
+    unit_grads = jnp.concatenate([array.reshape(2, 16, 64, rank) for array in unit_grads], axis=2)
+    kept = jnp.concatenate([lax.dynamic_index_in_dim(unit_grads, c, 0, keepdims=False), kept], axis=1)
+    other = jnp.concatenate([lax.dynamic_index_in_dim(unit_grads, 1 - c, 0, keepdims=False), other], axis=1)
+    early_sum = sum_plane(kept, other, "y").astype(bf16)
     early_all = lax.all_gather(early_sum, ALL, axis=0, tiled=False)
 
     grad_qkv = inner_rows(features(normed_g, y), gather_near(grad_low_qkv, "y"))
-    late = [
-        by_rows(inner_rows(grad_query, low_qkv[:, :rank])),
-        by_rows(inner_rows(grad_key, low_qkv[:, rank : 2 * rank])),
-        by_rows(inner_rows(grad_value, low_qkv[:, 2 * rank :])),
-        by_rows(grad_qkv[:, :rank]),
-        by_rows(grad_qkv[:, rank : 2 * rank]),
-        by_rows(grad_qkv[:, 2 * rank :]),
-    ]
-    terms = jnp.concatenate(late, axis=1)
-    terms = terms.reshape(16, 2, terms.shape[1], rank)
-    kept = lax.dynamic_index_in_dim(terms, c, 1, keepdims=False)
-    given = lax.dynamic_index_in_dim(terms, 1 - c, 1, keepdims=False).astype(bf16)
-    terms = (kept + swap_cores(given).astype(f32)).reshape(4, 4, -1, rank)
-    late_sum = sum_ring(sum_ring(terms, "z"), "x").astype(bf16)
+    kept, other = by_cores(
+        [
+            inner_rows(grad_query, low_qkv[:, :rank]),
+            inner_rows(grad_key, low_qkv[:, rank : 2 * rank]),
+            inner_rows(grad_value, low_qkv[:, 2 * rank :]),
+            grad_qkv[:, :rank],
+            grad_qkv[:, rank : 2 * rank],
+            grad_qkv[:, 2 * rank :],
+        ]
+    )
+    g_gate, g_up, g_down_shrink, g_out_shrink, g_out_expand, g_down_expand, g_gateup = unpack_early(early_all)
+    late_sum = (sum_plane(kept, other, "x") + zero_of(g_gateup)).astype(bf16)
     late_all = gather_ring(gather_ring(gather_ring(late_sum, "x"), "z"), "y")
     late_all = late_all.reshape(4, 16, -1, rank)
-    g_gate, g_up, g_down_shrink, g_out_shrink, g_out_expand, g_down_expand, g_gateup = unpack_early(early_all)
     late_other = swap_cores(late_all)
-    late_all = after(late_all, g_gate, g_gateup)
     g_q, g_k, g_v, g_qkv = unpack_late(c.reshape(1).astype(jnp.int32), late_all, late_other)
     return (
         from_rows(output),

time: 898 us -> 835 us (0.930)
  waiting for transfers between devices: 433 us -> 352 us
  starting transfers between devices: 134 us -> 161 us
  Pallas kernels: 116 us -> 102 us
    reduce_scatter x2 -> x0, waiting for transfers between devices: 64.3 us -> none  [the longest x1 38.5 us: reduce_units(): lax.psum_scatter(unit_terms, OVER_X, scatter_dimension=0, tiled=False)]
    ppermute x63 -> x69, starting transfers between devices: 86.4 us -> 119 us  [shift(): lax.ppermute(value, RING[ring], [(i, (i + step) % 4) for i in range(4)])]
    ppermute x1, waiting for transfers between devices: 68.9 us -> 40 us  [gather_row(): partner = lax.ppermute(line, CORNER, PARTNER)]
    ppermute x2, waiting for transfers between devices: 31.1 us -> 48.1 us  [sum_row(): lax.ppermute(value, CORNER, pairs)]
    ppermute x63 -> x69, waiting for transfers between devices: 212 us -> 229 us  [shift(): lax.ppermute(value, RING[ring], [(i, (i + step) % 4) for i in range(4)])]
    ppermute x2, waiting for transfers between devices: 37.1 us -> 21.8 us  [gather_row(): ahead = [lax.ppermute(line, CORNER, pairs) for pairs in LATER]]
    pallas_call x2 -> x1, Pallas kernels: 55 us -> 45.7 us  [feed_forward(): pl.pallas_call(ffn_kernel, grid_spec=pltpu.PrefetchScalarGridSpec(num_sca...]
    unnamed x176 -> x181, local copies, waits for them, and re-layouts: 23.3 us -> 21.8 us
  transfers between devices with their start and end apart: 88 -> 92, of which waited for: 45 -> 50; matrix products, arithmetic and copies ran while one was open for 19% -> 17% of each run, Pallas kernels for 7% -> 4%
where the time goes in v1:
time: 835 us; the launch traced here: 823 us
  waiting for transfers between devices  352 us (42%)
  starting transfers between devices  161 us (19%)
  Pallas kernels  102 us (12%)
  local copies, waits for them, and re-layouts  80 us (10%)
  other arithmetic  54.3 us (7%)
  matrix products  53.2 us (6%)
  between operations  20.1 us (2%)
    ppermute x69, waiting for transfers between devices, shift(): lax.ppermute(value, RING[ring], [(i, (i + step) % 4) for i in range(4)])  229 us
    ppermute x69, starting transfers between devices, shift(): lax.ppermute(value, RING[ring], [(i, (i + step) % 4) for i in range(4)])  119 us
    ppermute x2, waiting for transfers between devices, sum_row(): lax.ppermute(value, CORNER, pairs)  48.1 us
    pallas_call x1, Pallas kernels, feed_forward(): pl.pallas_call(ffn_kernel, grid_spec=pltpu.PrefetchScalarGridSpec(num_sca...  45.7 us
    ppermute x1, waiting for transfers between devices, gather_row(): partner = lax.ppermute(line, CORNER, PARTNER)  40 us
    dot_general x11, matrix products, product(): return jnp.dot(left, right, preferred_element_type=f32)  26 us
    unnamed x181, local copies, waits for them, and re-layouts  21.8 us
    ppermute x2, waiting for transfers between devices, gather_row(): ahead = [lax.ppermute(line, CORNER, pairs) for pairs in LATER]  21.8 us
  transfers between devices with their start and end apart: 92, of which 50 were waited for; matrix products, arithmetic and copies ran while one was open for 17% of the time, Pallas kernels for 4%

profile of v1, /device:TPU:1, one launch (start us, length us, event | category | flops | bytes accessed | tf_op | source)
XLA Modules:
  0.0 822.8 jit_solution(13796754118650250567)
XLA Ops:
  14.0 5.0 all-to-all-start
  26.1 4.4 all-to-all-start.1
  33.2 7.0 all-to-all-done.1
  45.2 3.0 collective-permute-start.2
  48.7 6.0 collective-permute-done.5
  59.0 13.0 %collective-permute-done.7 = bf16[128,2048]{1,0:T(8,128)(2,1)S(1)} collective-permute-done((bf16[128,2048]{1,0:T(8,128)(2,1)S(1)}, bf16[128,2048]{1,0:T(8,128)(2,1)S(1)}, u32[]{:S(2)}, u32[]{:S(2)}) %collective-permute-start.7) | collective-permute-done | bytes 524320 | tf_op jit(solution)/shard_map/ppermute | solution.py:73
  72.2 4.3 collective-permute-done.4
  80.4 3.3 collective-permute-done.8
  86.4 5.5 collective-permute-done.10
  91.9 3.0 collective-permute-start.11
  98.1 12.4 %collective-permute-done.11 = bf16[4,128,512]{2,1,0:T(8,128)(2,1)S(1)} collective-permute-done((bf16[4,128,512]{2,1,0:T(8,128)(2,1)S(1)}, bf16[4,128,512]{2,1,0:T(8,128)(2,1)S(1)}, u32[]{:S(2)}, u32[]{:S(2)}) %collective-permute-start.11) | collective-permute-done | bytes 524320 | tf_op jit(solution)/shard_map/ppermute | solution.py:73
  113.8 9.8 %collective-permute-done.13 = bf16[4,128,512]{2,1,0:T(8,128)(2,1)S(1)} collective-permute-done((bf16[4,128,512]{2,1,0:T(8,128)(2,1)S(1)}, bf16[4,128,512]{2,1,0:T(8,128)(2,1)S(1)}, u32[]{:S(2)}, u32[]{:S(2)}) %collective-permute-start.13) | collective-permute-done | bytes 524320 | tf_op jit(solution)/shard_map/ppermute | solution.py:73
  130.3 3.2 fusion.3
  134.7 2.9 fusion.177
  137.5 4.2 broadcast_select_fusion
  145.6 12.0 %collective-permute-done.15 = bf16[512,512]{1,0:T(8,128)(2,1)S(1)} collective-permute-done((bf16[512,512]{1,0:T(8,128)(2,1)S(1)}, bf16[512,512]{1,0:T(8,128)(2,1)S(1)}, u32[]{:S(2)}, u32[]{:S(2)}) %collective-permute-start.15) | collective-permute-done | bytes 524320 | tf_op jit(solution)/shard_map/ppermute | solution.py:73
  159.3 11.8 %collective-permute-done.17 = bf16[512,512]{1,0:T(8,128)(2,1)S(1)} collective-permute-done((bf16[512,512]{1,0:T(8,128)(2,1)S(1)}, bf16[512,512]{1,0:T(8,128)(2,1)S(1)}, u32[]{:S(2)}, u32[]{:S(2)}) %collective-permute-start.17) | collective-permute-done | bytes 524320 | tf_op jit(solution)/shard_map/ppermute | solution.py:73
  173.3 4.1 collective-permute-start.19
  178.8 40.0 %collective-permute-done.18.refs_1_ = bf16[4,512,512]{2,1,0:T(8,128)(2,1)S(1)} collective-permute-done((bf16[4,512,512]{2,1,0:T(8,128)(2,1)S(1)}, bf16[4,512,512]{2,1,0:T(8,128)(2,1)S(1)}, u32[]{:S(2)}, u32[]{:S(2)}) %collective-permute-start.18) | collective-permute-done | bytes 2097184 | tf_op jit(solution)/shard_map/ppermute | solution.py:129
  219.4 21.8 %collective-permute-done.19.refs_2_ = bf16[4,512,512]{2,1,0:T(8,128)(2,1)S(1)} collective-permute-done((bf16[4,512,512]{2,1,0:T(8,128)(2,1)S(1)}, bf16[4,512,512]{2,1,0:T(8,128)(2,1)S(1)}, u32[]{:S(2)}, u32[]{:S(2)}) %collective-permute-start.19) | collective-permute-done | bytes 2097184 | tf_op jit(solution)/shard_map/ppermute | solution.py:128
  257.9 2.8 reshape.604
  264.8 14.9 %attend.1 = (f32[512,512]{1,0:T(8,128)S(1)}, f32[2,512,1]{2,1,0:T(8,128)S(1)}) custom-call(s32[64]{0:T(128)S(1)} %pad_add_fusion.2.active, bf16[512,512]{1,0:T(8,128)(2,1)S(1)} %fusion.28.q_ref, s32[512,1]{1,0:T(8,128)S(1)} %copy.152.pos_ref, s32[512,1]{1,0:T(8,128)S(1)} %copy.153.start_ref, s32[16,1,512]{2,1,0:T(1,128)S(1)} %reshape.605.kpos_ref, ...), custom_call_target="tpu_custom_call" | custom-call | flops 6442450944 | bytes 10485760 | tf_op jit(solution)/shard_map/attend/pallas_call | solution.py:280
  285.3 7.7 collective-permute-done.23
  302.4 5.4 multiply_reduce_fusion.1
  308.5 7.5 collective-permute-start.26
  319.1 18.9 %collective-permute-done.26 = bf16[128,2048]{1,0:T(8,128)(2,1)S(1)} collective-permute-done((bf16[128,2048]{1,0:T(8,128)(2,1)S(1)}, bf16[128,2048]{1,0:T(8,128)(2,1)S(1)}, u32[]{:S(2)}, u32[]{:S(2)}) %collective-permute-start.26) | collective-permute-done | bytes 524320 | tf_op jit(solution)/shard_map/ppermute | solution.py:73
  338.0 4.3 collective-permute-done.28
  345.5 45.7 %feed_forward.1 = (bf16[512,2048]{1,0:T(8,128)(2,1)}, bf16[512,2432]{1,0:T(8,128)(2,1)}, f32[2,1024,128]{2,1,0:T(8,128)}, f32[2,1024,128]{2,1,0:T(8,128)}, f32[2,1024,128]{2,1,0:T(8,128)}) custom-call(s32[1]{0:T(128)} %bitcast.37.at, bf16[512,2048]{1,0:T(8,128)(2,1)} %pad_maximum_fusion.2.nm_ref, bf16[512,2048]{1,0:T(8,128)(2,1)} %copy-done.55, ...), custom_call_target="tpu_custom_call" | custom-call | flops 30064771072 | bytes 41943040 | tf_op jit(solution)/shard_map/feed_forward/pallas_call | solution.py:401
  394.3 2.9 collective-permute-start.31
  400.6 10.1 %collective-permute-done.29 = bf16[128,2432]{1,0:T(8,128)(2,1)} collective-permute-done((bf16[128,2432]{1,0:T(8,128)(2,1)}, bf16[128,2432]{1,0:T(8,128)(2,1)}, u32[]{:S(2)}, u32[]{:S(2)}) %collective-permute-start.29) | collective-permute-done | bytes 622624 | tf_op jit(solution)/shard_map/ppermute | solution.py:73
  410.7 14.3 %collective-permute-done.30 = bf16[128,2432]{1,0:T(8,128)(2,1)} collective-permute-done((bf16[128,2432]{1,0:T(8,128)(2,1)}, bf16[128,2432]{1,0:T(8,128)(2,1)}, u32[]{:S(2)}, u32[]{:S(2)}) %collective-permute-start.30) | collective-permute-done | bytes 622624 | tf_op jit(solution)/shard_map/ppermute | solution.py:73
  431.5 2.9 fusion.155
  441.8 3.7 collective-permute-done.34
  449.9 19.9 %attend_back.1 = (f32[512,512]{1,0:T(8,128)S(1)}, bf16[4,512,512]{2,1,0:T(8,128)(2,1)}, bf16[4,512,512]{2,1,0:T(8,128)(2,1)}, bf16[4,512,512]{2,1,0:T(8,128)(2,1)}, bf16[4,512,512]{2,1,0:T(8,128)(2,1)}) custom-call(s32[64]{0:T(128)S(1)} %pad_add_fusion.2.active, bf16[512,512]{1,0:T(8,128)(2,1)S(1)} %fusion.28.q_ref, s32[512,1]{1,0:T(8,128)S(1)} %copy-done.6, ...), custom_call_target="tpu_custom_call" | custom-call | flops 12884901888 | bytes 20971520 | tf_op jit(solution)/shard_map/attend_back/pallas_call | solution.py:305
  470.9 5.8 collective-permute-start.67
  490.1 4.2 collective-permute-done.65
  516.2 6.0 collective-permute-start.71
  524.6 3.8 collective-permute-done.71
  528.5 6.4 collective-permute-done.72
  543.5 4.0 collective-permute-start.36
  552.7 3.5 add_convert_fusion.1
  560.6 2.8 reshape.611
  566.2 33.7 %collective-permute-done.38 = bf16[4,512,512]{2,1,0:T(8,128)(2,1)} collective-permute-done((bf16[4,512,512]{2,1,0:T(8,128)(2,1)}, bf16[4,512,512]{2,1,0:T(8,128)(2,1)}, u32[]{:S(2)}, u32[]{:S(2)}) %collective-permute-start.38) | collective-permute-done | bytes 2097184 | tf_op jit(solution)/shard_map/ppermute | solution.py:136
  599.9 14.4 %collective-permute-done.39 = bf16[4,512,512]{2,1,0:T(8,128)(2,1)} collective-permute-done((bf16[4,512,512]{2,1,0:T(8,128)(2,1)}, bf16[4,512,512]{2,1,0:T(8,128)(2,1)}, u32[]{:S(2)}, u32[]{:S(2)}) %collective-permute-start.39) | collective-permute-done | bytes 2097184 | tf_op jit(solution)/shard_map/ppermute | solution.py:136
  614.3 3.9 collective-permute-done.37
  618.2 7.2 fusion.163
  626.7 2.8 collective-permute-start.42
  633.3 9.1 %collective-permute-done.40 = bf16[512,512]{1,0:T(8,128)(2,1)} collective-permute-done((bf16[512,512]{1,0:T(8,128)(2,1)}, bf16[512,512]{1,0:T(8,128)(2,1)}, u32[]{:S(2)}, u32[]{:S(2)}) %collective-permute-start.40) | collective-permute-done | bytes 524320 | tf_op jit(solution)/shard_map/ppermute | solution.py:73
  642.3 10.9 %collective-permute-done.41 = bf16[512,512]{1,0:T(8,128)(2,1)} collective-permute-done((bf16[512,512]{1,0:T(8,128)(2,1)}, bf16[512,512]{1,0:T(8,128)(2,1)}, u32[]{:S(2)}, u32[]{:S(2)}) %collective-permute-start.41) | collective-permute-done | bytes 524320 | tf_op jit(solution)/shard_map/ppermute | solution.py:73
  663.4 2.9 fusion.43
  666.3 3.0 add_convert_fusion
  675.1 3.0 collective-permute-done.55
  681.3 2.9 collective-permute-start.57
  690.7 13.0 %collective-permute-start.59 = (bf16[4,80,128]{2,1,0:T(8,128)(2,1)S(1)}, bf16[4,80,128]{2,1,0:T(8,128)(2,1)S(1)}, u32[]{:S(2)}, u32[]{:S(2)}) collective-permute-start(bf16[4,80,128]{2,1,0:T(8,128)(2,1)S(1)} %get-tuple-element.117), channel_id=1, source_target_pairs={{0,64},{32,96},{64,0},{96,32},{1,65},{33,97},{65,1},{97,33},{2,66}... | collective-permute-start | bytes 245768 | tf_op jit(solution)/shard_map/ppermute | solution.py:73
  703.7 9.1 %collective-permute-start.60 = (bf16[4,80,128]{2,1,0:T(8,128)(2,1)S(1)}, bf16[4,80,128]{2,1,0:T(8,128)(2,1)S(1)}, u32[]{:S(2)}, u32[]{:S(2)}) collective-permute-start(bf16[4,80,128]{2,1,0:T(8,128)(2,1)S(1)} %get-tuple-element.116), channel_id=1, source_target_pairs={{0,96},{32,0},{64,32},{96,64},{1,97},{33,1},{65,33},{97,65},{2,98}... | collective-permute-start | bytes 245768 | tf_op jit(solution)/shard_map/ppermute | solution.py:73
  718.6 14.7 %unpack_early.1 = (f32[128,8192]{1,0:T(8,128)}, f32[128,8192]{1,0:T(8,128)}, f32[8192,128]{1,0:T(8,128)}, f32[2048,128]{1,0:T(8,128)}, f32[128,2048]{1,0:T(8,128...) custom-call(bf16[128,272,128]{2,1,0:T(8,128)(2,1)} %bitcast.291), custom_call_target="tpu_custom_call" | custom-call | flops 1048576 | bytes 28311552 | tf_op jit(solution)/shard_map/unpack_early/pallas_call | solution.py:467
  741.4 18.7 %collective-permute-done.78 = bf16[80,128]{1,0:T(8,128)(2,1)S(1)} collective-permute-done((bf16[80,128]{1,0:T(8,128)(2,1)S(1)}, bf16[80,128]{1,0:T(8,128)(2,1)S(1)}, u32[]{:S(2)}, u32[]{:S(2)}) %collective-permute-start.78) | collective-permute-done | bytes 20512 | tf_op jit(solution)/shard_map/ppermute | solution.py:73
  760.1 3.5 collective-permute-done.79
  763.6 11.5 %collective-permute-start.80 = (bf16[4,80,128]{2,1,0:T(8,128)(2,1)S(1)}, bf16[4,80,128]{2,1,0:T(8,128)(2,1)S(1)}, u32[]{:S(2)}, u32[]{:S(2)}) collective-permute-start(bf16[4,80,128]{2,1,0:T(8,128)(2,1)S(1)} %bitcast_dynamic-update-slice_fusion.19), channel_id=1, source_target_pairs={{0,96},{32,0},{64,32},{96,64},{1,97},{33,1},{65,33},{97,65},{2,98}... | collective-permute-start | bytes 245768 | tf_op jit(solution)/shard_map/ppermute | solution.py:73
  785.8 3.8 collective-permute-done.83
  789.7 3.1 collective-permute-done.84
  792.9 5.9 collective-permute-done.85
  798.8 4.5 collective-permute-start.86
  809.3 6.7 unpack_late.1
  (528 shorter events, 240.1 us)
Async XLA Ops:
  7.2 237.2 %all-gather.5.cloned.1.call-start = ((), (), s32[]{:S(2)}) async-start(), calls=%async_computation.2 | async-start | bytes 8454144 | tf_op jit(solution)/shard_map/all_gather | solution.py:620
  9.8 20.7 %collective-permute-start = (bf16[64,2048]{1,0:T(8,128)(2,1)}, bf16[64,2048]{1,0:T(8,128)(2,1)S(1)}, u32[]{:S(2)}, u32[]{:S(2)}) collective-permute-start(bf16[64,2048]{1,0:T(8,128)(2,1)} %get-tuple-element.145), channel_id=1, source_target_pairs={{0,1},{1,0},{2,3},{3,2},{4,5},{5,4},{6,7},{7,6},{8,9},{9,8},{10,11... | collective-permute-start | bytes 786440 | tf_op jit(solution)/shard_map/ppermute | solution.py:69
  12.9 18.3 %collective-permute-start.1 = (bf16[64,2048]{1,0:T(8,128)(2,1)}, bf16[64,2048]{1,0:T(8,128)(2,1)}, u32[]{:S(2)}, u32[]{:S(2)}) collective-permute-start(bf16[64,2048]{1,0:T(8,128)(2,1)} %get-tuple-element.143), channel_id=1, source_target_pairs={{0,1},{1,0},{2,3},{3,2},{4,5},{5,4},{6,7},{7,6},{8,9},{9,8},{10,11... | collective-permute-start | bytes 786440 | tf_op jit(solution)/shard_map/ppermute | solution.py:69
  14.0 12.1 %all-to-all-start = ((bf16[8,16,512]{2,1,0:T(8,128)(2,1)}), bf16[8,16,512]{2,1,0:T(8,128)(2,1)S(1)}, u32[]{:S(2)}, u32[]{:S(2)}) async-start(bf16[8,16,512]{2,1,0:T(8,128)(2,1)} %bitcast.7), calls=%async_computation | async-start | bytes 262144 | tf_op jit(solution)/shard_map/all_to_all | solution.py:607
  26.1 14.1 %all-to-all-start.1 = ((bf16[8,16,2048]{2,1,0:T(8,128)(2,1)}), bf16[8,16,2048]{2,1,0:T(8,128)(2,1)S(1)}, u32[]{:S(2)}, u32[]{:S(2)}) async-start(bf16[8,16,2048]{2,1,0:T(8,128)(2,1)} %pad_maximum_fusion.7), calls=%async_computation.1 | async-start | bytes 1048576 | tf_op jit(solution)/shard_map/all_to_all | solution.py:609
  30.5 315.0 %all-gather.7.cloned.1.call-start = ((), (), s32[]{:S(2)}) async-start(), calls=%async_computation.3 | async-start | bytes 25952256 | tf_op jit(solution)/shard_map/all_gather | solution.py:641
  40.2 14.6 %collective-permute-start.5 = (bf16[128,2048]{1,0:T(8,128)(2,1)S(1)}, bf16[128,2048]{1,0:T(8,128)(2,1)}, u32[]{:S(2)}, u32[]{:S(2)}) collective-permute-start(bf16[128,2048]{1,0:T(8,128)(2,1)S(1)} %pad_maximum_fusion.6), channel_id=1, source_target_pairs={{0,24},{8,0},{16,8},{24,16},{1,25},{9,1},{17,9},{25,17},{2,26},{10... | collective-permute-start | bytes 1572872 | tf_op jit(solution)/shard_map/ppermute | solution.py:73
  42.6 15.3 %collective-permute-start.6 = (bf16[128,2048]{1,0:T(8,128)(2,1)S(1)}, bf16[128,2048]{1,0:T(8,128)(2,1)}, u32[]{:S(2)}, u32[]{:S(2)}) collective-permute-start(bf16[128,2048]{1,0:T(8,128)(2,1)S(1)} %pad_maximum_fusion.6), channel_id=1, source_target_pairs={{0,16},{8,24},{16,0},{24,8},{1,17},{9,25},{17,1},{25,9},{2,18},{10... | collective-permute-start | bytes 1572872 | tf_op jit(solution)/shard_map/ppermute | solution.py:73
  43.9 28.0 %collective-permute-start.7 = (bf16[128,2048]{1,0:T(8,128)(2,1)S(1)}, bf16[128,2048]{1,0:T(8,128)(2,1)S(1)}, u32[]{:S(2)}, u32[]{:S(2)}) collective-permute-start(bf16[128,2048]{1,0:T(8,128)(2,1)S(1)} %pad_maximum_fusion.6), channel_id=1, source_target_pairs={{0,8},{8,16},{16,24},{24,0},{1,9},{9,17},{17,25},{25,1},{2,10},{10... | collective-permute-start | bytes 1572872 | tf_op jit(solution)/shard_map/ppermute | solution.py:73
  45.2 26.8 %collective-permute-start.2 = (bf16[128,2048]{1,0:T(8,128)(2,1)S(1)}, bf16[128,2048]{1,0:T(8,128)(2,1)S(1)}, u32[]{:S(2)}, u32[]{:S(2)}) collective-permute-start(bf16[128,2048]{1,0:T(8,128)(2,1)S(1)} %copy-done.38), channel_id=1, source_target_pairs={{0,6},{2,0},{4,2},{6,4},{1,7},{3,1},{5,3},{7,5},{8,14},{10,8},{12,... | collective-permute-start | bytes 1572872 | tf_op jit(solution)/shard_map/ppermute | solution.py:73
  48.2 23.9 %collective-permute-start.3 = (bf16[128,2048]{1,0:T(8,128)(2,1)S(1)}, bf16[128,2048]{1,0:T(8,128)(2,1)S(1)}, u32[]{:S(2)}, u32[]{:S(2)}) collective-permute-start(bf16[128,2048]{1,0:T(8,128)(2,1)S(1)} %copy-done.38), channel_id=1, source_target_pairs={{0,4},{2,6},{4,0},{6,2},{1,5},{3,7},{5,1},{7,3},{8,12},{10,14},{12... | collective-permute-start | bytes 1572872 | tf_op jit(solution)/shard_map/ppermute | solution.py:73
  54.8 21.7 %collective-permute-start.4 = (bf16[128,2048]{1,0:T(8,128)(2,1)S(1)}, bf16[128,2048]{1,0:T(8,128)(2,1)S(1)}, u32[]{:S(2)}, u32[]{:S(2)}) collective-permute-start(bf16[128,2048]{1,0:T(8,128)(2,1)S(1)} %copy-done.38), channel_id=1, source_target_pairs={{0,2},{2,4},{4,6},{6,0},{1,3},{3,5},{5,7},{7,1},{8,10},{10,12},{12... | collective-permute-start | bytes 1572872 | tf_op jit(solution)/shard_map/ppermute | solution.py:73
  79.7 12.1 %collective-permute-start.10 = (bf16[128,512]{1,0:T(8,128)(2,1)S(1)}, bf16[128,512]{1,0:T(8,128)(2,1)S(1)}, u32[]{:S(2)}, u32[]{:S(2)}) collective-permute-start(bf16[128,512]{1,0:T(8,128)(2,1)S(1)} %bitcast.325), channel_id=1, source_target_pairs={{0,8},{8,16},{16,24},{24,0},{1,9},{9,17},{17,25},{25,1},{2,10},{10... | collective-permute-start | bytes 393224 | tf_op jit(solution)/shard_map/ppermute | solution.py:73
  91.9 18.7 %collective-permute-start.11 = (bf16[4,128,512]{2,1,0:T(8,128)(2,1)S(1)}, bf16[4,128,512]{2,1,0:T(8,128)(2,1)S(1)}, u32[]{:S(2)}, u32[]{:S(2)}) collective-permute-start(bf16[4,128,512]{2,1,0:T(8,128)(2,1)S(1)} %bitcast_dynamic-update-slice_fusion.11), channel_id=1, source_target_pairs={{0,96},{32,0},{64,32},{96,64},{1,97},{33,1},{65,33},{97,65},{2,98}... | collective-permute-start | bytes 1572872 | tf_op jit(solution)/shard_map/ppermute | solution.py:73
  95.1 16.8 %collective-permute-start.12 = (bf16[4,128,512]{2,1,0:T(8,128)(2,1)S(1)}, bf16[4,128,512]{2,1,0:T(8,128)(2,1)}, u32[]{:S(2)}, u32[]{:S(2)}) collective-permute-start(bf16[4,128,512]{2,1,0:T(8,128)(2,1)S(1)} %bitcast_dynamic-update-slice_fusion.11), channel_id=1, source_target_pairs={{0,64},{32,96},{64,0},{96,32},{1,65},{33,97},{65,1},{97,33},{2,66}... | collective-permute-start | bytes 1572872 | tf_op jit(solution)/shard_map/ppermute | solution.py:73
  95.2 28.3 %collective-permute-start.13 = (bf16[4,128,512]{2,1,0:T(8,128)(2,1)S(1)}, bf16[4,128,512]{2,1,0:T(8,128)(2,1)S(1)}, u32[]{:S(2)}, u32[]{:S(2)}) collective-permute-start(bf16[4,128,512]{2,1,0:T(8,128)(2,1)S(1)} %bitcast_dynamic-update-slice_fusion.11), channel_id=1, source_target_pairs={{0,32},{32,64},{64,96},{96,0},{1,33},{33,65},{65,97},{97,1},{2,34}... | collective-permute-start | bytes 1572872 | tf_op jit(solution)/shard_map/ppermute | solution.py:73
  124.4 13.2 %collective-permute-start.14 = (bf16[2048,512]{1,0:T(8,128)(2,1)}, bf16[2048,512]{1,0:T(8,128)(2,1)}, u32[]{:S(2)}, u32[]{:S(2)}) collective-permute-start(bf16[2048,512]{1,0:T(8,128)(2,1)} %bitcast.20), channel_id=1, source_target_pairs={{0,1},{1,0},{2,3},{3,2},{4,5},{5,4},{6,7},{7,6},{8,9},{9,8},{10,11... | collective-permute-start | bytes 6291464 | tf_op jit(solution)/shard_map/ppermute | solution.py:69
  144.0 13.6 %collective-permute-start.15 = (bf16[512,512]{1,0:T(8,128)(2,1)S(1)}, bf16[512,512]{1,0:T(8,128)(2,1)S(1)}, u32[]{:S(2)}, u32[]{:S(2)}) collective-permute-start(bf16[512,512]{1,0:T(8,128)(2,1)S(1)} %get-tuple-element.139), channel_id=1, source_target_pairs={{0,24},{8,0},{16,8},{24,16},{1,25},{9,1},{17,9},{25,17},{2,26},{10... | collective-permute-start | bytes 1572872 | tf_op jit(solution)/shard_map/ppermute | solution.py:73
  144.6 14.7 %collective-permute-start.16 = (bf16[512,512]{1,0:T(8,128)(2,1)S(1)}, bf16[512,512]{1,0:T(8,128)(2,1)S(1)}, u32[]{:S(2)}, u32[]{:S(2)}) collective-permute-start(bf16[512,512]{1,0:T(8,128)(2,1)S(1)} %get-tuple-element.139), channel_id=1, source_target_pairs={{0,16},{8,24},{16,0},{24,8},{1,17},{9,25},{17,1},{25,9},{2,18},{10... | collective-permute-start | bytes 1572872 | tf_op jit(solution)/shard_map/ppermute | solution.py:73
  145.1 26.0 %collective-permute-start.17 = (bf16[512,512]{1,0:T(8,128)(2,1)S(1)}, bf16[512,512]{1,0:T(8,128)(2,1)S(1)}, u32[]{:S(2)}, u32[]{:S(2)}) collective-permute-start(bf16[512,512]{1,0:T(8,128)(2,1)S(1)} %get-tuple-element.139), channel_id=1, source_target_pairs={{0,8},{8,16},{16,24},{24,0},{1,9},{9,17},{17,25},{25,1},{2,10},{10... | collective-permute-start | bytes 1572872 | tf_op jit(solution)/shard_map/ppermute | solution.py:73
  171.4 47.4 %collective-permute-start.18 = (bf16[4,512,512]{2,1,0:T(8,128)(2,1)S(1)}, bf16[4,512,512]{2,1,0:T(8,128)(2,1)S(1)}, u32[]{:S(2)}, u32[]{:S(2)}) collective-permute-start(bf16[4,512,512]{2,1,0:T(8,128)(2,1)S(1)} %pad_maximum_fusion.1.refs_0_), channel_id=1, source_target_pairs={{0,32},{1,33},{32,0},{33,1},{64,96},{65,97},{96,64},{97,65},{2,34}... | collective-permute-start | bytes 6291464 | tf_op jit(solution)/shard_map/ppermute | solution.py:129
  173.3 67.9 %collective-permute-start.19 = (bf16[4,512,512]{2,1,0:T(8,128)(2,1)S(1)}, bf16[4,512,512]{2,1,0:T(8,128)(2,1)S(1)}, u32[]{:S(2)}, u32[]{:S(2)}) collective-permute-start(bf16[4,512,512]{2,1,0:T(8,128)(2,1)S(1)} %pad_maximum_fusion.1.refs_0_), channel_id=1, source_target_pairs={{1,64},{33,96},{3,66},{35,98},{5,68},{37,100},{7,70},{39,102},{9,7... | collective-permute-start | bytes 6291464 | tf_op jit(solution)/shard_map/ppermute | solution.py:128
  177.4 65.7 %collective-permute-start.20 = (bf16[4,512,512]{2,1,0:T(8,128)(2,1)S(1)}, bf16[4,512,512]{2,1,0:T(8,128)(2,1)S(1)}, u32[]{:S(2)}, u32[]{:S(2)}) collective-permute-start(bf16[4,512,512]{2,1,0:T(8,128)(2,1)S(1)} %pad_maximum_fusion.1.refs_0_), channel_id=1, source_target_pairs={{1,96},{33,64},{3,98},{35,66},{5,100},{37,68},{7,102},{39,70},{9,1... | collective-permute-start | bytes 6291464 | tf_op jit(solution)/shard_map/ppermute | solution.py:128
  247.3 471.2 %all-gather.9.cloned.1.call-start = ((), (), s32[]{:S(2)}) async-start(), calls=%async_computation.4 | async-start | bytes 8982528 | tf_op jit(solution)/shard_map/all_gather | solution.py:764
  249.4 14.7 %collective-permute-start.21 = (bf16[4,512,512]{2,1,0:T(8,128)(2,1)}, bf16[4,512,512]{2,1,0:T(8,128)(2,1)}, u32[]{:S(2)}, u32[]{:S(2)}) collective-permute-start(bf16[4,512,512]{2,1,0:T(8,128)(2,1)} %copy-done.1), channel_id=1, source_target_pairs={{0,1},{2,3},{4,5},{6,7},{8,9},{10,11},{12,13},{14,15},{16,17},{18,... | collective-permute-start | bytes 6291464 | tf_op jit(solution)/shard_map/ppermute | solution.py:130
  250.7 13.4 %collective-permute-start.22 = (bf16[4,512,512]{2,1,0:T(8,128)(2,1)}, bf16[4,512,512]{2,1,0:T(8,128)(2,1)}, u32[]{:S(2)}, u32[]{:S(2)}) collective-permute-start(bf16[4,512,512]{2,1,0:T(8,128)(2,1)} %copy-done.78), channel_id=1, source_target_pairs={{0,1},{2,3},{4,5},{6,7},{8,9},{10,11},{12,13},{14,15},{16,17},{18,... | collective-permute-start | bytes 6291464 | tf_op jit(solution)/shard_map/ppermute | solution.py:130
  280.8 12.2 %collective-permute-start.23 = (bf16[128,512]{1,0:T(8,128)(2,1)S(1)}, bf16[128,512]{1,0:T(8,128)(2,1)S(1)}, u32[]{:S(2)}, u32[]{:S(2)}) collective-permute-start(bf16[128,512]{1,0:T(8,128)(2,1)S(1)} %get-tuple-element.137), channel_id=1, source_target_pairs={{0,2},{2,4},{4,6},{6,0},{1,3},{3,5},{5,7},{7,1},{8,10},{10,12},{12... | collective-permute-start | bytes 393224 | tf_op jit(solution)/shard_map/ppermute | solution.py:73
  280.9 12.8 %collective-permute-start.24 = (bf16[128,512]{1,0:T(8,128)(2,1)S(1)}, bf16[128,512]{1,0:T(8,128)(2,1)S(1)}, u32[]{:S(2)}, u32[]{:S(2)}) collective-permute-start(bf16[128,512]{1,0:T(8,128)(2,1)S(1)} %get-tuple-element.136), channel_id=1, source_target_pairs={{0,4},{2,6},{4,0},{6,2},{1,5},{3,7},{5,1},{7,3},{8,12},{10,14},{12... | collective-permute-start | bytes 393224 | tf_op jit(solution)/shard_map/ppermute | solution.py:73
  281.9 14.8 %collective-permute-start.25 = (bf16[128,512]{1,0:T(8,128)(2,1)S(1)}, bf16[128,512]{1,0:T(8,128)(2,1)S(1)}, u32[]{:S(2)}, u32[]{:S(2)}) collective-permute-start(bf16[128,512]{1,0:T(8,128)(2,1)S(1)} %get-tuple-element.135), channel_id=1, source_target_pairs={{0,6},{2,0},{4,2},{6,4},{1,7},{3,1},{5,3},{7,5},{8,14},{10,8},{12,... | collective-permute-start | bytes 393224 | tf_op jit(solution)/shard_map/ppermute | solution.py:73
  308.5 29.5 %collective-permute-start.26 = (bf16[128,2048]{1,0:T(8,128)(2,1)S(1)}, bf16[128,2048]{1,0:T(8,128)(2,1)S(1)}, u32[]{:S(2)}, u32[]{:S(2)}) collective-permute-start(bf16[128,2048]{1,0:T(8,128)(2,1)S(1)} %multiply_convert_fusion.1), channel_id=1, source_target_pairs={{0,24},{8,0},{16,8},{24,16},{1,25},{9,1},{17,9},{25,17},{2,26},{10... | collective-permute-start | bytes 1572872 | tf_op jit(solution)/shard_map/ppermute | solution.py:73
  316.0 22.0 %collective-permute-start.27 = (bf16[128,2048]{1,0:T(8,128)(2,1)S(1)}, bf16[128,2048]{1,0:T(8,128)(2,1)S(1)}, u32[]{:S(2)}, u32[]{:S(2)}) collective-permute-start(bf16[128,2048]{1,0:T(8,128)(2,1)S(1)} %multiply_convert_fusion.1), channel_id=1, source_target_pairs={{0,16},{8,24},{16,0},{24,8},{1,17},{9,25},{17,1},{25,9},{2,18},{10... | collective-permute-start | bytes 1572872 | tf_op jit(solution)/shard_map/ppermute | solution.py:73
  316.0 26.3 %collective-permute-start.28 = (bf16[128,2048]{1,0:T(8,128)(2,1)S(1)}, bf16[128,2048]{1,0:T(8,128)(2,1)S(1)}, u32[]{:S(2)}, u32[]{:S(2)}) collective-permute-start(bf16[128,2048]{1,0:T(8,128)(2,1)S(1)} %multiply_convert_fusion.1), channel_id=1, source_target_pairs={{0,8},{8,16},{16,24},{24,0},{1,9},{9,17},{17,25},{25,1},{2,10},{10... | collective-permute-start | bytes 1572872 | tf_op jit(solution)/shard_map/ppermute | solution.py:73
  393.9 16.8 %collective-permute-start.29 = (bf16[128,2432]{1,0:T(8,128)(2,1)}, bf16[128,2432]{1,0:T(8,128)(2,1)}, u32[]{:S(2)}, u32[]{:S(2)}) collective-permute-start(bf16[128,2432]{1,0:T(8,128)(2,1)} %get-tuple-element.90), channel_id=1, source_target_pairs={{0,16},{8,24},{16,0},{24,8},{1,17},{9,25},{17,1},{25,9},{2,18},{10... | collective-permute-start | bytes 1867784 | tf_op jit(solution)/shard_map/ppermute | solution.py:73
  394.3 30.7 %collective-permute-start.30 = (bf16[128,2432]{1,0:T(8,128)(2,1)}, bf16[128,2432]{1,0:T(8,128)(2,1)}, u32[]{:S(2)}, u32[]{:S(2)}) collective-permute-start(bf16[128,2432]{1,0:T(8,128)(2,1)} %get-tuple-element.92), channel_id=1, source_target_pairs={{0,8},{8,16},{16,24},{24,0},{1,9},{9,17},{17,25},{25,1},{2,10},{10... | collective-permute-start | bytes 1867784 | tf_op jit(solution)/shard_map/ppermute | solution.py:73
  394.3 30.7 %collective-permute-start.31 = (bf16[128,2432]{1,0:T(8,128)(2,1)}, bf16[128,2432]{1,0:T(8,128)(2,1)}, u32[]{:S(2)}, u32[]{:S(2)}) collective-permute-start(bf16[128,2432]{1,0:T(8,128)(2,1)} %get-tuple-element.91), channel_id=1, source_target_pairs={{0,24},{8,0},{16,8},{24,16},{1,25},{9,1},{17,9},{25,17},{2,26},{10... | collective-permute-start | bytes 1867784 | tf_op jit(solution)/shard_map/ppermute | solution.py:73
  470.9 11.0 %collective-permute-start.67 = (bf16[128,384]{1,0:T(8,128)(2,1)S(1)}, bf16[128,384]{1,0:T(8,128)(2,1)S(1)}, u32[]{:S(2)}, u32[]{:S(2)}) collective-permute-start(bf16[128,384]{1,0:T(8,128)(2,1)S(1)} %maximum_add_fusion.3), channel_id=1, source_target_pairs={{0,24},{8,0},{16,8},{24,16},{1,25},{9,1},{17,9},{25,17},{2,26},{10... | collective-permute-start | bytes 294920 | tf_op jit(solution)/shard_map/ppermute | solution.py:73
  481.7 12.5 %collective-permute-start.65 = (bf16[512,256]{0,1:T(8,128)(2,1)S(1)}, bf16[512,256]{0,1:T(8,128)(2,1)S(1)}, u32[]{:S(2)}, u32[]{:S(2)}) collective-permute-start(bf16[512,256]{0,1:T(8,128)(2,1)S(1)} %get-tuple-element.107), channel_id=1, source_target_pairs={{0,8},{8,16},{16,24},{24,0},{1,9},{9,17},{17,25},{25,1},{2,10},{10... | collective-permute-start | bytes 786440 | tf_op jit(solution)/shard_map/ppermute | solution.py:73
  482.0 12.3 %collective-permute-start.66 = (bf16[512,256]{0,1:T(8,128)(2,1)S(1)}, bf16[512,256]{0,1:T(8,128)(2,1)S(1)}, u32[]{:S(2)}, u32[]{:S(2)}) collective-permute-start(bf16[512,256]{0,1:T(8,128)(2,1)S(1)} %get-tuple-element.106), channel_id=1, source_target_pairs={{0,24},{8,0},{16,8},{24,16},{1,25},{9,1},{17,9},{25,17},{2,26},{10... | collective-permute-start | bytes 786440 | tf_op jit(solution)/shard_map/ppermute | solution.py:73
  516.2 12.3 %collective-permute-start.71 = (bf16[4,272,128]{2,1,0:T(8,128)(2,1)}, bf16[4,272,128]{2,1,0:T(8,128)(2,1)}, u32[]{:S(2)}, u32[]{:S(2)}) collective-permute-start(bf16[4,272,128]{2,1,0:T(8,128)(2,1)} %get-tuple-element.93), channel_id=1, source_target_pairs={{0,32},{32,64},{64,96},{96,0},{1,33},{33,65},{65,97},{97,1},{2,34}... | collective-permute-start | bytes 835592 | tf_op jit(solution)/shard_map/ppermute | solution.py:73
  522.2 12.6 %collective-permute-start.72 = (bf16[4,272,128]{2,1,0:T(8,128)(2,1)S(1)}, bf16[4,272,128]{2,1,0:T(8,128)(2,1)}, u32[]{:S(2)}, u32[]{:S(2)}) collective-permute-start(bf16[4,272,128]{2,1,0:T(8,128)(2,1)S(1)} %get-tuple-element.95), channel_id=1, source_target_pairs={{0,64},{32,96},{64,0},{96,32},{1,65},{33,97},{65,1},{97,33},{2,66}... | collective-permute-start | bytes 835592 | tf_op jit(solution)/shard_map/ppermute | solution.py:73
  522.3 13.0 %collective-permute-start.73 = (bf16[4,272,128]{2,1,0:T(8,128)(2,1)S(1)}, bf16[4,272,128]{2,1,0:T(8,128)(2,1)}, u32[]{:S(2)}, u32[]{:S(2)}) collective-permute-start(bf16[4,272,128]{2,1,0:T(8,128)(2,1)S(1)} %get-tuple-element.94), channel_id=1, source_target_pairs={{0,96},{32,0},{64,32},{96,64},{1,97},{33,1},{65,33},{97,65},{2,98}... | collective-permute-start | bytes 835592 | tf_op jit(solution)/shard_map/ppermute | solution.py:73
  547.5 18.7 %collective-permute-start.35 = (bf16[4,512,512]{2,1,0:T(8,128)(2,1)}, bf16[4,512,512]{2,1,0:T(8,128)(2,1)}, u32[]{:S(2)}, u32[]{:S(2)}) collective-permute-start(bf16[4,512,512]{2,1,0:T(8,128)(2,1)} %get-tuple-element.55), channel_id=1, source_target_pairs={{1,0},{3,2},{5,4},{7,6},{9,8},{11,10},{13,12},{15,14},{17,16},{19,... | collective-permute-start | bytes 6291464 | tf_op jit(solution)/shard_map/ppermute | solution.py:135
  550.1 49.8 %collective-permute-start.38 = (bf16[4,512,512]{2,1,0:T(8,128)(2,1)}, bf16[4,512,512]{2,1,0:T(8,128)(2,1)}, u32[]{:S(2)}, u32[]{:S(2)}) collective-permute-start(bf16[4,512,512]{2,1,0:T(8,128)(2,1)} %get-tuple-element.55), channel_id=1, source_target_pairs={{64,1},{96,33},{66,3},{98,35},{68,5},{100,37},{70,7},{102,39},{72,... | collective-permute-start | bytes 6291464 | tf_op jit(solution)/shard_map/ppermute | solution.py:136
  551.4 62.9 %collective-permute-start.39 = (bf16[4,512,512]{2,1,0:T(8,128)(2,1)}, bf16[4,512,512]{2,1,0:T(8,128)(2,1)}, u32[]{:S(2)}, u32[]{:S(2)}) collective-permute-start(bf16[4,512,512]{2,1,0:T(8,128)(2,1)} %get-tuple-element.57), channel_id=1, source_target_pairs={{96,1},{64,33},{98,3},{66,35},{100,5},{68,37},{102,7},{70,39},{104... | collective-permute-start | bytes 6291464 | tf_op jit(solution)/shard_map/ppermute | solution.py:136
  556.3 62.0 %collective-permute-start.37 = (bf16[4,512,512]{2,1,0:T(8,128)(2,1)}, bf16[4,512,512]{2,1,0:T(8,128)(2,1)}, u32[]{:S(2)}, u32[]{:S(2)}) collective-permute-start(bf16[4,512,512]{2,1,0:T(8,128)(2,1)} %add_convert_fusion.1), channel_id=1, source_target_pairs={{0,32},{1,33},{32,0},{33,1},{64,96},{65,97},{96,64},{97,65},{2,34}... | collective-permute-start | bytes 6291464 | tf_op jit(solution)/shard_map/ppermute | solution.py:138
  626.6 15.7 %collective-permute-start.40 = (bf16[512,512]{1,0:T(8,128)(2,1)}, bf16[512,512]{1,0:T(8,128)(2,1)}, u32[]{:S(2)}, u32[]{:S(2)}) collective-permute-start(bf16[512,512]{1,0:T(8,128)(2,1)} %get-tuple-element.102), channel_id=1, source_target_pairs={{0,16},{8,24},{16,0},{24,8},{1,17},{9,25},{17,1},{25,9},{2,18},{10... | collective-permute-start | bytes 1572872 | tf_op jit(solution)/shard_map/ppermute | solution.py:73
  626.6 26.6 %collective-permute-start.41 = (bf16[512,512]{1,0:T(8,128)(2,1)}, bf16[512,512]{1,0:T(8,128)(2,1)}, u32[]{:S(2)}, u32[]{:S(2)}) collective-permute-start(bf16[512,512]{1,0:T(8,128)(2,1)} %get-tuple-element.104), channel_id=1, source_target_pairs={{0,8},{8,16},{16,24},{24,0},{1,9},{9,17},{17,25},{25,1},{2,10},{10... | collective-permute-start | bytes 1572872 | tf_op jit(solution)/shard_map/ppermute | solution.py:73
  626.7 26.6 %collective-permute-start.42 = (bf16[512,512]{1,0:T(8,128)(2,1)}, bf16[512,512]{1,0:T(8,128)(2,1)}, u32[]{:S(2)}, u32[]{:S(2)}) collective-permute-start(bf16[512,512]{1,0:T(8,128)(2,1)} %get-tuple-element.103), channel_id=1, source_target_pairs={{0,24},{8,0},{16,8},{24,16},{1,25},{9,1},{17,9},{25,17},{2,26},{10... | collective-permute-start | bytes 1572872 | tf_op jit(solution)/shard_map/ppermute | solution.py:73
  658.4 12.1 %collective-permute-start.46 = (bf16[128,384]{0,1:T(8,128)(2,1)}, bf16[128,384]{0,1:T(8,128)(2,1)}, u32[]{:S(2)}, u32[]{:S(2)}) collective-permute-start(bf16[128,384]{0,1:T(8,128)(2,1)} %get-tuple-element.146), channel_id=1, source_target_pairs={{0,4},{2,6},{4,0},{6,2},{1,5},{3,7},{5,1},{7,3},{8,12},{10,14},{12... | collective-permute-start | bytes 294920 | tf_op jit(solution)/shard_map/ppermute | solution.py:73
  658.4 12.1 %collective-permute-start.47 = (bf16[128,384]{0,1:T(8,128)(2,1)}, bf16[128,384]{0,1:T(8,128)(2,1)}, u32[]{:S(2)}, u32[]{:S(2)}) collective-permute-start(bf16[128,384]{0,1:T(8,128)(2,1)} %get-tuple-element.148), channel_id=1, source_target_pairs={{0,2},{2,4},{4,6},{6,0},{1,3},{3,5},{5,7},{7,1},{8,10},{10,12},{12... | collective-permute-start | bytes 294920 | tf_op jit(solution)/shard_map/ppermute | solution.py:73
  684.3 19.4 %collective-permute-start.43 = (bf16[128,2048]{1,0:T(8,128)(2,1)S(1)}, bf16[128,2048]{1,0:T(8,128)(2,1)S(1)}, u32[]{:S(2)}, u32[]{:S(2)}) collective-permute-start(bf16[128,2048]{1,0:T(8,128)(2,1)S(1)} %get-tuple-element.99), channel_id=1, source_target_pairs={{0,4},{2,6},{4,0},{6,2},{1,5},{3,7},{5,1},{7,3},{8,12},{10,14},{12... | collective-permute-start | bytes 1572872 | tf_op jit(solution)/shard_map/ppermute | solution.py:73
  685.4 27.4 %collective-permute-start.44 = (bf16[128,2048]{1,0:T(8,128)(2,1)S(1)}, bf16[128,2048]{1,0:T(8,128)(2,1)S(1)}, u32[]{:S(2)}, u32[]{:S(2)}) collective-permute-start(bf16[128,2048]{1,0:T(8,128)(2,1)S(1)} %get-tuple-element.101), channel_id=1, source_target_pairs={{0,2},{2,4},{4,6},{6,0},{1,3},{3,5},{5,7},{7,1},{8,10},{10,12},{12... | collective-permute-start | bytes 1572872 | tf_op jit(solution)/shard_map/ppermute | solution.py:73
  685.4 27.4 %collective-permute-start.45 = (bf16[128,2048]{1,0:T(8,128)(2,1)S(1)}, bf16[128,2048]{1,0:T(8,128)(2,1)S(1)}, u32[]{:S(2)}, u32[]{:S(2)}) collective-permute-start(bf16[128,2048]{1,0:T(8,128)(2,1)S(1)} %get-tuple-element.100), channel_id=1, source_target_pairs={{0,6},{2,0},{4,2},{6,4},{1,7},{3,1},{5,3},{7,5},{8,14},{10,8},{12,... | collective-permute-start | bytes 1572872 | tf_op jit(solution)/shard_map/ppermute | solution.py:73
  688.2 26.3 %collective-permute-start.58 = (bf16[4,80,128]{2,1,0:T(8,128)(2,1)S(1)}, bf16[4,80,128]{2,1,0:T(8,128)(2,1)S(1)}, u32[]{:S(2)}, u32[]{:S(2)}) collective-permute-start(bf16[4,80,128]{2,1,0:T(8,128)(2,1)S(1)} %get-tuple-element.115), channel_id=1, source_target_pairs={{0,32},{32,64},{64,96},{96,0},{1,33},{33,65},{65,97},{97,1},{2,34}... | collective-permute-start | bytes 245768 | tf_op jit(solution)/shard_map/ppermute | solution.py:73
  690.7 23.8 %collective-permute-start.59 = (bf16[4,80,128]{2,1,0:T(8,128)(2,1)S(1)}, bf16[4,80,128]{2,1,0:T(8,128)(2,1)S(1)}, u32[]{:S(2)}, u32[]{:S(2)}) collective-permute-start(bf16[4,80,128]{2,1,0:T(8,128)(2,1)S(1)} %get-tuple-element.117), channel_id=1, source_target_pairs={{0,64},{32,96},{64,0},{96,32},{1,65},{33,97},{65,1},{97,33},{2,66}... | collective-permute-start | bytes 245768 | tf_op jit(solution)/shard_map/ppermute | solution.py:73
  714.6 20.5 %collective-permute-start.61 = (bf16[80,128]{1,0:T(8,128)(2,1)S(1)}, bf16[80,128]{1,0:T(8,128)(2,1)S(1)}, u32[]{:S(2)}, u32[]{:S(2)}) collective-permute-start(bf16[80,128]{1,0:T(8,128)(2,1)S(1)} %get-tuple-element.154), channel_id=1, source_target_pairs={{0,8},{8,16},{16,24},{24,0},{1,9},{9,17},{17,25},{25,1},{2,10},{10... | collective-permute-start | bytes 61448 | tf_op jit(solution)/shard_map/ppermute | solution.py:73
  714.7 20.4 %collective-permute-start.62 = (bf16[80,128]{1,0:T(8,128)(2,1)S(1)}, bf16[80,128]{1,0:T(8,128)(2,1)S(1)}, u32[]{:S(2)}, u32[]{:S(2)}) collective-permute-start(bf16[80,128]{1,0:T(8,128)(2,1)S(1)} %get-tuple-element.156), channel_id=1, source_target_pairs={{0,16},{8,24},{16,0},{24,8},{1,17},{9,25},{17,1},{25,9},{2,18},{10... | collective-permute-start | bytes 61448 | tf_op jit(solution)/shard_map/ppermute | solution.py:73
  716.8 18.3 %collective-permute-start.63 = (bf16[80,128]{1,0:T(8,128)(2,1)S(1)}, bf16[80,128]{1,0:T(8,128)(2,1)S(1)}, u32[]{:S(2)}, u32[]{:S(2)}) collective-permute-start(bf16[80,128]{1,0:T(8,128)(2,1)S(1)} %get-tuple-element.155), channel_id=1, source_target_pairs={{0,24},{8,0},{16,8},{24,16},{1,25},{9,1},{17,9},{25,17},{2,26},{10... | collective-permute-start | bytes 61448 | tf_op jit(solution)/shard_map/ppermute | solution.py:73
  736.2 67.3 %collective-permute-start.49 = (bf16[128,2048]{1,0:T(8,128)(2,1)}, bf16[128,2048]{1,0:T(8,128)(2,1)S(1)}, u32[]{:S(2)}, u32[]{:S(2)}) collective-permute-start(bf16[128,2048]{1,0:T(8,128)(2,1)} %get-tuple-element.96), channel_id=1, source_target_pairs={{0,16},{8,24},{16,0},{24,8},{1,17},{9,25},{17,1},{25,9},{2,18},{10... | collective-permute-start | bytes 1572872 | tf_op jit(solution)/shard_map/ppermute | solution.py:73
  738.2 65.3 %collective-permute-start.50 = (bf16[128,2048]{1,0:T(8,128)(2,1)}, bf16[128,2048]{1,0:T(8,128)(2,1)S(1)}, u32[]{:S(2)}, u32[]{:S(2)}) collective-permute-start(bf16[128,2048]{1,0:T(8,128)(2,1)} %get-tuple-element.98), channel_id=1, source_target_pairs={{0,8},{8,16},{16,24},{24,0},{1,9},{9,17},{17,25},{25,1},{2,10},{10... | collective-permute-start | bytes 1572872 | tf_op jit(solution)/shard_map/ppermute | solution.py:73
  738.7 64.8 %collective-permute-start.51 = (bf16[128,2048]{1,0:T(8,128)(2,1)}, bf16[128,2048]{1,0:T(8,128)(2,1)S(1)}, u32[]{:S(2)}, u32[]{:S(2)}) collective-permute-start(bf16[128,2048]{1,0:T(8,128)(2,1)} %get-tuple-element.97), channel_id=1, source_target_pairs={{0,24},{8,0},{16,8},{24,16},{1,25},{9,1},{17,9},{25,17},{2,26},{10... | collective-permute-start | bytes 1572872 | tf_op jit(solution)/shard_map/ppermute | solution.py:73
  740.9 19.2 %collective-permute-start.78 = (bf16[80,128]{1,0:T(8,128)(2,1)S(1)}, bf16[80,128]{1,0:T(8,128)(2,1)S(1)}, u32[]{:S(2)}, u32[]{:S(2)}) collective-permute-start(bf16[80,128]{1,0:T(8,128)(2,1)S(1)} %get-tuple-element.79), channel_id=1, source_target_pairs={{0,16},{8,24},{16,0},{24,8},{1,17},{9,25},{17,1},{25,9},{2,18},{10... | collective-permute-start | bytes 61448 | tf_op jit(solution)/shard_map/ppermute | solution.py:73
  740.9 22.8 %collective-permute-start.79 = (bf16[80,128]{1,0:T(8,128)(2,1)S(1)}, bf16[80,128]{1,0:T(8,128)(2,1)S(1)}, u32[]{:S(2)}, u32[]{:S(2)}) collective-permute-start(bf16[80,128]{1,0:T(8,128)(2,1)S(1)} %get-tuple-element.79), channel_id=1, source_target_pairs={{0,8},{8,16},{16,24},{24,0},{1,9},{9,17},{17,25},{25,1},{2,10},{10... | collective-permute-start | bytes 61448 | tf_op jit(solution)/shard_map/ppermute | solution.py:73
  763.6 13.6 %collective-permute-start.80 = (bf16[4,80,128]{2,1,0:T(8,128)(2,1)S(1)}, bf16[4,80,128]{2,1,0:T(8,128)(2,1)S(1)}, u32[]{:S(2)}, u32[]{:S(2)}) collective-permute-start(bf16[4,80,128]{2,1,0:T(8,128)(2,1)S(1)} %bitcast_dynamic-update-slice_fusion.19), channel_id=1, source_target_pairs={{0,96},{32,0},{64,32},{96,64},{1,97},{33,1},{65,33},{97,65},{2,98}... | collective-permute-start | bytes 245768 | tf_op jit(solution)/shard_map/ppermute | solution.py:73
  (111 other events, 1738.2 us)
Sparse Core Ops, SparseCore 0:
  11.1 106.0 all-gather.4
  247.5 95.2 all-gather.6
  543.6 79.1 all-gather.8

commit v2 on v1

--- a/solution.py
+++ b/solution.py
@@ -131,15 +131,16 @@
     return line, partner, ahead[0], ahead[1], beside[0], beside[1]
 
 
-def sum_row(own, own_partner, prev, prev_partner):
+def sum_row(own, own_partner, prev, prev_partner, beside):
     got = [lax.ppermute(value, "c", [(1, 0)]) for value in (prev_partner, prev)]
     terms = [lax.ppermute(value, CORNER, pairs) for value, pairs in zip((prev, prev_partner), EARLIER)]
     sent = (own_partner.astype(f32) + got[0].astype(f32)).astype(bf16)
     terms = [got[1], lax.ppermute(sent, CORNER, PARTNER)] + terms
+    start = zero_of(sent)
     line = own.astype(f32)
     for term in terms:
         line = line + term.astype(f32)
-    sent = line.astype(bf16)
+    sent = (line + beside(start)).astype(bf16)
     total = line[0]
     for step in (2, 1, 3):
         total = total + shift(sent[step], "x", step).astype(f32)
@@ -343,9 +344,7 @@
     pick_ref,
     result_ref,
     back_ref,
-    gge_ref,
-    gue_ref,
-    gds_ref,
+    units_ref,
     nmp,
     result,
     grad,
@@ -381,9 +380,9 @@
     low[:, :rank] += times_transposed(grad_gate, ge)
     low[:, rank : 2 * rank] += times_transposed(grad_up, ue)
     low[:, 2 * rank :] += product(active_units, ds)
-    gge_ref[0] = inner_rows(grad_gate, low_gate)
-    gue_ref[0] = inner_rows(grad_up, low_up)
-    gds_ref[0] = inner_rows(active_units, gld_ref[...])
+    units_ref[0, :, 0, :64] = inner_rows(grad_gate, low_gate).reshape(4, 64, rank)
+    units_ref[0, :, 0, 64:128] = inner_rows(grad_up, low_up).reshape(4, 64, rank)
+    units_ref[0, :, 0, 128:] = inner_rows(active_units, gld_ref[...]).reshape(4, 64, rank)
 
     @pl.when(step == 2 * UNITS // CHUNK - 1)
     def _():
@@ -397,7 +396,7 @@
 def feed_forward(at, normed_mid, cot, low_gu, grad_low_down, weights, expands, perm, picks):
     rank = low_gu.shape[1] // 2
     steps = UNITS // CHUNK
-    unit_spec = pl.BlockSpec((1, CHUNK, rank), lambda i, at: (i // steps, i % steps, 0))
+    unit_spec = pl.BlockSpec((1, 4, 1, 192, rank), lambda i, at: (i % steps, 0, i // steps, 0, 0))
     return pl.pallas_call(
         ffn_kernel,
         grid_spec=pltpu.PrefetchScalarGridSpec(
@@ -417,7 +416,7 @@
                 whole((GROUP, GROUP)),
                 pl.BlockSpec((1, 2 * CHUNK, CHUNK), lambda i, at: (i // steps, 0, 0)),
             ],
-            out_specs=[whole((GROUP, 2048)), whole((GROUP, 2048 + 3 * rank)), unit_spec, unit_spec, unit_spec],
+            out_specs=[whole((GROUP, 2048)), whole((GROUP, 2048 + 3 * rank)), unit_spec],
             scratch_shapes=[
                 pltpu.VMEM((GROUP, 2048), bf16),
                 pltpu.VMEM((GROUP, 2048), f32),
@@ -428,8 +427,8 @@
         out_shape=[
             jax.ShapeDtypeStruct((GROUP, 2048), bf16),
             jax.ShapeDtypeStruct((GROUP, 2048 + 3 * rank), bf16),
-        ]
-        + [jax.ShapeDtypeStruct((2, UNITS, rank), f32)] * 3,
+            jax.ShapeDtypeStruct((4, 4, 2, 192, rank), f32),
+        ],
         compiler_params=pltpu.CompilerParams(vmem_limit_bytes=60 << 20),
         cost_estimate=pl.CostEstimate(flops=28 << 30, bytes_accessed=40 << 20, transcendentals=2 << 20),
         name="feed_forward",
@@ -461,9 +460,6 @@
 
 
 def unpack_early(everyone):
-    def rows_at(i):
-        return (i % 4) * 4 + i // 4
-
     return pl.pallas_call(
         early_kernel,
         grid=(16,),
@@ -472,10 +468,10 @@
             pl.BlockSpec((128, 512), lambda i: (0, i)),
             pl.BlockSpec((128, 512), lambda i: (0, i)),
             pl.BlockSpec((512, 128), lambda i: (i, 0)),
-            pl.BlockSpec((128, 128), lambda i: (rows_at(i), 0)),
-            pl.BlockSpec((128, 128), lambda i: (0, rows_at(i))),
-            pl.BlockSpec((128, 128), lambda i: (0, rows_at(i))),
-            pl.BlockSpec((128, 256), lambda i: (rows_at(i), 0)),
+            pl.BlockSpec((128, 128), lambda i: (i, 0)),
+            pl.BlockSpec((128, 128), lambda i: (0, i)),
+            pl.BlockSpec((128, 128), lambda i: (0, i)),
+            pl.BlockSpec((128, 256), lambda i: (i, 0)),
         ],
         out_shape=[
             jax.ShapeDtypeStruct(shape, f32)
@@ -589,9 +585,11 @@
         owner = jnp.sum(inside.astype(jnp.int32) * adapter[None, :], axis=1)
         return (owner[:, None] == (jnp.arange(rank, dtype=jnp.int32) // RANK)[None, :]).astype(f32)
 
-    tile_low, tile_high = jnp.min(tiles_pos, axis=1), jnp.max(tiles_pos, axis=1)
-    active = (tile_low <= jnp.max(group_pos)) & (tile_high >= jnp.min(group_start))
-    active = step_tables(active.astype(jnp.int32), c)
+    key_runs, pos_runs, start_runs = tiles_pos.reshape(64, 128), group_pos.reshape(4, 128), group_start.reshape(4, 128)
+    key_low, key_high = jnp.min(key_runs, axis=1)[:, None], jnp.max(key_runs, axis=1)[:, None]
+    seen = (key_low <= jnp.max(pos_runs, axis=1)[None, :]) & (key_high >= jnp.min(start_runs, axis=1)[None, :])
+    active = jnp.max(seen.astype(jnp.int32).reshape(16, 16), axis=1)
+    active = step_tables(active, c)
     select_y = selected(group_pos)
     select_x = selected(own_row.reshape(2, 4, 4, 128)[0, :, 0].reshape(GROUP))
     select = select_y[:128]
@@ -636,7 +634,7 @@
     key = (key_heads * cos_table + rotate(key_heads) * sin_table).astype(bf16).reshape(GROUP, 256)
 
     lines = gather_row(jnp.concatenate([key, value_lin.astype(bf16)], axis=1))
-    waited = zero_of(lines[1]) + zero_of(lines[2]) + zero_of(lines[3]) + zero_of(wo)
+    waited = zero_of(lines[1]) + zero_of(lines[2]) + zero_of(lines[3]) + zero_of(lines[4]) + zero_of(wo)
     ffn = jnp.concatenate([gate_up, w_down], axis=0) + waited.astype(bf16)
     ffn = lax.all_gather(ffn, OVER_X, axis=0, tiled=False).reshape(16, 2, 192, 2048)
     attended = (query, group_pos[:, None], group_start[:, None], tiles_pos.reshape(16, 1, GROUP)) + lines
@@ -665,7 +663,7 @@
     picks = jnp.stack(
         [(wide[:, None] == (narrow // 64 * 128 + core * 64 + narrow % 64)[None, :]).astype(bf16) for core in (0, 1)]
     )
-    result, back_part, *unit_grads = feed_forward(
+    result, back_part, unit_grads = feed_forward(
         x.reshape(1).astype(jnp.int32),
         normed_mid_g,
         cot_g,
@@ -701,7 +699,16 @@
 
     dout = slices_near(grad_mixed)
     dq, *terms = attend_back(active, *attended, mixed_f, lse, dout)
-    dkv = sum_row(*terms)
+    unit_sum = lax.psum_scatter(
+        unit_grads.reshape(32, 192, rank), OVER_X, scatter_dimension=0, tiled=False
+    )
+    aheads = []
+
+    def beside(start):
+        aheads.append(sum_tokens(result + start.astype(bf16), "x"))
+        return zero_of(aheads[0]) + zero_of(unit_sum)
+
+    dkv = sum_row(*terms, beside)
     dk, dv = dkv[:, :HEAD_SIZE], dkv[:, HEAD_SIZE:]
     query_back = (dq * factor).astype(bf16).astype(f32).reshape(GROUP, 2, HEAD_SIZE)
     key_back = dk.astype(bf16).astype(f32).reshape(GROUP, 1, HEAD_SIZE)
@@ -723,8 +730,7 @@
     for_other = jnp.where(c == 0, grad_kv, grad_query)
     grad_normed_part = times_transposed(for_mine, qkv_mine) + times_transposed(for_other, qkv_other)
     grad_normed = sum_tokens(grad_normed_part, "y") + times_transposed(grad_low_qkv, qkv_shrink)
-    ahead = sum_tokens(after(result, grad_normed), "x")
-    output = (middle + ahead + product(low_down, down_expand)).astype(bf16)
+    output = (middle + aheads[0] + product(low_down, down_expand)).astype(bf16)
     grad_input = (grad_middle + norm_back(inputs, scale_in, gain_attn, grad_normed)).astype(bf16)
 
     def features(array, at):
@@ -739,28 +745,16 @@
         terms = kept + swap_cores(given.astype(bf16)).astype(f32)
         return sum_ring(sum_ring(terms.reshape(4, 4, -1, rank), "z"), ring)
 
-    attended_back = zero_of(dq)
-    low_near = jnp.concatenate([low_down, grad_low_gu], axis=1) + attended_back.astype(bf16)
-    low_near = gather_near(low_near, "x")
-    grad_gateup = inner_rows(features(normed_mid_g, x), low_near[:, rank:])
-    out_terms = jnp.concatenate([inner_rows(mixed_tok, grad_low_out), inner_rows(grad_attn_out, low_out)], axis=1)
-    out_terms = (out_terms + attended_back).astype(bf16).reshape(4, 512, 2 * rank)
-    out_terms = sum_near(
-        [lax.dynamic_index_in_dim(out_terms, (x + step) % 4, 0, keepdims=False) for step in range(4)], "x"
-    )
-    kept, other = by_cores(
-        [
-            out_terms[:, :rank],
-            out_terms[:, rank:],
-            inner_rows(features(cot_g, x), low_near[:, :rank]),
-            grad_gateup[:, :rank],
-            grad_gateup[:, rank:],
-        ]
-    )
-    unit_grads = jnp.concatenate([array.reshape(2, 16, 64, rank) for array in unit_grads], axis=2)
-    kept = jnp.concatenate([lax.dynamic_index_in_dim(unit_grads, c, 0, keepdims=False), kept], axis=1)
-    other = jnp.concatenate([lax.dynamic_index_in_dim(unit_grads, 1 - c, 0, keepdims=False), other], axis=1)
-    early_sum = sum_plane(kept, other, "y").astype(bf16)
+    row_terms = [
+        inner_rows(mixed_tok, grad_low_out),
+        inner_rows(grad_attn_out, low_out),
+        inner_rows(cot, low_down),
+        inner_rows(normed_mid, grad_low_gu[:, :rank]),
+        inner_rows(normed_mid, grad_low_gu[:, rank:]),
+    ]
+    row_terms = jnp.concatenate([array.reshape(128, 16, rank) for array in row_terms], axis=1)
+    row_sum = lax.psum_scatter(row_terms, ALL, scatter_dimension=0, tiled=False)
+    early_sum = (jnp.concatenate([unit_sum, row_sum], axis=0) + zero_of(dkv)).astype(bf16)
     early_all = lax.all_gather(early_sum, ALL, axis=0, tiled=False)
 
     grad_qkv = inner_rows(features(normed_g, y), gather_near(grad_low_qkv, "y"))
@@ -775,8 +769,9 @@
         ]
     )
     g_gate, g_up, g_down_shrink, g_out_shrink, g_out_expand, g_down_expand, g_gateup = unpack_early(early_all)
-    late_sum = (sum_plane(kept, other, "x") + zero_of(g_gateup)).astype(bf16)
-    late_all = gather_ring(gather_ring(gather_ring(late_sum, "x"), "z"), "y")
+    late_sum = sum_plane(kept, other, "x").astype(bf16)
+    late_all = gather_ring(gather_ring(late_sum, "x"), "z") + zero_of(g_gateup).astype(bf16)
+    late_all = gather_ring(late_all, "y")
     late_all = late_all.reshape(4, 16, -1, rank)
     late_other = swap_cores(late_all)
     g_q, g_k, g_v, g_qkv = unpack_late(c.reshape(1).astype(jnp.int32), late_all, late_other)

time: 835 us -> 1290 us (1.54)
  waiting for transfers between devices: 352 us -> 854 us
  local copies, waits for them, and re-layouts: 80 us -> 63.5 us
  starting transfers between devices: 161 us -> 147 us
    reduce_scatter x0 -> x2, waiting for transfers between devices: none -> 545 us  [the longest x1 545 us: local(): row_sum = lax.psum_scatter(row_terms, ALL, scatter_dimension=0, tiled=False)]
    ppermute x2, waiting for transfers between devices: 48.1 us -> 0.01 us  [sum_row(): lax.ppermute(value, CORNER, pairs)]
    ppermute x69 -> x57, starting transfers between devices: 119 us -> 98.4 us  [shift(): lax.ppermute(value, RING[ring], [(i, (i + step) % 4) for i in range(4)])]
    ppermute x69 -> x57, waiting for transfers between devices: 229 us -> 239 us  [shift(): lax.ppermute(value, RING[ring], [(i, (i + step) % 4) for i in range(4)])]
  transfers between devices with their start and end apart: 92 -> 81, of which waited for: 50 -> 47; matrix products, arithmetic and copies ran while one was open for 17% -> 12% of each run, Pallas kernels for 4% -> 4%
where the time goes in v2:
time: 1290 us; the launch traced here: 1280 us
  waiting for transfers between devices  854 us (66%)
  starting transfers between devices  147 us (11%)
  Pallas kernels  98.4 us (8%)
  local copies, waits for them, and re-layouts  63.5 us (5%)
  matrix products  55.5 us (4%)
  other arithmetic  42 us (3%)
  between operations  23.2 us (2%)
    reduce_scatter x1, waiting for transfers between devices, local(): row_sum = lax.psum_scatter(row_terms, ALL, scatter_dimension=0, tiled=False)  545 us
    ppermute x57, waiting for transfers between devices, shift(): lax.ppermute(value, RING[ring], [(i, (i + step) % 4) for i in range(4)])  239 us
    ppermute x57, starting transfers between devices, shift(): lax.ppermute(value, RING[ring], [(i, (i + step) % 4) for i in range(4)])  98.4 us
    pallas_call x1, Pallas kernels, feed_forward(): pl.pallas_call(ffn_kernel, grid_spec=pltpu.PrefetchScalarGridSpec(num_sca...  45.7 us
    ppermute x1, waiting for transfers between devices, gather_row(): partner = lax.ppermute(line, CORNER, PARTNER)  37.4 us
    dot_general x11, matrix products, product(): return jnp.dot(left, right, preferred_element_type=f32)  25.8 us
  transfers between devices with their start and end apart: 81, of which 47 were waited for; matrix products, arithmetic and copies ran while one was open for 12% of the time, Pallas kernels for 4%

profile of v2, /device:TPU:1, one launch (start us, length us, event | category | flops | bytes accessed | tf_op | source)
XLA Modules:
  0.0 1283.7 jit_solution(15103560686215756438)
XLA Ops:
  14.0 5.0 all-to-all-start
  26.1 4.4 all-to-all-start.1
  33.3 6.9 all-to-all-done.1
  45.2 3.0 collective-permute-start.2
  48.7 6.0 collective-permute-done.5
  59.0 13.0 %collective-permute-done.7 = bf16[128,2048]{1,0:T(8,128)(2,1)S(1)} collective-permute-done((bf16[128,2048]{1,0:T(8,128)(2,1)S(1)}, bf16[128,2048]{1,0:T(8,128)(2,1)S(1)}, u32[]{:S(2)}, u32[]{:S(2)}) %collective-permute-start.7) | collective-permute-done | bytes 524320 | tf_op jit(solution)/shard_map/ppermute | solution.py:73
  72.2 4.3 collective-permute-done.4
  76.5 2.7 collective-permute-start.8
  80.4 3.3 collective-permute-done.8
  86.4 5.5 collective-permute-done.10
  91.9 3.0 collective-permute-start.11
  98.1 12.4 collective-permute-done.11
  113.8 9.8 collective-permute-done.13
  128.9 3.2 fusion.2
  133.3 2.9 fusion.141
  136.2 4.2 broadcast_select_fusion
  144.2 12.0 collective-permute-done.15
  157.9 11.8 collective-permute-done.17
  171.9 4.1 collective-permute-start.19
  180.1 37.4 %collective-permute-done.18.refs_1_ = bf16[4,512,512]{2,1,0:T(8,128)(2,1)S(1)} collective-permute-done((bf16[4,512,512]{2,1,0:T(8,128)(2,1)S(1)}, bf16[4,512,512]{2,1,0:T(8,128)(2,1)S(1)}, u32[]{:S(2)}, u32[]{:S(2)}) %collective-permute-start.18) | collective-permute-done | bytes 2097184 | tf_op jit(solution)/shard_map/ppermute | solution.py:129
  218.0 21.8 %collective-permute-done.19.refs_2_ = bf16[4,512,512]{2,1,0:T(8,128)(2,1)S(1)} collective-permute-done((bf16[4,512,512]{2,1,0:T(8,128)(2,1)S(1)}, bf16[4,512,512]{2,1,0:T(8,128)(2,1)S(1)}, u32[]{:S(2)}, u32[]{:S(2)}) %collective-permute-start.19) | collective-permute-done | bytes 2097184 | tf_op jit(solution)/shard_map/ppermute | solution.py:128
  255.5 2.9 reshape.641
  262.5 12.7 attend.1
  290.5 5.5 multiply_reduce_fusion.1
  296.8 27.8 %collective-permute-start.26 = (bf16[128,2048]{1,0:T(8,128)(2,1)S(1)}, bf16[128,2048]{1,0:T(8,128)(2,1)S(1)}, u32[]{:S(2)}, u32[]{:S(2)}) collective-permute-start(bf16[128,2048]{1,0:T(8,128)(2,1)S(1)} %multiply_convert_fusion.1), channel_id=1, source_target_pairs={{0,24},{8,0},{16,8},{24,16},{1,25},{9,1},{17,9},{25,17},{2,26},{10... | collective-permute-start | bytes 1572872 | tf_op jit(solution)/shard_map/ppermute | solution.py:73
  328.0 9.6 collective-permute-done.26
  337.6 3.7 collective-permute-done.28
  344.5 45.7 %feed_forward.1 = (bf16[512,2048]{1,0:T(8,128)(2,1)}, bf16[512,2432]{1,0:T(8,128)(2,1)}, f32[4,4,2,192,128]{4,3,2,1,0:T(8,128)}) custom-call(s32[1]{0:T(128)} %bitcast.39.at, bf16[512,2048]{1,0:T(8,128)(2,1)} %pad_maximum_fusion.1.nm_ref, bf16[512,2048]{1,0:T(8,128)(2,1)} %copy-done.64, bf16[512,256]{1,0:T(8,128)(2,1)} %fusion.3.lgu_ref, ...), custom_call_target="tpu_custom_call" | custom-call | flops 30064771072 | bytes 41943040 | tf_op jit(solution)/shard_map/feed_forward/pallas_call | solution.py:400
  390.1 2.7 fusion.131
  393.0 2.9 collective-permute-start.30
  396.2 14.4 %collective-permute-done.29 = bf16[128,2432]{1,0:T(8,128)(2,1)} collective-permute-done((bf16[128,2432]{1,0:T(8,128)(2,1)}, bf16[128,2432]{1,0:T(8,128)(2,1)}, u32[]{:S(2)}, u32[]{:S(2)}) %collective-permute-start.29) | collective-permute-done | bytes 622624 | tf_op jit(solution)/shard_map/ppermute | solution.py:73
  410.6 10.4 collective-permute-done.30
  436.2 6.3 fusion.122
  449.2 6.4 collective-permute-done.34
  455.7 18.8 %attend_back.1 = (f32[512,512]{1,0:T(8,128)S(1)}, bf16[4,512,512]{2,1,0:T(8,128)(2,1)}, bf16[4,512,512]{2,1,0:T(8,128)(2,1)}, bf16[4,512,512]{2,1,0:T(8,128)(2,1)}, bf16[4,512,512]{2,1,0:T(8,128)(2,1)}) custom-call(s32[64]{0:T(128)S(1)} %pad_add_fusion.2.active, bf16[512,512]{1,0:T(8,128)(2,1)S(1)} %fusion.23.q_ref, s32[512,1]{1,0:T(8,128)S(1)} %copy-done.6, ...), custom_call_target="tpu_custom_call" | custom-call | flops 12884901888 | bytes 20971520 | tf_op jit(solution)/shard_map/attend_back/pallas_call | solution.py:306
  474.5 3.6 collective-permute-start.35
  478.1 2.7 collective-permute-start.40
  483.4 3.6 add_convert_fusion.2
  488.2 3.7 collective-permute-start.41
  492.9 14.9 %collective-permute-done.36 = bf16[128,2048]{1,0:T(8,128)(2,1)S(1)} collective-permute-done((bf16[128,2048]{1,0:T(8,128)(2,1)S(1)}, bf16[128,2048]{1,0:T(8,128)(2,1)S(1)}, u32[]{:S(2)}, u32[]{:S(2)}) %collective-permute-start.36) | collective-permute-done | bytes 524320 | tf_op jit(solution)/shard_map/ppermute | solution.py:73
  507.9 12.8 collective-permute-start.37
  520.6 15.6 %collective-permute-done.37 = bf16[128,2048]{1,0:T(8,128)(2,1)S(1)} collective-permute-done((bf16[128,2048]{1,0:T(8,128)(2,1)S(1)}, bf16[128,2048]{1,0:T(8,128)(2,1)S(1)}, u32[]{:S(2)}, u32[]{:S(2)}) %collective-permute-start.37) | collective-permute-done | bytes 524320 | tf_op jit(solution)/shard_map/ppermute | solution.py:73
  537.6 12.4 collective-permute-done.38
  554.3 5.6 add_convert_fusion.1
  564.4 9.6 collective-permute-done.44
  574.0 12.8 collective-permute-done.45
  589.0 544.6 %reduce-scatter.5.cloned.1.call-done = f32[1,80,128]{2,1,0:T(8,128)} async-done(((f32[128,80,128]{2,1,0:T(8,128)}), f32[1,80,128]{2,1,0:T(8,128)}) %reduce-scatter.5.cloned.1.call-update) | async-done | bytes 40976 | tf_op jit(solution)/shard_map/reduce_scatter | solution.py:756
  1136.9 2.8 reshape.648
  1150.2 2.7 collective-permute-start.52
  1162.1 3.4 collective-permute-done.55
  1168.2 10.2 collective-permute-start.57
  1180.5 2.7 collective-permute-start.60
  1183.2 2.9 fusion.30
  1190.5 3.1 add_convert_fusion
  1200.7 3.0 collective-permute-done.65
  1204.4 4.0 collective-permute-done.66
  1208.4 2.7 collective-permute-start.67
  1215.0 2.8 collective-permute-done.68
  1219.5 4.0 collective-permute-done.69
  1223.5 3.4 all-gather.8.cloned.1.call-done.all_ref
  1226.9 14.5 %unpack_early.1 = (f32[128,8192]{1,0:T(8,128)}, f32[128,8192]{1,0:T(8,128)}, f32[8192,128]{1,0:T(8,128)}, f32[2048,128]{1,0:T(8,128)}, f32[128,2048]{1,0:T(8,128...) custom-call(bf16[128,272,128]{2,1,0:T(8,128)(2,1)} %all-gather.8.cloned.1.call-done.all_ref), custom_call_target="tpu_custom_call" | custom-call | flops 1048576 | bytes 28311552 | tf_op jit(solution)/shard_map/unpack_early/pallas_call | solution.py:463
  1249.8 4.0 collective-permute-done.71
  1253.9 8.7 collective-permute-done.72
  1270.1 6.7 unpack_late.1
  (511 shorter events, 190.5 us)
Async XLA Ops:
  7.2 237.1 %all-gather.4.cloned.1.call-start = ((), (), s32[]{:S(2)}) async-start(), calls=%async_computation.4 | async-start | bytes 8454144 | tf_op jit(solution)/shard_map/all_gather | solution.py:618
  9.8 20.7 %collective-permute-start = (bf16[64,2048]{1,0:T(8,128)(2,1)}, bf16[64,2048]{1,0:T(8,128)(2,1)S(1)}, u32[]{:S(2)}, u32[]{:S(2)}) collective-permute-start(bf16[64,2048]{1,0:T(8,128)(2,1)} %get-tuple-element.128), channel_id=1, source_target_pairs={{0,1},{1,0},{2,3},{3,2},{4,5},{5,4},{6,7},{7,6},{8,9},{9,8},{10,11... | collective-permute-start | bytes 786440 | tf_op jit(solution)/shard_map/ppermute | solution.py:69
  13.0 18.3 %collective-permute-start.1 = (bf16[64,2048]{1,0:T(8,128)(2,1)}, bf16[64,2048]{1,0:T(8,128)(2,1)}, u32[]{:S(2)}, u32[]{:S(2)}) collective-permute-start(bf16[64,2048]{1,0:T(8,128)(2,1)} %get-tuple-element.126), channel_id=1, source_target_pairs={{0,1},{1,0},{2,3},{3,2},{4,5},{5,4},{6,7},{7,6},{8,9},{9,8},{10,11... | collective-permute-start | bytes 786440 | tf_op jit(solution)/shard_map/ppermute | solution.py:69
  14.0 12.1 all-to-all-start
  26.1 14.1 %all-to-all-start.1 = ((bf16[8,16,2048]{2,1,0:T(8,128)(2,1)}), bf16[8,16,2048]{2,1,0:T(8,128)(2,1)S(1)}, u32[]{:S(2)}, u32[]{:S(2)}) async-start(bf16[8,16,2048]{2,1,0:T(8,128)(2,1)} %pad_maximum_fusion.5), calls=%async_computation.1 | async-start | bytes 1048576 | tf_op jit(solution)/shard_map/all_to_all | solution.py:607
  30.5 314.0 %all-gather.6.cloned.1.call-start = ((), (), s32[]{:S(2)}) async-start(), calls=%async_computation.5 | async-start | bytes 25952256 | tf_op jit(solution)/shard_map/all_gather | solution.py:639
  40.2 14.6 %collective-permute-start.5 = (bf16[128,2048]{1,0:T(8,128)(2,1)S(1)}, bf16[128,2048]{1,0:T(8,128)(2,1)}, u32[]{:S(2)}, u32[]{:S(2)}) collective-permute-start(bf16[128,2048]{1,0:T(8,128)(2,1)S(1)} %pad_maximum_fusion.4), channel_id=1, source_target_pairs={{0,24},{8,0},{16,8},{24,16},{1,25},{9,1},{17,9},{25,17},{2,26},{10... | collective-permute-start | bytes 1572872 | tf_op jit(solution)/shard_map/ppermute | solution.py:73
  42.6 15.3 %collective-permute-start.6 = (bf16[128,2048]{1,0:T(8,128)(2,1)S(1)}, bf16[128,2048]{1,0:T(8,128)(2,1)}, u32[]{:S(2)}, u32[]{:S(2)}) collective-permute-start(bf16[128,2048]{1,0:T(8,128)(2,1)S(1)} %pad_maximum_fusion.4), channel_id=1, source_target_pairs={{0,16},{8,24},{16,0},{24,8},{1,17},{9,25},{17,1},{25,9},{2,18},{10... | collective-permute-start | bytes 1572872 | tf_op jit(solution)/shard_map/ppermute | solution.py:73
  43.9 28.0 %collective-permute-start.7 = (bf16[128,2048]{1,0:T(8,128)(2,1)S(1)}, bf16[128,2048]{1,0:T(8,128)(2,1)S(1)}, u32[]{:S(2)}, u32[]{:S(2)}) collective-permute-start(bf16[128,2048]{1,0:T(8,128)(2,1)S(1)} %pad_maximum_fusion.4), channel_id=1, source_target_pairs={{0,8},{8,16},{16,24},{24,0},{1,9},{9,17},{17,25},{25,1},{2,10},{10... | collective-permute-start | bytes 1572872 | tf_op jit(solution)/shard_map/ppermute | solution.py:73
  45.2 26.8 %collective-permute-start.2 = (bf16[128,2048]{1,0:T(8,128)(2,1)S(1)}, bf16[128,2048]{1,0:T(8,128)(2,1)S(1)}, u32[]{:S(2)}, u32[]{:S(2)}) collective-permute-start(bf16[128,2048]{1,0:T(8,128)(2,1)S(1)} %copy-done.40), channel_id=1, source_target_pairs={{0,6},{2,0},{4,2},{6,4},{1,7},{3,1},{5,3},{7,5},{8,14},{10,8},{12,... | collective-permute-start | bytes 1572872 | tf_op jit(solution)/shard_map/ppermute | solution.py:73
  48.2 23.9 %collective-permute-start.3 = (bf16[128,2048]{1,0:T(8,128)(2,1)S(1)}, bf16[128,2048]{1,0:T(8,128)(2,1)S(1)}, u32[]{:S(2)}, u32[]{:S(2)}) collective-permute-start(bf16[128,2048]{1,0:T(8,128)(2,1)S(1)} %copy-done.40), channel_id=1, source_target_pairs={{0,4},{2,6},{4,0},{6,2},{1,5},{3,7},{5,1},{7,3},{8,12},{10,14},{12... | collective-permute-start | bytes 1572872 | tf_op jit(solution)/shard_map/ppermute | solution.py:73
  54.8 21.7 %collective-permute-start.4 = (bf16[128,2048]{1,0:T(8,128)(2,1)S(1)}, bf16[128,2048]{1,0:T(8,128)(2,1)S(1)}, u32[]{:S(2)}, u32[]{:S(2)}) collective-permute-start(bf16[128,2048]{1,0:T(8,128)(2,1)S(1)} %copy-done.40), channel_id=1, source_target_pairs={{0,2},{2,4},{4,6},{6,0},{1,3},{3,5},{5,7},{7,1},{8,10},{10,12},{12... | collective-permute-start | bytes 1572872 | tf_op jit(solution)/shard_map/ppermute | solution.py:73
  76.5 7.3 collective-permute-start.8
  79.2 7.1 collective-permute-start.9
  79.7 12.1 collective-permute-start.10
  91.9 18.7 %collective-permute-start.11 = (bf16[4,128,512]{2,1,0:T(8,128)(2,1)S(1)}, bf16[4,128,512]{2,1,0:T(8,128)(2,1)S(1)}, u32[]{:S(2)}, u32[]{:S(2)}) collective-permute-start(bf16[4,128,512]{2,1,0:T(8,128)(2,1)S(1)} %bitcast_dynamic-update-slice_fusion.11), channel_id=1, source_target_pairs={{0,96},{32,0},{64,32},{96,64},{1,97},{33,1},{65,33},{97,65},{2,98}... | collective-permute-start | bytes 1572872 | tf_op jit(solution)/shard_map/ppermute | solution.py:73
  95.1 16.8 %collective-permute-start.12 = (bf16[4,128,512]{2,1,0:T(8,128)(2,1)S(1)}, bf16[4,128,512]{2,1,0:T(8,128)(2,1)}, u32[]{:S(2)}, u32[]{:S(2)}) collective-permute-start(bf16[4,128,512]{2,1,0:T(8,128)(2,1)S(1)} %bitcast_dynamic-update-slice_fusion.11), channel_id=1, source_target_pairs={{0,64},{32,96},{64,0},{96,32},{1,65},{33,97},{65,1},{97,33},{2,66}... | collective-permute-start | bytes 1572872 | tf_op jit(solution)/shard_map/ppermute | solution.py:73
  95.2 28.3 %collective-permute-start.13 = (bf16[4,128,512]{2,1,0:T(8,128)(2,1)S(1)}, bf16[4,128,512]{2,1,0:T(8,128)(2,1)S(1)}, u32[]{:S(2)}, u32[]{:S(2)}) collective-permute-start(bf16[4,128,512]{2,1,0:T(8,128)(2,1)S(1)} %bitcast_dynamic-update-slice_fusion.11), channel_id=1, source_target_pairs={{0,32},{32,64},{64,96},{96,0},{1,33},{33,65},{65,97},{97,1},{2,34}... | collective-permute-start | bytes 1572872 | tf_op jit(solution)/shard_map/ppermute | solution.py:73
  124.4 11.8 collective-permute-start.14
  142.6 13.6 %collective-permute-start.15 = (bf16[512,512]{1,0:T(8,128)(2,1)S(1)}, bf16[512,512]{1,0:T(8,128)(2,1)S(1)}, u32[]{:S(2)}, u32[]{:S(2)}) collective-permute-start(bf16[512,512]{1,0:T(8,128)(2,1)S(1)} %get-tuple-element.122), channel_id=1, source_target_pairs={{0,24},{8,0},{16,8},{24,16},{1,25},{9,1},{17,9},{25,17},{2,26},{10... | collective-permute-start | bytes 1572872 | tf_op jit(solution)/shard_map/ppermute | solution.py:73
  143.2 14.7 %collective-permute-start.16 = (bf16[512,512]{1,0:T(8,128)(2,1)S(1)}, bf16[512,512]{1,0:T(8,128)(2,1)S(1)}, u32[]{:S(2)}, u32[]{:S(2)}) collective-permute-start(bf16[512,512]{1,0:T(8,128)(2,1)S(1)} %get-tuple-element.122), channel_id=1, source_target_pairs={{0,16},{8,24},{16,0},{24,8},{1,17},{9,25},{17,1},{25,9},{2,18},{10... | collective-permute-start | bytes 1572872 | tf_op jit(solution)/shard_map/ppermute | solution.py:73
  143.8 26.0 %collective-permute-start.17 = (bf16[512,512]{1,0:T(8,128)(2,1)S(1)}, bf16[512,512]{1,0:T(8,128)(2,1)S(1)}, u32[]{:S(2)}, u32[]{:S(2)}) collective-permute-start(bf16[512,512]{1,0:T(8,128)(2,1)S(1)} %get-tuple-element.122), channel_id=1, source_target_pairs={{0,8},{8,16},{16,24},{24,0},{1,9},{9,17},{17,25},{25,1},{2,10},{10... | collective-permute-start | bytes 1572872 | tf_op jit(solution)/shard_map/ppermute | solution.py:73
  170.1 47.4 %collective-permute-start.18 = (bf16[4,512,512]{2,1,0:T(8,128)(2,1)S(1)}, bf16[4,512,512]{2,1,0:T(8,128)(2,1)S(1)}, u32[]{:S(2)}, u32[]{:S(2)}) collective-permute-start(bf16[4,512,512]{2,1,0:T(8,128)(2,1)S(1)} %pad_maximum_fusion.refs_0_), channel_id=1, source_target_pairs={{0,32},{1,33},{32,0},{33,1},{64,96},{65,97},{96,64},{97,65},{2,34}... | collective-permute-start | bytes 6291464 | tf_op jit(solution)/shard_map/ppermute | solution.py:129
  171.9 67.9 %collective-permute-start.19 = (bf16[4,512,512]{2,1,0:T(8,128)(2,1)S(1)}, bf16[4,512,512]{2,1,0:T(8,128)(2,1)S(1)}, u32[]{:S(2)}, u32[]{:S(2)}) collective-permute-start(bf16[4,512,512]{2,1,0:T(8,128)(2,1)S(1)} %pad_maximum_fusion.refs_0_), channel_id=1, source_target_pairs={{1,64},{33,96},{3,66},{35,98},{5,68},{37,100},{7,70},{39,102},{9,7... | collective-permute-start | bytes 6291464 | tf_op jit(solution)/shard_map/ppermute | solution.py:128
  176.0 65.7 %collective-permute-start.20 = (bf16[4,512,512]{2,1,0:T(8,128)(2,1)S(1)}, bf16[4,512,512]{2,1,0:T(8,128)(2,1)S(1)}, u32[]{:S(2)}, u32[]{:S(2)}) collective-permute-start(bf16[4,512,512]{2,1,0:T(8,128)(2,1)S(1)} %pad_maximum_fusion.refs_0_), channel_id=1, source_target_pairs={{1,96},{33,64},{3,98},{35,66},{5,100},{37,68},{7,102},{39,70},{9,1... | collective-permute-start | bytes 6291464 | tf_op jit(solution)/shard_map/ppermute | solution.py:128
  177.4 65.5 %collective-permute-start.21 = (bf16[4,512,512]{2,1,0:T(8,128)(2,1)S(1)}, bf16[4,512,512]{2,1,0:T(8,128)(2,1)S(1)}, u32[]{:S(2)}, u32[]{:S(2)}) collective-permute-start(bf16[4,512,512]{2,1,0:T(8,128)(2,1)S(1)} %pad_maximum_fusion.refs_0_), channel_id=1, source_target_pairs={{0,1},{2,3},{4,5},{6,7},{8,9},{10,11},{12,13},{14,15},{16,17},{18,... | collective-permute-start | bytes 6291464 | tf_op jit(solution)/shard_map/ppermute | solution.py:130
  247.2 304.6 %reduce-scatter.3.cloned.1.call-start = ((), (), s32[]{:S(2)}) async-start(), calls=%async_computation.6 | async-start | bytes 3244032 | tf_op jit(solution)/shard_map/reduce_scatter | solution.py:702
  248.7 13.1 %collective-permute-start.22 = (bf16[4,512,512]{2,1,0:T(8,128)(2,1)}, bf16[4,512,512]{2,1,0:T(8,128)(2,1)}, u32[]{:S(2)}, u32[]{:S(2)}) collective-permute-start(bf16[4,512,512]{2,1,0:T(8,128)(2,1)} %copy-done.83), channel_id=1, source_target_pairs={{0,1},{2,3},{4,5},{6,7},{8,9},{10,11},{12,13},{14,15},{16,17},{18,... | collective-permute-start | bytes 6291464 | tf_op jit(solution)/shard_map/ppermute | solution.py:130
  276.4 6.5 collective-permute-start.23
  276.5 7.1 collective-permute-start.24
  277.6 6.7 collective-permute-start.25
  296.8 40.8 %collective-permute-start.26 = (bf16[128,2048]{1,0:T(8,128)(2,1)S(1)}, bf16[128,2048]{1,0:T(8,128)(2,1)S(1)}, u32[]{:S(2)}, u32[]{:S(2)}) collective-permute-start(bf16[128,2048]{1,0:T(8,128)(2,1)S(1)} %multiply_convert_fusion.1), channel_id=1, source_target_pairs={{0,24},{8,0},{16,8},{24,16},{1,25},{9,1},{17,9},{25,17},{2,26},{10... | collective-permute-start | bytes 1572872 | tf_op jit(solution)/shard_map/ppermute | solution.py:73
  324.6 13.0 %collective-permute-start.27 = (bf16[128,2048]{1,0:T(8,128)(2,1)S(1)}, bf16[128,2048]{1,0:T(8,128)(2,1)S(1)}, u32[]{:S(2)}, u32[]{:S(2)}) collective-permute-start(bf16[128,2048]{1,0:T(8,128)(2,1)S(1)} %multiply_convert_fusion.1), channel_id=1, source_target_pairs={{0,16},{8,24},{16,0},{24,8},{1,17},{9,25},{17,1},{25,9},{2,18},{10... | collective-permute-start | bytes 1572872 | tf_op jit(solution)/shard_map/ppermute | solution.py:73
  324.6 16.7 %collective-permute-start.28 = (bf16[128,2048]{1,0:T(8,128)(2,1)S(1)}, bf16[128,2048]{1,0:T(8,128)(2,1)S(1)}, u32[]{:S(2)}, u32[]{:S(2)}) collective-permute-start(bf16[128,2048]{1,0:T(8,128)(2,1)S(1)} %multiply_convert_fusion.1), channel_id=1, source_target_pairs={{0,8},{8,16},{16,24},{24,0},{1,9},{9,17},{17,25},{25,1},{2,10},{10... | collective-permute-start | bytes 1572872 | tf_op jit(solution)/shard_map/ppermute | solution.py:73
  392.9 17.7 %collective-permute-start.29 = (bf16[128,2432]{1,0:T(8,128)(2,1)}, bf16[128,2432]{1,0:T(8,128)(2,1)}, u32[]{:S(2)}, u32[]{:S(2)}) collective-permute-start(bf16[128,2432]{1,0:T(8,128)(2,1)} %get-tuple-element.86), channel_id=1, source_target_pairs={{0,16},{8,24},{16,0},{24,8},{1,17},{9,25},{17,1},{25,9},{2,18},{10... | collective-permute-start | bytes 1867784 | tf_op jit(solution)/shard_map/ppermute | solution.py:73
  393.0 28.0 %collective-permute-start.30 = (bf16[128,2432]{1,0:T(8,128)(2,1)}, bf16[128,2432]{1,0:T(8,128)(2,1)}, u32[]{:S(2)}, u32[]{:S(2)}) collective-permute-start(bf16[128,2432]{1,0:T(8,128)(2,1)} %get-tuple-element.88), channel_id=1, source_target_pairs={{0,8},{8,16},{16,24},{24,0},{1,9},{9,17},{17,25},{25,1},{2,10},{10... | collective-permute-start | bytes 1867784 | tf_op jit(solution)/shard_map/ppermute | solution.py:73
  395.9 27.6 %collective-permute-start.31 = (bf16[128,2432]{1,0:T(8,128)(2,1)}, bf16[128,2432]{1,0:T(8,128)(2,1)}, u32[]{:S(2)}, u32[]{:S(2)}) collective-permute-start(bf16[128,2432]{1,0:T(8,128)(2,1)} %get-tuple-element.87), channel_id=1, source_target_pairs={{0,24},{8,0},{16,8},{24,16},{1,25},{9,1},{17,9},{25,17},{2,26},{10... | collective-permute-start | bytes 1867784 | tf_op jit(solution)/shard_map/ppermute | solution.py:73
  395.9 737.7 %reduce-scatter.5.cloned.1.call-start = ((), (), s32[]{:S(2)}) async-start(), calls=%async_computation.7 | async-start | bytes 5283840 | tf_op jit(solution)/shard_map/reduce_scatter | solution.py:756
  436.0 790.8 %all-gather.8.cloned.1.call-start = ((), (), s32[]{:S(2)}) async-start(), calls=%async_computation.8 | async-start | bytes 8982528 | tf_op jit(solution)/shard_map/all_gather | solution.py:758
  444.5 11.1 collective-permute-start.34
  474.5 8.9 collective-permute-start.35
  478.1 76.2 %collective-permute-start.40 = (bf16[4,512,512]{2,1,0:T(8,128)(2,1)}, bf16[4,512,512]{2,1,0:T(8,128)(2,1)}, u32[]{:S(2)}, u32[]{:S(2)}) collective-permute-start(bf16[4,512,512]{2,1,0:T(8,128)(2,1)} %get-tuple-element.54), channel_id=1, source_target_pairs={{1,0},{3,2},{5,4},{7,6},{9,8},{11,10},{13,12},{15,14},{17,16},{19,... | collective-permute-start | bytes 6291464 | tf_op jit(solution)/shard_map/ppermute | solution.py:135
  480.8 73.5 %collective-permute-start.42 = (bf16[4,512,512]{2,1,0:T(8,128)(2,1)}, bf16[4,512,512]{2,1,0:T(8,128)(2,1)}, u32[]{:S(2)}, u32[]{:S(2)}) collective-permute-start(bf16[4,512,512]{2,1,0:T(8,128)(2,1)} %get-tuple-element.54), channel_id=1, source_target_pairs={{64,1},{96,33},{66,3},{98,35},{68,5},{100,37},{70,7},{102,39},{72,... | collective-permute-start | bytes 6291464 | tf_op jit(solution)/shard_map/ppermute | solution.py:136
  482.1 72.3 %collective-permute-start.43 = (bf16[4,512,512]{2,1,0:T(8,128)(2,1)}, bf16[4,512,512]{2,1,0:T(8,128)(2,1)}, u32[]{:S(2)}, u32[]{:S(2)}) collective-permute-start(bf16[4,512,512]{2,1,0:T(8,128)(2,1)} %get-tuple-element.51), channel_id=1, source_target_pairs={{96,1},{64,33},{98,3},{66,35},{100,5},{68,37},{102,7},{70,39},{104... | collective-permute-start | bytes 6291464 | tf_op jit(solution)/shard_map/ppermute | solution.py:136
  488.2 66.1 %collective-permute-start.41 = (bf16[4,512,512]{2,1,0:T(8,128)(2,1)}, bf16[4,512,512]{2,1,0:T(8,128)(2,1)}, u32[]{:S(2)}, u32[]{:S(2)}) collective-permute-start(bf16[4,512,512]{2,1,0:T(8,128)(2,1)} %add_convert_fusion.2), channel_id=1, source_target_pairs={{0,32},{1,33},{32,0},{33,1},{64,96},{65,97},{96,64},{97,65},{2,34}... | collective-permute-start | bytes 6291464 | tf_op jit(solution)/shard_map/ppermute | solution.py:138
  492.8 15.0 %collective-permute-start.36 = (bf16[128,2048]{1,0:T(8,128)(2,1)S(1)}, bf16[128,2048]{1,0:T(8,128)(2,1)S(1)}, u32[]{:S(2)}, u32[]{:S(2)}) collective-permute-start(bf16[128,2048]{1,0:T(8,128)(2,1)S(1)} %get-tuple-element.95), channel_id=1, source_target_pairs={{0,16},{8,24},{16,0},{24,8},{1,17},{9,25},{17,1},{25,9},{2,18},{10... | collective-permute-start | bytes 1572872 | tf_op jit(solution)/shard_map/ppermute | solution.py:73
  507.9 28.3 %collective-permute-start.37 = (bf16[128,2048]{1,0:T(8,128)(2,1)S(1)}, bf16[128,2048]{1,0:T(8,128)(2,1)S(1)}, u32[]{:S(2)}, u32[]{:S(2)}) collective-permute-start(bf16[128,2048]{1,0:T(8,128)(2,1)S(1)} %get-tuple-element.97), channel_id=1, source_target_pairs={{0,8},{8,16},{16,24},{24,0},{1,9},{9,17},{17,25},{25,1},{2,10},{10... | collective-permute-start | bytes 1572872 | tf_op jit(solution)/shard_map/ppermute | solution.py:73
  536.2 13.8 %collective-permute-start.38 = (bf16[128,2048]{1,0:T(8,128)(2,1)S(1)}, bf16[128,2048]{1,0:T(8,128)(2,1)S(1)}, u32[]{:S(2)}, u32[]{:S(2)}) collective-permute-start(bf16[128,2048]{1,0:T(8,128)(2,1)S(1)} %get-tuple-element.96), channel_id=1, source_target_pairs={{0,24},{8,0},{16,8},{24,16},{1,25},{9,1},{17,9},{25,17},{2,26},{10... | collective-permute-start | bytes 1572872 | tf_op jit(solution)/shard_map/ppermute | solution.py:73
  560.1 13.9 %collective-permute-start.44 = (bf16[512,512]{1,0:T(8,128)(2,1)S(1)}, bf16[512,512]{1,0:T(8,128)(2,1)S(1)}, u32[]{:S(2)}, u32[]{:S(2)}) collective-permute-start(bf16[512,512]{1,0:T(8,128)(2,1)S(1)} %get-tuple-element.92), channel_id=1, source_target_pairs={{0,16},{8,24},{16,0},{24,8},{1,17},{9,25},{17,1},{25,9},{2,18},{10... | collective-permute-start | bytes 1572872 | tf_op jit(solution)/shard_map/ppermute | solution.py:73
  561.7 25.0 %collective-permute-start.45 = (bf16[512,512]{1,0:T(8,128)(2,1)S(1)}, bf16[512,512]{1,0:T(8,128)(2,1)S(1)}, u32[]{:S(2)}, u32[]{:S(2)}) collective-permute-start(bf16[512,512]{1,0:T(8,128)(2,1)S(1)} %get-tuple-element.94), channel_id=1, source_target_pairs={{0,8},{8,16},{16,24},{24,0},{1,9},{9,17},{17,25},{25,1},{2,10},{10... | collective-permute-start | bytes 1572872 | tf_op jit(solution)/shard_map/ppermute | solution.py:73
  563.0 23.8 %collective-permute-start.46 = (bf16[512,512]{1,0:T(8,128)(2,1)S(1)}, bf16[512,512]{1,0:T(8,128)(2,1)S(1)}, u32[]{:S(2)}, u32[]{:S(2)}) collective-permute-start(bf16[512,512]{1,0:T(8,128)(2,1)S(1)} %get-tuple-element.93), channel_id=1, source_target_pairs={{0,24},{8,0},{16,8},{24,16},{1,25},{9,1},{17,9},{25,17},{2,26},{10... | collective-permute-start | bytes 1572872 | tf_op jit(solution)/shard_map/ppermute | solution.py:73
  1150.2 6.1 collective-permute-start.51
  1150.2 6.1 collective-permute-start.52
  1168.2 11.7 collective-permute-start.57
  1179.2 86.8 %collective-permute-start.39 = (bf16[64,2048]{1,0:T(8,128)(2,1)}, bf16[64,2048]{1,0:T(8,128)(2,1)}, u32[]{:S(2)}, u32[]{:S(2)}) collective-permute-start(bf16[64,2048]{1,0:T(8,128)(2,1)} %get-tuple-element.113), channel_id=1, source_target_pairs={{0,1},{1,0},{2,3},{3,2},{4,5},{5,4},{6,7},{7,6},{8,9},{9,8},{10,11... | collective-permute-start | bytes 786440 | tf_op jit(solution)/shard_map/ppermute | solution.py:69
  1180.1 7.0 collective-permute-start.58
  1180.2 7.0 collective-permute-start.59
  1180.5 7.1 collective-permute-start.60
  1196.5 47.3 %collective-permute-start.47 = (bf16[128,2048]{1,0:T(8,128)(2,1)}, bf16[128,2048]{1,0:T(8,128)(2,1)}, u32[]{:S(2)}, u32[]{:S(2)}) collective-permute-start(bf16[128,2048]{1,0:T(8,128)(2,1)} %get-tuple-element.89), channel_id=1, source_target_pairs={{0,4},{2,6},{4,0},{6,2},{1,5},{3,7},{5,1},{7,3},{8,12},{10,14},{12... | collective-permute-start | bytes 1572872 | tf_op jit(solution)/shard_map/ppermute | solution.py:73
  1196.6 47.2 %collective-permute-start.48 = (bf16[128,2048]{1,0:T(8,128)(2,1)}, bf16[128,2048]{1,0:T(8,128)(2,1)}, u32[]{:S(2)}, u32[]{:S(2)}) collective-permute-start(bf16[128,2048]{1,0:T(8,128)(2,1)} %get-tuple-element.91), channel_id=1, source_target_pairs={{0,2},{2,4},{4,6},{6,0},{1,3},{3,5},{5,7},{7,1},{8,10},{10,12},{12... | collective-permute-start | bytes 1572872 | tf_op jit(solution)/shard_map/ppermute | solution.py:73
  1197.1 46.7 %collective-permute-start.49 = (bf16[128,2048]{1,0:T(8,128)(2,1)}, bf16[128,2048]{1,0:T(8,128)(2,1)}, u32[]{:S(2)}, u32[]{:S(2)}) collective-permute-start(bf16[128,2048]{1,0:T(8,128)(2,1)} %get-tuple-element.90), channel_id=1, source_target_pairs={{0,6},{2,0},{4,2},{6,4},{1,7},{3,1},{5,3},{7,5},{8,14},{10,8},{12,... | collective-permute-start | bytes 1572872 | tf_op jit(solution)/shard_map/ppermute | solution.py:73
  1246.2 7.6 collective-permute-start.71
  1247.1 15.5 %collective-permute-start.72 = (bf16[4,4,80,128]{3,2,1,0:T(8,128)(2,1)S(1)}, bf16[4,4,80,128]{3,2,1,0:T(8,128)(2,1)S(1)}, u32[]{:S(2)}, u32[]{:S(2)}) collective-permute-start(bf16[4,4,80,128]{3,2,1,0:T(8,128)(2,1)S(1)} %get-tuple-element.73), channel_id=1, source_target_pairs={{0,2},{2,4},{4,6},{6,0},{1,3},{3,5},{5,7},{7,1},{8,10},{10,12},{12... | collective-permute-start | bytes 983048 | tf_op jit(solution)/shard_map/ppermute | solution.py:73
  1262.6 6.4 collective-permute-start.73
  (104 other events, 2148.7 us)
Sparse Core Ops, SparseCore 0:
  11.1 106.0 all-gather.3
  247.3 92.3 all-gather.5
  396.1 81.5 reduce-scatter.2
  480.0 653.5 reduce-scatter.4
  1137.0 89.8 all-gather.7

commit v3 on v2

--- a/solution.py
+++ b/solution.py
@@ -753,8 +753,10 @@
         inner_rows(normed_mid, grad_low_gu[:, rank:]),
     ]
     row_terms = jnp.concatenate([array.reshape(128, 16, rank) for array in row_terms], axis=1)
-    row_sum = lax.psum_scatter(row_terms, ALL, scatter_dimension=0, tiled=False)
-    early_sum = (jnp.concatenate([unit_sum, row_sum], axis=0) + zero_of(dkv)).astype(bf16)
+    row_terms = jnp.swapaxes(row_terms.reshape(4, 4, 8, 80, rank), 1, 2).reshape(32, 320, rank)
+    row_sum = lax.psum_scatter(row_terms, OVER_X, scatter_dimension=0, tiled=False)
+    row_sum = sum_ring((row_sum + zero_of(dkv)).reshape(4, 80, rank), "x")
+    early_sum = jnp.concatenate([unit_sum, row_sum], axis=0).astype(bf16)
     early_all = lax.all_gather(early_sum, ALL, axis=0, tiled=False)
 
     grad_qkv = inner_rows(features(normed_g, y), gather_near(grad_low_qkv, "y"))

time: 1290 us -> 739 us (0.57)
  waiting for transfers between devices: 854 us -> 321 us
  starting transfers between devices: 147 us -> 133 us
    reduce_scatter x1, waiting for transfers between devices: 545 us -> 14.3 us  [local(): lax.psum_scatter(row_terms, OVER_X, scatter_dimension=0, tiled=False)]
    ppermute x57 -> x60, starting transfers between devices: 98.4 us -> 83.7 us  [shift(): lax.ppermute(value, RING[ring], [(i, (i + step) % 4) for i in range(4)])]
    ppermute x57 -> x60, waiting for transfers between devices: 239 us -> 228 us  [shift(): lax.ppermute(value, RING[ring], [(i, (i + step) % 4) for i in range(4)])]
  transfers between devices with their start and end apart: 81 -> 84, of which waited for: 47 -> 46; matrix products, arithmetic and copies ran while one was open for 12% -> 19% of each run, Pallas kernels for 4% -> 5%
where the time goes in v3:
time: 739 us; the launch traced here: 725 us
  waiting for transfers between devices  321 us (43%)
  starting transfers between devices  133 us (18%)
  Pallas kernels  89.9 us (12%)
  local copies, waits for them, and re-layouts  66.6 us (9%)
  matrix products  50.5 us (7%)
  other arithmetic  41 us (6%)
  between operations  22.9 us (3%)
    ppermute x60, waiting for transfers between devices, shift(): lax.ppermute(value, RING[ring], [(i, (i + step) % 4) for i in range(4)])  228 us
    ppermute x60, starting transfers between devices, shift(): lax.ppermute(value, RING[ring], [(i, (i + step) % 4) for i in range(4)])  83.7 us
    pallas_call x1, Pallas kernels, feed_forward(): pl.pallas_call(ffn_kernel, grid_spec=pltpu.PrefetchScalarGridSpec(num_sca...  45.6 us
    ppermute x1, waiting for transfers between devices, gather_row(): partner = lax.ppermute(line, CORNER, PARTNER)  37.4 us
    dot_general x11, matrix products, product(): return jnp.dot(left, right, preferred_element_type=f32)  25.6 us
    ppermute x2, waiting for transfers between devices, gather_row(): ahead = [lax.ppermute(line, CORNER, pairs) for pairs in LATER]  21.8 us
    ppermute x7, starting transfers between devices, swap_cores(): return lax.ppermute(value, 'c', [(0, 1), (1, 0)])  19.1 us
    dot_general x11, matrix products, times_transposed(): lax.dot_general(left, right, (((1,), (1,)), ((), ())), preferred_element_...  16.9 us
  transfers between devices with their start and end apart: 84, of which 46 were waited for; matrix products, arithmetic and copies ran while one was open for 19% of the time, Pallas kernels for 5%

profile of v3, /device:TPU:1, one launch (start us, length us, event | category | flops | bytes accessed | tf_op | source)
XLA Modules:
  0.0 724.8 jit_solution(880092617689841952)
XLA Ops:
  14.0 5.0 all-to-all-start
  26.1 4.4 all-to-all-start.1
  33.2 7.0 all-to-all-done.1
  45.2 3.0 collective-permute-start.2
  48.7 6.0 collective-permute-done.5
  59.0 13.0 %collective-permute-done.7 = bf16[128,2048]{1,0:T(8,128)(2,1)S(1)} collective-permute-done((bf16[128,2048]{1,0:T(8,128)(2,1)S(1)}, bf16[128,2048]{1,0:T(8,128)(2,1)S(1)}, u32[]{:S(2)}, u32[]{:S(2)}) %collective-permute-start.7) | collective-permute-done | bytes 524320 | tf_op jit(solution)/shard_map/ppermute | solution.py:73
  72.2 4.3 collective-permute-done.4
  76.5 2.7 collective-permute-start.8
  80.4 3.3 collective-permute-done.8
  83.8 2.6 collective-permute-done.9
  86.4 5.5 collective-permute-done.10
  91.9 3.0 collective-permute-start.11
  98.1 12.4 %collective-permute-done.11 = bf16[4,128,512]{2,1,0:T(8,128)(2,1)S(1)} collective-permute-done((bf16[4,128,512]{2,1,0:T(8,128)(2,1)S(1)}, bf16[4,128,512]{2,1,0:T(8,128)(2,1)S(1)}, u32[]{:S(2)}, u32[]{:S(2)}) %collective-permute-start.11) | collective-permute-done | bytes 524320 | tf_op jit(solution)/shard_map/ppermute | solution.py:73
  113.8 9.8 %collective-permute-done.13 = bf16[4,128,512]{2,1,0:T(8,128)(2,1)S(1)} collective-permute-done((bf16[4,128,512]{2,1,0:T(8,128)(2,1)S(1)}, bf16[4,128,512]{2,1,0:T(8,128)(2,1)S(1)}, u32[]{:S(2)}, u32[]{:S(2)}) %collective-permute-start.13) | collective-permute-done | bytes 524320 | tf_op jit(solution)/shard_map/ppermute | solution.py:73
  128.9 3.2 fusion.2
  133.3 2.9 fusion.147
  136.2 4.2 broadcast_select_fusion
  144.2 12.0 %collective-permute-done.15 = bf16[512,512]{1,0:T(8,128)(2,1)S(1)} collective-permute-done((bf16[512,512]{1,0:T(8,128)(2,1)S(1)}, bf16[512,512]{1,0:T(8,128)(2,1)S(1)}, u32[]{:S(2)}, u32[]{:S(2)}) %collective-permute-start.15) | collective-permute-done | bytes 524320 | tf_op jit(solution)/shard_map/ppermute | solution.py:73
  157.9 11.8 %collective-permute-done.17 = bf16[512,512]{1,0:T(8,128)(2,1)S(1)} collective-permute-done((bf16[512,512]{1,0:T(8,128)(2,1)S(1)}, bf16[512,512]{1,0:T(8,128)(2,1)S(1)}, u32[]{:S(2)}, u32[]{:S(2)}) %collective-permute-start.17) | collective-permute-done | bytes 524320 | tf_op jit(solution)/shard_map/ppermute | solution.py:73
  171.9 4.1 collective-permute-start.19
  180.1 37.4 %collective-permute-done.18.refs_1_ = bf16[4,512,512]{2,1,0:T(8,128)(2,1)S(1)} collective-permute-done((bf16[4,512,512]{2,1,0:T(8,128)(2,1)S(1)}, bf16[4,512,512]{2,1,0:T(8,128)(2,1)S(1)}, u32[]{:S(2)}, u32[]{:S(2)}) %collective-permute-start.18) | collective-permute-done | bytes 2097184 | tf_op jit(solution)/shard_map/ppermute | solution.py:129
  218.0 21.8 %collective-permute-done.19.refs_2_ = bf16[4,512,512]{2,1,0:T(8,128)(2,1)S(1)} collective-permute-done((bf16[4,512,512]{2,1,0:T(8,128)(2,1)S(1)}, bf16[4,512,512]{2,1,0:T(8,128)(2,1)S(1)}, u32[]{:S(2)}, u32[]{:S(2)}) %collective-permute-start.19) | collective-permute-done | bytes 2097184 | tf_op jit(solution)/shard_map/ppermute | solution.py:128
  255.5 2.9 reshape.655
  262.5 8.5 %attend.1 = (f32[512,512]{1,0:T(8,128)S(1)}, f32[2,512,1]{2,1,0:T(8,128)S(1)}) custom-call(s32[64]{0:T(128)S(1)} %pad_add_fusion.2.active, bf16[512,512]{1,0:T(8,128)(2,1)S(1)} %fusion.23.q_ref, s32[512,1]{1,0:T(8,128)S(1)} %copy.139.pos_ref, s32[512,1]{1,0:T(8,128)S(1)} %copy.140.start_ref, s32[16,1,512]{2,1,0:T(1,128)S(1)} %reshape.656.kpos_ref, ...), custom_call_target="tpu_custom_call" | custom-call | flops 6442450944 | bytes 10485760 | tf_op jit(solution)/shard_map/attend/pallas_call | solution.py:281
  286.1 5.0 multiply_reduce_fusion.1
  291.8 5.5 collective-permute-start.26
  300.7 18.1 %collective-permute-done.26 = bf16[128,2048]{1,0:T(8,128)(2,1)S(1)} collective-permute-done((bf16[128,2048]{1,0:T(8,128)(2,1)S(1)}, bf16[128,2048]{1,0:T(8,128)(2,1)S(1)}, u32[]{:S(2)}, u32[]{:S(2)}) %collective-permute-start.26) | collective-permute-done | bytes 524320 | tf_op jit(solution)/shard_map/ppermute | solution.py:73
  318.8 5.2 collective-permute-done.28
  327.2 12.2 %all-gather.6.cloned.1.call-done = bf16[32,192,2048]{2,1,0:T(8,128)(2,1)} async-done(((bf16[1,192,2048]{2,1,0:T(8,128)(2,1)}), bf16[32,192,2048]{2,1,0:T(8,128)(2,1)}) %all-gather.6.cloned.1.call-update) | async-done | bytes 25165840 | tf_op jit(solution)/shard_map/all_gather | solution.py:639
  339.5 45.6 %feed_forward.1 = (bf16[512,2048]{1,0:T(8,128)(2,1)}, bf16[512,2432]{1,0:T(8,128)(2,1)}, f32[4,4,2,192,128]{4,3,2,1,0:T(8,128)}) custom-call(s32[1]{0:T(128)} %bitcast.39.at, bf16[512,2048]{1,0:T(8,128)(2,1)} %pad_maximum_fusion.1.nm_ref, bf16[512,2048]{1,0:T(8,128)(2,1)} %copy-done.62, bf16[512,256]{1,0:T(8,128)(2,1)} %fusion.3.lgu_ref, ...), custom_call_target="tpu_custom_call" | custom-call | flops 30064771072 | bytes 41943040 | tf_op jit(solution)/shard_map/feed_forward/pallas_call | solution.py:400
  385.0 2.7 fusion.137
  387.8 2.7 collective-permute-start.29
  393.5 11.6 %collective-permute-done.29 = bf16[128,2432]{1,0:T(8,128)(2,1)} collective-permute-done((bf16[128,2432]{1,0:T(8,128)(2,1)}, bf16[128,2432]{1,0:T(8,128)(2,1)}, u32[]{:S(2)}, u32[]{:S(2)}) %collective-permute-start.29) | collective-permute-done | bytes 622624 | tf_op jit(solution)/shard_map/ppermute | solution.py:73
  405.0 13.9 %collective-permute-done.30 = bf16[128,2432]{1,0:T(8,128)(2,1)} collective-permute-done((bf16[128,2432]{1,0:T(8,128)(2,1)}, bf16[128,2432]{1,0:T(8,128)(2,1)}, u32[]{:S(2)}, u32[]{:S(2)}) %collective-permute-start.30) | collective-permute-done | bytes 622624 | tf_op jit(solution)/shard_map/ppermute | solution.py:73
  424.0 2.9 fusion.128
  433.6 2.9 copy.147
  436.5 2.9 collective-permute-done.34
  442.7 14.5 %attend_back.1 = (f32[512,512]{1,0:T(8,128)S(1)}, bf16[4,512,512]{2,1,0:T(8,128)(2,1)}, bf16[4,512,512]{2,1,0:T(8,128)(2,1)}, bf16[4,512,512]{2,1,0:T(8,128)(2,1)}, bf16[4,512,512]{2,1,0:T(8,128)(2,1)}) custom-call(s32[64]{0:T(128)S(1)} %pad_add_fusion.2.active, bf16[512,512]{1,0:T(8,128)(2,1)S(1)} %fusion.23.q_ref, s32[512,1]{1,0:T(8,128)S(1)} %copy-done.6, ...), custom_call_target="tpu_custom_call" | custom-call | flops 12884901888 | bytes 20971520 | tf_op jit(solution)/shard_map/attend_back/pallas_call | solution.py:306
  459.8 2.6 collective-permute-start.40
  465.1 3.6 add_convert_fusion.2
  473.0 3.3 collective-permute-start.36
  476.3 11.7 %collective-permute-done.36 = bf16[128,2048]{1,0:T(8,128)(2,1)S(1)} collective-permute-done((bf16[128,2048]{1,0:T(8,128)(2,1)S(1)}, bf16[128,2048]{1,0:T(8,128)(2,1)S(1)}, u32[]{:S(2)}, u32[]{:S(2)}) %collective-permute-start.36) | collective-permute-done | bytes 524320 | tf_op jit(solution)/shard_map/ppermute | solution.py:73
  488.0 3.5 collective-permute-start.37
  491.5 11.0 %collective-permute-done.37 = bf16[128,2048]{1,0:T(8,128)(2,1)S(1)} collective-permute-done((bf16[128,2048]{1,0:T(8,128)(2,1)S(1)}, bf16[128,2048]{1,0:T(8,128)(2,1)S(1)}, u32[]{:S(2)}, u32[]{:S(2)}) %collective-permute-start.37) | collective-permute-done | bytes 524320 | tf_op jit(solution)/shard_map/ppermute | solution.py:73
  504.5 11.8 %collective-permute-done.38 = bf16[128,2048]{1,0:T(8,128)(2,1)S(1)} collective-permute-done((bf16[128,2048]{1,0:T(8,128)(2,1)S(1)}, bf16[128,2048]{1,0:T(8,128)(2,1)S(1)}, u32[]{:S(2)}, u32[]{:S(2)}) %collective-permute-start.38) | collective-permute-done | bytes 524320 | tf_op jit(solution)/shard_map/ppermute | solution.py:73
  520.7 5.7 add_convert_fusion.1
  531.5 8.5 %collective-permute-done.44 = bf16[512,512]{1,0:T(8,128)(2,1)S(1)} collective-permute-done((bf16[512,512]{1,0:T(8,128)(2,1)S(1)}, bf16[512,512]{1,0:T(8,128)(2,1)S(1)}, u32[]{:S(2)}, u32[]{:S(2)}) %collective-permute-start.44) | collective-permute-done | bytes 524320 | tf_op jit(solution)/shard_map/ppermute | solution.py:73
  540.0 13.2 %collective-permute-done.45 = bf16[512,512]{1,0:T(8,128)(2,1)S(1)} collective-permute-done((bf16[512,512]{1,0:T(8,128)(2,1)S(1)}, bf16[512,512]{1,0:T(8,128)(2,1)S(1)}, u32[]{:S(2)}, u32[]{:S(2)}) %collective-permute-start.45) | collective-permute-done | bytes 524320 | tf_op jit(solution)/shard_map/ppermute | solution.py:73
  555.5 14.3 %reduce-scatter.5.cloned.1.call-done = f32[1,320,128]{2,1,0:T(8,128)} async-done(((f32[32,320,128]{2,1,0:T(8,128)}), f32[1,320,128]{2,1,0:T(8,128)}) %reduce-scatter.5.cloned.1.call-update) | async-done | bytes 163856 | tf_op jit(solution)/shard_map/reduce_scatter | solution.py:757
  579.8 2.8 reshape.662
  611.3 9.4 %collective-permute-start.57 = (bf16[16,80,128]{2,1,0:T(8,128)(2,1)S(1)}, bf16[16,80,128]{2,1,0:T(8,128)(2,1)S(1)}, u32[]{:S(2)}, u32[]{:S(2)}) collective-permute-start(bf16[16,80,128]{2,1,0:T(8,128)(2,1)S(1)} %fusion.42), channel_id=1, source_target_pairs={{0,1},{1,0},{2,3},{3,2},{4,5},{5,4},{6,7},{7,6},{8,9},{9,8},{10,11... | collective-permute-start | bytes 983048 | tf_op jit(solution)/shard_map/ppermute | solution.py:69
  625.0 2.9 fusion.30
  629.8 3.5 collective-permute-start.62
  633.3 2.9 add_convert_fusion
  642.3 2.9 collective-permute-start.65
  648.2 3.5 collective-permute-done.66
  651.7 3.4 collective-permute-start.67
  658.5 3.2 collective-permute-done.68
  662.9 5.1 collective-permute-done.69
  668.0 14.5 %unpack_early.1 = (f32[128,8192]{1,0:T(8,128)}, f32[128,8192]{1,0:T(8,128)}, f32[8192,128]{1,0:T(8,128)}, f32[2048,128]{1,0:T(8,128)}, f32[128,2048]{1,0:T(8,128...) custom-call(bf16[128,272,128]{2,1,0:T(8,128)(2,1)} %all-gather.8.cloned.1.call-done.all_ref), custom_call_target="tpu_custom_call" | custom-call | flops 1048576 | bytes 28311552 | tf_op jit(solution)/shard_map/unpack_early/pallas_call | solution.py:463
  690.9 4.2 collective-permute-done.74
  695.1 4.8 collective-permute-done.75
  700.0 6.3 collective-permute-start.76
  711.4 6.7 unpack_late.1
  (523 shorter events, 199.9 us)
Async XLA Ops:
  7.2 237.1 %all-gather.4.cloned.1.call-start = ((), (), s32[]{:S(2)}) async-start(), calls=%async_computation.4 | async-start | bytes 8454144 | tf_op jit(solution)/shard_map/all_gather | solution.py:618
  9.8 20.7 %collective-permute-start = (bf16[64,2048]{1,0:T(8,128)(2,1)}, bf16[64,2048]{1,0:T(8,128)(2,1)S(1)}, u32[]{:S(2)}, u32[]{:S(2)}) collective-permute-start(bf16[64,2048]{1,0:T(8,128)(2,1)} %get-tuple-element.128), channel_id=1, source_target_pairs={{0,1},{1,0},{2,3},{3,2},{4,5},{5,4},{6,7},{7,6},{8,9},{9,8},{10,11... | collective-permute-start | bytes 786440 | tf_op jit(solution)/shard_map/ppermute | solution.py:69
  13.0 18.3 %collective-permute-start.1 = (bf16[64,2048]{1,0:T(8,128)(2,1)}, bf16[64,2048]{1,0:T(8,128)(2,1)}, u32[]{:S(2)}, u32[]{:S(2)}) collective-permute-start(bf16[64,2048]{1,0:T(8,128)(2,1)} %get-tuple-element.126), channel_id=1, source_target_pairs={{0,1},{1,0},{2,3},{3,2},{4,5},{5,4},{6,7},{7,6},{8,9},{9,8},{10,11... | collective-permute-start | bytes 786440 | tf_op jit(solution)/shard_map/ppermute | solution.py:69
  14.0 12.1 %all-to-all-start = ((bf16[8,16,512]{2,1,0:T(8,128)(2,1)}), bf16[8,16,512]{2,1,0:T(8,128)(2,1)S(1)}, u32[]{:S(2)}, u32[]{:S(2)}) async-start(bf16[8,16,512]{2,1,0:T(8,128)(2,1)} %bitcast.9), calls=%async_computation | async-start | bytes 262144 | tf_op jit(solution)/shard_map/all_to_all | solution.py:605
  26.1 14.1 %all-to-all-start.1 = ((bf16[8,16,2048]{2,1,0:T(8,128)(2,1)}), bf16[8,16,2048]{2,1,0:T(8,128)(2,1)S(1)}, u32[]{:S(2)}, u32[]{:S(2)}) async-start(bf16[8,16,2048]{2,1,0:T(8,128)(2,1)} %pad_maximum_fusion.5), calls=%async_computation.1 | async-start | bytes 1048576 | tf_op jit(solution)/shard_map/all_to_all | solution.py:607
  30.5 309.0 %all-gather.6.cloned.1.call-start = ((), (), s32[]{:S(2)}) async-start(), calls=%async_computation.5 | async-start | bytes 25952256 | tf_op jit(solution)/shard_map/all_gather | solution.py:639
  40.2 14.6 %collective-permute-start.5 = (bf16[128,2048]{1,0:T(8,128)(2,1)S(1)}, bf16[128,2048]{1,0:T(8,128)(2,1)}, u32[]{:S(2)}, u32[]{:S(2)}) collective-permute-start(bf16[128,2048]{1,0:T(8,128)(2,1)S(1)} %pad_maximum_fusion.4), channel_id=1, source_target_pairs={{0,24},{8,0},{16,8},{24,16},{1,25},{9,1},{17,9},{25,17},{2,26},{10... | collective-permute-start | bytes 1572872 | tf_op jit(solution)/shard_map/ppermute | solution.py:73
  42.6 15.3 %collective-permute-start.6 = (bf16[128,2048]{1,0:T(8,128)(2,1)S(1)}, bf16[128,2048]{1,0:T(8,128)(2,1)}, u32[]{:S(2)}, u32[]{:S(2)}) collective-permute-start(bf16[128,2048]{1,0:T(8,128)(2,1)S(1)} %pad_maximum_fusion.4), channel_id=1, source_target_pairs={{0,16},{8,24},{16,0},{24,8},{1,17},{9,25},{17,1},{25,9},{2,18},{10... | collective-permute-start | bytes 1572872 | tf_op jit(solution)/shard_map/ppermute | solution.py:73
  43.9 28.0 %collective-permute-start.7 = (bf16[128,2048]{1,0:T(8,128)(2,1)S(1)}, bf16[128,2048]{1,0:T(8,128)(2,1)S(1)}, u32[]{:S(2)}, u32[]{:S(2)}) collective-permute-start(bf16[128,2048]{1,0:T(8,128)(2,1)S(1)} %pad_maximum_fusion.4), channel_id=1, source_target_pairs={{0,8},{8,16},{16,24},{24,0},{1,9},{9,17},{17,25},{25,1},{2,10},{10... | collective-permute-start | bytes 1572872 | tf_op jit(solution)/shard_map/ppermute | solution.py:73
  45.2 26.8 %collective-permute-start.2 = (bf16[128,2048]{1,0:T(8,128)(2,1)S(1)}, bf16[128,2048]{1,0:T(8,128)(2,1)S(1)}, u32[]{:S(2)}, u32[]{:S(2)}) collective-permute-start(bf16[128,2048]{1,0:T(8,128)(2,1)S(1)} %copy-done.40), channel_id=1, source_target_pairs={{0,6},{2,0},{4,2},{6,4},{1,7},{3,1},{5,3},{7,5},{8,14},{10,8},{12,... | collective-permute-start | bytes 1572872 | tf_op jit(solution)/shard_map/ppermute | solution.py:73
  48.2 23.9 %collective-permute-start.3 = (bf16[128,2048]{1,0:T(8,128)(2,1)S(1)}, bf16[128,2048]{1,0:T(8,128)(2,1)S(1)}, u32[]{:S(2)}, u32[]{:S(2)}) collective-permute-start(bf16[128,2048]{1,0:T(8,128)(2,1)S(1)} %copy-done.40), channel_id=1, source_target_pairs={{0,4},{2,6},{4,0},{6,2},{1,5},{3,7},{5,1},{7,3},{8,12},{10,14},{12... | collective-permute-start | bytes 1572872 | tf_op jit(solution)/shard_map/ppermute | solution.py:73
  54.8 21.7 %collective-permute-start.4 = (bf16[128,2048]{1,0:T(8,128)(2,1)S(1)}, bf16[128,2048]{1,0:T(8,128)(2,1)S(1)}, u32[]{:S(2)}, u32[]{:S(2)}) collective-permute-start(bf16[128,2048]{1,0:T(8,128)(2,1)S(1)} %copy-done.40), channel_id=1, source_target_pairs={{0,2},{2,4},{4,6},{6,0},{1,3},{3,5},{5,7},{7,1},{8,10},{10,12},{12... | collective-permute-start | bytes 1572872 | tf_op jit(solution)/shard_map/ppermute | solution.py:73
  76.5 7.3 %collective-permute-start.8 = (bf16[128,512]{1,0:T(8,128)(2,1)S(1)}, bf16[128,512]{1,0:T(8,128)(2,1)S(1)}, u32[]{:S(2)}, u32[]{:S(2)}) collective-permute-start(bf16[128,512]{1,0:T(8,128)(2,1)S(1)} %bitcast.300), channel_id=1, source_target_pairs={{0,24},{8,0},{16,8},{24,16},{1,25},{9,1},{17,9},{25,17},{2,26},{10... | collective-permute-start | bytes 393224 | tf_op jit(solution)/shard_map/ppermute | solution.py:73
  79.2 7.1 collective-permute-start.9
  79.7 12.1 %collective-permute-start.10 = (bf16[128,512]{1,0:T(8,128)(2,1)S(1)}, bf16[128,512]{1,0:T(8,128)(2,1)S(1)}, u32[]{:S(2)}, u32[]{:S(2)}) collective-permute-start(bf16[128,512]{1,0:T(8,128)(2,1)S(1)} %bitcast.302), channel_id=1, source_target_pairs={{0,8},{8,16},{16,24},{24,0},{1,9},{9,17},{17,25},{25,1},{2,10},{10... | collective-permute-start | bytes 393224 | tf_op jit(solution)/shard_map/ppermute | solution.py:73
  91.9 18.7 %collective-permute-start.11 = (bf16[4,128,512]{2,1,0:T(8,128)(2,1)S(1)}, bf16[4,128,512]{2,1,0:T(8,128)(2,1)S(1)}, u32[]{:S(2)}, u32[]{:S(2)}) collective-permute-start(bf16[4,128,512]{2,1,0:T(8,128)(2,1)S(1)} %bitcast_dynamic-update-slice_fusion.11), channel_id=1, source_target_pairs={{0,96},{32,0},{64,32},{96,64},{1,97},{33,1},{65,33},{97,65},{2,98}... | collective-permute-start | bytes 1572872 | tf_op jit(solution)/shard_map/ppermute | solution.py:73
  95.1 16.8 %collective-permute-start.12 = (bf16[4,128,512]{2,1,0:T(8,128)(2,1)S(1)}, bf16[4,128,512]{2,1,0:T(8,128)(2,1)}, u32[]{:S(2)}, u32[]{:S(2)}) collective-permute-start(bf16[4,128,512]{2,1,0:T(8,128)(2,1)S(1)} %bitcast_dynamic-update-slice_fusion.11), channel_id=1, source_target_pairs={{0,64},{32,96},{64,0},{96,32},{1,65},{33,97},{65,1},{97,33},{2,66}... | collective-permute-start | bytes 1572872 | tf_op jit(solution)/shard_map/ppermute | solution.py:73
  95.2 28.3 %collective-permute-start.13 = (bf16[4,128,512]{2,1,0:T(8,128)(2,1)S(1)}, bf16[4,128,512]{2,1,0:T(8,128)(2,1)S(1)}, u32[]{:S(2)}, u32[]{:S(2)}) collective-permute-start(bf16[4,128,512]{2,1,0:T(8,128)(2,1)S(1)} %bitcast_dynamic-update-slice_fusion.11), channel_id=1, source_target_pairs={{0,32},{32,64},{64,96},{96,0},{1,33},{33,65},{65,97},{97,1},{2,34}... | collective-permute-start | bytes 1572872 | tf_op jit(solution)/shard_map/ppermute | solution.py:73
  124.4 11.8 %collective-permute-start.14 = (bf16[2048,512]{1,0:T(8,128)(2,1)}, bf16[2048,512]{1,0:T(8,128)(2,1)}, u32[]{:S(2)}, u32[]{:S(2)}) collective-permute-start(bf16[2048,512]{1,0:T(8,128)(2,1)} %bitcast.22), channel_id=1, source_target_pairs={{0,1},{1,0},{2,3},{3,2},{4,5},{5,4},{6,7},{7,6},{8,9},{9,8},{10,11... | collective-permute-start | bytes 6291464 | tf_op jit(solution)/shard_map/ppermute | solution.py:69
  142.6 13.6 %collective-permute-start.15 = (bf16[512,512]{1,0:T(8,128)(2,1)S(1)}, bf16[512,512]{1,0:T(8,128)(2,1)S(1)}, u32[]{:S(2)}, u32[]{:S(2)}) collective-permute-start(bf16[512,512]{1,0:T(8,128)(2,1)S(1)} %get-tuple-element.122), channel_id=1, source_target_pairs={{0,24},{8,0},{16,8},{24,16},{1,25},{9,1},{17,9},{25,17},{2,26},{10... | collective-permute-start | bytes 1572872 | tf_op jit(solution)/shard_map/ppermute | solution.py:73
  143.2 14.7 %collective-permute-start.16 = (bf16[512,512]{1,0:T(8,128)(2,1)S(1)}, bf16[512,512]{1,0:T(8,128)(2,1)S(1)}, u32[]{:S(2)}, u32[]{:S(2)}) collective-permute-start(bf16[512,512]{1,0:T(8,128)(2,1)S(1)} %get-tuple-element.122), channel_id=1, source_target_pairs={{0,16},{8,24},{16,0},{24,8},{1,17},{9,25},{17,1},{25,9},{2,18},{10... | collective-permute-start | bytes 1572872 | tf_op jit(solution)/shard_map/ppermute | solution.py:73
  143.8 26.0 %collective-permute-start.17 = (bf16[512,512]{1,0:T(8,128)(2,1)S(1)}, bf16[512,512]{1,0:T(8,128)(2,1)S(1)}, u32[]{:S(2)}, u32[]{:S(2)}) collective-permute-start(bf16[512,512]{1,0:T(8,128)(2,1)S(1)} %get-tuple-element.122), channel_id=1, source_target_pairs={{0,8},{8,16},{16,24},{24,0},{1,9},{9,17},{17,25},{25,1},{2,10},{10... | collective-permute-start | bytes 1572872 | tf_op jit(solution)/shard_map/ppermute | solution.py:73
  170.1 47.4 %collective-permute-start.18 = (bf16[4,512,512]{2,1,0:T(8,128)(2,1)S(1)}, bf16[4,512,512]{2,1,0:T(8,128)(2,1)S(1)}, u32[]{:S(2)}, u32[]{:S(2)}) collective-permute-start(bf16[4,512,512]{2,1,0:T(8,128)(2,1)S(1)} %pad_maximum_fusion.refs_0_), channel_id=1, source_target_pairs={{0,32},{1,33},{32,0},{33,1},{64,96},{65,97},{96,64},{97,65},{2,34}... | collective-permute-start | bytes 6291464 | tf_op jit(solution)/shard_map/ppermute | solution.py:129
  171.9 67.9 %collective-permute-start.19 = (bf16[4,512,512]{2,1,0:T(8,128)(2,1)S(1)}, bf16[4,512,512]{2,1,0:T(8,128)(2,1)S(1)}, u32[]{:S(2)}, u32[]{:S(2)}) collective-permute-start(bf16[4,512,512]{2,1,0:T(8,128)(2,1)S(1)} %pad_maximum_fusion.refs_0_), channel_id=1, source_target_pairs={{1,64},{33,96},{3,66},{35,98},{5,68},{37,100},{7,70},{39,102},{9,7... | collective-permute-start | bytes 6291464 | tf_op jit(solution)/shard_map/ppermute | solution.py:128
  176.0 65.7 %collective-permute-start.20 = (bf16[4,512,512]{2,1,0:T(8,128)(2,1)S(1)}, bf16[4,512,512]{2,1,0:T(8,128)(2,1)S(1)}, u32[]{:S(2)}, u32[]{:S(2)}) collective-permute-start(bf16[4,512,512]{2,1,0:T(8,128)(2,1)S(1)} %pad_maximum_fusion.refs_0_), channel_id=1, source_target_pairs={{1,96},{33,64},{3,98},{35,66},{5,100},{37,68},{7,102},{39,70},{9,1... | collective-permute-start | bytes 6291464 | tf_op jit(solution)/shard_map/ppermute | solution.py:128
  177.4 65.5 %collective-permute-start.21 = (bf16[4,512,512]{2,1,0:T(8,128)(2,1)S(1)}, bf16[4,512,512]{2,1,0:T(8,128)(2,1)S(1)}, u32[]{:S(2)}, u32[]{:S(2)}) collective-permute-start(bf16[4,512,512]{2,1,0:T(8,128)(2,1)S(1)} %pad_maximum_fusion.refs_0_), channel_id=1, source_target_pairs={{0,1},{2,3},{4,5},{6,7},{8,9},{10,11},{12,13},{14,15},{16,17},{18,... | collective-permute-start | bytes 6291464 | tf_op jit(solution)/shard_map/ppermute | solution.py:130
  247.2 271.0 %reduce-scatter.3.cloned.1.call-start = ((), (), s32[]{:S(2)}) async-start(), calls=%async_computation.6 | async-start | bytes 3244032 | tf_op jit(solution)/shard_map/reduce_scatter | solution.py:702
  248.7 13.1 %collective-permute-start.22 = (bf16[4,512,512]{2,1,0:T(8,128)(2,1)}, bf16[4,512,512]{2,1,0:T(8,128)(2,1)}, u32[]{:S(2)}, u32[]{:S(2)}) collective-permute-start(bf16[4,512,512]{2,1,0:T(8,128)(2,1)} %copy-done.81), channel_id=1, source_target_pairs={{0,1},{2,3},{4,5},{6,7},{8,9},{10,11},{12,13},{14,15},{16,17},{18,... | collective-permute-start | bytes 6291464 | tf_op jit(solution)/shard_map/ppermute | solution.py:130
  272.3 7.1 collective-permute-start.24
  273.4 6.7 collective-permute-start.25
  291.8 27.1 %collective-permute-start.26 = (bf16[128,2048]{1,0:T(8,128)(2,1)S(1)}, bf16[128,2048]{1,0:T(8,128)(2,1)S(1)}, u32[]{:S(2)}, u32[]{:S(2)}) collective-permute-start(bf16[128,2048]{1,0:T(8,128)(2,1)S(1)} %multiply_convert_fusion.1), channel_id=1, source_target_pairs={{0,24},{8,0},{16,8},{24,16},{1,25},{9,1},{17,9},{25,17},{2,26},{10... | collective-permute-start | bytes 1572872 | tf_op jit(solution)/shard_map/ppermute | solution.py:73
  297.3 21.5 %collective-permute-start.27 = (bf16[128,2048]{1,0:T(8,128)(2,1)S(1)}, bf16[128,2048]{1,0:T(8,128)(2,1)S(1)}, u32[]{:S(2)}, u32[]{:S(2)}) collective-permute-start(bf16[128,2048]{1,0:T(8,128)(2,1)S(1)} %multiply_convert_fusion.1), channel_id=1, source_target_pairs={{0,16},{8,24},{16,0},{24,8},{1,17},{9,25},{17,1},{25,9},{2,18},{10... | collective-permute-start | bytes 1572872 | tf_op jit(solution)/shard_map/ppermute | solution.py:73
  297.3 26.7 %collective-permute-start.28 = (bf16[128,2048]{1,0:T(8,128)(2,1)S(1)}, bf16[128,2048]{1,0:T(8,128)(2,1)S(1)}, u32[]{:S(2)}, u32[]{:S(2)}) collective-permute-start(bf16[128,2048]{1,0:T(8,128)(2,1)S(1)} %multiply_convert_fusion.1), channel_id=1, source_target_pairs={{0,8},{8,16},{16,24},{24,0},{1,9},{9,17},{17,25},{25,1},{2,10},{10... | collective-permute-start | bytes 1572872 | tf_op jit(solution)/shard_map/ppermute | solution.py:73
  387.8 17.2 %collective-permute-start.29 = (bf16[128,2432]{1,0:T(8,128)(2,1)}, bf16[128,2432]{1,0:T(8,128)(2,1)}, u32[]{:S(2)}, u32[]{:S(2)}) collective-permute-start(bf16[128,2432]{1,0:T(8,128)(2,1)} %get-tuple-element.86), channel_id=1, source_target_pairs={{0,16},{8,24},{16,0},{24,8},{1,17},{9,25},{17,1},{25,9},{2,18},{10... | collective-permute-start | bytes 1867784 | tf_op jit(solution)/shard_map/ppermute | solution.py:73
  390.5 28.4 %collective-permute-start.30 = (bf16[128,2432]{1,0:T(8,128)(2,1)}, bf16[128,2432]{1,0:T(8,128)(2,1)}, u32[]{:S(2)}, u32[]{:S(2)}) collective-permute-start(bf16[128,2432]{1,0:T(8,128)(2,1)} %get-tuple-element.88), channel_id=1, source_target_pairs={{0,8},{8,16},{16,24},{24,0},{1,9},{9,17},{17,25},{25,1},{2,10},{10... | collective-permute-start | bytes 1867784 | tf_op jit(solution)/shard_map/ppermute | solution.py:73
  390.8 28.1 %collective-permute-start.31 = (bf16[128,2432]{1,0:T(8,128)(2,1)}, bf16[128,2432]{1,0:T(8,128)(2,1)}, u32[]{:S(2)}, u32[]{:S(2)}) collective-permute-start(bf16[128,2432]{1,0:T(8,128)(2,1)} %get-tuple-element.87), channel_id=1, source_target_pairs={{0,24},{8,0},{16,8},{24,16},{1,25},{9,1},{17,9},{25,17},{2,26},{10... | collective-permute-start | bytes 1867784 | tf_op jit(solution)/shard_map/ppermute | solution.py:73
  393.2 176.5 %reduce-scatter.5.cloned.1.call-start = ((), (), s32[]{:S(2)}) async-start(), calls=%async_computation.7 | async-start | bytes 5406720 | tf_op jit(solution)/shard_map/reduce_scatter | solution.py:757
  427.3 9.2 %collective-permute-start.32 = (bf16[128,512]{1,0:T(8,128)(2,1)S(1)}, bf16[128,512]{1,0:T(8,128)(2,1)S(1)}, u32[]{:S(2)}, u32[]{:S(2)}) collective-permute-start(bf16[128,512]{1,0:T(8,128)(2,1)S(1)} %get-tuple-element.117), channel_id=1, source_target_pairs={{0,6},{2,0},{4,2},{6,4},{1,7},{3,1},{5,3},{7,5},{8,14},{10,8},{12,... | collective-permute-start | bytes 393224 | tf_op jit(solution)/shard_map/ppermute | solution.py:73
  429.8 6.8 collective-permute-start.33
  430.3 9.1 %collective-permute-start.34 = (bf16[128,512]{1,0:T(8,128)(2,1)S(1)}, bf16[128,512]{1,0:T(8,128)(2,1)S(1)}, u32[]{:S(2)}, u32[]{:S(2)}) collective-permute-start(bf16[128,512]{1,0:T(8,128)(2,1)S(1)} %get-tuple-element.115), channel_id=1, source_target_pairs={{0,2},{2,4},{4,6},{6,0},{1,3},{3,5},{5,7},{7,1},{8,10},{10,12},{12... | collective-permute-start | bytes 393224 | tf_op jit(solution)/shard_map/ppermute | solution.py:73
  436.5 231.5 %all-gather.8.cloned.1.call-start = ((), (), s32[]{:S(2)}) async-start(), calls=%async_computation.8 | async-start | bytes 8982528 | tf_op jit(solution)/shard_map/all_gather | solution.py:760
  457.2 7.8 %collective-permute-start.35 = (bf16[4,512,512]{2,1,0:T(8,128)(2,1)}, bf16[4,512,512]{2,1,0:T(8,128)(2,1)S(1)}, u32[]{:S(2)}, u32[]{:S(2)}) collective-permute-start(bf16[4,512,512]{2,1,0:T(8,128)(2,1)} %get-tuple-element.51), channel_id=1, source_target_pairs={{1,0},{3,2},{5,4},{7,6},{9,8},{11,10},{13,12},{15,14},{17,16},{19,... | collective-permute-start | bytes 6291464 | tf_op jit(solution)/shard_map/ppermute | solution.py:135
  459.8 60.9 %collective-permute-start.40 = (bf16[4,512,512]{2,1,0:T(8,128)(2,1)}, bf16[4,512,512]{2,1,0:T(8,128)(2,1)}, u32[]{:S(2)}, u32[]{:S(2)}) collective-permute-start(bf16[4,512,512]{2,1,0:T(8,128)(2,1)} %get-tuple-element.54), channel_id=1, source_target_pairs={{1,0},{3,2},{5,4},{7,6},{9,8},{11,10},{13,12},{15,14},{17,16},{19,... | collective-permute-start | bytes 6291464 | tf_op jit(solution)/shard_map/ppermute | solution.py:135
  462.5 58.2 %collective-permute-start.42 = (bf16[4,512,512]{2,1,0:T(8,128)(2,1)}, bf16[4,512,512]{2,1,0:T(8,128)(2,1)}, u32[]{:S(2)}, u32[]{:S(2)}) collective-permute-start(bf16[4,512,512]{2,1,0:T(8,128)(2,1)} %get-tuple-element.54), channel_id=1, source_target_pairs={{64,1},{96,33},{66,3},{98,35},{68,5},{100,37},{70,7},{102,39},{72,... | collective-permute-start | bytes 6291464 | tf_op jit(solution)/shard_map/ppermute | solution.py:136
  463.8 56.9 %collective-permute-start.43 = (bf16[4,512,512]{2,1,0:T(8,128)(2,1)}, bf16[4,512,512]{2,1,0:T(8,128)(2,1)}, u32[]{:S(2)}, u32[]{:S(2)}) collective-permute-start(bf16[4,512,512]{2,1,0:T(8,128)(2,1)} %get-tuple-element.51), channel_id=1, source_target_pairs={{96,1},{64,33},{98,3},{66,35},{100,5},{68,37},{102,7},{70,39},{104... | collective-permute-start | bytes 6291464 | tf_op jit(solution)/shard_map/ppermute | solution.py:136
  469.9 50.8 %collective-permute-start.41 = (bf16[4,512,512]{2,1,0:T(8,128)(2,1)}, bf16[4,512,512]{2,1,0:T(8,128)(2,1)}, u32[]{:S(2)}, u32[]{:S(2)}) collective-permute-start(bf16[4,512,512]{2,1,0:T(8,128)(2,1)} %add_convert_fusion.2), channel_id=1, source_target_pairs={{0,32},{1,33},{32,0},{33,1},{64,96},{65,97},{96,64},{97,65},{2,34}... | collective-permute-start | bytes 6291464 | tf_op jit(solution)/shard_map/ppermute | solution.py:138
  473.0 15.0 %collective-permute-start.36 = (bf16[128,2048]{1,0:T(8,128)(2,1)S(1)}, bf16[128,2048]{1,0:T(8,128)(2,1)S(1)}, u32[]{:S(2)}, u32[]{:S(2)}) collective-permute-start(bf16[128,2048]{1,0:T(8,128)(2,1)S(1)} %get-tuple-element.95), channel_id=1, source_target_pairs={{0,16},{8,24},{16,0},{24,8},{1,17},{9,25},{17,1},{25,9},{2,18},{10... | collective-permute-start | bytes 1572872 | tf_op jit(solution)/shard_map/ppermute | solution.py:73
  488.0 14.5 %collective-permute-start.37 = (bf16[128,2048]{1,0:T(8,128)(2,1)S(1)}, bf16[128,2048]{1,0:T(8,128)(2,1)S(1)}, u32[]{:S(2)}, u32[]{:S(2)}) collective-permute-start(bf16[128,2048]{1,0:T(8,128)(2,1)S(1)} %get-tuple-element.97), channel_id=1, source_target_pairs={{0,8},{8,16},{16,24},{24,0},{1,9},{9,17},{17,25},{25,1},{2,10},{10... | collective-permute-start | bytes 1572872 | tf_op jit(solution)/shard_map/ppermute | solution.py:73
  502.5 13.9 %collective-permute-start.38 = (bf16[128,2048]{1,0:T(8,128)(2,1)S(1)}, bf16[128,2048]{1,0:T(8,128)(2,1)S(1)}, u32[]{:S(2)}, u32[]{:S(2)}) collective-permute-start(bf16[128,2048]{1,0:T(8,128)(2,1)S(1)} %get-tuple-element.96), channel_id=1, source_target_pairs={{0,24},{8,0},{16,8},{24,16},{1,25},{9,1},{17,9},{25,17},{2,26},{10... | collective-permute-start | bytes 1572872 | tf_op jit(solution)/shard_map/ppermute | solution.py:73
  526.5 13.5 %collective-permute-start.44 = (bf16[512,512]{1,0:T(8,128)(2,1)S(1)}, bf16[512,512]{1,0:T(8,128)(2,1)S(1)}, u32[]{:S(2)}, u32[]{:S(2)}) collective-permute-start(bf16[512,512]{1,0:T(8,128)(2,1)S(1)} %get-tuple-element.92), channel_id=1, source_target_pairs={{0,16},{8,24},{16,0},{24,8},{1,17},{9,25},{17,1},{25,9},{2,18},{10... | collective-permute-start | bytes 1572872 | tf_op jit(solution)/shard_map/ppermute | solution.py:73
  528.9 24.4 %collective-permute-start.45 = (bf16[512,512]{1,0:T(8,128)(2,1)S(1)}, bf16[512,512]{1,0:T(8,128)(2,1)S(1)}, u32[]{:S(2)}, u32[]{:S(2)}) collective-permute-start(bf16[512,512]{1,0:T(8,128)(2,1)S(1)} %get-tuple-element.94), channel_id=1, source_target_pairs={{0,8},{8,16},{16,24},{24,0},{1,9},{9,17},{17,25},{25,1},{2,10},{10... | collective-permute-start | bytes 1572872 | tf_op jit(solution)/shard_map/ppermute | solution.py:73
  529.2 24.0 %collective-permute-start.46 = (bf16[512,512]{1,0:T(8,128)(2,1)S(1)}, bf16[512,512]{1,0:T(8,128)(2,1)S(1)}, u32[]{:S(2)}, u32[]{:S(2)}) collective-permute-start(bf16[512,512]{1,0:T(8,128)(2,1)S(1)} %get-tuple-element.93), channel_id=1, source_target_pairs={{0,24},{8,0},{16,8},{24,16},{1,25},{9,1},{17,9},{25,17},{2,26},{10... | collective-permute-start | bytes 1572872 | tf_op jit(solution)/shard_map/ppermute | solution.py:73
  593.1 7.2 collective-permute-start.50
  611.3 10.8 %collective-permute-start.57 = (bf16[16,80,128]{2,1,0:T(8,128)(2,1)S(1)}, bf16[16,80,128]{2,1,0:T(8,128)(2,1)S(1)}, u32[]{:S(2)}, u32[]{:S(2)}) collective-permute-start(bf16[16,80,128]{2,1,0:T(8,128)(2,1)S(1)} %fusion.42), channel_id=1, source_target_pairs={{0,1},{1,0},{2,3},{3,2},{4,5},{5,4},{6,7},{7,6},{8,9},{9,8},{10,11... | collective-permute-start | bytes 983048 | tf_op jit(solution)/shard_map/ppermute | solution.py:69
  621.5 85.8 %collective-permute-start.39 = (bf16[64,2048]{1,0:T(8,128)(2,1)}, bf16[64,2048]{1,0:T(8,128)(2,1)}, u32[]{:S(2)}, u32[]{:S(2)}) collective-permute-start(bf16[64,2048]{1,0:T(8,128)(2,1)} %get-tuple-element.113), channel_id=1, source_target_pairs={{0,1},{1,0},{2,3},{3,2},{4,5},{5,4},{6,7},{7,6},{8,9},{9,8},{10,11... | collective-permute-start | bytes 786440 | tf_op jit(solution)/shard_map/ppermute | solution.py:69
  622.2 7.0 collective-permute-start.58
  622.3 6.9 collective-permute-start.59
  629.4 6.9 collective-permute-start.61
  639.2 46.0 %collective-permute-start.47 = (bf16[128,2048]{1,0:T(8,128)(2,1)}, bf16[128,2048]{1,0:T(8,128)(2,1)}, u32[]{:S(2)}, u32[]{:S(2)}) collective-permute-start(bf16[128,2048]{1,0:T(8,128)(2,1)} %get-tuple-element.89), channel_id=1, source_target_pairs={{0,4},{2,6},{4,0},{6,2},{1,5},{3,7},{5,1},{7,3},{8,12},{10,14},{12... | collective-permute-start | bytes 1572872 | tf_op jit(solution)/shard_map/ppermute | solution.py:73
  639.6 45.5 %collective-permute-start.48 = (bf16[128,2048]{1,0:T(8,128)(2,1)}, bf16[128,2048]{1,0:T(8,128)(2,1)}, u32[]{:S(2)}, u32[]{:S(2)}) collective-permute-start(bf16[128,2048]{1,0:T(8,128)(2,1)} %get-tuple-element.91), channel_id=1, source_target_pairs={{0,2},{2,4},{4,6},{6,0},{1,3},{3,5},{5,7},{7,1},{8,10},{10,12},{12... | collective-permute-start | bytes 1572872 | tf_op jit(solution)/shard_map/ppermute | solution.py:73
  640.0 45.2 %collective-permute-start.49 = (bf16[128,2048]{1,0:T(8,128)(2,1)}, bf16[128,2048]{1,0:T(8,128)(2,1)}, u32[]{:S(2)}, u32[]{:S(2)}) collective-permute-start(bf16[128,2048]{1,0:T(8,128)(2,1)} %get-tuple-element.90), channel_id=1, source_target_pairs={{0,6},{2,0},{4,2},{6,4},{1,7},{3,1},{5,3},{7,5},{8,14},{10,8},{12,... | collective-permute-start | bytes 1572872 | tf_op jit(solution)/shard_map/ppermute | solution.py:73
  687.5 7.6 %collective-permute-start.74 = (bf16[4,4,80,128]{3,2,1,0:T(8,128)(2,1)S(1)}, bf16[4,4,80,128]{3,2,1,0:T(8,128)(2,1)S(1)}, u32[]{:S(2)}, u32[]{:S(2)}) collective-permute-start(bf16[4,4,80,128]{3,2,1,0:T(8,128)(2,1)S(1)} %get-tuple-element.73), channel_id=1, source_target_pairs={{0,4},{2,6},{4,0},{6,2},{1,5},{3,7},{5,1},{7,3},{8,12},{10,14},{12... | collective-permute-start | bytes 983048 | tf_op jit(solution)/shard_map/ppermute | solution.py:73
  688.0 12.0 %collective-permute-start.75 = (bf16[4,4,80,128]{3,2,1,0:T(8,128)(2,1)S(1)}, bf16[4,4,80,128]{3,2,1,0:T(8,128)(2,1)S(1)}, u32[]{:S(2)}, u32[]{:S(2)}) collective-permute-start(bf16[4,4,80,128]{3,2,1,0:T(8,128)(2,1)S(1)} %get-tuple-element.73), channel_id=1, source_target_pairs={{0,2},{2,4},{4,6},{6,0},{1,3},{3,5},{5,7},{7,1},{8,10},{10,12},{12... | collective-permute-start | bytes 983048 | tf_op jit(solution)/shard_map/ppermute | solution.py:73
  700.0 10.3 %collective-permute-start.76 = (bf16[4,16,80,128]{3,2,1,0:T(8,128)(2,1)S(1)}, bf16[4,16,80,128]{3,2,1,0:T(8,128)(2,1)S(1)}, u32[]{:S(2)}, u32[]{:S(2)}) collective-permute-start(bf16[4,16,80,128]{3,2,1,0:T(8,128)(2,1)S(1)} %bitcast.276), channel_id=1, source_target_pairs={{0,1},{1,0},{2,3},{3,2},{4,5},{5,4},{6,7},{7,6},{8,9},{9,8},{10,11... | collective-permute-start | bytes 3932168 | tf_op jit(solution)/shard_map/ppermute | solution.py:69
  (107 other events, 1537.2 us)
Sparse Core Ops, SparseCore 0:
  11.1 106.0 all-gather.3
  247.3 92.0 all-gather.5
  393.3 78.1 reduce-scatter.2
  475.6 94.1 reduce-scatter.4
  578.1 88.9 all-gather.7

commit v4 on v3

--- a/solution.py
+++ b/solution.py
@@ -188,7 +188,7 @@
             scores = jnp.where(allowed, scores, neg_big)
             top_old = top[head]
             top_new = jnp.maximum(top_old, jnp.max(scores, axis=-1, keepdims=True))
-            weights_p = jnp.where(allowed, jnp.exp(scores - top_new), 0.0)
+            weights_p = jnp.exp(scores - top_new)
             damping = jnp.exp(top_old - top_new)
             total[head] = total[head] * damping + jnp.sum(weights_p, axis=-1, keepdims=True)
             accum[head] = accum[head] * damping + product(weights_p.astype(bf16), tile_buf[:, HEAD_SIZE:])
@@ -447,16 +447,21 @@
     return found
 
 
+def turned(array):
+    at = lax.broadcasted_iota(jnp.int32, (128, 128), 0), lax.broadcasted_iota(jnp.int32, (128, 128), 1)
+    return times_transposed((at[0] == at[1]).astype(f32).astype(bf16), array)
+
+
 def early_kernel(all_ref, gate_ref, up_ref, down_ref, oshrink_ref, oexpand_ref, dexpand_ref, gateup_ref):
-    pieces = [piece.astype(f32).reshape(-1, 128) for piece in cut(all_ref[...], EARLY)]
-    gate_ref[...] = pieces[0].T
-    up_ref[...] = pieces[1].T
-    down_ref[...] = pieces[2]
-    oshrink_ref[...] = pieces[3]
-    oexpand_ref[...] = pieces[4].T
-    dexpand_ref[...] = pieces[5].T
-    gateup_ref[:, :128] = pieces[6]
-    gateup_ref[:, 128:] = pieces[7]
+    pieces = [piece.reshape(-1, 128) for piece in cut(all_ref[...], EARLY)]
+    gate_ref[...] = turned(pieces[0])
+    up_ref[...] = turned(pieces[1])
+    down_ref[...] = pieces[2].astype(f32)
+    oshrink_ref[...] = pieces[3].astype(f32)
+    oexpand_ref[...] = turned(pieces[4])
+    dexpand_ref[...] = turned(pieces[5])
+    gateup_ref[:, :128] = pieces[6].astype(f32)
+    gateup_ref[:, 128:] = pieces[7].astype(f32)
 
 
 def unpack_early(everyone):
@@ -488,9 +493,9 @@
     pieces = [
         jnp.stack(pair, axis=1).reshape(-1, 128) for pair in zip(cut(first, LATE), cut(second, LATE))
     ]
-    q_ref[...] = pieces[0].T
-    k_ref[...] = pieces[1].T
-    v_ref[...] = pieces[2].T
+    q_ref[...] = turned(pieces[0].astype(bf16))
+    k_ref[...] = turned(pieces[1].astype(bf16))
+    v_ref[...] = turned(pieces[2].astype(bf16))
     for at in range(3):
         low_ref[:, at * 128 : (at + 1) * 128] = pieces[3 + at]
 
@@ -604,14 +609,13 @@
     qkv_parts = jnp.transpose(jnp.stack([heads_q, heads_kv], axis=2), (1, 2, 0, 3)).reshape(8, 16, 512)
     qkv_parts = lax.all_to_all(qkv_parts, ("y", "c"), split_axis=0, concat_axis=0, tiled=True).reshape(128, 512)
     gate_up = jnp.concatenate([column_slices(w_gate), column_slices(w_up)], axis=2)
-    gate_up = lax.all_to_all(after(gate_up, qkv_parts), ("x", "c"), split_axis=0, concat_axis=0, tiled=True).reshape(128, 2048)
     def columns_of(array, width):
         return lax.dynamic_slice_in_dim(array, y * width, width, 1)
 
     inputs = hidden.astype(f32)
     scale_in = row_scale(inputs)
     normed = (inputs * scale_in * gain_attn).astype(bf16)
-    normed, cot, qkv_parts, gate_up = lax.optimization_barrier((normed, cot, qkv_parts, gate_up))
+    normed, cot, qkv_parts = lax.optimization_barrier((normed, cot, qkv_parts))
     normed_g = gather_near(normed, "y")
     cot_g = gather_near(cot, "x")
     qkv_parts = after(qkv_parts, normed_g, cot_g)
@@ -634,6 +638,8 @@
     key = (key_heads * cos_table + rotate(key_heads) * sin_table).astype(bf16).reshape(GROUP, 256)
 
     lines = gather_row(jnp.concatenate([key, value_lin.astype(bf16)], axis=1))
+    gate_up = gate_up + zero_of(lines[0]).astype(bf16)
+    gate_up = lax.all_to_all(gate_up, ("x", "c"), split_axis=0, concat_axis=0, tiled=True).reshape(128, 2048)
     waited = zero_of(lines[1]) + zero_of(lines[2]) + zero_of(lines[3]) + zero_of(lines[4]) + zero_of(wo)
     ffn = jnp.concatenate([gate_up, w_down], axis=0) + waited.astype(bf16)
     ffn = lax.all_gather(ffn, OVER_X, axis=0, tiled=False).reshape(16, 2, 192, 2048)

time: 739 us -> 739 us (level); the launches traced: 725 us -> 733 us
  starting transfers between devices: 133 us -> 147 us
  waiting for transfers between devices: 321 us -> 309 us
    ppermute x1, waiting for transfers between devices: 37.4 us -> 18.1 us  [gather_row(): partner = lax.ppermute(line, CORNER, PARTNER)]
    all_gather x1, waiting for transfers between devices: 12.2 us -> 28.1 us  [local(): lax.all_gather(ffn, OVER_X, axis=0, tiled=False).reshape(16, 2, 192, 2048)]
    ppermute x1, starting transfers between devices: 2.13 us -> 12.7 us  [sum_row(): terms = [got[1], lax.ppermute(sent, CORNER, PARTNER)] + terms]
    reduce_scatter x1, waiting for transfers between devices: 14.3 us -> 6.12 us  [local(): lax.psum_scatter(row_terms, OVER_X, scatter_dimension=0, tiled=False)]
    unnamed x188 -> x178, local copies, waits for them, and re-layouts: 16.7 us -> 13.4 us
  transfers between devices with their start and end apart: 84 -> 84, of which waited for: 46 -> 43; matrix products, arithmetic and copies ran while one was open for 19% -> 20% of each run, Pallas kernels for 5% -> 5%
where the time goes in v4:
time: 739 us; the launch traced here: 733 us
  waiting for transfers between devices  309 us (42%)
  starting transfers between devices  147 us (20%)
  Pallas kernels  91 us (12%)
  local copies, waits for them, and re-layouts  68.7 us (9%)
  matrix products  52 us (7%)
  other arithmetic  42 us (6%)
  between operations  23.4 us (3%)
    ppermute x60, waiting for transfers between devices, shift(): lax.ppermute(value, RING[ring], [(i, (i + step) % 4) for i in range(4)])  228 us
    ppermute x60, starting transfers between devices, shift(): lax.ppermute(value, RING[ring], [(i, (i + step) % 4) for i in range(4)])  85.7 us
    pallas_call x1, Pallas kernels, feed_forward(): pl.pallas_call(ffn_kernel, grid_spec=pltpu.PrefetchScalarGridSpec(num_sca...  45.6 us
    all_gather x1, waiting for transfers between devices, local(): lax.all_gather(ffn, OVER_X, axis=0, tiled=False).reshape(16, 2, 192, 2048)  28.1 us
    dot_general x11, matrix products, product(): return jnp.dot(left, right, preferred_element_type=f32)  26.6 us
    ppermute x2, waiting for transfers between devices, gather_row(): ahead = [lax.ppermute(line, CORNER, pairs) for pairs in LATER]  20.1 us
    ppermute x1, waiting for transfers between devices, gather_row(): partner = lax.ppermute(line, CORNER, PARTNER)  18.1 us
    dot_general x11, matrix products, times_transposed(): lax.dot_general(left, right, (((1,), (1,)), ((), ())), preferred_element_...  17.5 us
  transfers between devices with their start and end apart: 84, of which 43 were waited for; matrix products, arithmetic and copies ran while one was open for 20% of the time, Pallas kernels for 5%

profile of v4, /device:TPU:1, one launch (start us, length us, event | category | flops | bytes accessed | tf_op | source)
XLA Modules:
  0.0 733.2 jit_solution(16611302787440013726)
XLA Ops:
  12.7 5.0 all-to-all-start
  23.0 2.5 collective-permute-start.5
  31.1 6.1 collective-permute-done.5
  37.9 3.5 collective-permute-done.6
  42.5 11.6 %collective-permute-done.7 = bf16[128,2048]{1,0:T(8,128)(2,1)S(1)} collective-permute-done((bf16[128,2048]{1,0:T(8,128)(2,1)S(1)}, bf16[128,2048]{1,0:T(8,128)(2,1)S(1)}, u32[]{:S(2)}, u32[]{:S(2)}) %collective-permute-start.7) | collective-permute-done | bytes 524320 | tf_op jit(solution)/shard_map/ppermute | solution.py:73
  54.4 5.9 collective-permute-start.9
  65.7 7.6 %collective-permute-start.11 = (bf16[4,128,512]{2,1,0:T(8,128)(2,1)S(1)}, bf16[4,128,512]{2,1,0:T(8,128)(2,1)S(1)}, u32[]{:S(2)}, u32[]{:S(2)}) collective-permute-start(bf16[4,128,512]{2,1,0:T(8,128)(2,1)S(1)} %bitcast_dynamic-update-slice_fusion.11), channel_id=1, source_target_pairs={{0,96},{32,0},{64,32},{96,64},{1,97},{33,1},{65,33},{97,65},{2,98}... | collective-permute-start | bytes 1572872 | tf_op jit(solution)/shard_map/ppermute | solution.py:73
  76.5 4.6 collective-permute-done.11
  82.0 3.1 collective-permute-done.12
  85.9 25.3 %collective-permute-done.13 = bf16[4,128,512]{2,1,0:T(8,128)(2,1)S(1)} collective-permute-done((bf16[4,128,512]{2,1,0:T(8,128)(2,1)S(1)}, bf16[4,128,512]{2,1,0:T(8,128)(2,1)S(1)}, u32[]{:S(2)}, u32[]{:S(2)}) %collective-permute-start.13) | collective-permute-done | bytes 524320 | tf_op jit(solution)/shard_map/ppermute | solution.py:73
  115.7 3.1 fusion.2
  119.9 2.9 fusion.147
  122.8 4.2 broadcast_select_fusion
  130.1 12.0 %collective-permute-done.15 = bf16[512,512]{1,0:T(8,128)(2,1)S(1)} collective-permute-done((bf16[512,512]{1,0:T(8,128)(2,1)S(1)}, bf16[512,512]{1,0:T(8,128)(2,1)S(1)}, u32[]{:S(2)}, u32[]{:S(2)}) %collective-permute-start.15) | collective-permute-done | bytes 524320 | tf_op jit(solution)/shard_map/ppermute | solution.py:73
  143.5 11.8 %collective-permute-done.17 = bf16[512,512]{1,0:T(8,128)(2,1)S(1)} collective-permute-done((bf16[512,512]{1,0:T(8,128)(2,1)S(1)}, bf16[512,512]{1,0:T(8,128)(2,1)S(1)}, u32[]{:S(2)}, u32[]{:S(2)}) %collective-permute-start.17) | collective-permute-done | bytes 524320 | tf_op jit(solution)/shard_map/ppermute | solution.py:73
  156.9 6.2 collective-permute-start.19
  163.1 2.6 collective-permute-start.20
  179.3 6.5 all-to-all-start.1
  185.8 18.1 %collective-permute-done.18.refs_1_ = bf16[4,512,512]{2,1,0:T(8,128)(2,1)} collective-permute-done((bf16[4,512,512]{2,1,0:T(8,128)(2,1)}, bf16[4,512,512]{2,1,0:T(8,128)(2,1)}, u32[]{:S(2)}, u32[]{:S(2)}) %collective-permute-start.18) | collective-permute-done | bytes 2097184 | tf_op jit(solution)/shard_map/ppermute | solution.py:129
  205.0 20.1 %collective-permute-done.19.refs_2_ = bf16[4,512,512]{2,1,0:T(8,128)(2,1)} collective-permute-done((bf16[4,512,512]{2,1,0:T(8,128)(2,1)}, bf16[4,512,512]{2,1,0:T(8,128)(2,1)}, u32[]{:S(2)}, u32[]{:S(2)}) %collective-permute-start.19) | collective-permute-done | bytes 2097184 | tf_op jit(solution)/shard_map/ppermute | solution.py:128
  243.7 2.8 reshape.654
  250.2 8.9 %attend.1 = (f32[512,512]{1,0:T(8,128)S(1)}, f32[2,512,1]{2,1,0:T(8,128)S(1)}) custom-call(s32[64]{0:T(128)S(1)} %pad_add_fusion.2.active, bf16[512,512]{1,0:T(8,128)(2,1)S(1)} %fusion.23.q_ref, s32[512,1]{1,0:T(8,128)S(1)} %copy.137.pos_ref, s32[512,1]{1,0:T(8,128)S(1)} %copy.138.start_ref, s32[16,1,512]{2,1,0:T(1,128)S(1)} %reshape.655.kpos_ref, ...), custom_call_target="tpu_custom_call" | custom-call | flops 6442450944 | bytes 10485760 | tf_op jit(solution)/shard_map/attend/pallas_call | solution.py:281
  260.2 3.2 collective-permute-start.23
  276.0 6.4 multiply_reduce_fusion.1
  283.2 2.8 collective-permute-start.26
  289.7 7.3 collective-permute-done.26
  297.1 4.5 collective-permute-done.28
  304.8 28.1 %all-gather.6.cloned.1.call-done = bf16[32,192,2048]{2,1,0:T(8,128)(2,1)} async-done(((bf16[1,192,2048]{2,1,0:T(8,128)(2,1)}), bf16[32,192,2048]{2,1,0:T(8,128)(2,1)}) %all-gather.6.cloned.1.call-update) | async-done | bytes 25165840 | tf_op jit(solution)/shard_map/all_gather | solution.py:645
  332.9 45.6 %feed_forward.1 = (bf16[512,2048]{1,0:T(8,128)(2,1)}, bf16[512,2432]{1,0:T(8,128)(2,1)}, f32[4,4,2,192,128]{4,3,2,1,0:T(8,128)}) custom-call(s32[1]{0:T(128)} %bitcast.36.at, bf16[512,2048]{1,0:T(8,128)(2,1)} %pad_maximum_fusion.1.nm_ref, bf16[512,2048]{1,0:T(8,128)(2,1)} %copy-done.60, bf16[512,256]{1,0:T(8,128)(2,1)} %fusion.3.lgu_ref, ...), custom_call_target="tpu_custom_call" | custom-call | flops 30064771072 | bytes 41943040 | tf_op jit(solution)/shard_map/feed_forward/pallas_call | solution.py:400
  378.6 2.7 fusion.137
  381.3 2.6 collective-permute-start.29
  386.9 11.7 %collective-permute-done.29 = bf16[128,2432]{1,0:T(8,128)(2,1)} collective-permute-done((bf16[128,2432]{1,0:T(8,128)(2,1)}, bf16[128,2432]{1,0:T(8,128)(2,1)}, u32[]{:S(2)}, u32[]{:S(2)}) %collective-permute-start.29) | collective-permute-done | bytes 622624 | tf_op jit(solution)/shard_map/ppermute | solution.py:73
  398.6 13.9 %collective-permute-done.30 = bf16[128,2432]{1,0:T(8,128)(2,1)} collective-permute-done((bf16[128,2432]{1,0:T(8,128)(2,1)}, bf16[128,2432]{1,0:T(8,128)(2,1)}, u32[]{:S(2)}, u32[]{:S(2)}) %collective-permute-start.30) | collective-permute-done | bytes 622624 | tf_op jit(solution)/shard_map/ppermute | solution.py:73
  417.7 2.9 fusion.128
  420.9 2.4 collective-permute-start.32
  427.1 2.9 copy.147
  430.1 2.5 collective-permute-done.34
  436.1 14.5 %attend_back.1 = (f32[512,512]{1,0:T(8,128)S(1)}, bf16[4,512,512]{2,1,0:T(8,128)(2,1)}, bf16[4,512,512]{2,1,0:T(8,128)(2,1)}, bf16[4,512,512]{2,1,0:T(8,128)(2,1)}, bf16[4,512,512]{2,1,0:T(8,128)(2,1)}) custom-call(s32[64]{0:T(128)S(1)} %pad_add_fusion.2.active, bf16[512,512]{1,0:T(8,128)(2,1)S(1)} %fusion.23.q_ref, s32[512,1]{1,0:T(8,128)S(1)} %copy-done.4, ...), custom_call_target="tpu_custom_call" | custom-call | flops 12884901888 | bytes 20971520 | tf_op jit(solution)/shard_map/attend_back/pallas_call | solution.py:306
  450.6 6.2 collective-permute-start.35
  456.8 2.7 collective-permute-start.40
  462.1 3.7 add_convert_fusion.2
  467.0 12.7 %collective-permute-start.41 = (bf16[4,512,512]{2,1,0:T(8,128)(2,1)}, bf16[4,512,512]{2,1,0:T(8,128)(2,1)}, u32[]{:S(2)}, u32[]{:S(2)}) collective-permute-start(bf16[4,512,512]{2,1,0:T(8,128)(2,1)} %add_convert_fusion.2), channel_id=1, source_target_pairs={{0,32},{1,33},{32,0},{33,1},{64,96},{65,97},{96,64},{97,65},{2,34}... | collective-permute-start | bytes 6291464 | tf_op jit(solution)/shard_map/ppermute | solution.py:138
  480.7 14.8 %collective-permute-done.36 = bf16[128,2048]{1,0:T(8,128)(2,1)S(1)} collective-permute-done((bf16[128,2048]{1,0:T(8,128)(2,1)S(1)}, bf16[128,2048]{1,0:T(8,128)(2,1)S(1)}, u32[]{:S(2)}, u32[]{:S(2)}) %collective-permute-start.36) | collective-permute-done | bytes 524320 | tf_op jit(solution)/shard_map/ppermute | solution.py:73
  495.5 14.3 %collective-permute-done.37 = bf16[128,2048]{1,0:T(8,128)(2,1)S(1)} collective-permute-done((bf16[128,2048]{1,0:T(8,128)(2,1)S(1)}, bf16[128,2048]{1,0:T(8,128)(2,1)S(1)}, u32[]{:S(2)}, u32[]{:S(2)}) %collective-permute-start.37) | collective-permute-done | bytes 524320 | tf_op jit(solution)/shard_map/ppermute | solution.py:73
  510.3 12.3 %collective-permute-done.38 = bf16[128,2048]{1,0:T(8,128)(2,1)S(1)} collective-permute-done((bf16[128,2048]{1,0:T(8,128)(2,1)S(1)}, bf16[128,2048]{1,0:T(8,128)(2,1)S(1)}, u32[]{:S(2)}, u32[]{:S(2)}) %collective-permute-start.38) | collective-permute-done | bytes 524320 | tf_op jit(solution)/shard_map/ppermute | solution.py:73
  526.9 6.1 add_convert_fusion.1
  535.9 10.2 %collective-permute-done.44 = bf16[512,512]{1,0:T(8,128)(2,1)S(1)} collective-permute-done((bf16[512,512]{1,0:T(8,128)(2,1)S(1)}, bf16[512,512]{1,0:T(8,128)(2,1)S(1)}, u32[]{:S(2)}, u32[]{:S(2)}) %collective-permute-start.44) | collective-permute-done | bytes 524320 | tf_op jit(solution)/shard_map/ppermute | solution.py:73
  546.1 13.2 %collective-permute-done.45 = bf16[512,512]{1,0:T(8,128)(2,1)S(1)} collective-permute-done((bf16[512,512]{1,0:T(8,128)(2,1)S(1)}, bf16[512,512]{1,0:T(8,128)(2,1)S(1)}, u32[]{:S(2)}, u32[]{:S(2)}) %collective-permute-start.45) | collective-permute-done | bytes 524320 | tf_op jit(solution)/shard_map/ppermute | solution.py:73
  561.6 6.1 reduce-scatter.5.cloned.1.call-done
  569.9 2.4 collective-permute-start.71
  577.7 2.8 reshape.665
  609.3 9.5 %collective-permute-start.57 = (bf16[16,80,128]{2,1,0:T(8,128)(2,1)S(1)}, bf16[16,80,128]{2,1,0:T(8,128)(2,1)S(1)}, u32[]{:S(2)}, u32[]{:S(2)}) collective-permute-start(bf16[16,80,128]{2,1,0:T(8,128)(2,1)S(1)} %fusion.42), channel_id=1, source_target_pairs={{0,1},{1,0},{2,3},{3,2},{4,5},{5,4},{6,7},{7,6},{8,9},{9,8},{10,11... | collective-permute-start | bytes 983048 | tf_op jit(solution)/shard_map/ppermute | solution.py:69
  620.4 9.3 %collective-permute-start.59 = (bf16[4,80,128]{2,1,0:T(8,128)(2,1)S(1)}, bf16[4,80,128]{2,1,0:T(8,128)(2,1)S(1)}, u32[]{:S(2)}, u32[]{:S(2)}) collective-permute-start(bf16[4,80,128]{2,1,0:T(8,128)(2,1)S(1)} %get-tuple-element.103), channel_id=1, source_target_pairs={{0,64},{32,96},{64,0},{96,32},{1,65},{33,97},{65,1},{97,33},{2,66}... | collective-permute-start | bytes 245768 | tf_op jit(solution)/shard_map/ppermute | solution.py:73
  631.7 2.9 fusion.30
  638.8 3.5 add_convert_fusion
  652.8 3.1 collective-permute-done.66
  661.7 3.1 collective-permute-done.68
  665.3 5.0 collective-permute-done.69
  670.4 5.5 all-gather.8.cloned.1.call-done.all_ref
  675.9 15.0 %unpack_early.1 = (f32[128,8192]{1,0:T(8,128)}, f32[128,8192]{1,0:T(8,128)}, f32[8192,128]{1,0:T(8,128)}, f32[2048,128]{1,0:T(8,128)}, f32[128,2048]{1,0:T(8,128...) custom-call(bf16[128,272,128]{2,1,0:T(8,128)(2,1)} %all-gather.8.cloned.1.call-done.all_ref), custom_call_target="tpu_custom_call" | custom-call | flops 1048576 | bytes 28311552 | tf_op jit(solution)/shard_map/unpack_early/pallas_call | solution.py:468
  697.3 2.6 collective-permute-done.73
  700.0 3.6 collective-permute-done.74
  703.6 10.0 %collective-permute-done.75 = bf16[4,4,80,128]{3,2,1,0:T(8,128)(2,1)S(1)} collective-permute-done((bf16[4,4,80,128]{3,2,1,0:T(8,128)(2,1)S(1)}, bf16[4,4,80,128]{3,2,1,0:T(8,128)(2,1)S(1)}, u32[]{:S(2)}, u32[]{:S(2)}) %collective-permute-start.75) | collective-permute-done | bytes 327712 | tf_op jit(solution)/shard_map/ppermute | solution.py:73
  719.6 7.0 unpack_late.1
  (514 shorter events, 193.7 us)
Async XLA Ops:
  7.2 224.1 %all-gather.4.cloned.1.call-start = ((), (), s32[]{:S(2)}) async-start(), calls=%async_computation.4 | async-start | bytes 8454144 | tf_op jit(solution)/shard_map/all_gather | solution.py:622
  9.1 9.4 %collective-permute-start = (bf16[64,2048]{1,0:T(8,128)(2,1)S(1)}, bf16[64,2048]{1,0:T(8,128)(2,1)S(1)}, u32[]{:S(2)}, u32[]{:S(2)}) collective-permute-start(bf16[64,2048]{1,0:T(8,128)(2,1)S(1)} %get-tuple-element.124), channel_id=1, source_target_pairs={{0,1},{1,0},{2,3},{3,2},{4,5},{5,4},{6,7},{7,6},{8,9},{9,8},{10,11... | collective-permute-start | bytes 786440 | tf_op jit(solution)/shard_map/ppermute | solution.py:69
  11.6 7.8 %collective-permute-start.1 = (bf16[64,2048]{1,0:T(8,128)(2,1)S(1)}, bf16[64,2048]{1,0:T(8,128)(2,1)}, u32[]{:S(2)}, u32[]{:S(2)}) collective-permute-start(bf16[64,2048]{1,0:T(8,128)(2,1)S(1)} %get-tuple-element.122), channel_id=1, source_target_pairs={{0,1},{1,0},{2,3},{3,2},{4,5},{5,4},{6,7},{7,6},{8,9},{9,8},{10,11... | collective-permute-start | bytes 786440 | tf_op jit(solution)/shard_map/ppermute | solution.py:69
  12.7 10.3 %all-to-all-start = ((bf16[8,16,512]{2,1,0:T(8,128)(2,1)}), bf16[8,16,512]{2,1,0:T(8,128)(2,1)S(1)}, u32[]{:S(2)}, u32[]{:S(2)}) async-start(bf16[8,16,512]{2,1,0:T(8,128)(2,1)} %bitcast.9), calls=%async_computation | async-start | bytes 262144 | tf_op jit(solution)/shard_map/all_to_all | solution.py:610
  23.0 14.2 %collective-permute-start.5 = (bf16[128,2048]{1,0:T(8,128)(2,1)S(1)}, bf16[128,2048]{1,0:T(8,128)(2,1)S(1)}, u32[]{:S(2)}, u32[]{:S(2)}) collective-permute-start(bf16[128,2048]{1,0:T(8,128)(2,1)S(1)} %pad_maximum_fusion.4), channel_id=1, source_target_pairs={{0,24},{8,0},{16,8},{24,16},{1,25},{9,1},{17,9},{25,17},{2,26},{10... | collective-permute-start | bytes 1572872 | tf_op jit(solution)/shard_map/ppermute | solution.py:73
  27.0 14.4 %collective-permute-start.6 = (bf16[128,2048]{1,0:T(8,128)(2,1)S(1)}, bf16[128,2048]{1,0:T(8,128)(2,1)}, u32[]{:S(2)}, u32[]{:S(2)}) collective-permute-start(bf16[128,2048]{1,0:T(8,128)(2,1)S(1)} %pad_maximum_fusion.4), channel_id=1, source_target_pairs={{0,16},{8,24},{16,0},{24,8},{1,17},{9,25},{17,1},{25,9},{2,18},{10... | collective-permute-start | bytes 1572872 | tf_op jit(solution)/shard_map/ppermute | solution.py:73
  28.2 25.9 %collective-permute-start.7 = (bf16[128,2048]{1,0:T(8,128)(2,1)S(1)}, bf16[128,2048]{1,0:T(8,128)(2,1)S(1)}, u32[]{:S(2)}, u32[]{:S(2)}) collective-permute-start(bf16[128,2048]{1,0:T(8,128)(2,1)S(1)} %pad_maximum_fusion.4), channel_id=1, source_target_pairs={{0,8},{8,16},{16,24},{24,0},{1,9},{9,17},{17,25},{25,1},{2,10},{10... | collective-permute-start | bytes 1572872 | tf_op jit(solution)/shard_map/ppermute | solution.py:73
  29.0 25.2 %collective-permute-start.2 = (bf16[128,2048]{1,0:T(8,128)(2,1)S(1)}, bf16[128,2048]{1,0:T(8,128)(2,1)S(1)}, u32[]{:S(2)}, u32[]{:S(2)}) collective-permute-start(bf16[128,2048]{1,0:T(8,128)(2,1)S(1)} %fusion.9), channel_id=1, source_target_pairs={{0,6},{2,0},{4,2},{6,4},{1,7},{3,1},{5,3},{7,5},{8,14},{10,8},{12,... | collective-permute-start | bytes 1572872 | tf_op jit(solution)/shard_map/ppermute | solution.py:73
  29.9 24.3 %collective-permute-start.3 = (bf16[128,2048]{1,0:T(8,128)(2,1)S(1)}, bf16[128,2048]{1,0:T(8,128)(2,1)S(1)}, u32[]{:S(2)}, u32[]{:S(2)}) collective-permute-start(bf16[128,2048]{1,0:T(8,128)(2,1)S(1)} %fusion.9), channel_id=1, source_target_pairs={{0,4},{2,6},{4,0},{6,2},{1,5},{3,7},{5,1},{7,3},{8,12},{10,14},{12... | collective-permute-start | bytes 1572872 | tf_op jit(solution)/shard_map/ppermute | solution.py:73
  37.2 17.1 %collective-permute-start.4 = (bf16[128,2048]{1,0:T(8,128)(2,1)S(1)}, bf16[128,2048]{1,0:T(8,128)(2,1)S(1)}, u32[]{:S(2)}, u32[]{:S(2)}) collective-permute-start(bf16[128,2048]{1,0:T(8,128)(2,1)S(1)} %fusion.9), channel_id=1, source_target_pairs={{0,2},{2,4},{4,6},{6,0},{1,3},{3,5},{5,7},{7,1},{8,10},{10,12},{12... | collective-permute-start | bytes 1572872 | tf_op jit(solution)/shard_map/ppermute | solution.py:73
  54.4 7.8 %collective-permute-start.8 = (bf16[128,512]{1,0:T(8,128)(2,1)S(1)}, bf16[128,512]{1,0:T(8,128)(2,1)S(1)}, u32[]{:S(2)}, u32[]{:S(2)}) collective-permute-start(bf16[128,512]{1,0:T(8,128)(2,1)S(1)} %bitcast.299), channel_id=1, source_target_pairs={{0,24},{8,0},{16,8},{24,16},{1,25},{9,1},{17,9},{25,17},{2,26},{10... | collective-permute-start | bytes 393224 | tf_op jit(solution)/shard_map/ppermute | solution.py:73
  54.4 8.9 %collective-permute-start.9 = (bf16[128,512]{1,0:T(8,128)(2,1)S(1)}, bf16[128,512]{1,0:T(8,128)(2,1)S(1)}, u32[]{:S(2)}, u32[]{:S(2)}) collective-permute-start(bf16[128,512]{1,0:T(8,128)(2,1)S(1)} %bitcast.300), channel_id=1, source_target_pairs={{0,16},{8,24},{16,0},{24,8},{1,17},{9,25},{17,1},{25,9},{2,18},{10... | collective-permute-start | bytes 393224 | tf_op jit(solution)/shard_map/ppermute | solution.py:73
  65.7 15.5 %collective-permute-start.11 = (bf16[4,128,512]{2,1,0:T(8,128)(2,1)S(1)}, bf16[4,128,512]{2,1,0:T(8,128)(2,1)S(1)}, u32[]{:S(2)}, u32[]{:S(2)}) collective-permute-start(bf16[4,128,512]{2,1,0:T(8,128)(2,1)S(1)} %bitcast_dynamic-update-slice_fusion.11), channel_id=1, source_target_pairs={{0,96},{32,0},{64,32},{96,64},{1,97},{33,1},{65,33},{97,65},{2,98}... | collective-permute-start | bytes 1572872 | tf_op jit(solution)/shard_map/ppermute | solution.py:73
  73.5 11.6 %collective-permute-start.12 = (bf16[4,128,512]{2,1,0:T(8,128)(2,1)S(1)}, bf16[4,128,512]{2,1,0:T(8,128)(2,1)S(1)}, u32[]{:S(2)}, u32[]{:S(2)}) collective-permute-start(bf16[4,128,512]{2,1,0:T(8,128)(2,1)S(1)} %bitcast_dynamic-update-slice_fusion.11), channel_id=1, source_target_pairs={{0,64},{32,96},{64,0},{96,32},{1,65},{33,97},{65,1},{97,33},{2,66}... | collective-permute-start | bytes 1572872 | tf_op jit(solution)/shard_map/ppermute | solution.py:73
  74.0 37.2 %collective-permute-start.13 = (bf16[4,128,512]{2,1,0:T(8,128)(2,1)S(1)}, bf16[4,128,512]{2,1,0:T(8,128)(2,1)S(1)}, u32[]{:S(2)}, u32[]{:S(2)}) collective-permute-start(bf16[4,128,512]{2,1,0:T(8,128)(2,1)S(1)} %bitcast_dynamic-update-slice_fusion.11), channel_id=1, source_target_pairs={{0,32},{32,64},{64,96},{96,0},{1,33},{33,65},{65,97},{97,1},{2,34}... | collective-permute-start | bytes 1572872 | tf_op jit(solution)/shard_map/ppermute | solution.py:73
  112.1 10.7 %collective-permute-start.14 = (bf16[2048,512]{1,0:T(8,128)(2,1)}, bf16[2048,512]{1,0:T(8,128)(2,1)}, u32[]{:S(2)}, u32[]{:S(2)}) collective-permute-start(bf16[2048,512]{1,0:T(8,128)(2,1)} %bitcast.19), channel_id=1, source_target_pairs={{0,1},{1,0},{2,3},{3,2},{4,5},{5,4},{6,7},{7,6},{8,9},{9,8},{10,11... | collective-permute-start | bytes 6291464 | tf_op jit(solution)/shard_map/ppermute | solution.py:69
  128.5 13.6 %collective-permute-start.15 = (bf16[512,512]{1,0:T(8,128)(2,1)S(1)}, bf16[512,512]{1,0:T(8,128)(2,1)S(1)}, u32[]{:S(2)}, u32[]{:S(2)}) collective-permute-start(bf16[512,512]{1,0:T(8,128)(2,1)S(1)} %get-tuple-element.118), channel_id=1, source_target_pairs={{0,24},{8,0},{16,8},{24,16},{1,25},{9,1},{17,9},{25,17},{2,26},{10... | collective-permute-start | bytes 1572872 | tf_op jit(solution)/shard_map/ppermute | solution.py:73
  128.6 14.9 %collective-permute-start.16 = (bf16[512,512]{1,0:T(8,128)(2,1)S(1)}, bf16[512,512]{1,0:T(8,128)(2,1)S(1)}, u32[]{:S(2)}, u32[]{:S(2)}) collective-permute-start(bf16[512,512]{1,0:T(8,128)(2,1)S(1)} %get-tuple-element.118), channel_id=1, source_target_pairs={{0,16},{8,24},{16,0},{24,8},{1,17},{9,25},{17,1},{25,9},{2,18},{10... | collective-permute-start | bytes 1572872 | tf_op jit(solution)/shard_map/ppermute | solution.py:73
  128.7 26.6 %collective-permute-start.17 = (bf16[512,512]{1,0:T(8,128)(2,1)S(1)}, bf16[512,512]{1,0:T(8,128)(2,1)S(1)}, u32[]{:S(2)}, u32[]{:S(2)}) collective-permute-start(bf16[512,512]{1,0:T(8,128)(2,1)S(1)} %get-tuple-element.118), channel_id=1, source_target_pairs={{0,8},{8,16},{16,24},{24,0},{1,9},{9,17},{17,25},{25,1},{2,10},{10... | collective-permute-start | bytes 1572872 | tf_op jit(solution)/shard_map/ppermute | solution.py:73
  156.9 47.0 %collective-permute-start.18 = (bf16[4,512,512]{2,1,0:T(8,128)(2,1)}, bf16[4,512,512]{2,1,0:T(8,128)(2,1)}, u32[]{:S(2)}, u32[]{:S(2)}) collective-permute-start(bf16[4,512,512]{2,1,0:T(8,128)(2,1)} %pad_maximum_fusion.refs_0_), channel_id=1, source_target_pairs={{0,32},{1,33},{32,0},{33,1},{64,96},{65,97},{96,64},{97,65},{2,34}... | collective-permute-start | bytes 6291464 | tf_op jit(solution)/shard_map/ppermute | solution.py:129
  156.9 68.2 %collective-permute-start.19 = (bf16[4,512,512]{2,1,0:T(8,128)(2,1)}, bf16[4,512,512]{2,1,0:T(8,128)(2,1)}, u32[]{:S(2)}, u32[]{:S(2)}) collective-permute-start(bf16[4,512,512]{2,1,0:T(8,128)(2,1)} %pad_maximum_fusion.refs_0_), channel_id=1, source_target_pairs={{1,64},{33,96},{3,66},{35,98},{5,68},{37,100},{7,70},{39,102},{9,7... | collective-permute-start | bytes 6291464 | tf_op jit(solution)/shard_map/ppermute | solution.py:128
  163.1 64.5 %collective-permute-start.20 = (bf16[4,512,512]{2,1,0:T(8,128)(2,1)}, bf16[4,512,512]{2,1,0:T(8,128)(2,1)}, u32[]{:S(2)}, u32[]{:S(2)}) collective-permute-start(bf16[4,512,512]{2,1,0:T(8,128)(2,1)} %pad_maximum_fusion.refs_0_), channel_id=1, source_target_pairs={{1,96},{33,64},{3,98},{35,66},{5,100},{37,68},{7,102},{39,70},{9,1... | collective-permute-start | bytes 6291464 | tf_op jit(solution)/shard_map/ppermute | solution.py:128
  165.8 63.7 %collective-permute-start.21 = (bf16[4,512,512]{2,1,0:T(8,128)(2,1)}, bf16[4,512,512]{2,1,0:T(8,128)(2,1)}, u32[]{:S(2)}, u32[]{:S(2)}) collective-permute-start(bf16[4,512,512]{2,1,0:T(8,128)(2,1)} %pad_maximum_fusion.refs_0_), channel_id=1, source_target_pairs={{0,1},{2,3},{4,5},{6,7},{8,9},{10,11},{12,13},{14,15},{16,17},{18,... | collective-permute-start | bytes 6291464 | tf_op jit(solution)/shard_map/ppermute | solution.py:130
  179.3 53.9 %all-to-all-start.1 = ((bf16[8,16,2048]{2,1,0:T(8,128)(2,1)}), bf16[8,16,2048]{2,1,0:T(8,128)(2,1)}, u32[]{:S(2)}, u32[]{:S(2)}) async-start(bf16[8,16,2048]{2,1,0:T(8,128)(2,1)} %maximum_add_fusion.1), calls=%async_computation.1 | async-start | bytes 1048576 | tf_op jit(solution)/shard_map/all_to_all | solution.py:642
  185.8 147.1 %all-gather.6.cloned.1.call-start = ((), (), s32[]{:S(2)}) async-start(), calls=%async_computation.5 | async-start | bytes 25952256 | tf_op jit(solution)/shard_map/all_gather | solution.py:645
  235.4 289.0 %reduce-scatter.3.cloned.1.call-start = ((), (), s32[]{:S(2)}) async-start(), calls=%async_computation.6 | async-start | bytes 3244032 | tf_op jit(solution)/shard_map/reduce_scatter | solution.py:708
  236.9 13.3 %collective-permute-start.22 = (bf16[4,512,512]{2,1,0:T(8,128)(2,1)}, bf16[4,512,512]{2,1,0:T(8,128)(2,1)}, u32[]{:S(2)}, u32[]{:S(2)}) collective-permute-start(bf16[4,512,512]{2,1,0:T(8,128)(2,1)} %collective-permute-done.18.refs_1_), channel_id=1, source_target_pairs={{0,1},{2,3},{4,5},{6,7},{8,9},{10,11},{12,13},{14,15},{16,17},{18,... | collective-permute-start | bytes 6291464 | tf_op jit(solution)/shard_map/ppermute | solution.py:130
  260.2 8.8 %collective-permute-start.23 = (bf16[128,512]{1,0:T(8,128)(2,1)S(1)}, bf16[128,512]{1,0:T(8,128)(2,1)S(1)}, u32[]{:S(2)}, u32[]{:S(2)}) collective-permute-start(bf16[128,512]{1,0:T(8,128)(2,1)S(1)} %get-tuple-element.116), channel_id=1, source_target_pairs={{0,2},{2,4},{4,6},{6,0},{1,3},{3,5},{5,7},{7,1},{8,10},{10,12},{12... | collective-permute-start | bytes 393224 | tf_op jit(solution)/shard_map/ppermute | solution.py:73
  263.4 6.3 collective-permute-start.24
  283.2 13.8 %collective-permute-start.26 = (bf16[128,2048]{1,0:T(8,128)(2,1)S(1)}, bf16[128,2048]{1,0:T(8,128)(2,1)S(1)}, u32[]{:S(2)}, u32[]{:S(2)}) collective-permute-start(bf16[128,2048]{1,0:T(8,128)(2,1)S(1)} %multiply_convert_fusion.1), channel_id=1, source_target_pairs={{0,24},{8,0},{16,8},{24,16},{1,25},{9,1},{17,9},{25,17},{2,26},{10... | collective-permute-start | bytes 1572872 | tf_op jit(solution)/shard_map/ppermute | solution.py:73
  286.0 11.1 %collective-permute-start.27 = (bf16[128,2048]{1,0:T(8,128)(2,1)S(1)}, bf16[128,2048]{1,0:T(8,128)(2,1)S(1)}, u32[]{:S(2)}, u32[]{:S(2)}) collective-permute-start(bf16[128,2048]{1,0:T(8,128)(2,1)S(1)} %multiply_convert_fusion.1), channel_id=1, source_target_pairs={{0,16},{8,24},{16,0},{24,8},{1,17},{9,25},{17,1},{25,9},{2,18},{10... | collective-permute-start | bytes 1572872 | tf_op jit(solution)/shard_map/ppermute | solution.py:73
  286.4 15.2 %collective-permute-start.28 = (bf16[128,2048]{1,0:T(8,128)(2,1)S(1)}, bf16[128,2048]{1,0:T(8,128)(2,1)S(1)}, u32[]{:S(2)}, u32[]{:S(2)}) collective-permute-start(bf16[128,2048]{1,0:T(8,128)(2,1)S(1)} %multiply_convert_fusion.1), channel_id=1, source_target_pairs={{0,8},{8,16},{16,24},{24,0},{1,9},{9,17},{17,25},{25,1},{2,10},{10... | collective-permute-start | bytes 1572872 | tf_op jit(solution)/shard_map/ppermute | solution.py:73
  381.3 17.2 %collective-permute-start.29 = (bf16[128,2432]{1,0:T(8,128)(2,1)}, bf16[128,2432]{1,0:T(8,128)(2,1)}, u32[]{:S(2)}, u32[]{:S(2)}) collective-permute-start(bf16[128,2432]{1,0:T(8,128)(2,1)} %get-tuple-element.82), channel_id=1, source_target_pairs={{0,16},{8,24},{16,0},{24,8},{1,17},{9,25},{17,1},{25,9},{2,18},{10... | collective-permute-start | bytes 1867784 | tf_op jit(solution)/shard_map/ppermute | solution.py:73
  383.9 28.5 %collective-permute-start.30 = (bf16[128,2432]{1,0:T(8,128)(2,1)}, bf16[128,2432]{1,0:T(8,128)(2,1)}, u32[]{:S(2)}, u32[]{:S(2)}) collective-permute-start(bf16[128,2432]{1,0:T(8,128)(2,1)} %get-tuple-element.84), channel_id=1, source_target_pairs={{0,8},{8,16},{16,24},{24,0},{1,9},{9,17},{17,25},{25,1},{2,10},{10... | collective-permute-start | bytes 1867784 | tf_op jit(solution)/shard_map/ppermute | solution.py:73
  385.0 27.6 %collective-permute-start.31 = (bf16[128,2432]{1,0:T(8,128)(2,1)}, bf16[128,2432]{1,0:T(8,128)(2,1)}, u32[]{:S(2)}, u32[]{:S(2)}) collective-permute-start(bf16[128,2432]{1,0:T(8,128)(2,1)} %get-tuple-element.83), channel_id=1, source_target_pairs={{0,24},{8,0},{16,8},{24,16},{1,25},{9,1},{17,9},{25,17},{2,26},{10... | collective-permute-start | bytes 1867784 | tf_op jit(solution)/shard_map/ppermute | solution.py:73
  386.6 181.1 %reduce-scatter.5.cloned.1.call-start = ((), (), s32[]{:S(2)}) async-start(), calls=%async_computation.7 | async-start | bytes 5406720 | tf_op jit(solution)/shard_map/reduce_scatter | solution.py:763
  420.9 9.1 %collective-permute-start.32 = (bf16[128,512]{1,0:T(8,128)(2,1)S(1)}, bf16[128,512]{1,0:T(8,128)(2,1)S(1)}, u32[]{:S(2)}, u32[]{:S(2)}) collective-permute-start(bf16[128,512]{1,0:T(8,128)(2,1)S(1)} %get-tuple-element.113), channel_id=1, source_target_pairs={{0,6},{2,0},{4,2},{6,4},{1,7},{3,1},{5,3},{7,5},{8,14},{10,8},{12,... | collective-permute-start | bytes 393224 | tf_op jit(solution)/shard_map/ppermute | solution.py:73
  423.3 6.8 collective-permute-start.33
  423.9 8.8 %collective-permute-start.34 = (bf16[128,512]{1,0:T(8,128)(2,1)S(1)}, bf16[128,512]{1,0:T(8,128)(2,1)S(1)}, u32[]{:S(2)}, u32[]{:S(2)}) collective-permute-start(bf16[128,512]{1,0:T(8,128)(2,1)S(1)} %get-tuple-element.111), channel_id=1, source_target_pairs={{0,2},{2,4},{4,6},{6,0},{1,3},{3,5},{5,7},{7,1},{8,10},{10,12},{12... | collective-permute-start | bytes 393224 | tf_op jit(solution)/shard_map/ppermute | solution.py:73
  430.0 245.8 %all-gather.8.cloned.1.call-start = ((), (), s32[]{:S(2)}) async-start(), calls=%async_computation.8 | async-start | bytes 8982528 | tf_op jit(solution)/shard_map/all_gather | solution.py:766
  450.6 11.5 %collective-permute-start.35 = (bf16[4,512,512]{2,1,0:T(8,128)(2,1)}, bf16[4,512,512]{2,1,0:T(8,128)(2,1)S(1)}, u32[]{:S(2)}, u32[]{:S(2)}) collective-permute-start(bf16[4,512,512]{2,1,0:T(8,128)(2,1)} %get-tuple-element.47), channel_id=1, source_target_pairs={{1,0},{3,2},{5,4},{7,6},{9,8},{11,10},{13,12},{15,14},{17,16},{19,... | collective-permute-start | bytes 6291464 | tf_op jit(solution)/shard_map/ppermute | solution.py:135
  456.8 70.0 %collective-permute-start.40 = (bf16[4,512,512]{2,1,0:T(8,128)(2,1)}, bf16[4,512,512]{2,1,0:T(8,128)(2,1)}, u32[]{:S(2)}, u32[]{:S(2)}) collective-permute-start(bf16[4,512,512]{2,1,0:T(8,128)(2,1)} %get-tuple-element.50), channel_id=1, source_target_pairs={{1,0},{3,2},{5,4},{7,6},{9,8},{11,10},{13,12},{15,14},{17,16},{19,... | collective-permute-start | bytes 6291464 | tf_op jit(solution)/shard_map/ppermute | solution.py:135
  459.5 67.3 %collective-permute-start.42 = (bf16[4,512,512]{2,1,0:T(8,128)(2,1)}, bf16[4,512,512]{2,1,0:T(8,128)(2,1)}, u32[]{:S(2)}, u32[]{:S(2)}) collective-permute-start(bf16[4,512,512]{2,1,0:T(8,128)(2,1)} %get-tuple-element.50), channel_id=1, source_target_pairs={{64,1},{96,33},{66,3},{98,35},{68,5},{100,37},{70,7},{102,39},{72,... | collective-permute-start | bytes 6291464 | tf_op jit(solution)/shard_map/ppermute | solution.py:136
  460.8 66.1 %collective-permute-start.43 = (bf16[4,512,512]{2,1,0:T(8,128)(2,1)}, bf16[4,512,512]{2,1,0:T(8,128)(2,1)}, u32[]{:S(2)}, u32[]{:S(2)}) collective-permute-start(bf16[4,512,512]{2,1,0:T(8,128)(2,1)} %get-tuple-element.47), channel_id=1, source_target_pairs={{96,1},{64,33},{98,3},{66,35},{100,5},{68,37},{102,7},{70,39},{104... | collective-permute-start | bytes 6291464 | tf_op jit(solution)/shard_map/ppermute | solution.py:136
  467.0 59.9 %collective-permute-start.41 = (bf16[4,512,512]{2,1,0:T(8,128)(2,1)}, bf16[4,512,512]{2,1,0:T(8,128)(2,1)}, u32[]{:S(2)}, u32[]{:S(2)}) collective-permute-start(bf16[4,512,512]{2,1,0:T(8,128)(2,1)} %add_convert_fusion.2), channel_id=1, source_target_pairs={{0,32},{1,33},{32,0},{33,1},{64,96},{65,97},{96,64},{97,65},{2,34}... | collective-permute-start | bytes 6291464 | tf_op jit(solution)/shard_map/ppermute | solution.py:138
  480.6 14.9 %collective-permute-start.36 = (bf16[128,2048]{1,0:T(8,128)(2,1)S(1)}, bf16[128,2048]{1,0:T(8,128)(2,1)S(1)}, u32[]{:S(2)}, u32[]{:S(2)}) collective-permute-start(bf16[128,2048]{1,0:T(8,128)(2,1)S(1)} %get-tuple-element.91), channel_id=1, source_target_pairs={{0,16},{8,24},{16,0},{24,8},{1,17},{9,25},{17,1},{25,9},{2,18},{10... | collective-permute-start | bytes 1572872 | tf_op jit(solution)/shard_map/ppermute | solution.py:73
  495.5 14.3 %collective-permute-start.37 = (bf16[128,2048]{1,0:T(8,128)(2,1)S(1)}, bf16[128,2048]{1,0:T(8,128)(2,1)S(1)}, u32[]{:S(2)}, u32[]{:S(2)}) collective-permute-start(bf16[128,2048]{1,0:T(8,128)(2,1)S(1)} %get-tuple-element.93), channel_id=1, source_target_pairs={{0,8},{8,16},{16,24},{24,0},{1,9},{9,17},{17,25},{25,1},{2,10},{10... | collective-permute-start | bytes 1572872 | tf_op jit(solution)/shard_map/ppermute | solution.py:73
  509.9 12.7 %collective-permute-start.38 = (bf16[128,2048]{1,0:T(8,128)(2,1)S(1)}, bf16[128,2048]{1,0:T(8,128)(2,1)S(1)}, u32[]{:S(2)}, u32[]{:S(2)}) collective-permute-start(bf16[128,2048]{1,0:T(8,128)(2,1)S(1)} %get-tuple-element.92), channel_id=1, source_target_pairs={{0,24},{8,0},{16,8},{24,16},{1,25},{9,1},{17,9},{25,17},{2,26},{10... | collective-permute-start | bytes 1572872 | tf_op jit(solution)/shard_map/ppermute | solution.py:73
  533.1 13.0 %collective-permute-start.44 = (bf16[512,512]{1,0:T(8,128)(2,1)S(1)}, bf16[512,512]{1,0:T(8,128)(2,1)S(1)}, u32[]{:S(2)}, u32[]{:S(2)}) collective-permute-start(bf16[512,512]{1,0:T(8,128)(2,1)S(1)} %get-tuple-element.88), channel_id=1, source_target_pairs={{0,16},{8,24},{16,0},{24,8},{1,17},{9,25},{17,1},{25,9},{2,18},{10... | collective-permute-start | bytes 1572872 | tf_op jit(solution)/shard_map/ppermute | solution.py:73
  533.2 26.1 %collective-permute-start.45 = (bf16[512,512]{1,0:T(8,128)(2,1)S(1)}, bf16[512,512]{1,0:T(8,128)(2,1)S(1)}, u32[]{:S(2)}, u32[]{:S(2)}) collective-permute-start(bf16[512,512]{1,0:T(8,128)(2,1)S(1)} %get-tuple-element.90), channel_id=1, source_target_pairs={{0,8},{8,16},{16,24},{24,0},{1,9},{9,17},{17,25},{25,1},{2,10},{10... | collective-permute-start | bytes 1572872 | tf_op jit(solution)/shard_map/ppermute | solution.py:73
  534.7 24.7 %collective-permute-start.46 = (bf16[512,512]{1,0:T(8,128)(2,1)S(1)}, bf16[512,512]{1,0:T(8,128)(2,1)S(1)}, u32[]{:S(2)}, u32[]{:S(2)}) collective-permute-start(bf16[512,512]{1,0:T(8,128)(2,1)S(1)} %get-tuple-element.89), channel_id=1, source_target_pairs={{0,24},{8,0},{16,8},{24,16},{1,25},{9,1},{17,9},{25,17},{2,26},{10... | collective-permute-start | bytes 1572872 | tf_op jit(solution)/shard_map/ppermute | solution.py:73
  591.0 7.4 %collective-permute-start.50 = (bf16[128,384]{0,1:T(8,128)(2,1)}, bf16[128,384]{0,1:T(8,128)(2,1)}, u32[]{:S(2)}, u32[]{:S(2)}) collective-permute-start(bf16[128,384]{0,1:T(8,128)(2,1)} %get-tuple-element.125), channel_id=1, source_target_pairs={{0,4},{2,6},{4,0},{6,2},{1,5},{3,7},{5,1},{7,3},{8,12},{10,14},{12... | collective-permute-start | bytes 294920 | tf_op jit(solution)/shard_map/ppermute | solution.py:73
  601.4 6.1 collective-permute-start.56
  609.3 10.9 %collective-permute-start.57 = (bf16[16,80,128]{2,1,0:T(8,128)(2,1)S(1)}, bf16[16,80,128]{2,1,0:T(8,128)(2,1)S(1)}, u32[]{:S(2)}, u32[]{:S(2)}) collective-permute-start(bf16[16,80,128]{2,1,0:T(8,128)(2,1)S(1)} %fusion.42), channel_id=1, source_target_pairs={{0,1},{1,0},{2,3},{3,2},{4,5},{5,4},{6,7},{7,6},{8,9},{9,8},{10,11... | collective-permute-start | bytes 983048 | tf_op jit(solution)/shard_map/ppermute | solution.py:69
  619.6 96.0 %collective-permute-start.39 = (bf16[64,2048]{1,0:T(8,128)(2,1)}, bf16[64,2048]{1,0:T(8,128)(2,1)}, u32[]{:S(2)}, u32[]{:S(2)}) collective-permute-start(bf16[64,2048]{1,0:T(8,128)(2,1)} %get-tuple-element.109), channel_id=1, source_target_pairs={{0,1},{1,0},{2,3},{3,2},{4,5},{5,4},{6,7},{7,6},{8,9},{9,8},{10,11... | collective-permute-start | bytes 786440 | tf_op jit(solution)/shard_map/ppermute | solution.py:69
  620.3 14.3 %collective-permute-start.58 = (bf16[4,80,128]{2,1,0:T(8,128)(2,1)S(1)}, bf16[4,80,128]{2,1,0:T(8,128)(2,1)S(1)}, u32[]{:S(2)}, u32[]{:S(2)}) collective-permute-start(bf16[4,80,128]{2,1,0:T(8,128)(2,1)S(1)} %get-tuple-element.101), channel_id=1, source_target_pairs={{0,32},{32,64},{64,96},{96,0},{1,33},{33,65},{65,97},{97,1},{2,34}... | collective-permute-start | bytes 245768 | tf_op jit(solution)/shard_map/ppermute | solution.py:73
  620.4 14.2 %collective-permute-start.59 = (bf16[4,80,128]{2,1,0:T(8,128)(2,1)S(1)}, bf16[4,80,128]{2,1,0:T(8,128)(2,1)S(1)}, u32[]{:S(2)}, u32[]{:S(2)}) collective-permute-start(bf16[4,80,128]{2,1,0:T(8,128)(2,1)S(1)} %get-tuple-element.103), channel_id=1, source_target_pairs={{0,64},{32,96},{64,0},{96,32},{1,65},{33,97},{65,1},{97,33},{2,66}... | collective-permute-start | bytes 245768 | tf_op jit(solution)/shard_map/ppermute | solution.py:73
  634.7 7.6 %collective-permute-start.61 = (bf16[80,128]{1,0:T(8,128)(2,1)S(1)}, bf16[80,128]{1,0:T(8,128)(2,1)S(1)}, u32[]{:S(2)}, u32[]{:S(2)}) collective-permute-start(bf16[80,128]{1,0:T(8,128)(2,1)S(1)} %get-tuple-element.136), channel_id=1, source_target_pairs={{0,8},{8,16},{16,24},{24,0},{1,9},{9,17},{17,25},{25,1},{2,10},{10... | collective-permute-start | bytes 61448 | tf_op jit(solution)/shard_map/ppermute | solution.py:73
  644.2 49.1 %collective-permute-start.47 = (bf16[128,2048]{1,0:T(8,128)(2,1)}, bf16[128,2048]{1,0:T(8,128)(2,1)}, u32[]{:S(2)}, u32[]{:S(2)}) collective-permute-start(bf16[128,2048]{1,0:T(8,128)(2,1)} %get-tuple-element.85), channel_id=1, source_target_pairs={{0,4},{2,6},{4,0},{6,2},{1,5},{3,7},{5,1},{7,3},{8,12},{10,14},{12... | collective-permute-start | bytes 1572872 | tf_op jit(solution)/shard_map/ppermute | solution.py:73
  644.7 48.7 %collective-permute-start.48 = (bf16[128,2048]{1,0:T(8,128)(2,1)}, bf16[128,2048]{1,0:T(8,128)(2,1)}, u32[]{:S(2)}, u32[]{:S(2)}) collective-permute-start(bf16[128,2048]{1,0:T(8,128)(2,1)} %get-tuple-element.87), channel_id=1, source_target_pairs={{0,2},{2,4},{4,6},{6,0},{1,3},{3,5},{5,7},{7,1},{8,10},{10,12},{12... | collective-permute-start | bytes 1572872 | tf_op jit(solution)/shard_map/ppermute | solution.py:73
  645.3 48.1 %collective-permute-start.49 = (bf16[128,2048]{1,0:T(8,128)(2,1)}, bf16[128,2048]{1,0:T(8,128)(2,1)}, u32[]{:S(2)}, u32[]{:S(2)}) collective-permute-start(bf16[128,2048]{1,0:T(8,128)(2,1)} %get-tuple-element.86), channel_id=1, source_target_pairs={{0,6},{2,0},{4,2},{6,4},{1,7},{3,1},{5,3},{7,5},{8,14},{10,8},{12,... | collective-permute-start | bytes 1572872 | tf_op jit(solution)/shard_map/ppermute | solution.py:73
  693.2 6.7 collective-permute-start.73
  695.7 7.9 %collective-permute-start.74 = (bf16[4,4,80,128]{3,2,1,0:T(8,128)(2,1)S(1)}, bf16[4,4,80,128]{3,2,1,0:T(8,128)(2,1)S(1)}, u32[]{:S(2)}, u32[]{:S(2)}) collective-permute-start(bf16[4,4,80,128]{3,2,1,0:T(8,128)(2,1)S(1)} %get-tuple-element.69), channel_id=1, source_target_pairs={{0,4},{2,6},{4,0},{6,2},{1,5},{3,7},{5,1},{7,3},{8,12},{10,14},{12... | collective-permute-start | bytes 983048 | tf_op jit(solution)/shard_map/ppermute | solution.py:73
  696.0 17.6 %collective-permute-start.75 = (bf16[4,4,80,128]{3,2,1,0:T(8,128)(2,1)S(1)}, bf16[4,4,80,128]{3,2,1,0:T(8,128)(2,1)S(1)}, u32[]{:S(2)}, u32[]{:S(2)}) collective-permute-start(bf16[4,4,80,128]{3,2,1,0:T(8,128)(2,1)S(1)} %get-tuple-element.69), channel_id=1, source_target_pairs={{0,2},{2,4},{4,6},{6,0},{1,3},{3,5},{5,7},{7,1},{8,10},{10,12},{12... | collective-permute-start | bytes 983048 | tf_op jit(solution)/shard_map/ppermute | solution.py:73
  (102 other events, 1412.3 us)
Sparse Core Ops, SparseCore 0:
  11.1 102.8 all-gather.3
  235.5 97.3 all-gather.5
  386.8 79.5 reduce-scatter.2
  470.3 97.3 reduce-scatter.4
  576.0 99.7 all-gather.7

commit v5 on v4

--- a/solution.py
+++ b/solution.py
@@ -81,9 +81,9 @@
     return jnp.concatenate([value] + [shift(value, ring, -step) for step in (1, 2, 3)], axis=axis)
 
 
-def gather_ring(value, ring):
+def gather_ring(value, ring, base=0.0):
     at = place_in(ring)
-    whole_ring = jnp.zeros((4,) + value.shape, value.dtype)
+    whole_ring = jnp.full((4,) + value.shape, base, value.dtype)
     whole_ring = lax.dynamic_update_index_in_dim(whole_ring, value, at, 0)
     for step in (1, 2, 3):
         got = shift(value, ring, -step)
@@ -183,9 +183,12 @@
     def _():
         load_tile(step // 4, tile_buf, *refs[:6])
         allowed = allowed_mask(pos_ref[...], start_ref[...], kpos_ref[0])
+        both = [
+            times_transposed(q_ref[:, head * HEAD_SIZE : (head + 1) * HEAD_SIZE], tile_buf[:, :HEAD_SIZE])
+            for head in range(2)
+        ]
         for head in range(2):
-            scores = times_transposed(q_ref[:, head * HEAD_SIZE : (head + 1) * HEAD_SIZE], tile_buf[:, :HEAD_SIZE])
-            scores = jnp.where(allowed, scores, neg_big)
+            scores = jnp.where(allowed, both[head], neg_big)
             top_old = top[head]
             top_new = jnp.maximum(top_old, jnp.max(scores, axis=-1, keepdims=True))
             weights_p = jnp.exp(scores - top_new)
@@ -619,9 +622,9 @@
     normed_g = gather_near(normed, "y")
     cot_g = gather_near(cot, "x")
     qkv_parts = after(qkv_parts, normed_g, cot_g)
-    wo = lax.all_gather(w_out, ALL, axis=0, tiled=True)
     qkv_mine = gather_ring(gather_ring(qkv_parts, "x"), "z").reshape(2048, 512)
     qkv_other = swap_cores(qkv_mine)
+    wo = lax.all_gather(w_out + zero_of(qkv_mine).astype(bf16), ALL, axis=0, tiled=True)
     q_expand = columns_of(query_expand, 512)
     k_expand = columns_of(key_expand, 256)
     v_expand = columns_of(value_expand, 256)
@@ -778,8 +781,8 @@
     )
     g_gate, g_up, g_down_shrink, g_out_shrink, g_out_expand, g_down_expand, g_gateup = unpack_early(early_all)
     late_sum = sum_plane(kept, other, "x").astype(bf16)
-    late_all = gather_ring(gather_ring(late_sum, "x"), "z") + zero_of(g_gateup).astype(bf16)
-    late_all = gather_ring(late_all, "y")
+    late_all = gather_ring(gather_ring(late_sum, "x"), "z")
+    late_all = gather_ring(late_all, "y", zero_of(g_gateup).astype(bf16))
     late_all = late_all.reshape(4, 16, -1, rank)
     late_other = swap_cores(late_all)
     g_q, g_k, g_v, g_qkv = unpack_late(c.reshape(1).astype(jnp.int32), late_all, late_other)

time: 739 us -> 753 us (1.019)
  waiting for transfers between devices: 309 us -> 296 us
  local copies, waits for them, and re-layouts: 68.7 us -> 80.5 us
  Pallas kernels: 91 us -> 98.7 us
    ppermute x1, waiting for transfers between devices: 18.1 us -> 37.2 us  [gather_row(): partner = lax.ppermute(line, CORNER, PARTNER)]
    all_gather x1, waiting for transfers between devices: 28.1 us -> 10.1 us  [local(): lax.all_gather(ffn, OVER_X, axis=0, tiled=False).reshape(16, 2, 192, 2048)]
    broadcast_in_dim x4 -> x12, local copies, waits for them, and re-layouts: 1.83 us -> 12.4 us  [the longest x3 5.11 us: local(): heads = lax.dynamic_update_index_in_dim(heads, got, (y - step) % 4, 0)]
    ppermute x7, starting transfers between devices: 13.8 us -> 23.2 us  [swap_cores(): return lax.ppermute(value, 'c', [(0, 1), (1, 0)])]
    ppermute x60, waiting for transfers between devices: 228 us -> 220 us  [shift(): lax.ppermute(value, RING[ring], [(i, (i + step) % 4) for i in range(4)])]
    unnamed x178 -> x180, local copies, waits for them, and re-layouts: 13.4 us -> 16.9 us
  transfers between devices with their start and end apart: 84 -> 84, of which waited for: 43 -> 40; matrix products, arithmetic and copies ran while one was open for 20% -> 20% of each run, Pallas kernels for 5% -> 6%
where the time goes in v5:
time: 753 us; the launch traced here: 744 us
  waiting for transfers between devices  296 us (39%)
  starting transfers between devices  153 us (20%)
  Pallas kernels  98.7 us (13%)
  local copies, waits for them, and re-layouts  80.5 us (11%)
  matrix products  49.2 us (7%)
  other arithmetic  41.7 us (6%)
  between operations  24 us (3%)
    ppermute x60, waiting for transfers between devices, shift(): lax.ppermute(value, RING[ring], [(i, (i + step) % 4) for i in range(4)])  220 us
    ppermute x60, starting transfers between devices, shift(): lax.ppermute(value, RING[ring], [(i, (i + step) % 4) for i in range(4)])  83.3 us
    pallas_call x1, Pallas kernels, feed_forward(): pl.pallas_call(ffn_kernel, grid_spec=pltpu.PrefetchScalarGridSpec(num_sca...  45.6 us
    ppermute x1, waiting for transfers between devices, gather_row(): partner = lax.ppermute(line, CORNER, PARTNER)  37.2 us
    dot_general x11, matrix products, product(): return jnp.dot(left, right, preferred_element_type=f32)  24.9 us
    ppermute x7, starting transfers between devices, swap_cores(): return lax.ppermute(value, 'c', [(0, 1), (1, 0)])  23.2 us
    ppermute x2, waiting for transfers between devices, gather_row(): ahead = [lax.ppermute(line, CORNER, pairs) for pairs in LATER]  20.1 us
    pallas_call x1, Pallas kernels, attend_back(): pl.pallas_call(attend_back_kernel, grid_spec=pltpu.PrefetchScalarGridSpec...  18 us
  transfers between devices with their start and end apart: 84, of which 40 were waited for; matrix products, arithmetic and copies ran while one was open for 20% of the time, Pallas kernels for 6%

profile of v5, /device:TPU:1, one launch (start us, length us, event | category | flops | bytes accessed | tf_op | source)
XLA Modules:
  0.0 744.0 jit_solution(16687147694894374299)
XLA Ops:
  12.0 5.0 all-to-all-start
  19.5 2.9 all-to-all-done
  22.4 2.5 collective-permute-start.5
  28.9 7.1 collective-permute-done.5
  38.7 12.7 %collective-permute-done.7 = bf16[128,2048]{1,0:T(8,128)(2,1)S(1)} collective-permute-done((bf16[128,2048]{1,0:T(8,128)(2,1)S(1)}, bf16[128,2048]{1,0:T(8,128)(2,1)S(1)}, u32[]{:S(2)}, u32[]{:S(2)}) %collective-permute-start.7) | collective-permute-done | bytes 524320 | tf_op jit(solution)/shard_map/ppermute | solution.py:73
  54.2 4.2 collective-permute-start.9
  60.8 2.7 collective-permute-done.10
  63.5 3.8 collective-permute-start.11
  70.6 9.0 %collective-permute-done.11 = bf16[4,128,512]{1,2,0:T(8,128)(2,1)} collective-permute-done((bf16[4,128,512]{1,2,0:T(8,128)(2,1)S(1)}, bf16[4,128,512]{1,2,0:T(8,128)(2,1)}, u32[]{:S(2)}, u32[]{:S(2)}) %collective-permute-start.11) | collective-permute-done | bytes 524320 | tf_op jit(solution)/shard_map/ppermute | solution.py:73
  82.9 8.2 %collective-permute-done.13 = bf16[4,128,512]{1,2,0:T(8,128)(2,1)} collective-permute-done((bf16[4,128,512]{1,2,0:T(8,128)(2,1)S(1)}, bf16[4,128,512]{1,2,0:T(8,128)(2,1)}, u32[]{:S(2)}, u32[]{:S(2)}) %collective-permute-start.13) | collective-permute-done | bytes 524320 | tf_op jit(solution)/shard_map/ppermute | solution.py:73
  98.2 3.4 collective-permute-start.14
  105.2 3.0 fusion.2
  109.4 3.5 fusion.146
  112.9 4.9 broadcast_select_fusion
  122.1 12.0 %collective-permute-done.15 = bf16[512,512]{1,0:T(8,128)(2,1)S(1)} collective-permute-done((bf16[512,512]{1,0:T(8,128)(2,1)S(1)}, bf16[512,512]{1,0:T(8,128)(2,1)S(1)}, u32[]{:S(2)}, u32[]{:S(2)}) %collective-permute-start.15) | collective-permute-done | bytes 524320 | tf_op jit(solution)/shard_map/ppermute | solution.py:73
  135.6 11.5 %collective-permute-done.17 = bf16[512,512]{1,0:T(8,128)(2,1)S(1)} collective-permute-done((bf16[512,512]{1,0:T(8,128)(2,1)S(1)}, bf16[512,512]{1,0:T(8,128)(2,1)S(1)}, u32[]{:S(2)}, u32[]{:S(2)}) %collective-permute-start.17) | collective-permute-done | bytes 524320 | tf_op jit(solution)/shard_map/ppermute | solution.py:73
  148.8 8.3 %collective-permute-start.19 = (bf16[4,512,512]{2,1,0:T(8,128)(2,1)}, bf16[4,512,512]{2,1,0:T(8,128)(2,1)}, u32[]{:S(2)}, u32[]{:S(2)}) collective-permute-start(bf16[4,512,512]{2,1,0:T(8,128)(2,1)} %pad_maximum_fusion.refs_0_), channel_id=1, source_target_pairs={{1,64},{33,96},{3,66},{35,98},{5,68},{37,100},{7,70},{39,102},{9,7... | collective-permute-start | bytes 6291464 | tf_op jit(solution)/shard_map/ppermute | solution.py:128
  157.1 2.6 collective-permute-start.20
  166.1 5.9 all-to-all-start.1
  172.0 37.2 %collective-permute-done.18.refs_1_ = bf16[4,512,512]{2,1,0:T(8,128)(2,1)} collective-permute-done((bf16[4,512,512]{2,1,0:T(8,128)(2,1)}, bf16[4,512,512]{2,1,0:T(8,128)(2,1)}, u32[]{:S(2)}, u32[]{:S(2)}) %collective-permute-start.18) | collective-permute-done | bytes 2097184 | tf_op jit(solution)/shard_map/ppermute | solution.py:129
  210.4 20.1 %collective-permute-done.19.refs_2_ = bf16[4,512,512]{2,1,0:T(8,128)(2,1)} collective-permute-done((bf16[4,512,512]{2,1,0:T(8,128)(2,1)}, bf16[4,512,512]{2,1,0:T(8,128)(2,1)}, u32[]{:S(2)}, u32[]{:S(2)}) %collective-permute-start.19) | collective-permute-done | bytes 2097184 | tf_op jit(solution)/shard_map/ppermute | solution.py:128
  253.0 13.1 %attend.1 = (f32[512,512]{1,0:T(8,128)S(1)}, f32[2,512,1]{2,1,0:T(8,128)S(1)}) custom-call(s32[64]{0:T(128)S(1)} %pad_add_fusion.2.active, bf16[512,512]{1,0:T(8,128)(2,1)S(1)} %fusion.23.q_ref, s32[512,1]{1,0:T(8,128)S(1)} %copy.171.pos_ref, s32[512,1]{1,0:T(8,128)S(1)} %copy.172.start_ref, s32[16,1,512]{2,1,0:T(1,128)S(1)} %reshape.660.kpos_ref, ...), custom_call_target="tpu_custom_call" | custom-call | flops 6442450944 | bytes 10485760 | tf_op jit(solution)/shard_map/attend/pallas_call | solution.py:284
  268.0 4.3 collective-permute-start.23
  272.3 2.9 collective-permute-start.24
  289.0 5.6 multiply_reduce_fusion.1
  295.3 7.2 collective-permute-start.26
  305.9 15.3 %collective-permute-done.26 = bf16[128,2048]{1,0:T(8,128)(2,1)S(1)} collective-permute-done((bf16[128,2048]{1,0:T(8,128)(2,1)S(1)}, bf16[128,2048]{1,0:T(8,128)(2,1)S(1)}, u32[]{:S(2)}, u32[]{:S(2)}) %collective-permute-start.26) | collective-permute-done | bytes 524320 | tf_op jit(solution)/shard_map/ppermute | solution.py:73
  321.2 4.3 collective-permute-done.28
  328.7 10.1 %all-gather.6.cloned.1.call-done = bf16[32,192,2048]{2,1,0:T(8,128)(2,1)} async-done(((bf16[1,192,2048]{2,1,0:T(8,128)(2,1)}), bf16[32,192,2048]{2,1,0:T(8,128)(2,1)}) %all-gather.6.cloned.1.call-update) | async-done | bytes 25165840 | tf_op jit(solution)/shard_map/all_gather | solution.py:648
  338.8 45.6 %feed_forward.1 = (bf16[512,2048]{1,0:T(8,128)(2,1)}, bf16[512,2432]{1,0:T(8,128)(2,1)}, f32[4,4,2,192,128]{4,3,2,1,0:T(8,128)}) custom-call(s32[1]{0:T(128)} %bitcast.38.at, bf16[512,2048]{1,0:T(8,128)(2,1)} %pad_maximum_fusion.1.nm_ref, bf16[512,2048]{1,0:T(8,128)(2,1)} %copy-done.60, bf16[512,256]{1,0:T(8,128)(2,1)} %fusion.3.lgu_ref, ...), custom_call_target="tpu_custom_call" | custom-call | flops 30064771072 | bytes 41943040 | tf_op jit(solution)/shard_map/feed_forward/pallas_call | solution.py:403
  384.4 2.7 fusion.136
  387.2 2.6 collective-permute-start.29
  392.8 11.7 %collective-permute-done.29 = bf16[128,2432]{1,0:T(8,128)(2,1)} collective-permute-done((bf16[128,2432]{1,0:T(8,128)(2,1)}, bf16[128,2432]{1,0:T(8,128)(2,1)}, u32[]{:S(2)}, u32[]{:S(2)}) %collective-permute-start.29) | collective-permute-done | bytes 622624 | tf_op jit(solution)/shard_map/ppermute | solution.py:73
  404.4 13.9 %collective-permute-done.30 = bf16[128,2432]{1,0:T(8,128)(2,1)} collective-permute-done((bf16[128,2432]{1,0:T(8,128)(2,1)}, bf16[128,2432]{1,0:T(8,128)(2,1)}, u32[]{:S(2)}, u32[]{:S(2)}) %collective-permute-start.30) | collective-permute-done | bytes 622624 | tf_op jit(solution)/shard_map/ppermute | solution.py:73
  423.4 2.9 fusion.127
  426.7 2.5 collective-permute-start.32
  433.0 2.9 copy.182
  436.0 3.0 collective-permute-done.34
  442.2 18.0 %attend_back.1 = (f32[512,512]{1,0:T(8,128)S(1)}, bf16[4,512,512]{2,1,0:T(8,128)(2,1)}, bf16[4,512,512]{2,1,0:T(8,128)(2,1)}, bf16[4,512,512]{2,1,0:T(8,128)(2,1)}, bf16[4,512,512]{2,1,0:T(8,128)(2,1)}) custom-call(s32[64]{0:T(128)S(1)} %pad_add_fusion.2.active, bf16[512,512]{1,0:T(8,128)(2,1)S(1)} %fusion.23.q_ref, s32[512,1]{1,0:T(8,128)S(1)} %copy-done.4, ...), custom_call_target="tpu_custom_call" | custom-call | flops 12884901888 | bytes 20971520 | tf_op jit(solution)/shard_map/attend_back/pallas_call | solution.py:309
  460.2 2.5 collective-permute-start.35
  462.8 2.7 collective-permute-start.40
  468.0 3.7 add_convert_fusion.2
  472.9 14.2 %collective-permute-start.41 = (bf16[4,512,512]{2,1,0:T(8,128)(2,1)}, bf16[4,512,512]{2,1,0:T(8,128)(2,1)}, u32[]{:S(2)}, u32[]{:S(2)}) collective-permute-start(bf16[4,512,512]{2,1,0:T(8,128)(2,1)} %add_convert_fusion.2), channel_id=1, source_target_pairs={{0,32},{1,33},{32,0},{33,1},{64,96},{65,97},{96,64},{97,65},{2,34}... | collective-permute-start | bytes 6291464 | tf_op jit(solution)/shard_map/ppermute | solution.py:138
  488.1 14.8 %collective-permute-done.36 = bf16[128,2048]{1,0:T(8,128)(2,1)S(1)} collective-permute-done((bf16[128,2048]{1,0:T(8,128)(2,1)S(1)}, bf16[128,2048]{1,0:T(8,128)(2,1)S(1)}, u32[]{:S(2)}, u32[]{:S(2)}) %collective-permute-start.36) | collective-permute-done | bytes 524320 | tf_op jit(solution)/shard_map/ppermute | solution.py:73
  503.0 14.3 %collective-permute-done.37 = bf16[128,2048]{1,0:T(8,128)(2,1)S(1)} collective-permute-done((bf16[128,2048]{1,0:T(8,128)(2,1)S(1)}, bf16[128,2048]{1,0:T(8,128)(2,1)S(1)}, u32[]{:S(2)}, u32[]{:S(2)}) %collective-permute-start.37) | collective-permute-done | bytes 524320 | tf_op jit(solution)/shard_map/ppermute | solution.py:73
  517.7 12.3 %collective-permute-done.38 = bf16[128,2048]{1,0:T(8,128)(2,1)S(1)} collective-permute-done((bf16[128,2048]{1,0:T(8,128)(2,1)S(1)}, bf16[128,2048]{1,0:T(8,128)(2,1)S(1)}, u32[]{:S(2)}, u32[]{:S(2)}) %collective-permute-start.38) | collective-permute-done | bytes 524320 | tf_op jit(solution)/shard_map/ppermute | solution.py:73
  534.3 6.1 add_convert_fusion.1
  543.3 10.2 %collective-permute-done.44 = bf16[512,512]{1,0:T(8,128)(2,1)S(1)} collective-permute-done((bf16[512,512]{1,0:T(8,128)(2,1)S(1)}, bf16[512,512]{1,0:T(8,128)(2,1)S(1)}, u32[]{:S(2)}, u32[]{:S(2)}) %collective-permute-start.44) | collective-permute-done | bytes 524320 | tf_op jit(solution)/shard_map/ppermute | solution.py:73
  553.5 13.2 %collective-permute-done.45 = bf16[512,512]{1,0:T(8,128)(2,1)S(1)} collective-permute-done((bf16[512,512]{1,0:T(8,128)(2,1)S(1)}, bf16[512,512]{1,0:T(8,128)(2,1)S(1)}, u32[]{:S(2)}, u32[]{:S(2)}) %collective-permute-start.45) | collective-permute-done | bytes 524320 | tf_op jit(solution)/shard_map/ppermute | solution.py:73
  569.0 6.2 reduce-scatter.5.cloned.1.call-done
  585.2 2.8 reshape.670
  610.0 2.5 collective-permute-done.57
  616.6 9.9 %collective-permute-start.60 = (bf16[16,80,128]{2,1,0:T(8,128)(2,1)S(1)}, bf16[16,80,128]{2,1,0:T(8,128)(2,1)S(1)}, u32[]{:S(2)}, u32[]{:S(2)}) collective-permute-start(bf16[16,80,128]{2,1,0:T(8,128)(2,1)S(1)} %fusion.42), channel_id=1, source_target_pairs={{0,1},{1,0},{2,3},{3,2},{4,5},{5,4},{6,7},{7,6},{8,9},{9,8},{10,11... | collective-permute-start | bytes 983048 | tf_op jit(solution)/shard_map/ppermute | solution.py:69
  626.4 2.9 fusion.30
  629.5 8.0 %collective-permute-start.62 = (bf16[4,80,128]{2,1,0:T(8,128)(2,1)S(1)}, bf16[4,80,128]{2,1,0:T(8,128)(2,1)S(1)}, u32[]{:S(2)}, u32[]{:S(2)}) collective-permute-start(bf16[4,80,128]{2,1,0:T(8,128)(2,1)S(1)} %get-tuple-element.101), channel_id=1, source_target_pairs={{0,64},{32,96},{64,0},{96,32},{1,65},{33,97},{65,1},{97,33},{2,66}... | collective-permute-start | bytes 245768 | tf_op jit(solution)/shard_map/ppermute | solution.py:73
  639.6 2.9 add_convert_fusion
  646.2 2.5 collective-permute-start.49
  653.5 2.6 collective-permute-start.39
  657.3 8.1 %collective-permute-done.47 = bf16[128,2048]{1,0:T(8,128)(2,1)S(1)} collective-permute-done((bf16[128,2048]{1,0:T(8,128)(2,1)S(1)}, bf16[128,2048]{1,0:T(8,128)(2,1)S(1)}, u32[]{:S(2)}, u32[]{:S(2)}) %collective-permute-start.47) | collective-permute-done | bytes 524320 | tf_op jit(solution)/shard_map/ppermute | solution.py:73
  665.4 17.4 %collective-permute-done.48 = bf16[128,2048]{1,0:T(8,128)(2,1)S(1)} collective-permute-done((bf16[128,2048]{1,0:T(8,128)(2,1)S(1)}, bf16[128,2048]{1,0:T(8,128)(2,1)S(1)}, u32[]{:S(2)}, u32[]{:S(2)}) %collective-permute-start.48) | collective-permute-done | bytes 524320 | tf_op jit(solution)/shard_map/ppermute | solution.py:73
  685.7 2.9 collective-permute-done.68
  698.5 15.0 %unpack_early.1 = (f32[128,8192]{1,0:T(8,128)}, f32[128,8192]{1,0:T(8,128)}, f32[8192,128]{1,0:T(8,128)}, f32[2048,128]{1,0:T(8,128)}, f32[128,2048]{1,0:T(8,128...) custom-call(bf16[128,272,128]{2,1,0:T(8,128)(2,1)} %all-gather.8.cloned.1.call-done.all_ref), custom_call_target="tpu_custom_call" | custom-call | flops 1048576 | bytes 28311552 | tf_op jit(solution)/shard_map/unpack_early/pallas_call | solution.py:471
  720.0 5.3 collective-permute-start.76
  730.3 7.0 unpack_late.1
  (526 shorter events, 191.0 us)
Async XLA Ops:
  8.4 8.6 %collective-permute-start = (bf16[64,2048]{1,0:T(8,128)(2,1)S(1)}, bf16[64,2048]{1,0:T(8,128)(2,1)S(1)}, u32[]{:S(2)}, u32[]{:S(2)}) collective-permute-start(bf16[64,2048]{1,0:T(8,128)(2,1)S(1)} %get-tuple-element.123), channel_id=1, source_target_pairs={{0,1},{1,0},{2,3},{3,2},{4,5},{5,4},{6,7},{7,6},{8,9},{9,8},{10,11... | collective-permute-start | bytes 786440 | tf_op jit(solution)/shard_map/ppermute | solution.py:69
  11.0 7.1 collective-permute-start.1
  12.0 10.3 %all-to-all-start = ((bf16[8,16,512]{2,1,0:T(8,128)(2,1)}), bf16[8,16,512]{2,1,0:T(8,128)(2,1)S(1)}, u32[]{:S(2)}, u32[]{:S(2)}) async-start(bf16[8,16,512]{2,1,0:T(8,128)(2,1)} %bitcast.9), calls=%async_computation | async-start | bytes 262144 | tf_op jit(solution)/shard_map/all_to_all | solution.py:613
  17.1 219.6 %all-gather.4.cloned.1.call-start = ((), (), s32[]{:S(2)}) async-start(), calls=%async_computation.4 | async-start | bytes 8454144 | tf_op jit(solution)/shard_map/all_gather | solution.py:627
  22.4 13.6 %collective-permute-start.5 = (bf16[128,2048]{1,0:T(8,128)(2,1)S(1)}, bf16[128,2048]{1,0:T(8,128)(2,1)}, u32[]{:S(2)}, u32[]{:S(2)}) collective-permute-start(bf16[128,2048]{1,0:T(8,128)(2,1)S(1)} %pad_maximum_fusion.4), channel_id=1, source_target_pairs={{0,24},{8,0},{16,8},{24,16},{1,25},{9,1},{17,9},{25,17},{2,26},{10... | collective-permute-start | bytes 1572872 | tf_op jit(solution)/shard_map/ppermute | solution.py:73
  24.8 13.8 %collective-permute-start.6 = (bf16[128,2048]{1,0:T(8,128)(2,1)S(1)}, bf16[128,2048]{1,0:T(8,128)(2,1)S(1)}, u32[]{:S(2)}, u32[]{:S(2)}) collective-permute-start(bf16[128,2048]{1,0:T(8,128)(2,1)S(1)} %pad_maximum_fusion.4), channel_id=1, source_target_pairs={{0,16},{8,24},{16,0},{24,8},{1,17},{9,25},{17,1},{25,9},{2,18},{10... | collective-permute-start | bytes 1572872 | tf_op jit(solution)/shard_map/ppermute | solution.py:73
  25.4 26.1 %collective-permute-start.7 = (bf16[128,2048]{1,0:T(8,128)(2,1)S(1)}, bf16[128,2048]{1,0:T(8,128)(2,1)S(1)}, u32[]{:S(2)}, u32[]{:S(2)}) collective-permute-start(bf16[128,2048]{1,0:T(8,128)(2,1)S(1)} %pad_maximum_fusion.4), channel_id=1, source_target_pairs={{0,8},{8,16},{16,24},{24,0},{1,9},{9,17},{17,25},{25,1},{2,10},{10... | collective-permute-start | bytes 1572872 | tf_op jit(solution)/shard_map/ppermute | solution.py:73
  26.8 24.6 %collective-permute-start.2 = (bf16[128,2048]{1,0:T(8,128)(2,1)S(1)}, bf16[128,2048]{1,0:T(8,128)(2,1)S(1)}, u32[]{:S(2)}, u32[]{:S(2)}) collective-permute-start(bf16[128,2048]{1,0:T(8,128)(2,1)S(1)} %fusion.9), channel_id=1, source_target_pairs={{0,6},{2,0},{4,2},{6,4},{1,7},{3,1},{5,3},{7,5},{8,14},{10,8},{12,... | collective-permute-start | bytes 1572872 | tf_op jit(solution)/shard_map/ppermute | solution.py:73
  27.7 24.6 %collective-permute-start.3 = (bf16[128,2048]{1,0:T(8,128)(2,1)S(1)}, bf16[128,2048]{1,0:T(8,128)(2,1)S(1)}, u32[]{:S(2)}, u32[]{:S(2)}) collective-permute-start(bf16[128,2048]{1,0:T(8,128)(2,1)S(1)} %fusion.9), channel_id=1, source_target_pairs={{0,4},{2,6},{4,0},{6,2},{1,5},{3,7},{5,1},{7,3},{8,12},{10,14},{12... | collective-permute-start | bytes 1572872 | tf_op jit(solution)/shard_map/ppermute | solution.py:73
  36.0 17.2 %collective-permute-start.4 = (bf16[128,2048]{1,0:T(8,128)(2,1)S(1)}, bf16[128,2048]{1,0:T(8,128)(2,1)S(1)}, u32[]{:S(2)}, u32[]{:S(2)}) collective-permute-start(bf16[128,2048]{1,0:T(8,128)(2,1)S(1)} %fusion.9), channel_id=1, source_target_pairs={{0,2},{2,4},{4,6},{6,0},{1,3},{3,5},{5,7},{7,1},{8,10},{10,12},{12... | collective-permute-start | bytes 1572872 | tf_op jit(solution)/shard_map/ppermute | solution.py:73
  63.5 16.1 %collective-permute-start.11 = (bf16[4,128,512]{1,2,0:T(8,128)(2,1)S(1)}, bf16[4,128,512]{1,2,0:T(8,128)(2,1)}, u32[]{:S(2)}, u32[]{:S(2)}) collective-permute-start(bf16[4,128,512]{1,2,0:T(8,128)(2,1)S(1)} %bitcast_dynamic-update-slice_fusion.4), channel_id=1, source_target_pairs={{0,96},{32,0},{64,32},{96,64},{1,97},{33,1},{65,33},{97,65},{2,98}... | collective-permute-start | bytes 1572872 | tf_op jit(solution)/shard_map/ppermute | solution.py:73
  67.3 13.5 %collective-permute-start.12 = (bf16[4,128,512]{1,2,0:T(8,128)(2,1)S(1)}, bf16[4,128,512]{1,2,0:T(8,128)(2,1)S(1)}, u32[]{:S(2)}, u32[]{:S(2)}) collective-permute-start(bf16[4,128,512]{1,2,0:T(8,128)(2,1)S(1)} %bitcast_dynamic-update-slice_fusion.4), channel_id=1, source_target_pairs={{0,64},{32,96},{64,0},{96,32},{1,65},{33,97},{65,1},{97,33},{2,66}... | collective-permute-start | bytes 1572872 | tf_op jit(solution)/shard_map/ppermute | solution.py:73
  67.3 23.7 %collective-permute-start.13 = (bf16[4,128,512]{1,2,0:T(8,128)(2,1)S(1)}, bf16[4,128,512]{1,2,0:T(8,128)(2,1)}, u32[]{:S(2)}, u32[]{:S(2)}) collective-permute-start(bf16[4,128,512]{1,2,0:T(8,128)(2,1)S(1)} %bitcast_dynamic-update-slice_fusion.4), channel_id=1, source_target_pairs={{0,32},{32,64},{64,96},{96,0},{1,33},{33,65},{65,97},{97,1},{2,34}... | collective-permute-start | bytes 1572872 | tf_op jit(solution)/shard_map/ppermute | solution.py:73
  98.2 14.6 %collective-permute-start.14 = (bf16[2048,512]{1,0:T(8,128)(2,1)}, bf16[2048,512]{1,0:T(8,128)(2,1)}, u32[]{:S(2)}, u32[]{:S(2)}) collective-permute-start(bf16[2048,512]{1,0:T(8,128)(2,1)} %bitcast.19), channel_id=1, source_target_pairs={{0,1},{1,0},{2,3},{3,2},{4,5},{5,4},{6,7},{7,6},{8,9},{9,8},{10,11... | collective-permute-start | bytes 6291464 | tf_op jit(solution)/shard_map/ppermute | solution.py:69
  120.1 14.0 %collective-permute-start.15 = (bf16[512,512]{1,0:T(8,128)(2,1)S(1)}, bf16[512,512]{1,0:T(8,128)(2,1)S(1)}, u32[]{:S(2)}, u32[]{:S(2)}) collective-permute-start(bf16[512,512]{1,0:T(8,128)(2,1)S(1)} %get-tuple-element.117), channel_id=1, source_target_pairs={{0,24},{8,0},{16,8},{24,16},{1,25},{9,1},{17,9},{25,17},{2,26},{10... | collective-permute-start | bytes 1572872 | tf_op jit(solution)/shard_map/ppermute | solution.py:73
  120.2 15.4 %collective-permute-start.16 = (bf16[512,512]{1,0:T(8,128)(2,1)S(1)}, bf16[512,512]{1,0:T(8,128)(2,1)S(1)}, u32[]{:S(2)}, u32[]{:S(2)}) collective-permute-start(bf16[512,512]{1,0:T(8,128)(2,1)S(1)} %get-tuple-element.117), channel_id=1, source_target_pairs={{0,16},{8,24},{16,0},{24,8},{1,17},{9,25},{17,1},{25,9},{2,18},{10... | collective-permute-start | bytes 1572872 | tf_op jit(solution)/shard_map/ppermute | solution.py:73
  122.1 25.0 %collective-permute-start.17 = (bf16[512,512]{1,0:T(8,128)(2,1)S(1)}, bf16[512,512]{1,0:T(8,128)(2,1)S(1)}, u32[]{:S(2)}, u32[]{:S(2)}) collective-permute-start(bf16[512,512]{1,0:T(8,128)(2,1)S(1)} %get-tuple-element.117), channel_id=1, source_target_pairs={{0,8},{8,16},{16,24},{24,0},{1,9},{9,17},{17,25},{25,1},{2,10},{10... | collective-permute-start | bytes 1572872 | tf_op jit(solution)/shard_map/ppermute | solution.py:73
  148.8 60.5 %collective-permute-start.18 = (bf16[4,512,512]{2,1,0:T(8,128)(2,1)}, bf16[4,512,512]{2,1,0:T(8,128)(2,1)}, u32[]{:S(2)}, u32[]{:S(2)}) collective-permute-start(bf16[4,512,512]{2,1,0:T(8,128)(2,1)} %pad_maximum_fusion.refs_0_), channel_id=1, source_target_pairs={{0,32},{1,33},{32,0},{33,1},{64,96},{65,97},{96,64},{97,65},{2,34}... | collective-permute-start | bytes 6291464 | tf_op jit(solution)/shard_map/ppermute | solution.py:129
  148.8 81.7 %collective-permute-start.19 = (bf16[4,512,512]{2,1,0:T(8,128)(2,1)}, bf16[4,512,512]{2,1,0:T(8,128)(2,1)}, u32[]{:S(2)}, u32[]{:S(2)}) collective-permute-start(bf16[4,512,512]{2,1,0:T(8,128)(2,1)} %pad_maximum_fusion.refs_0_), channel_id=1, source_target_pairs={{1,64},{33,96},{3,66},{35,98},{5,68},{37,100},{7,70},{39,102},{9,7... | collective-permute-start | bytes 6291464 | tf_op jit(solution)/shard_map/ppermute | solution.py:128
  157.1 75.8 %collective-permute-start.20 = (bf16[4,512,512]{2,1,0:T(8,128)(2,1)}, bf16[4,512,512]{2,1,0:T(8,128)(2,1)}, u32[]{:S(2)}, u32[]{:S(2)}) collective-permute-start(bf16[4,512,512]{2,1,0:T(8,128)(2,1)} %pad_maximum_fusion.refs_0_), channel_id=1, source_target_pairs={{1,96},{33,64},{3,98},{35,66},{5,100},{37,68},{7,102},{39,70},{9,1... | collective-permute-start | bytes 6291464 | tf_op jit(solution)/shard_map/ppermute | solution.py:128
  159.8 75.0 %collective-permute-start.21 = (bf16[4,512,512]{2,1,0:T(8,128)(2,1)}, bf16[4,512,512]{2,1,0:T(8,128)(2,1)}, u32[]{:S(2)}, u32[]{:S(2)}) collective-permute-start(bf16[4,512,512]{2,1,0:T(8,128)(2,1)} %pad_maximum_fusion.refs_0_), channel_id=1, source_target_pairs={{0,1},{2,3},{4,5},{6,7},{8,9},{10,11},{12,13},{14,15},{16,17},{18,... | collective-permute-start | bytes 6291464 | tf_op jit(solution)/shard_map/ppermute | solution.py:130
  166.1 72.4 %all-to-all-start.1 = ((bf16[8,16,2048]{2,1,0:T(8,128)(2,1)}), bf16[8,16,2048]{2,1,0:T(8,128)(2,1)S(1)}, u32[]{:S(2)}, u32[]{:S(2)}) async-start(bf16[8,16,2048]{2,1,0:T(8,128)(2,1)} %maximum_add_fusion.1), calls=%async_computation.1 | async-start | bytes 1048576 | tf_op jit(solution)/shard_map/all_to_all | solution.py:645
  172.0 166.8 %all-gather.6.cloned.1.call-start = ((), (), s32[]{:S(2)}) async-start(), calls=%async_computation.5 | async-start | bytes 25952256 | tf_op jit(solution)/shard_map/all_gather | solution.py:648
  239.6 292.2 %reduce-scatter.3.cloned.1.call-start = ((), (), s32[]{:S(2)}) async-start(), calls=%async_computation.6 | async-start | bytes 3244032 | tf_op jit(solution)/shard_map/reduce_scatter | solution.py:711
  241.5 11.5 %collective-permute-start.22 = (bf16[4,512,512]{2,1,0:T(8,128)(2,1)}, bf16[4,512,512]{2,1,0:T(8,128)(2,1)}, u32[]{:S(2)}, u32[]{:S(2)}) collective-permute-start(bf16[4,512,512]{2,1,0:T(8,128)(2,1)} %collective-permute-done.18.refs_1_), channel_id=1, source_target_pairs={{0,1},{2,3},{4,5},{6,7},{8,9},{10,11},{12,13},{14,15},{16,17},{18,... | collective-permute-start | bytes 6291464 | tf_op jit(solution)/shard_map/ppermute | solution.py:130
  268.0 11.0 %collective-permute-start.23 = (bf16[128,512]{1,0:T(8,128)(2,1)}, bf16[128,512]{1,0:T(8,128)(2,1)}, u32[]{:S(2)}, u32[]{:S(2)}) collective-permute-start(bf16[128,512]{1,0:T(8,128)(2,1)} %get-tuple-element.114), channel_id=1, source_target_pairs={{0,2},{2,4},{4,6},{6,0},{1,3},{3,5},{5,7},{7,1},{8,10},{10,12},{12... | collective-permute-start | bytes 393224 | tf_op jit(solution)/shard_map/ppermute | solution.py:73
  272.3 8.4 %collective-permute-start.24 = (bf16[128,512]{1,0:T(8,128)(2,1)}, bf16[128,512]{1,0:T(8,128)(2,1)}, u32[]{:S(2)}, u32[]{:S(2)}) collective-permute-start(bf16[128,512]{1,0:T(8,128)(2,1)} %get-tuple-element.113), channel_id=1, source_target_pairs={{0,4},{2,6},{4,0},{6,2},{1,5},{3,7},{5,1},{7,3},{8,12},{10,14},{12... | collective-permute-start | bytes 393224 | tf_op jit(solution)/shard_map/ppermute | solution.py:73
  275.2 7.2 collective-permute-start.25
  295.3 25.9 %collective-permute-start.26 = (bf16[128,2048]{1,0:T(8,128)(2,1)S(1)}, bf16[128,2048]{1,0:T(8,128)(2,1)S(1)}, u32[]{:S(2)}, u32[]{:S(2)}) collective-permute-start(bf16[128,2048]{1,0:T(8,128)(2,1)S(1)} %multiply_convert_fusion.1), channel_id=1, source_target_pairs={{0,24},{8,0},{16,8},{24,16},{1,25},{9,1},{17,9},{25,17},{2,26},{10... | collective-permute-start | bytes 1572872 | tf_op jit(solution)/shard_map/ppermute | solution.py:73
  302.4 18.7 %collective-permute-start.27 = (bf16[128,2048]{1,0:T(8,128)(2,1)S(1)}, bf16[128,2048]{1,0:T(8,128)(2,1)S(1)}, u32[]{:S(2)}, u32[]{:S(2)}) collective-permute-start(bf16[128,2048]{1,0:T(8,128)(2,1)S(1)} %multiply_convert_fusion.1), channel_id=1, source_target_pairs={{0,16},{8,24},{16,0},{24,8},{1,17},{9,25},{17,1},{25,9},{2,18},{10... | collective-permute-start | bytes 1572872 | tf_op jit(solution)/shard_map/ppermute | solution.py:73
  302.5 23.1 %collective-permute-start.28 = (bf16[128,2048]{1,0:T(8,128)(2,1)S(1)}, bf16[128,2048]{1,0:T(8,128)(2,1)S(1)}, u32[]{:S(2)}, u32[]{:S(2)}) collective-permute-start(bf16[128,2048]{1,0:T(8,128)(2,1)S(1)} %multiply_convert_fusion.1), channel_id=1, source_target_pairs={{0,8},{8,16},{16,24},{24,0},{1,9},{9,17},{17,25},{25,1},{2,10},{10... | collective-permute-start | bytes 1572872 | tf_op jit(solution)/shard_map/ppermute | solution.py:73
  387.2 17.2 %collective-permute-start.29 = (bf16[128,2432]{1,0:T(8,128)(2,1)}, bf16[128,2432]{1,0:T(8,128)(2,1)}, u32[]{:S(2)}, u32[]{:S(2)}) collective-permute-start(bf16[128,2432]{1,0:T(8,128)(2,1)} %get-tuple-element.80), channel_id=1, source_target_pairs={{0,16},{8,24},{16,0},{24,8},{1,17},{9,25},{17,1},{25,9},{2,18},{10... | collective-permute-start | bytes 1867784 | tf_op jit(solution)/shard_map/ppermute | solution.py:73
  389.8 28.5 %collective-permute-start.30 = (bf16[128,2432]{1,0:T(8,128)(2,1)}, bf16[128,2432]{1,0:T(8,128)(2,1)}, u32[]{:S(2)}, u32[]{:S(2)}) collective-permute-start(bf16[128,2432]{1,0:T(8,128)(2,1)} %get-tuple-element.82), channel_id=1, source_target_pairs={{0,8},{8,16},{16,24},{24,0},{1,9},{9,17},{17,25},{25,1},{2,10},{10... | collective-permute-start | bytes 1867784 | tf_op jit(solution)/shard_map/ppermute | solution.py:73
  390.2 28.1 %collective-permute-start.31 = (bf16[128,2432]{1,0:T(8,128)(2,1)}, bf16[128,2432]{1,0:T(8,128)(2,1)}, u32[]{:S(2)}, u32[]{:S(2)}) collective-permute-start(bf16[128,2432]{1,0:T(8,128)(2,1)} %get-tuple-element.81), channel_id=1, source_target_pairs={{0,24},{8,0},{16,8},{24,16},{1,25},{9,1},{17,9},{25,17},{2,26},{10... | collective-permute-start | bytes 1867784 | tf_op jit(solution)/shard_map/ppermute | solution.py:73
  392.5 182.6 %reduce-scatter.5.cloned.1.call-start = ((), (), s32[]{:S(2)}) async-start(), calls=%async_computation.7 | async-start | bytes 5406720 | tf_op jit(solution)/shard_map/reduce_scatter | solution.py:766
  426.7 9.3 %collective-permute-start.32 = (bf16[128,512]{1,0:T(8,128)(2,1)S(1)}, bf16[128,512]{1,0:T(8,128)(2,1)S(1)}, u32[]{:S(2)}, u32[]{:S(2)}) collective-permute-start(bf16[128,512]{1,0:T(8,128)(2,1)S(1)} %get-tuple-element.111), channel_id=1, source_target_pairs={{0,6},{2,0},{4,2},{6,4},{1,7},{3,1},{5,3},{7,5},{8,14},{10,8},{12,... | collective-permute-start | bytes 393224 | tf_op jit(solution)/shard_map/ppermute | solution.py:73
  429.2 6.8 collective-permute-start.33
  429.7 9.2 %collective-permute-start.34 = (bf16[128,512]{1,0:T(8,128)(2,1)S(1)}, bf16[128,512]{1,0:T(8,128)(2,1)S(1)}, u32[]{:S(2)}, u32[]{:S(2)}) collective-permute-start(bf16[128,512]{1,0:T(8,128)(2,1)S(1)} %get-tuple-element.109), channel_id=1, source_target_pairs={{0,2},{2,4},{4,6},{6,0},{1,3},{3,5},{5,7},{7,1},{8,10},{10,12},{12... | collective-permute-start | bytes 393224 | tf_op jit(solution)/shard_map/ppermute | solution.py:73
  435.9 262.6 %all-gather.8.cloned.1.call-start = ((), (), s32[]{:S(2)}) async-start(), calls=%async_computation.8 | async-start | bytes 8982528 | tf_op jit(solution)/shard_map/all_gather | solution.py:769
  460.2 7.8 %collective-permute-start.35 = (bf16[4,512,512]{2,1,0:T(8,128)(2,1)}, bf16[4,512,512]{2,1,0:T(8,128)(2,1)S(1)}, u32[]{:S(2)}, u32[]{:S(2)}) collective-permute-start(bf16[4,512,512]{2,1,0:T(8,128)(2,1)} %get-tuple-element.47), channel_id=1, source_target_pairs={{1,0},{3,2},{5,4},{7,6},{9,8},{11,10},{13,12},{15,14},{17,16},{19,... | collective-permute-start | bytes 6291464 | tf_op jit(solution)/shard_map/ppermute | solution.py:135
  462.8 71.5 %collective-permute-start.40 = (bf16[4,512,512]{2,1,0:T(8,128)(2,1)}, bf16[4,512,512]{2,1,0:T(8,128)(2,1)}, u32[]{:S(2)}, u32[]{:S(2)}) collective-permute-start(bf16[4,512,512]{2,1,0:T(8,128)(2,1)} %get-tuple-element.50), channel_id=1, source_target_pairs={{1,0},{3,2},{5,4},{7,6},{9,8},{11,10},{13,12},{15,14},{17,16},{19,... | collective-permute-start | bytes 6291464 | tf_op jit(solution)/shard_map/ppermute | solution.py:135
  465.4 68.8 %collective-permute-start.42 = (bf16[4,512,512]{2,1,0:T(8,128)(2,1)}, bf16[4,512,512]{2,1,0:T(8,128)(2,1)}, u32[]{:S(2)}, u32[]{:S(2)}) collective-permute-start(bf16[4,512,512]{2,1,0:T(8,128)(2,1)} %get-tuple-element.50), channel_id=1, source_target_pairs={{64,1},{96,33},{66,3},{98,35},{68,5},{100,37},{70,7},{102,39},{72,... | collective-permute-start | bytes 6291464 | tf_op jit(solution)/shard_map/ppermute | solution.py:136
  466.7 67.6 %collective-permute-start.43 = (bf16[4,512,512]{2,1,0:T(8,128)(2,1)}, bf16[4,512,512]{2,1,0:T(8,128)(2,1)}, u32[]{:S(2)}, u32[]{:S(2)}) collective-permute-start(bf16[4,512,512]{2,1,0:T(8,128)(2,1)} %get-tuple-element.47), channel_id=1, source_target_pairs={{96,1},{64,33},{98,3},{66,35},{100,5},{68,37},{102,7},{70,39},{104... | collective-permute-start | bytes 6291464 | tf_op jit(solution)/shard_map/ppermute | solution.py:136
  472.9 61.4 %collective-permute-start.41 = (bf16[4,512,512]{2,1,0:T(8,128)(2,1)}, bf16[4,512,512]{2,1,0:T(8,128)(2,1)}, u32[]{:S(2)}, u32[]{:S(2)}) collective-permute-start(bf16[4,512,512]{2,1,0:T(8,128)(2,1)} %add_convert_fusion.2), channel_id=1, source_target_pairs={{0,32},{1,33},{32,0},{33,1},{64,96},{65,97},{96,64},{97,65},{2,34}... | collective-permute-start | bytes 6291464 | tf_op jit(solution)/shard_map/ppermute | solution.py:138
  488.0 14.9 %collective-permute-start.36 = (bf16[128,2048]{1,0:T(8,128)(2,1)S(1)}, bf16[128,2048]{1,0:T(8,128)(2,1)S(1)}, u32[]{:S(2)}, u32[]{:S(2)}) collective-permute-start(bf16[128,2048]{1,0:T(8,128)(2,1)S(1)} %get-tuple-element.89), channel_id=1, source_target_pairs={{0,16},{8,24},{16,0},{24,8},{1,17},{9,25},{17,1},{25,9},{2,18},{10... | collective-permute-start | bytes 1572872 | tf_op jit(solution)/shard_map/ppermute | solution.py:73
  503.0 14.3 %collective-permute-start.37 = (bf16[128,2048]{1,0:T(8,128)(2,1)S(1)}, bf16[128,2048]{1,0:T(8,128)(2,1)S(1)}, u32[]{:S(2)}, u32[]{:S(2)}) collective-permute-start(bf16[128,2048]{1,0:T(8,128)(2,1)S(1)} %get-tuple-element.91), channel_id=1, source_target_pairs={{0,8},{8,16},{16,24},{24,0},{1,9},{9,17},{17,25},{25,1},{2,10},{10... | collective-permute-start | bytes 1572872 | tf_op jit(solution)/shard_map/ppermute | solution.py:73
  517.3 12.7 %collective-permute-start.38 = (bf16[128,2048]{1,0:T(8,128)(2,1)S(1)}, bf16[128,2048]{1,0:T(8,128)(2,1)S(1)}, u32[]{:S(2)}, u32[]{:S(2)}) collective-permute-start(bf16[128,2048]{1,0:T(8,128)(2,1)S(1)} %get-tuple-element.90), channel_id=1, source_target_pairs={{0,24},{8,0},{16,8},{24,16},{1,25},{9,1},{17,9},{25,17},{2,26},{10... | collective-permute-start | bytes 1572872 | tf_op jit(solution)/shard_map/ppermute | solution.py:73
  540.5 13.0 %collective-permute-start.44 = (bf16[512,512]{1,0:T(8,128)(2,1)S(1)}, bf16[512,512]{1,0:T(8,128)(2,1)S(1)}, u32[]{:S(2)}, u32[]{:S(2)}) collective-permute-start(bf16[512,512]{1,0:T(8,128)(2,1)S(1)} %get-tuple-element.86), channel_id=1, source_target_pairs={{0,16},{8,24},{16,0},{24,8},{1,17},{9,25},{17,1},{25,9},{2,18},{10... | collective-permute-start | bytes 1572872 | tf_op jit(solution)/shard_map/ppermute | solution.py:73
  540.6 26.1 %collective-permute-start.45 = (bf16[512,512]{1,0:T(8,128)(2,1)S(1)}, bf16[512,512]{1,0:T(8,128)(2,1)S(1)}, u32[]{:S(2)}, u32[]{:S(2)}) collective-permute-start(bf16[512,512]{1,0:T(8,128)(2,1)S(1)} %get-tuple-element.88), channel_id=1, source_target_pairs={{0,8},{8,16},{16,24},{24,0},{1,9},{9,17},{17,25},{25,1},{2,10},{10... | collective-permute-start | bytes 1572872 | tf_op jit(solution)/shard_map/ppermute | solution.py:73
  542.1 24.6 %collective-permute-start.46 = (bf16[512,512]{1,0:T(8,128)(2,1)S(1)}, bf16[512,512]{1,0:T(8,128)(2,1)S(1)}, u32[]{:S(2)}, u32[]{:S(2)}) collective-permute-start(bf16[512,512]{1,0:T(8,128)(2,1)S(1)} %get-tuple-element.87), channel_id=1, source_target_pairs={{0,24},{8,0},{16,8},{24,16},{1,25},{9,1},{17,9},{25,17},{2,26},{10... | collective-permute-start | bytes 1572872 | tf_op jit(solution)/shard_map/ppermute | solution.py:73
  598.5 7.2 collective-permute-start.50
  616.6 12.7 %collective-permute-start.60 = (bf16[16,80,128]{2,1,0:T(8,128)(2,1)S(1)}, bf16[16,80,128]{2,1,0:T(8,128)(2,1)S(1)}, u32[]{:S(2)}, u32[]{:S(2)}) collective-permute-start(bf16[16,80,128]{2,1,0:T(8,128)(2,1)S(1)} %fusion.42), channel_id=1, source_target_pairs={{0,1},{1,0},{2,3},{3,2},{4,5},{5,4},{6,7},{7,6},{8,9},{9,8},{10,11... | collective-permute-start | bytes 983048 | tf_op jit(solution)/shard_map/ppermute | solution.py:69
  629.5 13.0 %collective-permute-start.61 = (bf16[4,80,128]{2,1,0:T(8,128)(2,1)S(1)}, bf16[4,80,128]{2,1,0:T(8,128)(2,1)S(1)}, u32[]{:S(2)}, u32[]{:S(2)}) collective-permute-start(bf16[4,80,128]{2,1,0:T(8,128)(2,1)S(1)} %get-tuple-element.99), channel_id=1, source_target_pairs={{0,32},{32,64},{64,96},{96,0},{1,33},{33,65},{65,97},{97,1},{2,34}... | collective-permute-start | bytes 245768 | tf_op jit(solution)/shard_map/ppermute | solution.py:73
  629.5 13.1 %collective-permute-start.62 = (bf16[4,80,128]{2,1,0:T(8,128)(2,1)S(1)}, bf16[4,80,128]{2,1,0:T(8,128)(2,1)S(1)}, u32[]{:S(2)}, u32[]{:S(2)}) collective-permute-start(bf16[4,80,128]{2,1,0:T(8,128)(2,1)S(1)} %get-tuple-element.101), channel_id=1, source_target_pairs={{0,64},{32,96},{64,0},{96,32},{1,65},{33,97},{65,1},{97,33},{2,66}... | collective-permute-start | bytes 245768 | tf_op jit(solution)/shard_map/ppermute | solution.py:73
  642.7 7.8 %collective-permute-start.64 = (bf16[80,128]{1,0:T(8,128)(2,1)S(1)}, bf16[80,128]{1,0:T(8,128)(2,1)S(1)}, u32[]{:S(2)}, u32[]{:S(2)}) collective-permute-start(bf16[80,128]{1,0:T(8,128)(2,1)S(1)} %get-tuple-element.132), channel_id=1, source_target_pairs={{0,8},{8,16},{16,24},{24,0},{1,9},{9,17},{17,25},{25,1},{2,10},{10... | collective-permute-start | bytes 61448 | tf_op jit(solution)/shard_map/ppermute | solution.py:73
  644.9 20.5 %collective-permute-start.47 = (bf16[128,2048]{1,0:T(8,128)(2,1)S(1)}, bf16[128,2048]{1,0:T(8,128)(2,1)S(1)}, u32[]{:S(2)}, u32[]{:S(2)}) collective-permute-start(bf16[128,2048]{1,0:T(8,128)(2,1)S(1)} %get-tuple-element.83), channel_id=1, source_target_pairs={{0,4},{2,6},{4,0},{6,2},{1,5},{3,7},{5,1},{7,3},{8,12},{10,14},{12... | collective-permute-start | bytes 1572872 | tf_op jit(solution)/shard_map/ppermute | solution.py:73
  646.0 36.8 %collective-permute-start.48 = (bf16[128,2048]{1,0:T(8,128)(2,1)S(1)}, bf16[128,2048]{1,0:T(8,128)(2,1)S(1)}, u32[]{:S(2)}, u32[]{:S(2)}) collective-permute-start(bf16[128,2048]{1,0:T(8,128)(2,1)S(1)} %get-tuple-element.85), channel_id=1, source_target_pairs={{0,2},{2,4},{4,6},{6,0},{1,3},{3,5},{5,7},{7,1},{8,10},{10,12},{12... | collective-permute-start | bytes 1572872 | tf_op jit(solution)/shard_map/ppermute | solution.py:73
  646.2 36.6 %collective-permute-start.49 = (bf16[128,2048]{1,0:T(8,128)(2,1)S(1)}, bf16[128,2048]{1,0:T(8,128)(2,1)S(1)}, u32[]{:S(2)}, u32[]{:S(2)}) collective-permute-start(bf16[128,2048]{1,0:T(8,128)(2,1)S(1)} %get-tuple-element.84), channel_id=1, source_target_pairs={{0,6},{2,0},{4,2},{6,4},{1,7},{3,1},{5,3},{7,5},{8,14},{10,8},{12,... | collective-permute-start | bytes 1572872 | tf_op jit(solution)/shard_map/ppermute | solution.py:73
  653.5 72.7 %collective-permute-start.39 = (bf16[64,2048]{1,0:T(8,128)(2,1)}, bf16[64,2048]{1,0:T(8,128)(2,1)}, u32[]{:S(2)}, u32[]{:S(2)}) collective-permute-start(bf16[64,2048]{1,0:T(8,128)(2,1)} %get-tuple-element.107), channel_id=1, source_target_pairs={{0,1},{1,0},{2,3},{3,2},{4,5},{5,4},{6,7},{7,6},{8,9},{9,8},{10,11... | collective-permute-start | bytes 786440 | tf_op jit(solution)/shard_map/ppermute | solution.py:69
  656.2 29.6 %collective-permute-start.67 = (bf16[80,128]{1,0:T(8,128)(2,1)S(1)}, bf16[80,128]{1,0:T(8,128)(2,1)S(1)}, u32[]{:S(2)}, u32[]{:S(2)}) collective-permute-start(bf16[80,128]{1,0:T(8,128)(2,1)S(1)} %get-tuple-element.69), channel_id=1, source_target_pairs={{0,24},{8,0},{16,8},{24,16},{1,25},{9,1},{17,9},{25,17},{2,26},{10... | collective-permute-start | bytes 61448 | tf_op jit(solution)/shard_map/ppermute | solution.py:73
  697.0 19.8 %collective-permute-start.73 = (bf16[4,4,80,128]{3,2,1,0:T(8,128)(2,1)}, bf16[4,4,80,128]{3,2,1,0:T(8,128)(2,1)}, u32[]{:S(2)}, u32[]{:S(2)}) collective-permute-start(bf16[4,4,80,128]{3,2,1,0:T(8,128)(2,1)} %bitcast_dynamic-update-slice_fusion.8), channel_id=1, source_target_pairs={{0,6},{2,0},{4,2},{6,4},{1,7},{3,1},{5,3},{7,5},{8,14},{10,8},{12,... | collective-permute-start | bytes 983048 | tf_op jit(solution)/shard_map/ppermute | solution.py:73
  697.6 20.3 %collective-permute-start.74 = (bf16[4,4,80,128]{3,2,1,0:T(8,128)(2,1)}, bf16[4,4,80,128]{3,2,1,0:T(8,128)(2,1)}, u32[]{:S(2)}, u32[]{:S(2)}) collective-permute-start(bf16[4,4,80,128]{3,2,1,0:T(8,128)(2,1)} %bitcast_dynamic-update-slice_fusion.8), channel_id=1, source_target_pairs={{0,4},{2,6},{4,0},{6,2},{1,5},{3,7},{5,1},{7,3},{8,12},{10,14},{12... | collective-permute-start | bytes 983048 | tf_op jit(solution)/shard_map/ppermute | solution.py:73
  698.3 20.7 %collective-permute-start.75 = (bf16[4,4,80,128]{3,2,1,0:T(8,128)(2,1)}, bf16[4,4,80,128]{3,2,1,0:T(8,128)(2,1)}, u32[]{:S(2)}, u32[]{:S(2)}) collective-permute-start(bf16[4,4,80,128]{3,2,1,0:T(8,128)(2,1)} %bitcast_dynamic-update-slice_fusion.8), channel_id=1, source_target_pairs={{0,2},{2,4},{4,6},{6,0},{1,3},{3,5},{5,7},{7,1},{8,10},{10,12},{12... | collective-permute-start | bytes 983048 | tf_op jit(solution)/shard_map/ppermute | solution.py:73
  720.0 9.3 %collective-permute-start.76 = (bf16[4,16,80,128]{3,2,1,0:T(8,128)(2,1)S(1)}, bf16[4,16,80,128]{3,2,1,0:T(8,128)(2,1)S(1)}, u32[]{:S(2)}, u32[]{:S(2)}) collective-permute-start(bf16[4,16,80,128]{3,2,1,0:T(8,128)(2,1)S(1)} %bitcast.269), channel_id=1, source_target_pairs={{0,1},{1,0},{2,3},{3,2},{4,5},{5,4},{6,7},{7,6},{8,9},{9,8},{10,11... | collective-permute-start | bytes 3932168 | tf_op jit(solution)/shard_map/ppermute | solution.py:69
  (103 other events, 1197.5 us)
Sparse Core Ops, SparseCore 0:
  97.5 98.3 all-gather.3
  239.7 99.0 all-gather.5
  392.6 77.6 reduce-scatter.2
  474.4 100.7 reduce-scatter.4
  583.5 101.4 all-gather.7

commit v6 on v5

--- a/solution.py
+++ b/solution.py
@@ -91,9 +91,9 @@
     return whole_ring
 
 
-def sum_near(blocks, ring):
+def sum_near(blocks, ring, base=0.0):
     got = [shift(blocks[step], ring, step) for step in (2, 1, 3)]
-    total = blocks[0].astype(f32)
+    total = blocks[0].astype(f32) + base
     for term in got:
         total = total + term.astype(f32)
     return total
@@ -624,7 +624,7 @@
     qkv_parts = after(qkv_parts, normed_g, cot_g)
     qkv_mine = gather_ring(gather_ring(qkv_parts, "x"), "z").reshape(2048, 512)
     qkv_other = swap_cores(qkv_mine)
-    wo = lax.all_gather(w_out + zero_of(qkv_mine).astype(bf16), ALL, axis=0, tiled=True)
+    wo = lax.all_gather(w_out, ALL, axis=0, tiled=True)
     q_expand = columns_of(query_expand, 512)
     k_expand = columns_of(key_expand, 256)
     v_expand = columns_of(value_expand, 256)
@@ -684,9 +684,9 @@
         picks,
     )
 
-    def sum_tokens(part, ring):
+    def sum_tokens(part, ring, base=0.0):
         sent = part.astype(bf16)
-        return sum_near([sent[i * 128 : (i + 1) * 128] for i in range(4)], ring)
+        return sum_near([sent[i * 128 : (i + 1) * 128] for i in range(4)], ring, base)
 
     back = sum_tokens(back_part, "x")
     back, back_low, low_down_sum = back[:, :2048], back[:, 2048 : 2048 + 2 * rank], back[:, 2048 + 2 * rank :]
@@ -738,10 +738,6 @@
     for_mine = jnp.where(c == 0, grad_query, grad_kv)
     for_other = jnp.where(c == 0, grad_kv, grad_query)
     grad_normed_part = times_transposed(for_mine, qkv_mine) + times_transposed(for_other, qkv_other)
-    grad_normed = sum_tokens(grad_normed_part, "y") + times_transposed(grad_low_qkv, qkv_shrink)
-    output = (middle + aheads[0] + product(low_down, down_expand)).astype(bf16)
-    grad_input = (grad_middle + norm_back(inputs, scale_in, gain_attn, grad_normed)).astype(bf16)
-
     def features(array, at):
         return lax.dynamic_slice_in_dim(array, at * 512, 512, 1)
 
@@ -782,6 +778,9 @@
     g_gate, g_up, g_down_shrink, g_out_shrink, g_out_expand, g_down_expand, g_gateup = unpack_early(early_all)
     late_sum = sum_plane(kept, other, "x").astype(bf16)
     late_all = gather_ring(gather_ring(late_sum, "x"), "z")
+    grad_normed = sum_tokens(grad_normed_part, "y", zero_of(late_all)) + times_transposed(grad_low_qkv, qkv_shrink)
+    output = (middle + aheads[0] + product(low_down, down_expand)).astype(bf16)
+    grad_input = (grad_middle + norm_back(inputs, scale_in, gain_attn, grad_normed)).astype(bf16)
     late_all = gather_ring(late_all, "y", zero_of(g_gateup).astype(bf16))
     late_all = late_all.reshape(4, 16, -1, rank)
     late_other = swap_cores(late_all)

time: 753 us -> 736 us (0.977)
  starting transfers between devices: 153 us -> 144 us
    ppermute x1, waiting for transfers between devices: 37.2 us -> 18.2 us  [gather_row(): partner = lax.ppermute(line, CORNER, PARTNER)]
    ppermute x1, starting transfers between devices: 14.2 us -> 3.88 us  [sum_row(): terms = [got[1], lax.ppermute(sent, CORNER, PARTNER)] + terms]
    broadcast_in_dim x8 -> x0, local copies, waits for them, and re-layouts: 9.85 us -> none  [the longest x3 5.11 us: local(): heads = lax.dynamic_update_index_in_dim(heads, got, (y - step) % 4, 0)]
    unnamed x180 -> x176, local copies, waits for them, and re-layouts: 16.9 us -> 13.2 us
  transfers between devices with their start and end apart: 84 -> 84, of which waited for: 40 -> 40; matrix products, arithmetic and copies ran while one was open for 20% -> 21% of each run, Pallas kernels for 6% -> 6%
where the time goes in v6:
time: 736 us; the launch traced here: 724 us
  waiting for transfers between devices  290 us (39%)
  starting transfers between devices  144 us (20%)
  Pallas kernels  98.5 us (13%)
  local copies, waits for them, and re-layouts  76.1 us (10%)
  matrix products  49.6 us (7%)
  other arithmetic  41.5 us (6%)
  between operations  24.1 us (3%)
    ppermute x60, waiting for transfers between devices, shift(): lax.ppermute(value, RING[ring], [(i, (i + step) % 4) for i in range(4)])  221 us
    ppermute x60, starting transfers between devices, shift(): lax.ppermute(value, RING[ring], [(i, (i + step) % 4) for i in range(4)])  87.9 us
    pallas_call x1, Pallas kernels, feed_forward(): pl.pallas_call(ffn_kernel, grid_spec=pltpu.PrefetchScalarGridSpec(num_sca...  45.6 us
    dot_general x11, matrix products, product(): return jnp.dot(left, right, preferred_element_type=f32)  25.3 us
    ppermute x7, starting transfers between devices, swap_cores(): return lax.ppermute(value, 'c', [(0, 1), (1, 0)])  21.7 us
    ppermute x2, waiting for transfers between devices, gather_row(): ahead = [lax.ppermute(line, CORNER, pairs) for pairs in LATER]  20 us
    ppermute x1, waiting for transfers between devices, gather_row(): partner = lax.ppermute(line, CORNER, PARTNER)  18.2 us
    pallas_call x1, Pallas kernels, attend_back(): pl.pallas_call(attend_back_kernel, grid_spec=pltpu.PrefetchScalarGridSpec...  18.1 us
  transfers between devices with their start and end apart: 84, of which 40 were waited for; matrix products, arithmetic and copies ran while one was open for 21% of the time, Pallas kernels for 6%

profile of v6, /device:TPU:1, one launch (start us, length us, event | category | flops | bytes accessed | tf_op | source)
XLA Modules:
  0.0 723.6 jit_solution(10376624505748091541)
XLA Ops:
  12.7 5.0 all-to-all-start
  23.0 2.5 collective-permute-start.5
  31.1 6.1 collective-permute-done.5
  37.9 3.5 collective-permute-done.6
  42.5 11.6 %collective-permute-done.7 = bf16[128,2048]{1,0:T(8,128)(2,1)S(1)} collective-permute-done((bf16[128,2048]{1,0:T(8,128)(2,1)S(1)}, bf16[128,2048]{1,0:T(8,128)(2,1)S(1)}, u32[]{:S(2)}, u32[]{:S(2)}) %collective-permute-start.7) | collective-permute-done | bytes 524320 | tf_op jit(solution)/shard_map/ppermute | solution.py:73
  54.4 5.9 collective-permute-start.9
  63.2 2.6 collective-permute-done.10
  65.8 7.4 %collective-permute-start.11 = (bf16[4,128,512]{2,1,0:T(8,128)(2,1)S(1)}, bf16[4,128,512]{2,1,0:T(8,128)(2,1)S(1)}, u32[]{:S(2)}, u32[]{:S(2)}) collective-permute-start(bf16[4,128,512]{2,1,0:T(8,128)(2,1)S(1)} %bitcast_dynamic-update-slice_fusion.11), channel_id=1, source_target_pairs={{0,96},{32,0},{64,32},{96,64},{1,97},{33,1},{65,33},{97,65},{2,98}... | collective-permute-start | bytes 1572872 | tf_op jit(solution)/shard_map/ppermute | solution.py:73
  76.4 4.4 collective-permute-done.11
  81.6 3.2 collective-permute-done.12
  85.6 25.4 %collective-permute-done.13 = bf16[4,128,512]{2,1,0:T(8,128)(2,1)S(1)} collective-permute-done((bf16[4,128,512]{2,1,0:T(8,128)(2,1)S(1)}, bf16[4,128,512]{2,1,0:T(8,128)(2,1)S(1)}, u32[]{:S(2)}, u32[]{:S(2)}) %collective-permute-start.13) | collective-permute-done | bytes 524320 | tf_op jit(solution)/shard_map/ppermute | solution.py:73
  115.7 3.1 fusion.2
  119.9 2.9 fusion.147
  122.8 4.2 broadcast_select_fusion
  130.1 12.0 %collective-permute-done.15 = bf16[512,512]{1,0:T(8,128)(2,1)S(1)} collective-permute-done((bf16[512,512]{1,0:T(8,128)(2,1)S(1)}, bf16[512,512]{1,0:T(8,128)(2,1)S(1)}, u32[]{:S(2)}, u32[]{:S(2)}) %collective-permute-start.15) | collective-permute-done | bytes 524320 | tf_op jit(solution)/shard_map/ppermute | solution.py:73
  143.5 11.9 %collective-permute-done.17 = bf16[512,512]{1,0:T(8,128)(2,1)S(1)} collective-permute-done((bf16[512,512]{1,0:T(8,128)(2,1)S(1)}, bf16[512,512]{1,0:T(8,128)(2,1)S(1)}, u32[]{:S(2)}, u32[]{:S(2)}) %collective-permute-start.17) | collective-permute-done | bytes 524320 | tf_op jit(solution)/shard_map/ppermute | solution.py:73
  156.9 6.1 collective-permute-start.19
  163.0 2.7 collective-permute-start.20
  179.2 6.5 all-to-all-start.1
  185.7 18.2 %collective-permute-done.18.refs_1_ = bf16[4,512,512]{2,1,0:T(8,128)(2,1)} collective-permute-done((bf16[4,512,512]{2,1,0:T(8,128)(2,1)}, bf16[4,512,512]{2,1,0:T(8,128)(2,1)}, u32[]{:S(2)}, u32[]{:S(2)}) %collective-permute-start.18) | collective-permute-done | bytes 2097184 | tf_op jit(solution)/shard_map/ppermute | solution.py:129
  205.2 20.0 %collective-permute-done.19.refs_2_ = bf16[4,512,512]{2,1,0:T(8,128)(2,1)} collective-permute-done((bf16[4,512,512]{2,1,0:T(8,128)(2,1)}, bf16[4,512,512]{2,1,0:T(8,128)(2,1)}, u32[]{:S(2)}, u32[]{:S(2)}) %collective-permute-start.19) | collective-permute-done | bytes 2097184 | tf_op jit(solution)/shard_map/ppermute | solution.py:128
  243.7 2.8 reshape.658
  250.3 12.8 %attend.1 = (f32[512,512]{1,0:T(8,128)S(1)}, f32[2,512,1]{2,1,0:T(8,128)S(1)}) custom-call(s32[64]{0:T(128)S(1)} %pad_add_fusion.2.active, bf16[512,512]{1,0:T(8,128)(2,1)S(1)} %fusion.23.q_ref, s32[512,1]{1,0:T(8,128)S(1)} %copy.137.pos_ref, s32[512,1]{1,0:T(8,128)S(1)} %copy.138.start_ref, s32[16,1,512]{2,1,0:T(1,128)S(1)} %reshape.659.kpos_ref, ...), custom_call_target="tpu_custom_call" | custom-call | flops 6442450944 | bytes 10485760 | tf_op jit(solution)/shard_map/attend/pallas_call | solution.py:284
  264.3 2.4 collective-permute-start.23
  280.2 5.2 multiply_reduce_fusion.1
  290.5 9.8 %collective-permute-done.26 = bf16[128,2048]{1,0:T(8,128)(2,1)S(1)} collective-permute-done((bf16[128,2048]{1,0:T(8,128)(2,1)S(1)}, bf16[128,2048]{1,0:T(8,128)(2,1)S(1)}, u32[]{:S(2)}, u32[]{:S(2)}) %collective-permute-start.26) | collective-permute-done | bytes 524320 | tf_op jit(solution)/shard_map/ppermute | solution.py:73
  300.3 12.8 %collective-permute-done.28 = bf16[128,2048]{1,0:T(8,128)(2,1)S(1)} collective-permute-done((bf16[128,2048]{1,0:T(8,128)(2,1)S(1)}, bf16[128,2048]{1,0:T(8,128)(2,1)S(1)}, u32[]{:S(2)}, u32[]{:S(2)}) %collective-permute-start.28) | collective-permute-done | bytes 524320 | tf_op jit(solution)/shard_map/ppermute | solution.py:73
  316.3 15.4 %all-gather.6.cloned.1.call-done = bf16[32,192,2048]{2,1,0:T(8,128)(2,1)} async-done(((bf16[1,192,2048]{2,1,0:T(8,128)(2,1)}), bf16[32,192,2048]{2,1,0:T(8,128)(2,1)}) %all-gather.6.cloned.1.call-update) | async-done | bytes 25165840 | tf_op jit(solution)/shard_map/all_gather | solution.py:648
  331.7 45.6 %feed_forward.1 = (bf16[512,2048]{1,0:T(8,128)(2,1)}, bf16[512,2432]{1,0:T(8,128)(2,1)}, f32[4,4,2,192,128]{4,3,2,1,0:T(8,128)}) custom-call(s32[1]{0:T(128)} %bitcast.36.at, bf16[512,2048]{1,0:T(8,128)(2,1)} %pad_maximum_fusion.1.nm_ref, bf16[512,2048]{1,0:T(8,128)(2,1)} %copy-done.59, bf16[512,256]{1,0:T(8,128)(2,1)} %fusion.3.lgu_ref, ...), custom_call_target="tpu_custom_call" | custom-call | flops 30064771072 | bytes 41943040 | tf_op jit(solution)/shard_map/feed_forward/pallas_call | solution.py:403
  377.3 2.7 fusion.137
  380.0 2.7 collective-permute-start.29
  385.7 11.6 %collective-permute-done.29 = bf16[128,2432]{1,0:T(8,128)(2,1)} collective-permute-done((bf16[128,2432]{1,0:T(8,128)(2,1)}, bf16[128,2432]{1,0:T(8,128)(2,1)}, u32[]{:S(2)}, u32[]{:S(2)}) %collective-permute-start.29) | collective-permute-done | bytes 622624 | tf_op jit(solution)/shard_map/ppermute | solution.py:73
  397.3 13.9 %collective-permute-done.30 = bf16[128,2432]{1,0:T(8,128)(2,1)} collective-permute-done((bf16[128,2432]{1,0:T(8,128)(2,1)}, bf16[128,2432]{1,0:T(8,128)(2,1)}, u32[]{:S(2)}, u32[]{:S(2)}) %collective-permute-start.30) | collective-permute-done | bytes 622624 | tf_op jit(solution)/shard_map/ppermute | solution.py:73
  416.2 2.9 fusion.128
  419.5 2.5 collective-permute-start.32
  425.8 2.9 copy.147
  428.8 2.9 collective-permute-done.34
  434.9 18.1 %attend_back.1 = (f32[512,512]{1,0:T(8,128)S(1)}, bf16[4,512,512]{2,1,0:T(8,128)(2,1)}, bf16[4,512,512]{2,1,0:T(8,128)(2,1)}, bf16[4,512,512]{2,1,0:T(8,128)(2,1)}, bf16[4,512,512]{2,1,0:T(8,128)(2,1)}) custom-call(s32[64]{0:T(128)S(1)} %pad_add_fusion.2.active, bf16[512,512]{1,0:T(8,128)(2,1)S(1)} %fusion.23.q_ref, s32[512,1]{1,0:T(8,128)S(1)} %copy-done.4, ...), custom_call_target="tpu_custom_call" | custom-call | flops 12884901888 | bytes 20971520 | tf_op jit(solution)/shard_map/attend_back/pallas_call | solution.py:309
  454.4 2.7 collective-permute-start.40
  459.7 3.7 add_convert_fusion.2
  464.6 3.9 collective-permute-start.41
  469.4 4.4 collective-permute-start.36
  473.9 11.6 %collective-permute-done.36 = bf16[128,2048]{1,0:T(8,128)(2,1)S(1)} collective-permute-done((bf16[128,2048]{1,0:T(8,128)(2,1)S(1)}, bf16[128,2048]{1,0:T(8,128)(2,1)S(1)}, u32[]{:S(2)}, u32[]{:S(2)}) %collective-permute-start.36) | collective-permute-done | bytes 524320 | tf_op jit(solution)/shard_map/ppermute | solution.py:73
  485.5 7.3 %collective-permute-start.37 = (bf16[128,2048]{1,0:T(8,128)(2,1)S(1)}, bf16[128,2048]{1,0:T(8,128)(2,1)S(1)}, u32[]{:S(2)}, u32[]{:S(2)}) collective-permute-start(bf16[128,2048]{1,0:T(8,128)(2,1)S(1)} %get-tuple-element.91), channel_id=1, source_target_pairs={{0,8},{8,16},{16,24},{24,0},{1,9},{9,17},{17,25},{25,1},{2,10},{10... | collective-permute-start | bytes 1572872 | tf_op jit(solution)/shard_map/ppermute | solution.py:73
  492.8 14.7 %collective-permute-done.37 = bf16[128,2048]{1,0:T(8,128)(2,1)S(1)} collective-permute-done((bf16[128,2048]{1,0:T(8,128)(2,1)S(1)}, bf16[128,2048]{1,0:T(8,128)(2,1)S(1)}, u32[]{:S(2)}, u32[]{:S(2)}) %collective-permute-start.37) | collective-permute-done | bytes 524320 | tf_op jit(solution)/shard_map/ppermute | solution.py:73
  509.1 11.3 %collective-permute-done.38 = bf16[128,2048]{1,0:T(8,128)(2,1)S(1)} collective-permute-done((bf16[128,2048]{1,0:T(8,128)(2,1)S(1)}, bf16[128,2048]{1,0:T(8,128)(2,1)S(1)}, u32[]{:S(2)}, u32[]{:S(2)}) %collective-permute-start.38) | collective-permute-done | bytes 524320 | tf_op jit(solution)/shard_map/ppermute | solution.py:73
  524.7 5.6 add_convert_fusion.1
  534.2 9.5 %collective-permute-done.44 = bf16[512,512]{1,0:T(8,128)(2,1)S(1)} collective-permute-done((bf16[512,512]{1,0:T(8,128)(2,1)S(1)}, bf16[512,512]{1,0:T(8,128)(2,1)S(1)}, u32[]{:S(2)}, u32[]{:S(2)}) %collective-permute-start.44) | collective-permute-done | bytes 524320 | tf_op jit(solution)/shard_map/ppermute | solution.py:73
  543.7 13.4 %collective-permute-done.45 = bf16[512,512]{1,0:T(8,128)(2,1)S(1)} collective-permute-done((bf16[512,512]{1,0:T(8,128)(2,1)S(1)}, bf16[512,512]{1,0:T(8,128)(2,1)S(1)}, u32[]{:S(2)}, u32[]{:S(2)}) %collective-permute-start.45) | collective-permute-done | bytes 524320 | tf_op jit(solution)/shard_map/ppermute | solution.py:73
  559.4 12.6 %reduce-scatter.5.cloned.1.call-done = f32[1,320,128]{2,1,0:T(8,128)} async-done(((f32[32,320,128]{2,1,0:T(8,128)}), f32[1,320,128]{2,1,0:T(8,128)}) %reduce-scatter.5.cloned.1.call-update) | async-done | bytes 163856 | tf_op jit(solution)/shard_map/reduce_scatter | solution.py:762
  582.0 2.8 reshape.669
  613.5 10.2 %collective-permute-start.53 = (bf16[16,80,128]{2,1,0:T(8,128)(2,1)S(1)}, bf16[16,80,128]{2,1,0:T(8,128)(2,1)S(1)}, u32[]{:S(2)}, u32[]{:S(2)}) collective-permute-start(bf16[16,80,128]{2,1,0:T(8,128)(2,1)S(1)} %fusion.42), channel_id=1, source_target_pairs={{0,1},{1,0},{2,3},{3,2},{4,5},{5,4},{6,7},{7,6},{8,9},{9,8},{10,11... | collective-permute-start | bytes 983048 | tf_op jit(solution)/shard_map/ppermute | solution.py:69
  625.4 2.9 collective-permute-start.55
  630.3 2.9 fusion.30
  633.4 2.7 collective-permute-start.58
  637.0 2.9 add_convert_fusion
  642.2 2.6 collective-permute-start.68
  645.7 3.9 collective-permute-done.61
  650.2 3.7 collective-permute-done.62
  659.4 3.3 collective-permute-done.64
  665.5 2.7 collective-permute-done.65
  675.6 15.0 %unpack_early.1 = (f32[128,8192]{1,0:T(8,128)}, f32[128,8192]{1,0:T(8,128)}, f32[8192,128]{1,0:T(8,128)}, f32[2048,128]{1,0:T(8,128)}, f32[128,2048]{1,0:T(8,128...) custom-call(bf16[128,272,128]{2,1,0:T(8,128)(2,1)} %all-gather.8.cloned.1.call-done.all_ref), custom_call_target="tpu_custom_call" | custom-call | flops 1048576 | bytes 28311552 | tf_op jit(solution)/shard_map/unpack_early/pallas_call | solution.py:471
  697.1 7.9 %collective-permute-start.76 = (bf16[4,16,80,128]{3,2,1,0:T(8,128)(2,1)S(1)}, bf16[4,16,80,128]{3,2,1,0:T(8,128)(2,1)S(1)}, u32[]{:S(2)}, u32[]{:S(2)}) collective-permute-start(bf16[4,16,80,128]{3,2,1,0:T(8,128)(2,1)S(1)} %bitcast.277), channel_id=1, source_target_pairs={{0,1},{1,0},{2,3},{3,2},{4,5},{5,4},{6,7},{7,6},{8,9},{9,8},{10,11... | collective-permute-start | bytes 3932168 | tf_op jit(solution)/shard_map/ppermute | solution.py:69
  710.0 7.0 unpack_late.1
  (513 shorter events, 196.3 us)
Async XLA Ops:
  7.2 224.1 %all-gather.4.cloned.1.call-start = ((), (), s32[]{:S(2)}) async-start(), calls=%async_computation.4 | async-start | bytes 8454144 | tf_op jit(solution)/shard_map/all_gather | solution.py:627
  9.1 9.4 %collective-permute-start = (bf16[64,2048]{1,0:T(8,128)(2,1)S(1)}, bf16[64,2048]{1,0:T(8,128)(2,1)S(1)}, u32[]{:S(2)}, u32[]{:S(2)}) collective-permute-start(bf16[64,2048]{1,0:T(8,128)(2,1)S(1)} %get-tuple-element.122), channel_id=1, source_target_pairs={{0,1},{1,0},{2,3},{3,2},{4,5},{5,4},{6,7},{7,6},{8,9},{9,8},{10,11... | collective-permute-start | bytes 786440 | tf_op jit(solution)/shard_map/ppermute | solution.py:69
  11.6 7.8 %collective-permute-start.1 = (bf16[64,2048]{1,0:T(8,128)(2,1)S(1)}, bf16[64,2048]{1,0:T(8,128)(2,1)}, u32[]{:S(2)}, u32[]{:S(2)}) collective-permute-start(bf16[64,2048]{1,0:T(8,128)(2,1)S(1)} %get-tuple-element.120), channel_id=1, source_target_pairs={{0,1},{1,0},{2,3},{3,2},{4,5},{5,4},{6,7},{7,6},{8,9},{9,8},{10,11... | collective-permute-start | bytes 786440 | tf_op jit(solution)/shard_map/ppermute | solution.py:69
  12.7 10.3 %all-to-all-start = ((bf16[8,16,512]{2,1,0:T(8,128)(2,1)}), bf16[8,16,512]{2,1,0:T(8,128)(2,1)S(1)}, u32[]{:S(2)}, u32[]{:S(2)}) async-start(bf16[8,16,512]{2,1,0:T(8,128)(2,1)} %bitcast.9), calls=%async_computation | async-start | bytes 262144 | tf_op jit(solution)/shard_map/all_to_all | solution.py:613
  23.0 14.2 %collective-permute-start.5 = (bf16[128,2048]{1,0:T(8,128)(2,1)S(1)}, bf16[128,2048]{1,0:T(8,128)(2,1)S(1)}, u32[]{:S(2)}, u32[]{:S(2)}) collective-permute-start(bf16[128,2048]{1,0:T(8,128)(2,1)S(1)} %pad_maximum_fusion.4), channel_id=1, source_target_pairs={{0,24},{8,0},{16,8},{24,16},{1,25},{9,1},{17,9},{25,17},{2,26},{10... | collective-permute-start | bytes 1572872 | tf_op jit(solution)/shard_map/ppermute | solution.py:73
  27.0 14.4 %collective-permute-start.6 = (bf16[128,2048]{1,0:T(8,128)(2,1)S(1)}, bf16[128,2048]{1,0:T(8,128)(2,1)}, u32[]{:S(2)}, u32[]{:S(2)}) collective-permute-start(bf16[128,2048]{1,0:T(8,128)(2,1)S(1)} %pad_maximum_fusion.4), channel_id=1, source_target_pairs={{0,16},{8,24},{16,0},{24,8},{1,17},{9,25},{17,1},{25,9},{2,18},{10... | collective-permute-start | bytes 1572872 | tf_op jit(solution)/shard_map/ppermute | solution.py:73
  28.2 25.9 %collective-permute-start.7 = (bf16[128,2048]{1,0:T(8,128)(2,1)S(1)}, bf16[128,2048]{1,0:T(8,128)(2,1)S(1)}, u32[]{:S(2)}, u32[]{:S(2)}) collective-permute-start(bf16[128,2048]{1,0:T(8,128)(2,1)S(1)} %pad_maximum_fusion.4), channel_id=1, source_target_pairs={{0,8},{8,16},{16,24},{24,0},{1,9},{9,17},{17,25},{25,1},{2,10},{10... | collective-permute-start | bytes 1572872 | tf_op jit(solution)/shard_map/ppermute | solution.py:73
  29.0 25.2 %collective-permute-start.2 = (bf16[128,2048]{1,0:T(8,128)(2,1)S(1)}, bf16[128,2048]{1,0:T(8,128)(2,1)S(1)}, u32[]{:S(2)}, u32[]{:S(2)}) collective-permute-start(bf16[128,2048]{1,0:T(8,128)(2,1)S(1)} %fusion.9), channel_id=1, source_target_pairs={{0,6},{2,0},{4,2},{6,4},{1,7},{3,1},{5,3},{7,5},{8,14},{10,8},{12,... | collective-permute-start | bytes 1572872 | tf_op jit(solution)/shard_map/ppermute | solution.py:73
  29.9 24.3 %collective-permute-start.3 = (bf16[128,2048]{1,0:T(8,128)(2,1)S(1)}, bf16[128,2048]{1,0:T(8,128)(2,1)S(1)}, u32[]{:S(2)}, u32[]{:S(2)}) collective-permute-start(bf16[128,2048]{1,0:T(8,128)(2,1)S(1)} %fusion.9), channel_id=1, source_target_pairs={{0,4},{2,6},{4,0},{6,2},{1,5},{3,7},{5,1},{7,3},{8,12},{10,14},{12... | collective-permute-start | bytes 1572872 | tf_op jit(solution)/shard_map/ppermute | solution.py:73
  37.2 17.1 %collective-permute-start.4 = (bf16[128,2048]{1,0:T(8,128)(2,1)S(1)}, bf16[128,2048]{1,0:T(8,128)(2,1)S(1)}, u32[]{:S(2)}, u32[]{:S(2)}) collective-permute-start(bf16[128,2048]{1,0:T(8,128)(2,1)S(1)} %fusion.9), channel_id=1, source_target_pairs={{0,2},{2,4},{4,6},{6,0},{1,3},{3,5},{5,7},{7,1},{8,10},{10,12},{12... | collective-permute-start | bytes 1572872 | tf_op jit(solution)/shard_map/ppermute | solution.py:73
  54.4 7.7 %collective-permute-start.8 = (bf16[128,512]{1,0:T(8,128)(2,1)S(1)}, bf16[128,512]{1,0:T(8,128)(2,1)S(1)}, u32[]{:S(2)}, u32[]{:S(2)}) collective-permute-start(bf16[128,512]{1,0:T(8,128)(2,1)S(1)} %bitcast.300), channel_id=1, source_target_pairs={{0,24},{8,0},{16,8},{24,16},{1,25},{9,1},{17,9},{25,17},{2,26},{10... | collective-permute-start | bytes 393224 | tf_op jit(solution)/shard_map/ppermute | solution.py:73
  54.4 8.8 %collective-permute-start.9 = (bf16[128,512]{1,0:T(8,128)(2,1)S(1)}, bf16[128,512]{1,0:T(8,128)(2,1)S(1)}, u32[]{:S(2)}, u32[]{:S(2)}) collective-permute-start(bf16[128,512]{1,0:T(8,128)(2,1)S(1)} %bitcast.301), channel_id=1, source_target_pairs={{0,16},{8,24},{16,0},{24,8},{1,17},{9,25},{17,1},{25,9},{2,18},{10... | collective-permute-start | bytes 393224 | tf_op jit(solution)/shard_map/ppermute | solution.py:73
  65.8 15.0 %collective-permute-start.11 = (bf16[4,128,512]{2,1,0:T(8,128)(2,1)S(1)}, bf16[4,128,512]{2,1,0:T(8,128)(2,1)S(1)}, u32[]{:S(2)}, u32[]{:S(2)}) collective-permute-start(bf16[4,128,512]{2,1,0:T(8,128)(2,1)S(1)} %bitcast_dynamic-update-slice_fusion.11), channel_id=1, source_target_pairs={{0,96},{32,0},{64,32},{96,64},{1,97},{33,1},{65,33},{97,65},{2,98}... | collective-permute-start | bytes 1572872 | tf_op jit(solution)/shard_map/ppermute | solution.py:73
  73.3 11.5 %collective-permute-start.12 = (bf16[4,128,512]{2,1,0:T(8,128)(2,1)S(1)}, bf16[4,128,512]{2,1,0:T(8,128)(2,1)S(1)}, u32[]{:S(2)}, u32[]{:S(2)}) collective-permute-start(bf16[4,128,512]{2,1,0:T(8,128)(2,1)S(1)} %bitcast_dynamic-update-slice_fusion.11), channel_id=1, source_target_pairs={{0,64},{32,96},{64,0},{96,32},{1,65},{33,97},{65,1},{97,33},{2,66}... | collective-permute-start | bytes 1572872 | tf_op jit(solution)/shard_map/ppermute | solution.py:73
  73.9 37.2 %collective-permute-start.13 = (bf16[4,128,512]{2,1,0:T(8,128)(2,1)S(1)}, bf16[4,128,512]{2,1,0:T(8,128)(2,1)S(1)}, u32[]{:S(2)}, u32[]{:S(2)}) collective-permute-start(bf16[4,128,512]{2,1,0:T(8,128)(2,1)S(1)} %bitcast_dynamic-update-slice_fusion.11), channel_id=1, source_target_pairs={{0,32},{32,64},{64,96},{96,0},{1,33},{33,65},{65,97},{97,1},{2,34}... | collective-permute-start | bytes 1572872 | tf_op jit(solution)/shard_map/ppermute | solution.py:73
  111.9 10.9 %collective-permute-start.14 = (bf16[2048,512]{1,0:T(8,128)(2,1)}, bf16[2048,512]{1,0:T(8,128)(2,1)}, u32[]{:S(2)}, u32[]{:S(2)}) collective-permute-start(bf16[2048,512]{1,0:T(8,128)(2,1)} %bitcast.19), channel_id=1, source_target_pairs={{0,1},{1,0},{2,3},{3,2},{4,5},{5,4},{6,7},{7,6},{8,9},{9,8},{10,11... | collective-permute-start | bytes 6291464 | tf_op jit(solution)/shard_map/ppermute | solution.py:69
  128.5 13.6 %collective-permute-start.15 = (bf16[512,512]{1,0:T(8,128)(2,1)S(1)}, bf16[512,512]{1,0:T(8,128)(2,1)S(1)}, u32[]{:S(2)}, u32[]{:S(2)}) collective-permute-start(bf16[512,512]{1,0:T(8,128)(2,1)S(1)} %get-tuple-element.116), channel_id=1, source_target_pairs={{0,24},{8,0},{16,8},{24,16},{1,25},{9,1},{17,9},{25,17},{2,26},{10... | collective-permute-start | bytes 1572872 | tf_op jit(solution)/shard_map/ppermute | solution.py:73
  128.7 14.7 %collective-permute-start.16 = (bf16[512,512]{1,0:T(8,128)(2,1)S(1)}, bf16[512,512]{1,0:T(8,128)(2,1)S(1)}, u32[]{:S(2)}, u32[]{:S(2)}) collective-permute-start(bf16[512,512]{1,0:T(8,128)(2,1)S(1)} %get-tuple-element.116), channel_id=1, source_target_pairs={{0,16},{8,24},{16,0},{24,8},{1,17},{9,25},{17,1},{25,9},{2,18},{10... | collective-permute-start | bytes 1572872 | tf_op jit(solution)/shard_map/ppermute | solution.py:73
  128.7 26.6 %collective-permute-start.17 = (bf16[512,512]{1,0:T(8,128)(2,1)S(1)}, bf16[512,512]{1,0:T(8,128)(2,1)S(1)}, u32[]{:S(2)}, u32[]{:S(2)}) collective-permute-start(bf16[512,512]{1,0:T(8,128)(2,1)S(1)} %get-tuple-element.116), channel_id=1, source_target_pairs={{0,8},{8,16},{16,24},{24,0},{1,9},{9,17},{17,25},{25,1},{2,10},{10... | collective-permute-start | bytes 1572872 | tf_op jit(solution)/shard_map/ppermute | solution.py:73
  156.9 47.0 %collective-permute-start.18 = (bf16[4,512,512]{2,1,0:T(8,128)(2,1)}, bf16[4,512,512]{2,1,0:T(8,128)(2,1)}, u32[]{:S(2)}, u32[]{:S(2)}) collective-permute-start(bf16[4,512,512]{2,1,0:T(8,128)(2,1)} %pad_maximum_fusion.refs_0_), channel_id=1, source_target_pairs={{0,32},{1,33},{32,0},{33,1},{64,96},{65,97},{96,64},{97,65},{2,34}... | collective-permute-start | bytes 6291464 | tf_op jit(solution)/shard_map/ppermute | solution.py:129
  156.9 68.2 %collective-permute-start.19 = (bf16[4,512,512]{2,1,0:T(8,128)(2,1)}, bf16[4,512,512]{2,1,0:T(8,128)(2,1)}, u32[]{:S(2)}, u32[]{:S(2)}) collective-permute-start(bf16[4,512,512]{2,1,0:T(8,128)(2,1)} %pad_maximum_fusion.refs_0_), channel_id=1, source_target_pairs={{1,64},{33,96},{3,66},{35,98},{5,68},{37,100},{7,70},{39,102},{9,7... | collective-permute-start | bytes 6291464 | tf_op jit(solution)/shard_map/ppermute | solution.py:128
  163.0 64.6 %collective-permute-start.20 = (bf16[4,512,512]{2,1,0:T(8,128)(2,1)}, bf16[4,512,512]{2,1,0:T(8,128)(2,1)}, u32[]{:S(2)}, u32[]{:S(2)}) collective-permute-start(bf16[4,512,512]{2,1,0:T(8,128)(2,1)} %pad_maximum_fusion.refs_0_), channel_id=1, source_target_pairs={{1,96},{33,64},{3,98},{35,66},{5,100},{37,68},{7,102},{39,70},{9,1... | collective-permute-start | bytes 6291464 | tf_op jit(solution)/shard_map/ppermute | solution.py:128
  165.7 63.8 %collective-permute-start.21 = (bf16[4,512,512]{2,1,0:T(8,128)(2,1)}, bf16[4,512,512]{2,1,0:T(8,128)(2,1)}, u32[]{:S(2)}, u32[]{:S(2)}) collective-permute-start(bf16[4,512,512]{2,1,0:T(8,128)(2,1)} %pad_maximum_fusion.refs_0_), channel_id=1, source_target_pairs={{0,1},{2,3},{4,5},{6,7},{8,9},{10,11},{12,13},{14,15},{16,17},{18,... | collective-permute-start | bytes 6291464 | tf_op jit(solution)/shard_map/ppermute | solution.py:130
  179.2 54.0 %all-to-all-start.1 = ((bf16[8,16,2048]{2,1,0:T(8,128)(2,1)}), bf16[8,16,2048]{2,1,0:T(8,128)(2,1)}, u32[]{:S(2)}, u32[]{:S(2)}) async-start(bf16[8,16,2048]{2,1,0:T(8,128)(2,1)} %maximum_add_fusion.1), calls=%async_computation.1 | async-start | bytes 1048576 | tf_op jit(solution)/shard_map/all_to_all | solution.py:645
  185.7 146.0 %all-gather.6.cloned.1.call-start = ((), (), s32[]{:S(2)}) async-start(), calls=%async_computation.5 | async-start | bytes 25952256 | tf_op jit(solution)/shard_map/all_gather | solution.py:648
  235.4 286.8 %reduce-scatter.3.cloned.1.call-start = ((), (), s32[]{:S(2)}) async-start(), calls=%async_computation.6 | async-start | bytes 3244032 | tf_op jit(solution)/shard_map/reduce_scatter | solution.py:711
  236.9 13.4 %collective-permute-start.22 = (bf16[4,512,512]{2,1,0:T(8,128)(2,1)}, bf16[4,512,512]{2,1,0:T(8,128)(2,1)}, u32[]{:S(2)}, u32[]{:S(2)}) collective-permute-start(bf16[4,512,512]{2,1,0:T(8,128)(2,1)} %collective-permute-done.18.refs_1_), channel_id=1, source_target_pairs={{0,1},{2,3},{4,5},{6,7},{8,9},{10,11},{12,13},{14,15},{16,17},{18,... | collective-permute-start | bytes 6291464 | tf_op jit(solution)/shard_map/ppermute | solution.py:130
  264.3 7.3 %collective-permute-start.23 = (bf16[128,512]{1,0:T(8,128)(2,1)S(1)}, bf16[128,512]{1,0:T(8,128)(2,1)S(1)}, u32[]{:S(2)}, u32[]{:S(2)}) collective-permute-start(bf16[128,512]{1,0:T(8,128)(2,1)S(1)} %get-tuple-element.114), channel_id=1, source_target_pairs={{0,2},{2,4},{4,6},{6,0},{1,3},{3,5},{5,7},{7,1},{8,10},{10,12},{12... | collective-permute-start | bytes 393224 | tf_op jit(solution)/shard_map/ppermute | solution.py:73
  266.7 7.0 collective-permute-start.24
  286.2 14.1 %collective-permute-start.26 = (bf16[128,2048]{1,0:T(8,128)(2,1)S(1)}, bf16[128,2048]{1,0:T(8,128)(2,1)S(1)}, u32[]{:S(2)}, u32[]{:S(2)}) collective-permute-start(bf16[128,2048]{1,0:T(8,128)(2,1)S(1)} %multiply_convert_fusion.1), channel_id=1, source_target_pairs={{0,24},{8,0},{16,8},{24,16},{1,25},{9,1},{17,9},{25,17},{2,26},{10... | collective-permute-start | bytes 1572872 | tf_op jit(solution)/shard_map/ppermute | solution.py:73
  286.3 14.0 %collective-permute-start.27 = (bf16[128,2048]{1,0:T(8,128)(2,1)S(1)}, bf16[128,2048]{1,0:T(8,128)(2,1)S(1)}, u32[]{:S(2)}, u32[]{:S(2)}) collective-permute-start(bf16[128,2048]{1,0:T(8,128)(2,1)S(1)} %multiply_convert_fusion.1), channel_id=1, source_target_pairs={{0,16},{8,24},{16,0},{24,8},{1,17},{9,25},{17,1},{25,9},{2,18},{10... | collective-permute-start | bytes 1572872 | tf_op jit(solution)/shard_map/ppermute | solution.py:73
  286.4 26.7 %collective-permute-start.28 = (bf16[128,2048]{1,0:T(8,128)(2,1)S(1)}, bf16[128,2048]{1,0:T(8,128)(2,1)S(1)}, u32[]{:S(2)}, u32[]{:S(2)}) collective-permute-start(bf16[128,2048]{1,0:T(8,128)(2,1)S(1)} %multiply_convert_fusion.1), channel_id=1, source_target_pairs={{0,8},{8,16},{16,24},{24,0},{1,9},{9,17},{17,25},{25,1},{2,10},{10... | collective-permute-start | bytes 1572872 | tf_op jit(solution)/shard_map/ppermute | solution.py:73
  380.0 17.2 %collective-permute-start.29 = (bf16[128,2432]{1,0:T(8,128)(2,1)}, bf16[128,2432]{1,0:T(8,128)(2,1)}, u32[]{:S(2)}, u32[]{:S(2)}) collective-permute-start(bf16[128,2432]{1,0:T(8,128)(2,1)} %get-tuple-element.80), channel_id=1, source_target_pairs={{0,16},{8,24},{16,0},{24,8},{1,17},{9,25},{17,1},{25,9},{2,18},{10... | collective-permute-start | bytes 1867784 | tf_op jit(solution)/shard_map/ppermute | solution.py:73
  382.7 28.4 %collective-permute-start.30 = (bf16[128,2432]{1,0:T(8,128)(2,1)}, bf16[128,2432]{1,0:T(8,128)(2,1)}, u32[]{:S(2)}, u32[]{:S(2)}) collective-permute-start(bf16[128,2432]{1,0:T(8,128)(2,1)} %get-tuple-element.82), channel_id=1, source_target_pairs={{0,8},{8,16},{16,24},{24,0},{1,9},{9,17},{17,25},{25,1},{2,10},{10... | collective-permute-start | bytes 1867784 | tf_op jit(solution)/shard_map/ppermute | solution.py:73
  383.0 28.1 %collective-permute-start.31 = (bf16[128,2432]{1,0:T(8,128)(2,1)}, bf16[128,2432]{1,0:T(8,128)(2,1)}, u32[]{:S(2)}, u32[]{:S(2)}) collective-permute-start(bf16[128,2432]{1,0:T(8,128)(2,1)} %get-tuple-element.81), channel_id=1, source_target_pairs={{0,24},{8,0},{16,8},{24,16},{1,25},{9,1},{17,9},{25,17},{2,26},{10... | collective-permute-start | bytes 1867784 | tf_op jit(solution)/shard_map/ppermute | solution.py:73
  385.4 186.5 %reduce-scatter.5.cloned.1.call-start = ((), (), s32[]{:S(2)}) async-start(), calls=%async_computation.7 | async-start | bytes 5406720 | tf_op jit(solution)/shard_map/reduce_scatter | solution.py:762
  419.5 9.3 %collective-permute-start.32 = (bf16[128,512]{1,0:T(8,128)(2,1)S(1)}, bf16[128,512]{1,0:T(8,128)(2,1)S(1)}, u32[]{:S(2)}, u32[]{:S(2)}) collective-permute-start(bf16[128,512]{1,0:T(8,128)(2,1)S(1)} %get-tuple-element.111), channel_id=1, source_target_pairs={{0,6},{2,0},{4,2},{6,4},{1,7},{3,1},{5,3},{7,5},{8,14},{10,8},{12,... | collective-permute-start | bytes 393224 | tf_op jit(solution)/shard_map/ppermute | solution.py:73
  422.0 6.8 collective-permute-start.33
  422.5 9.2 %collective-permute-start.34 = (bf16[128,512]{1,0:T(8,128)(2,1)S(1)}, bf16[128,512]{1,0:T(8,128)(2,1)S(1)}, u32[]{:S(2)}, u32[]{:S(2)}) collective-permute-start(bf16[128,512]{1,0:T(8,128)(2,1)S(1)} %get-tuple-element.109), channel_id=1, source_target_pairs={{0,2},{2,4},{4,6},{6,0},{1,3},{3,5},{5,7},{7,1},{8,10},{10,12},{12... | collective-permute-start | bytes 393224 | tf_op jit(solution)/shard_map/ppermute | solution.py:73
  428.7 246.9 %all-gather.8.cloned.1.call-start = ((), (), s32[]{:S(2)}) async-start(), calls=%async_computation.8 | async-start | bytes 8982528 | tf_op jit(solution)/shard_map/all_gather | solution.py:765
  453.0 6.7 collective-permute-start.35
  454.4 70.2 %collective-permute-start.40 = (bf16[4,512,512]{2,1,0:T(8,128)(2,1)}, bf16[4,512,512]{2,1,0:T(8,128)(2,1)}, u32[]{:S(2)}, u32[]{:S(2)}) collective-permute-start(bf16[4,512,512]{2,1,0:T(8,128)(2,1)} %get-tuple-element.50), channel_id=1, source_target_pairs={{1,0},{3,2},{5,4},{7,6},{9,8},{11,10},{13,12},{15,14},{17,16},{19,... | collective-permute-start | bytes 6291464 | tf_op jit(solution)/shard_map/ppermute | solution.py:135
  457.1 67.6 %collective-permute-start.42 = (bf16[4,512,512]{2,1,0:T(8,128)(2,1)}, bf16[4,512,512]{2,1,0:T(8,128)(2,1)}, u32[]{:S(2)}, u32[]{:S(2)}) collective-permute-start(bf16[4,512,512]{2,1,0:T(8,128)(2,1)} %get-tuple-element.50), channel_id=1, source_target_pairs={{64,1},{96,33},{66,3},{98,35},{68,5},{100,37},{70,7},{102,39},{72,... | collective-permute-start | bytes 6291464 | tf_op jit(solution)/shard_map/ppermute | solution.py:136
  458.4 66.3 %collective-permute-start.43 = (bf16[4,512,512]{2,1,0:T(8,128)(2,1)}, bf16[4,512,512]{2,1,0:T(8,128)(2,1)}, u32[]{:S(2)}, u32[]{:S(2)}) collective-permute-start(bf16[4,512,512]{2,1,0:T(8,128)(2,1)} %get-tuple-element.47), channel_id=1, source_target_pairs={{96,1},{64,33},{98,3},{66,35},{100,5},{68,37},{102,7},{70,39},{104... | collective-permute-start | bytes 6291464 | tf_op jit(solution)/shard_map/ppermute | solution.py:136
  464.6 60.1 %collective-permute-start.41 = (bf16[4,512,512]{2,1,0:T(8,128)(2,1)}, bf16[4,512,512]{2,1,0:T(8,128)(2,1)}, u32[]{:S(2)}, u32[]{:S(2)}) collective-permute-start(bf16[4,512,512]{2,1,0:T(8,128)(2,1)} %add_convert_fusion.2), channel_id=1, source_target_pairs={{0,32},{1,33},{32,0},{33,1},{64,96},{65,97},{96,64},{97,65},{2,34}... | collective-permute-start | bytes 6291464 | tf_op jit(solution)/shard_map/ppermute | solution.py:138
  469.4 16.0 %collective-permute-start.36 = (bf16[128,2048]{1,0:T(8,128)(2,1)S(1)}, bf16[128,2048]{1,0:T(8,128)(2,1)S(1)}, u32[]{:S(2)}, u32[]{:S(2)}) collective-permute-start(bf16[128,2048]{1,0:T(8,128)(2,1)S(1)} %get-tuple-element.89), channel_id=1, source_target_pairs={{0,16},{8,24},{16,0},{24,8},{1,17},{9,25},{17,1},{25,9},{2,18},{10... | collective-permute-start | bytes 1572872 | tf_op jit(solution)/shard_map/ppermute | solution.py:73
  485.5 22.0 %collective-permute-start.37 = (bf16[128,2048]{1,0:T(8,128)(2,1)S(1)}, bf16[128,2048]{1,0:T(8,128)(2,1)S(1)}, u32[]{:S(2)}, u32[]{:S(2)}) collective-permute-start(bf16[128,2048]{1,0:T(8,128)(2,1)S(1)} %get-tuple-element.91), channel_id=1, source_target_pairs={{0,8},{8,16},{16,24},{24,0},{1,9},{9,17},{17,25},{25,1},{2,10},{10... | collective-permute-start | bytes 1572872 | tf_op jit(solution)/shard_map/ppermute | solution.py:73
  507.4 12.9 %collective-permute-start.38 = (bf16[128,2048]{1,0:T(8,128)(2,1)S(1)}, bf16[128,2048]{1,0:T(8,128)(2,1)S(1)}, u32[]{:S(2)}, u32[]{:S(2)}) collective-permute-start(bf16[128,2048]{1,0:T(8,128)(2,1)S(1)} %get-tuple-element.90), channel_id=1, source_target_pairs={{0,24},{8,0},{16,8},{24,16},{1,25},{9,1},{17,9},{25,17},{2,26},{10... | collective-permute-start | bytes 1572872 | tf_op jit(solution)/shard_map/ppermute | solution.py:73
  530.4 13.3 %collective-permute-start.44 = (bf16[512,512]{1,0:T(8,128)(2,1)S(1)}, bf16[512,512]{1,0:T(8,128)(2,1)S(1)}, u32[]{:S(2)}, u32[]{:S(2)}) collective-permute-start(bf16[512,512]{1,0:T(8,128)(2,1)S(1)} %get-tuple-element.86), channel_id=1, source_target_pairs={{0,16},{8,24},{16,0},{24,8},{1,17},{9,25},{17,1},{25,9},{2,18},{10... | collective-permute-start | bytes 1572872 | tf_op jit(solution)/shard_map/ppermute | solution.py:73
  531.6 25.5 %collective-permute-start.45 = (bf16[512,512]{1,0:T(8,128)(2,1)S(1)}, bf16[512,512]{1,0:T(8,128)(2,1)S(1)}, u32[]{:S(2)}, u32[]{:S(2)}) collective-permute-start(bf16[512,512]{1,0:T(8,128)(2,1)S(1)} %get-tuple-element.88), channel_id=1, source_target_pairs={{0,8},{8,16},{16,24},{24,0},{1,9},{9,17},{17,25},{25,1},{2,10},{10... | collective-permute-start | bytes 1572872 | tf_op jit(solution)/shard_map/ppermute | solution.py:73
  533.3 23.8 %collective-permute-start.46 = (bf16[512,512]{1,0:T(8,128)(2,1)S(1)}, bf16[512,512]{1,0:T(8,128)(2,1)S(1)}, u32[]{:S(2)}, u32[]{:S(2)}) collective-permute-start(bf16[512,512]{1,0:T(8,128)(2,1)S(1)} %get-tuple-element.87), channel_id=1, source_target_pairs={{0,24},{8,0},{16,8},{24,16},{1,25},{9,1},{17,9},{25,17},{2,26},{10... | collective-permute-start | bytes 1572872 | tf_op jit(solution)/shard_map/ppermute | solution.py:73
  595.3 7.4 %collective-permute-start.47 = (bf16[128,384]{0,1:T(8,128)(2,1)}, bf16[128,384]{0,1:T(8,128)(2,1)}, u32[]{:S(2)}, u32[]{:S(2)}) collective-permute-start(bf16[128,384]{0,1:T(8,128)(2,1)} %get-tuple-element.123), channel_id=1, source_target_pairs={{0,4},{2,6},{4,0},{6,2},{1,5},{3,7},{5,1},{7,3},{8,12},{10,14},{12... | collective-permute-start | bytes 294920 | tf_op jit(solution)/shard_map/ppermute | solution.py:73
  613.5 11.7 %collective-permute-start.53 = (bf16[16,80,128]{2,1,0:T(8,128)(2,1)S(1)}, bf16[16,80,128]{2,1,0:T(8,128)(2,1)S(1)}, u32[]{:S(2)}, u32[]{:S(2)}) collective-permute-start(bf16[16,80,128]{2,1,0:T(8,128)(2,1)S(1)} %fusion.42), channel_id=1, source_target_pairs={{0,1},{1,0},{2,3},{3,2},{4,5},{5,4},{6,7},{7,6},{8,9},{9,8},{10,11... | collective-permute-start | bytes 983048 | tf_op jit(solution)/shard_map/ppermute | solution.py:69
  624.6 81.3 %collective-permute-start.39 = (bf16[64,2048]{1,0:T(8,128)(2,1)}, bf16[64,2048]{1,0:T(8,128)(2,1)}, u32[]{:S(2)}, u32[]{:S(2)}) collective-permute-start(bf16[64,2048]{1,0:T(8,128)(2,1)} %get-tuple-element.107), channel_id=1, source_target_pairs={{0,1},{1,0},{2,3},{3,2},{4,5},{5,4},{6,7},{7,6},{8,9},{9,8},{10,11... | collective-permute-start | bytes 786440 | tf_op jit(solution)/shard_map/ppermute | solution.py:69
  625.3 7.9 %collective-permute-start.54 = (bf16[4,80,128]{2,1,0:T(8,128)(2,1)S(1)}, bf16[4,80,128]{2,1,0:T(8,128)(2,1)S(1)}, u32[]{:S(2)}, u32[]{:S(2)}) collective-permute-start(bf16[4,80,128]{2,1,0:T(8,128)(2,1)S(1)} %get-tuple-element.99), channel_id=1, source_target_pairs={{0,32},{32,64},{64,96},{96,0},{1,33},{33,65},{65,97},{97,1},{2,34}... | collective-permute-start | bytes 245768 | tf_op jit(solution)/shard_map/ppermute | solution.py:73
  625.4 7.8 %collective-permute-start.55 = (bf16[4,80,128]{2,1,0:T(8,128)(2,1)S(1)}, bf16[4,80,128]{2,1,0:T(8,128)(2,1)S(1)}, u32[]{:S(2)}, u32[]{:S(2)}) collective-permute-start(bf16[4,80,128]{2,1,0:T(8,128)(2,1)S(1)} %get-tuple-element.101), channel_id=1, source_target_pairs={{0,64},{32,96},{64,0},{96,32},{1,65},{33,97},{65,1},{97,33},{2,66}... | collective-permute-start | bytes 245768 | tf_op jit(solution)/shard_map/ppermute | solution.py:73
  633.3 6.5 collective-permute-start.57
  641.9 29.3 %collective-permute-start.66 = (bf16[128,2048]{1,0:T(8,128)(2,1)S(1)}, bf16[128,2048]{1,0:T(8,128)(2,1)S(1)}, u32[]{:S(2)}, u32[]{:S(2)}) collective-permute-start(bf16[128,2048]{1,0:T(8,128)(2,1)S(1)} %get-tuple-element.83), channel_id=1, source_target_pairs={{0,4},{2,6},{4,0},{6,2},{1,5},{3,7},{5,1},{7,3},{8,12},{10,14},{12... | collective-permute-start | bytes 1572872 | tf_op jit(solution)/shard_map/ppermute | solution.py:73
  642.0 31.8 %collective-permute-start.67 = (bf16[128,2048]{1,0:T(8,128)(2,1)S(1)}, bf16[128,2048]{1,0:T(8,128)(2,1)S(1)}, u32[]{:S(2)}, u32[]{:S(2)}) collective-permute-start(bf16[128,2048]{1,0:T(8,128)(2,1)S(1)} %get-tuple-element.85), channel_id=1, source_target_pairs={{0,2},{2,4},{4,6},{6,0},{1,3},{3,5},{5,7},{7,1},{8,10},{10,12},{12... | collective-permute-start | bytes 1572872 | tf_op jit(solution)/shard_map/ppermute | solution.py:73
  642.2 31.7 %collective-permute-start.68 = (bf16[128,2048]{1,0:T(8,128)(2,1)S(1)}, bf16[128,2048]{1,0:T(8,128)(2,1)S(1)}, u32[]{:S(2)}, u32[]{:S(2)}) collective-permute-start(bf16[128,2048]{1,0:T(8,128)(2,1)S(1)} %get-tuple-element.84), channel_id=1, source_target_pairs={{0,6},{2,0},{4,2},{6,4},{1,7},{3,1},{5,3},{7,5},{8,14},{10,8},{12,... | collective-permute-start | bytes 1572872 | tf_op jit(solution)/shard_map/ppermute | solution.py:73
  668.9 25.1 %collective-permute-start.73 = (bf16[4,4,80,128]{3,2,1,0:T(8,128)(2,1)}, bf16[4,4,80,128]{3,2,1,0:T(8,128)(2,1)}, u32[]{:S(2)}, u32[]{:S(2)}) collective-permute-start(bf16[4,4,80,128]{3,2,1,0:T(8,128)(2,1)} %bitcast_dynamic-update-slice_fusion.15), channel_id=1, source_target_pairs={{0,6},{2,0},{4,2},{6,4},{1,7},{3,1},{5,3},{7,5},{8,14},{10,8},{12,... | collective-permute-start | bytes 983048 | tf_op jit(solution)/shard_map/ppermute | solution.py:73
  671.3 23.7 %collective-permute-start.74 = (bf16[4,4,80,128]{3,2,1,0:T(8,128)(2,1)}, bf16[4,4,80,128]{3,2,1,0:T(8,128)(2,1)}, u32[]{:S(2)}, u32[]{:S(2)}) collective-permute-start(bf16[4,4,80,128]{3,2,1,0:T(8,128)(2,1)} %bitcast_dynamic-update-slice_fusion.15), channel_id=1, source_target_pairs={{0,4},{2,6},{4,0},{6,2},{1,5},{3,7},{5,1},{7,3},{8,12},{10,14},{12... | collective-permute-start | bytes 983048 | tf_op jit(solution)/shard_map/ppermute | solution.py:73
  673.8 22.2 %collective-permute-start.75 = (bf16[4,4,80,128]{3,2,1,0:T(8,128)(2,1)}, bf16[4,4,80,128]{3,2,1,0:T(8,128)(2,1)}, u32[]{:S(2)}, u32[]{:S(2)}) collective-permute-start(bf16[4,4,80,128]{3,2,1,0:T(8,128)(2,1)} %bitcast_dynamic-update-slice_fusion.15), channel_id=1, source_target_pairs={{0,2},{2,4},{4,6},{6,0},{1,3},{3,5},{5,7},{7,1},{8,10},{10,12},{12... | collective-permute-start | bytes 983048 | tf_op jit(solution)/shard_map/ppermute | solution.py:73
  697.1 11.9 %collective-permute-start.76 = (bf16[4,16,80,128]{3,2,1,0:T(8,128)(2,1)S(1)}, bf16[4,16,80,128]{3,2,1,0:T(8,128)(2,1)S(1)}, u32[]{:S(2)}, u32[]{:S(2)}) collective-permute-start(bf16[4,16,80,128]{3,2,1,0:T(8,128)(2,1)S(1)} %bitcast.277), channel_id=1, source_target_pairs={{0,1},{1,0},{2,3},{3,2},{4,5},{5,4},{6,7},{7,6},{8,9},{9,8},{10,11... | collective-permute-start | bytes 3932168 | tf_op jit(solution)/shard_map/ppermute | solution.py:69
  (101 other events, 1522.3 us)
Sparse Core Ops, SparseCore 0:
  11.1 102.6 all-gather.3
  235.5 96.1 all-gather.5
  385.5 78.2 reduce-scatter.2
  467.9 104.0 reduce-scatter.4
  580.3 90.7 all-gather.7

commit v7 on v6

--- a/solution.py
+++ b/solution.py
@@ -470,16 +470,16 @@
 def unpack_early(everyone):
     return pl.pallas_call(
         early_kernel,
-        grid=(16,),
-        in_specs=[pl.BlockSpec((8, sum(EARLY), 128), lambda i: (i, 0, 0))],
+        grid=(8,),
+        in_specs=[pl.BlockSpec((16, sum(EARLY), 128), lambda i: (i, 0, 0))],
         out_specs=[
-            pl.BlockSpec((128, 512), lambda i: (0, i)),
-            pl.BlockSpec((128, 512), lambda i: (0, i)),
-            pl.BlockSpec((512, 128), lambda i: (i, 0)),
-            pl.BlockSpec((128, 128), lambda i: (i, 0)),
-            pl.BlockSpec((128, 128), lambda i: (0, i)),
-            pl.BlockSpec((128, 128), lambda i: (0, i)),
-            pl.BlockSpec((128, 256), lambda i: (i, 0)),
+            pl.BlockSpec((128, 1024), lambda i: (0, i)),
+            pl.BlockSpec((128, 1024), lambda i: (0, i)),
+            pl.BlockSpec((1024, 128), lambda i: (i, 0)),
+            pl.BlockSpec((256, 128), lambda i: (i, 0)),
+            pl.BlockSpec((128, 256), lambda i: (0, i)),
+            pl.BlockSpec((128, 256), lambda i: (0, i)),
+            pl.BlockSpec((256, 256), lambda i: (i, 0)),
         ],
         out_shape=[
             jax.ShapeDtypeStruct(shape, f32)
@@ -504,18 +504,18 @@
 
 
 def unpack_late(core, mine, other):
-    half = pl.BlockSpec((1, 8, sum(LATE), 128), lambda i, core: (i // 2, i % 2, 0, 0))
+    half = pl.BlockSpec((1, 16, sum(LATE), 128), lambda i, core: (i, 0, 0, 0))
     return pl.pallas_call(
         late_kernel,
         grid_spec=pltpu.PrefetchScalarGridSpec(
             num_scalar_prefetch=1,
-            grid=(8,),
+            grid=(4,),
             in_specs=[half, half],
             out_specs=[
+                pl.BlockSpec((128, 512), lambda i, core: (0, i)),
                 pl.BlockSpec((128, 256), lambda i, core: (0, i)),
-                pl.BlockSpec((128, 128), lambda i, core: (0, i)),
-                pl.BlockSpec((128, 128), lambda i, core: (0, i)),
-                pl.BlockSpec((256, 384), lambda i, core: (i, 0)),
+                pl.BlockSpec((128, 256), lambda i, core: (0, i)),
+                pl.BlockSpec((512, 384), lambda i, core: (i, 0)),
             ],
         ),
         out_shape=[

time: 736 us -> 722 us (0.981)
  waiting for transfers between devices: 290 us -> 279 us
    ppermute x60, starting transfers between devices: 87.9 us -> 96.4 us  [shift(): lax.ppermute(value, RING[ring], [(i, (i + step) % 4) for i in range(4)])]
  transfers between devices with their start and end apart: 84 -> 84, of which waited for: 40 -> 43; matrix products, arithmetic and copies ran while one was open for 21% -> 21% of each run, Pallas kernels for 6% -> 6%
where the time goes in v7:
time: 722 us; the launch traced here: 715 us
  waiting for transfers between devices  279 us (39%)
  starting transfers between devices  147 us (20%)
  Pallas kernels  96.6 us (13%)
  local copies, waits for them, and re-layouts  76 us (11%)
  matrix products  49.9 us (7%)
  other arithmetic  42 us (6%)
  between operations  24 us (3%)
    ppermute x60, waiting for transfers between devices, shift(): lax.ppermute(value, RING[ring], [(i, (i + step) % 4) for i in range(4)])  216 us
    ppermute x60, starting transfers between devices, shift(): lax.ppermute(value, RING[ring], [(i, (i + step) % 4) for i in range(4)])  96.4 us
    pallas_call x1, Pallas kernels, feed_forward(): pl.pallas_call(ffn_kernel, grid_spec=pltpu.PrefetchScalarGridSpec(num_sca...  45.6 us
    dot_general x11, matrix products, product(): return jnp.dot(left, right, preferred_element_type=f32)  25.6 us
    ppermute x7, starting transfers between devices, swap_cores(): return lax.ppermute(value, 'c', [(0, 1), (1, 0)])  20.9 us
    ppermute x2, waiting for transfers between devices, gather_row(): ahead = [lax.ppermute(line, CORNER, pairs) for pairs in LATER]  20 us
    pallas_call x1, Pallas kernels, attend_back(): pl.pallas_call(attend_back_kernel, grid_spec=pltpu.PrefetchScalarGridSpec...  19.9 us
    ppermute x1, waiting for transfers between devices, gather_row(): partner = lax.ppermute(line, CORNER, PARTNER)  18.2 us
  transfers between devices with their start and end apart: 84, of which 43 were waited for; matrix products, arithmetic and copies ran while one was open for 21% of the time, Pallas kernels for 6%

profile of v7, /device:TPU:1, one launch (start us, length us, event | category | flops | bytes accessed | tf_op | source)
XLA Modules:
  0.0 714.9 jit_solution(15466383562806253538)
XLA Ops:
  12.7 5.0 all-to-all-start
  31.1 6.1 collective-permute-done.5
  37.9 3.5 collective-permute-done.6
  42.5 11.6 %collective-permute-done.7 = bf16[128,2048]{1,0:T(8,128)(2,1)S(1)} collective-permute-done((bf16[128,2048]{1,0:T(8,128)(2,1)S(1)}, bf16[128,2048]{1,0:T(8,128)(2,1)S(1)}, u32[]{:S(2)}, u32[]{:S(2)}) %collective-permute-start.7) | collective-permute-done | bytes 524320 | tf_op jit(solution)/shard_map/ppermute | solution.py:73
  54.4 5.9 collective-permute-start.9
  63.2 2.6 collective-permute-done.10
  65.8 7.4 %collective-permute-start.11 = (bf16[4,128,512]{2,1,0:T(8,128)(2,1)S(1)}, bf16[4,128,512]{2,1,0:T(8,128)(2,1)S(1)}, u32[]{:S(2)}, u32[]{:S(2)}) collective-permute-start(bf16[4,128,512]{2,1,0:T(8,128)(2,1)S(1)} %bitcast_dynamic-update-slice_fusion.11), channel_id=1, source_target_pairs={{0,96},{32,0},{64,32},{96,64},{1,97},{33,1},{65,33},{97,65},{2,98}... | collective-permute-start | bytes 1572872 | tf_op jit(solution)/shard_map/ppermute | solution.py:73
  76.4 4.4 collective-permute-done.11
  81.6 3.2 collective-permute-done.12
  85.6 25.4 %collective-permute-done.13 = bf16[4,128,512]{2,1,0:T(8,128)(2,1)S(1)} collective-permute-done((bf16[4,128,512]{2,1,0:T(8,128)(2,1)S(1)}, bf16[4,128,512]{2,1,0:T(8,128)(2,1)S(1)}, u32[]{:S(2)}, u32[]{:S(2)}) %collective-permute-start.13) | collective-permute-done | bytes 524320 | tf_op jit(solution)/shard_map/ppermute | solution.py:73
  115.7 3.1 fusion.2
  119.9 2.9 fusion.147
  122.8 4.2 broadcast_select_fusion
  130.1 12.0 %collective-permute-done.15 = bf16[512,512]{1,0:T(8,128)(2,1)S(1)} collective-permute-done((bf16[512,512]{1,0:T(8,128)(2,1)S(1)}, bf16[512,512]{1,0:T(8,128)(2,1)S(1)}, u32[]{:S(2)}, u32[]{:S(2)}) %collective-permute-start.15) | collective-permute-done | bytes 524320 | tf_op jit(solution)/shard_map/ppermute | solution.py:73
  143.5 11.9 %collective-permute-done.17 = bf16[512,512]{1,0:T(8,128)(2,1)S(1)} collective-permute-done((bf16[512,512]{1,0:T(8,128)(2,1)S(1)}, bf16[512,512]{1,0:T(8,128)(2,1)S(1)}, u32[]{:S(2)}, u32[]{:S(2)}) %collective-permute-start.17) | collective-permute-done | bytes 524320 | tf_op jit(solution)/shard_map/ppermute | solution.py:73
  156.9 6.1 collective-permute-start.19
  163.0 2.7 collective-permute-start.20
  179.2 6.5 all-to-all-start.1
  185.7 18.2 %collective-permute-done.18.refs_1_ = bf16[4,512,512]{2,1,0:T(8,128)(2,1)} collective-permute-done((bf16[4,512,512]{2,1,0:T(8,128)(2,1)}, bf16[4,512,512]{2,1,0:T(8,128)(2,1)}, u32[]{:S(2)}, u32[]{:S(2)}) %collective-permute-start.18) | collective-permute-done | bytes 2097184 | tf_op jit(solution)/shard_map/ppermute | solution.py:129
  205.2 20.0 %collective-permute-done.19.refs_2_ = bf16[4,512,512]{2,1,0:T(8,128)(2,1)} collective-permute-done((bf16[4,512,512]{2,1,0:T(8,128)(2,1)}, bf16[4,512,512]{2,1,0:T(8,128)(2,1)}, u32[]{:S(2)}, u32[]{:S(2)}) %collective-permute-start.19) | collective-permute-done | bytes 2097184 | tf_op jit(solution)/shard_map/ppermute | solution.py:128
  243.7 2.8 reshape.658
  250.3 14.9 %attend.1 = (f32[512,512]{1,0:T(8,128)S(1)}, f32[2,512,1]{2,1,0:T(8,128)S(1)}) custom-call(s32[64]{0:T(128)S(1)} %pad_add_fusion.2.active, bf16[512,512]{1,0:T(8,128)(2,1)S(1)} %fusion.23.q_ref, s32[512,1]{1,0:T(8,128)S(1)} %copy.137.pos_ref, s32[512,1]{1,0:T(8,128)S(1)} %copy.138.start_ref, s32[16,1,512]{2,1,0:T(1,128)S(1)} %reshape.659.kpos_ref, ...), custom_call_target="tpu_custom_call" | custom-call | flops 6442450944 | bytes 10485760 | tf_op jit(solution)/shard_map/attend/pallas_call | solution.py:284
  282.1 5.5 multiply_reduce_fusion.1
  293.3 9.2 %collective-permute-done.26 = bf16[128,2048]{1,0:T(8,128)(2,1)S(1)} collective-permute-done((bf16[128,2048]{1,0:T(8,128)(2,1)S(1)}, bf16[128,2048]{1,0:T(8,128)(2,1)S(1)}, u32[]{:S(2)}, u32[]{:S(2)}) %collective-permute-start.26) | collective-permute-done | bytes 524320 | tf_op jit(solution)/shard_map/ppermute | solution.py:73
  304.0 11.3 %collective-permute-done.28 = bf16[128,2048]{1,0:T(8,128)(2,1)S(1)} collective-permute-done((bf16[128,2048]{1,0:T(8,128)(2,1)S(1)}, bf16[128,2048]{1,0:T(8,128)(2,1)S(1)}, u32[]{:S(2)}, u32[]{:S(2)}) %collective-permute-start.28) | collective-permute-done | bytes 524320 | tf_op jit(solution)/shard_map/ppermute | solution.py:73
  318.6 12.8 %all-gather.6.cloned.1.call-done = bf16[32,192,2048]{2,1,0:T(8,128)(2,1)} async-done(((bf16[1,192,2048]{2,1,0:T(8,128)(2,1)}), bf16[32,192,2048]{2,1,0:T(8,128)(2,1)}) %all-gather.6.cloned.1.call-update) | async-done | bytes 25165840 | tf_op jit(solution)/shard_map/all_gather | solution.py:648
  331.4 45.6 %feed_forward.1 = (bf16[512,2048]{1,0:T(8,128)(2,1)}, bf16[512,2432]{1,0:T(8,128)(2,1)}, f32[4,4,2,192,128]{4,3,2,1,0:T(8,128)}) custom-call(s32[1]{0:T(128)} %bitcast.36.at, bf16[512,2048]{1,0:T(8,128)(2,1)} %pad_maximum_fusion.1.nm_ref, bf16[512,2048]{1,0:T(8,128)(2,1)} %copy-done.59, bf16[512,256]{1,0:T(8,128)(2,1)} %fusion.3.lgu_ref, ...), custom_call_target="tpu_custom_call" | custom-call | flops 30064771072 | bytes 41943040 | tf_op jit(solution)/shard_map/feed_forward/pallas_call | solution.py:403
  377.0 2.7 fusion.137
  379.7 2.7 collective-permute-start.29
  385.3 11.6 %collective-permute-done.29 = bf16[128,2432]{1,0:T(8,128)(2,1)} collective-permute-done((bf16[128,2432]{1,0:T(8,128)(2,1)}, bf16[128,2432]{1,0:T(8,128)(2,1)}, u32[]{:S(2)}, u32[]{:S(2)}) %collective-permute-start.29) | collective-permute-done | bytes 622624 | tf_op jit(solution)/shard_map/ppermute | solution.py:73
  396.9 13.9 %collective-permute-done.30 = bf16[128,2432]{1,0:T(8,128)(2,1)} collective-permute-done((bf16[128,2432]{1,0:T(8,128)(2,1)}, bf16[128,2432]{1,0:T(8,128)(2,1)}, u32[]{:S(2)}, u32[]{:S(2)}) %collective-permute-start.30) | collective-permute-done | bytes 622624 | tf_op jit(solution)/shard_map/ppermute | solution.py:73
  415.9 2.9 fusion.128
  419.2 2.5 collective-permute-start.32
  425.5 2.9 copy.147
  428.5 2.9 collective-permute-done.34
  434.6 19.9 %attend_back.1 = (f32[512,512]{1,0:T(8,128)S(1)}, bf16[4,512,512]{2,1,0:T(8,128)(2,1)}, bf16[4,512,512]{2,1,0:T(8,128)(2,1)}, bf16[4,512,512]{2,1,0:T(8,128)(2,1)}, bf16[4,512,512]{2,1,0:T(8,128)(2,1)}) custom-call(s32[64]{0:T(128)S(1)} %pad_add_fusion.2.active, bf16[512,512]{1,0:T(8,128)(2,1)S(1)} %fusion.23.q_ref, s32[512,1]{1,0:T(8,128)S(1)} %copy-done.4, ...), custom_call_target="tpu_custom_call" | custom-call | flops 12884901888 | bytes 20971520 | tf_op jit(solution)/shard_map/attend_back/pallas_call | solution.py:309
  456.0 2.7 collective-permute-start.40
  461.2 3.6 add_convert_fusion.2
  467.1 3.4 collective-permute-start.36
  470.4 11.6 %collective-permute-done.36 = bf16[128,2048]{1,0:T(8,128)(2,1)S(1)} collective-permute-done((bf16[128,2048]{1,0:T(8,128)(2,1)S(1)}, bf16[128,2048]{1,0:T(8,128)(2,1)S(1)}, u32[]{:S(2)}, u32[]{:S(2)}) %collective-permute-start.36) | collective-permute-done | bytes 524320 | tf_op jit(solution)/shard_map/ppermute | solution.py:73
  482.0 3.0 collective-permute-start.37
  485.0 11.6 %collective-permute-done.37 = bf16[128,2048]{1,0:T(8,128)(2,1)S(1)} collective-permute-done((bf16[128,2048]{1,0:T(8,128)(2,1)S(1)}, bf16[128,2048]{1,0:T(8,128)(2,1)S(1)}, u32[]{:S(2)}, u32[]{:S(2)}) %collective-permute-start.37) | collective-permute-done | bytes 524320 | tf_op jit(solution)/shard_map/ppermute | solution.py:73
  498.3 12.2 %collective-permute-done.38 = bf16[128,2048]{1,0:T(8,128)(2,1)S(1)} collective-permute-done((bf16[128,2048]{1,0:T(8,128)(2,1)S(1)}, bf16[128,2048]{1,0:T(8,128)(2,1)S(1)}, u32[]{:S(2)}, u32[]{:S(2)}) %collective-permute-start.38) | collective-permute-done | bytes 524320 | tf_op jit(solution)/shard_map/ppermute | solution.py:73
  514.8 6.1 add_convert_fusion.1
  521.0 3.0 collective-permute-start.44
  524.0 2.7 collective-permute-start.46
  526.7 8.6 %collective-permute-done.44 = bf16[512,512]{1,0:T(8,128)(2,1)S(1)} collective-permute-done((bf16[512,512]{1,0:T(8,128)(2,1)S(1)}, bf16[512,512]{1,0:T(8,128)(2,1)S(1)}, u32[]{:S(2)}, u32[]{:S(2)}) %collective-permute-start.44) | collective-permute-done | bytes 524320 | tf_op jit(solution)/shard_map/ppermute | solution.py:73
  535.3 12.3 %collective-permute-done.45 = bf16[512,512]{1,0:T(8,128)(2,1)S(1)} collective-permute-done((bf16[512,512]{1,0:T(8,128)(2,1)S(1)}, bf16[512,512]{1,0:T(8,128)(2,1)S(1)}, u32[]{:S(2)}, u32[]{:S(2)}) %collective-permute-start.45) | collective-permute-done | bytes 524320 | tf_op jit(solution)/shard_map/ppermute | solution.py:73
  549.9 8.8 %reduce-scatter.5.cloned.1.call-done = f32[1,320,128]{2,1,0:T(8,128)} async-done(((f32[32,320,128]{2,1,0:T(8,128)}), f32[1,320,128]{2,1,0:T(8,128)}) %reduce-scatter.5.cloned.1.call-update) | async-done | bytes 163856 | tf_op jit(solution)/shard_map/reduce_scatter | solution.py:762
  568.8 2.8 reshape.669
  600.0 10.1 %collective-permute-start.53 = (bf16[16,80,128]{2,1,0:T(8,128)(2,1)S(1)}, bf16[16,80,128]{2,1,0:T(8,128)(2,1)S(1)}, u32[]{:S(2)}, u32[]{:S(2)}) collective-permute-start(bf16[16,80,128]{2,1,0:T(8,128)(2,1)S(1)} %fusion.42), channel_id=1, source_target_pairs={{0,1},{1,0},{2,3},{3,2},{4,5},{5,4},{6,7},{7,6},{8,9},{9,8},{10,11... | collective-permute-start | bytes 983048 | tf_op jit(solution)/shard_map/ppermute | solution.py:69
  611.7 15.0 %collective-permute-start.55 = (bf16[4,80,128]{2,1,0:T(8,128)(2,1)S(1)}, bf16[4,80,128]{2,1,0:T(8,128)(2,1)S(1)}, u32[]{:S(2)}, u32[]{:S(2)}) collective-permute-start(bf16[4,80,128]{2,1,0:T(8,128)(2,1)S(1)} %get-tuple-element.101), channel_id=1, source_target_pairs={{0,64},{32,96},{64,0},{96,32},{1,65},{33,97},{65,1},{97,33},{2,66}... | collective-permute-start | bytes 245768 | tf_op jit(solution)/shard_map/ppermute | solution.py:73
  626.7 2.9 fusion.30
  633.7 2.9 add_convert_fusion
  639.4 2.6 collective-permute-start.68
  643.5 3.2 collective-permute-done.61
  647.7 3.3 collective-permute-done.62
  651.0 2.7 collective-permute-start.63
  657.8 2.5 collective-permute-done.64
  662.7 3.4 collective-permute-done.65
  668.9 2.6 collective-permute-done.67
  673.3 11.4 %unpack_early.1 = (f32[128,8192]{1,0:T(8,128)}, f32[128,8192]{1,0:T(8,128)}, f32[8192,128]{1,0:T(8,128)}, f32[2048,128]{1,0:T(8,128)}, f32[128,2048]{1,0:T(8,128...) custom-call(bf16[128,272,128]{2,1,0:T(8,128)(2,1)} %all-gather.8.cloned.1.call-done.all_ref), custom_call_target="tpu_custom_call" | custom-call | flops 1048576 | bytes 28311552 | tf_op jit(solution)/shard_map/unpack_early/pallas_call | solution.py:471
  691.1 7.2 %collective-permute-start.76 = (bf16[4,16,80,128]{3,2,1,0:T(8,128)(2,1)S(1)}, bf16[4,16,80,128]{3,2,1,0:T(8,128)(2,1)S(1)}, u32[]{:S(2)}, u32[]{:S(2)}) collective-permute-start(bf16[4,16,80,128]{3,2,1,0:T(8,128)(2,1)S(1)} %bitcast.277), channel_id=1, source_target_pairs={{0,1},{1,0},{2,3},{3,2},{4,5},{5,4},{6,7},{7,6},{8,9},{9,8},{10,11... | collective-permute-start | bytes 3932168 | tf_op jit(solution)/shard_map/ppermute | solution.py:69
  703.3 4.8 unpack_late.1
  (513 shorter events, 197.1 us)
Async XLA Ops:
  7.2 224.1 %all-gather.4.cloned.1.call-start = ((), (), s32[]{:S(2)}) async-start(), calls=%async_computation.4 | async-start | bytes 8454144 | tf_op jit(solution)/shard_map/all_gather | solution.py:627
  9.1 9.4 %collective-permute-start = (bf16[64,2048]{1,0:T(8,128)(2,1)S(1)}, bf16[64,2048]{1,0:T(8,128)(2,1)S(1)}, u32[]{:S(2)}, u32[]{:S(2)}) collective-permute-start(bf16[64,2048]{1,0:T(8,128)(2,1)S(1)} %get-tuple-element.122), channel_id=1, source_target_pairs={{0,1},{1,0},{2,3},{3,2},{4,5},{5,4},{6,7},{7,6},{8,9},{9,8},{10,11... | collective-permute-start | bytes 786440 | tf_op jit(solution)/shard_map/ppermute | solution.py:69
  11.6 7.8 %collective-permute-start.1 = (bf16[64,2048]{1,0:T(8,128)(2,1)S(1)}, bf16[64,2048]{1,0:T(8,128)(2,1)}, u32[]{:S(2)}, u32[]{:S(2)}) collective-permute-start(bf16[64,2048]{1,0:T(8,128)(2,1)S(1)} %get-tuple-element.120), channel_id=1, source_target_pairs={{0,1},{1,0},{2,3},{3,2},{4,5},{5,4},{6,7},{7,6},{8,9},{9,8},{10,11... | collective-permute-start | bytes 786440 | tf_op jit(solution)/shard_map/ppermute | solution.py:69
  12.7 10.3 %all-to-all-start = ((bf16[8,16,512]{2,1,0:T(8,128)(2,1)}), bf16[8,16,512]{2,1,0:T(8,128)(2,1)S(1)}, u32[]{:S(2)}, u32[]{:S(2)}) async-start(bf16[8,16,512]{2,1,0:T(8,128)(2,1)} %bitcast.9), calls=%async_computation | async-start | bytes 262144 | tf_op jit(solution)/shard_map/all_to_all | solution.py:613
  23.0 14.2 %collective-permute-start.5 = (bf16[128,2048]{1,0:T(8,128)(2,1)S(1)}, bf16[128,2048]{1,0:T(8,128)(2,1)S(1)}, u32[]{:S(2)}, u32[]{:S(2)}) collective-permute-start(bf16[128,2048]{1,0:T(8,128)(2,1)S(1)} %pad_maximum_fusion.4), channel_id=1, source_target_pairs={{0,24},{8,0},{16,8},{24,16},{1,25},{9,1},{17,9},{25,17},{2,26},{10... | collective-permute-start | bytes 1572872 | tf_op jit(solution)/shard_map/ppermute | solution.py:73
  27.0 14.4 %collective-permute-start.6 = (bf16[128,2048]{1,0:T(8,128)(2,1)S(1)}, bf16[128,2048]{1,0:T(8,128)(2,1)}, u32[]{:S(2)}, u32[]{:S(2)}) collective-permute-start(bf16[128,2048]{1,0:T(8,128)(2,1)S(1)} %pad_maximum_fusion.4), channel_id=1, source_target_pairs={{0,16},{8,24},{16,0},{24,8},{1,17},{9,25},{17,1},{25,9},{2,18},{10... | collective-permute-start | bytes 1572872 | tf_op jit(solution)/shard_map/ppermute | solution.py:73
  28.2 25.9 %collective-permute-start.7 = (bf16[128,2048]{1,0:T(8,128)(2,1)S(1)}, bf16[128,2048]{1,0:T(8,128)(2,1)S(1)}, u32[]{:S(2)}, u32[]{:S(2)}) collective-permute-start(bf16[128,2048]{1,0:T(8,128)(2,1)S(1)} %pad_maximum_fusion.4), channel_id=1, source_target_pairs={{0,8},{8,16},{16,24},{24,0},{1,9},{9,17},{17,25},{25,1},{2,10},{10... | collective-permute-start | bytes 1572872 | tf_op jit(solution)/shard_map/ppermute | solution.py:73
  29.0 25.2 %collective-permute-start.2 = (bf16[128,2048]{1,0:T(8,128)(2,1)S(1)}, bf16[128,2048]{1,0:T(8,128)(2,1)S(1)}, u32[]{:S(2)}, u32[]{:S(2)}) collective-permute-start(bf16[128,2048]{1,0:T(8,128)(2,1)S(1)} %fusion.9), channel_id=1, source_target_pairs={{0,6},{2,0},{4,2},{6,4},{1,7},{3,1},{5,3},{7,5},{8,14},{10,8},{12,... | collective-permute-start | bytes 1572872 | tf_op jit(solution)/shard_map/ppermute | solution.py:73
  29.9 24.3 %collective-permute-start.3 = (bf16[128,2048]{1,0:T(8,128)(2,1)S(1)}, bf16[128,2048]{1,0:T(8,128)(2,1)S(1)}, u32[]{:S(2)}, u32[]{:S(2)}) collective-permute-start(bf16[128,2048]{1,0:T(8,128)(2,1)S(1)} %fusion.9), channel_id=1, source_target_pairs={{0,4},{2,6},{4,0},{6,2},{1,5},{3,7},{5,1},{7,3},{8,12},{10,14},{12... | collective-permute-start | bytes 1572872 | tf_op jit(solution)/shard_map/ppermute | solution.py:73
  37.2 17.1 %collective-permute-start.4 = (bf16[128,2048]{1,0:T(8,128)(2,1)S(1)}, bf16[128,2048]{1,0:T(8,128)(2,1)S(1)}, u32[]{:S(2)}, u32[]{:S(2)}) collective-permute-start(bf16[128,2048]{1,0:T(8,128)(2,1)S(1)} %fusion.9), channel_id=1, source_target_pairs={{0,2},{2,4},{4,6},{6,0},{1,3},{3,5},{5,7},{7,1},{8,10},{10,12},{12... | collective-permute-start | bytes 1572872 | tf_op jit(solution)/shard_map/ppermute | solution.py:73
  54.4 7.7 %collective-permute-start.8 = (bf16[128,512]{1,0:T(8,128)(2,1)S(1)}, bf16[128,512]{1,0:T(8,128)(2,1)S(1)}, u32[]{:S(2)}, u32[]{:S(2)}) collective-permute-start(bf16[128,512]{1,0:T(8,128)(2,1)S(1)} %bitcast.300), channel_id=1, source_target_pairs={{0,24},{8,0},{16,8},{24,16},{1,25},{9,1},{17,9},{25,17},{2,26},{10... | collective-permute-start | bytes 393224 | tf_op jit(solution)/shard_map/ppermute | solution.py:73
  54.4 8.8 %collective-permute-start.9 = (bf16[128,512]{1,0:T(8,128)(2,1)S(1)}, bf16[128,512]{1,0:T(8,128)(2,1)S(1)}, u32[]{:S(2)}, u32[]{:S(2)}) collective-permute-start(bf16[128,512]{1,0:T(8,128)(2,1)S(1)} %bitcast.301), channel_id=1, source_target_pairs={{0,16},{8,24},{16,0},{24,8},{1,17},{9,25},{17,1},{25,9},{2,18},{10... | collective-permute-start | bytes 393224 | tf_op jit(solution)/shard_map/ppermute | solution.py:73
  65.8 15.0 %collective-permute-start.11 = (bf16[4,128,512]{2,1,0:T(8,128)(2,1)S(1)}, bf16[4,128,512]{2,1,0:T(8,128)(2,1)S(1)}, u32[]{:S(2)}, u32[]{:S(2)}) collective-permute-start(bf16[4,128,512]{2,1,0:T(8,128)(2,1)S(1)} %bitcast_dynamic-update-slice_fusion.11), channel_id=1, source_target_pairs={{0,96},{32,0},{64,32},{96,64},{1,97},{33,1},{65,33},{97,65},{2,98}... | collective-permute-start | bytes 1572872 | tf_op jit(solution)/shard_map/ppermute | solution.py:73
  73.3 11.5 %collective-permute-start.12 = (bf16[4,128,512]{2,1,0:T(8,128)(2,1)S(1)}, bf16[4,128,512]{2,1,0:T(8,128)(2,1)S(1)}, u32[]{:S(2)}, u32[]{:S(2)}) collective-permute-start(bf16[4,128,512]{2,1,0:T(8,128)(2,1)S(1)} %bitcast_dynamic-update-slice_fusion.11), channel_id=1, source_target_pairs={{0,64},{32,96},{64,0},{96,32},{1,65},{33,97},{65,1},{97,33},{2,66}... | collective-permute-start | bytes 1572872 | tf_op jit(solution)/shard_map/ppermute | solution.py:73
  73.9 37.2 %collective-permute-start.13 = (bf16[4,128,512]{2,1,0:T(8,128)(2,1)S(1)}, bf16[4,128,512]{2,1,0:T(8,128)(2,1)S(1)}, u32[]{:S(2)}, u32[]{:S(2)}) collective-permute-start(bf16[4,128,512]{2,1,0:T(8,128)(2,1)S(1)} %bitcast_dynamic-update-slice_fusion.11), channel_id=1, source_target_pairs={{0,32},{32,64},{64,96},{96,0},{1,33},{33,65},{65,97},{97,1},{2,34}... | collective-permute-start | bytes 1572872 | tf_op jit(solution)/shard_map/ppermute | solution.py:73
  111.9 10.9 %collective-permute-start.14 = (bf16[2048,512]{1,0:T(8,128)(2,1)}, bf16[2048,512]{1,0:T(8,128)(2,1)}, u32[]{:S(2)}, u32[]{:S(2)}) collective-permute-start(bf16[2048,512]{1,0:T(8,128)(2,1)} %bitcast.19), channel_id=1, source_target_pairs={{0,1},{1,0},{2,3},{3,2},{4,5},{5,4},{6,7},{7,6},{8,9},{9,8},{10,11... | collective-permute-start | bytes 6291464 | tf_op jit(solution)/shard_map/ppermute | solution.py:69
  128.5 13.6 %collective-permute-start.15 = (bf16[512,512]{1,0:T(8,128)(2,1)S(1)}, bf16[512,512]{1,0:T(8,128)(2,1)S(1)}, u32[]{:S(2)}, u32[]{:S(2)}) collective-permute-start(bf16[512,512]{1,0:T(8,128)(2,1)S(1)} %get-tuple-element.116), channel_id=1, source_target_pairs={{0,24},{8,0},{16,8},{24,16},{1,25},{9,1},{17,9},{25,17},{2,26},{10... | collective-permute-start | bytes 1572872 | tf_op jit(solution)/shard_map/ppermute | solution.py:73
  128.7 14.7 %collective-permute-start.16 = (bf16[512,512]{1,0:T(8,128)(2,1)S(1)}, bf16[512,512]{1,0:T(8,128)(2,1)S(1)}, u32[]{:S(2)}, u32[]{:S(2)}) collective-permute-start(bf16[512,512]{1,0:T(8,128)(2,1)S(1)} %get-tuple-element.116), channel_id=1, source_target_pairs={{0,16},{8,24},{16,0},{24,8},{1,17},{9,25},{17,1},{25,9},{2,18},{10... | collective-permute-start | bytes 1572872 | tf_op jit(solution)/shard_map/ppermute | solution.py:73
  128.7 26.6 %collective-permute-start.17 = (bf16[512,512]{1,0:T(8,128)(2,1)S(1)}, bf16[512,512]{1,0:T(8,128)(2,1)S(1)}, u32[]{:S(2)}, u32[]{:S(2)}) collective-permute-start(bf16[512,512]{1,0:T(8,128)(2,1)S(1)} %get-tuple-element.116), channel_id=1, source_target_pairs={{0,8},{8,16},{16,24},{24,0},{1,9},{9,17},{17,25},{25,1},{2,10},{10... | collective-permute-start | bytes 1572872 | tf_op jit(solution)/shard_map/ppermute | solution.py:73
  156.9 47.0 %collective-permute-start.18 = (bf16[4,512,512]{2,1,0:T(8,128)(2,1)}, bf16[4,512,512]{2,1,0:T(8,128)(2,1)}, u32[]{:S(2)}, u32[]{:S(2)}) collective-permute-start(bf16[4,512,512]{2,1,0:T(8,128)(2,1)} %pad_maximum_fusion.refs_0_), channel_id=1, source_target_pairs={{0,32},{1,33},{32,0},{33,1},{64,96},{65,97},{96,64},{97,65},{2,34}... | collective-permute-start | bytes 6291464 | tf_op jit(solution)/shard_map/ppermute | solution.py:129
  156.9 68.2 %collective-permute-start.19 = (bf16[4,512,512]{2,1,0:T(8,128)(2,1)}, bf16[4,512,512]{2,1,0:T(8,128)(2,1)}, u32[]{:S(2)}, u32[]{:S(2)}) collective-permute-start(bf16[4,512,512]{2,1,0:T(8,128)(2,1)} %pad_maximum_fusion.refs_0_), channel_id=1, source_target_pairs={{1,64},{33,96},{3,66},{35,98},{5,68},{37,100},{7,70},{39,102},{9,7... | collective-permute-start | bytes 6291464 | tf_op jit(solution)/shard_map/ppermute | solution.py:128
  163.0 64.6 %collective-permute-start.20 = (bf16[4,512,512]{2,1,0:T(8,128)(2,1)}, bf16[4,512,512]{2,1,0:T(8,128)(2,1)}, u32[]{:S(2)}, u32[]{:S(2)}) collective-permute-start(bf16[4,512,512]{2,1,0:T(8,128)(2,1)} %pad_maximum_fusion.refs_0_), channel_id=1, source_target_pairs={{1,96},{33,64},{3,98},{35,66},{5,100},{37,68},{7,102},{39,70},{9,1... | collective-permute-start | bytes 6291464 | tf_op jit(solution)/shard_map/ppermute | solution.py:128
  165.7 63.8 %collective-permute-start.21 = (bf16[4,512,512]{2,1,0:T(8,128)(2,1)}, bf16[4,512,512]{2,1,0:T(8,128)(2,1)}, u32[]{:S(2)}, u32[]{:S(2)}) collective-permute-start(bf16[4,512,512]{2,1,0:T(8,128)(2,1)} %pad_maximum_fusion.refs_0_), channel_id=1, source_target_pairs={{0,1},{2,3},{4,5},{6,7},{8,9},{10,11},{12,13},{14,15},{16,17},{18,... | collective-permute-start | bytes 6291464 | tf_op jit(solution)/shard_map/ppermute | solution.py:130
  179.2 54.0 %all-to-all-start.1 = ((bf16[8,16,2048]{2,1,0:T(8,128)(2,1)}), bf16[8,16,2048]{2,1,0:T(8,128)(2,1)}, u32[]{:S(2)}, u32[]{:S(2)}) async-start(bf16[8,16,2048]{2,1,0:T(8,128)(2,1)} %maximum_add_fusion.1), calls=%async_computation.1 | async-start | bytes 1048576 | tf_op jit(solution)/shard_map/all_to_all | solution.py:645
  185.7 145.7 %all-gather.6.cloned.1.call-start = ((), (), s32[]{:S(2)}) async-start(), calls=%async_computation.5 | async-start | bytes 25952256 | tf_op jit(solution)/shard_map/all_gather | solution.py:648
  235.4 276.8 %reduce-scatter.3.cloned.1.call-start = ((), (), s32[]{:S(2)}) async-start(), calls=%async_computation.6 | async-start | bytes 3244032 | tf_op jit(solution)/shard_map/reduce_scatter | solution.py:711
  236.9 13.4 %collective-permute-start.22 = (bf16[4,512,512]{2,1,0:T(8,128)(2,1)}, bf16[4,512,512]{2,1,0:T(8,128)(2,1)}, u32[]{:S(2)}, u32[]{:S(2)}) collective-permute-start(bf16[4,512,512]{2,1,0:T(8,128)(2,1)} %collective-permute-done.18.refs_1_), channel_id=1, source_target_pairs={{0,1},{2,3},{4,5},{6,7},{8,9},{10,11},{12,13},{14,15},{16,17},{18,... | collective-permute-start | bytes 6291464 | tf_op jit(solution)/shard_map/ppermute | solution.py:130
  266.4 7.3 %collective-permute-start.23 = (bf16[128,512]{1,0:T(8,128)(2,1)S(1)}, bf16[128,512]{1,0:T(8,128)(2,1)S(1)}, u32[]{:S(2)}, u32[]{:S(2)}) collective-permute-start(bf16[128,512]{1,0:T(8,128)(2,1)S(1)} %get-tuple-element.114), channel_id=1, source_target_pairs={{0,2},{2,4},{4,6},{6,0},{1,3},{3,5},{5,7},{7,1},{8,10},{10,12},{12... | collective-permute-start | bytes 393224 | tf_op jit(solution)/shard_map/ppermute | solution.py:73
  268.8 7.0 collective-permute-start.24
  288.4 14.1 %collective-permute-start.26 = (bf16[128,2048]{1,0:T(8,128)(2,1)S(1)}, bf16[128,2048]{1,0:T(8,128)(2,1)S(1)}, u32[]{:S(2)}, u32[]{:S(2)}) collective-permute-start(bf16[128,2048]{1,0:T(8,128)(2,1)S(1)} %multiply_convert_fusion.1), channel_id=1, source_target_pairs={{0,24},{8,0},{16,8},{24,16},{1,25},{9,1},{17,9},{25,17},{2,26},{10... | collective-permute-start | bytes 1572872 | tf_op jit(solution)/shard_map/ppermute | solution.py:73
  288.5 15.6 %collective-permute-start.27 = (bf16[128,2048]{1,0:T(8,128)(2,1)S(1)}, bf16[128,2048]{1,0:T(8,128)(2,1)S(1)}, u32[]{:S(2)}, u32[]{:S(2)}) collective-permute-start(bf16[128,2048]{1,0:T(8,128)(2,1)S(1)} %multiply_convert_fusion.1), channel_id=1, source_target_pairs={{0,16},{8,24},{16,0},{24,8},{1,17},{9,25},{17,1},{25,9},{2,18},{10... | collective-permute-start | bytes 1572872 | tf_op jit(solution)/shard_map/ppermute | solution.py:73
  290.5 24.8 %collective-permute-start.28 = (bf16[128,2048]{1,0:T(8,128)(2,1)S(1)}, bf16[128,2048]{1,0:T(8,128)(2,1)S(1)}, u32[]{:S(2)}, u32[]{:S(2)}) collective-permute-start(bf16[128,2048]{1,0:T(8,128)(2,1)S(1)} %multiply_convert_fusion.1), channel_id=1, source_target_pairs={{0,8},{8,16},{16,24},{24,0},{1,9},{9,17},{17,25},{25,1},{2,10},{10... | collective-permute-start | bytes 1572872 | tf_op jit(solution)/shard_map/ppermute | solution.py:73
  379.7 17.2 %collective-permute-start.29 = (bf16[128,2432]{1,0:T(8,128)(2,1)}, bf16[128,2432]{1,0:T(8,128)(2,1)}, u32[]{:S(2)}, u32[]{:S(2)}) collective-permute-start(bf16[128,2432]{1,0:T(8,128)(2,1)} %get-tuple-element.80), channel_id=1, source_target_pairs={{0,16},{8,24},{16,0},{24,8},{1,17},{9,25},{17,1},{25,9},{2,18},{10... | collective-permute-start | bytes 1867784 | tf_op jit(solution)/shard_map/ppermute | solution.py:73
  382.4 28.4 %collective-permute-start.30 = (bf16[128,2432]{1,0:T(8,128)(2,1)}, bf16[128,2432]{1,0:T(8,128)(2,1)}, u32[]{:S(2)}, u32[]{:S(2)}) collective-permute-start(bf16[128,2432]{1,0:T(8,128)(2,1)} %get-tuple-element.82), channel_id=1, source_target_pairs={{0,8},{8,16},{16,24},{24,0},{1,9},{9,17},{17,25},{25,1},{2,10},{10... | collective-permute-start | bytes 1867784 | tf_op jit(solution)/shard_map/ppermute | solution.py:73
  382.7 28.1 %collective-permute-start.31 = (bf16[128,2432]{1,0:T(8,128)(2,1)}, bf16[128,2432]{1,0:T(8,128)(2,1)}, u32[]{:S(2)}, u32[]{:S(2)}) collective-permute-start(bf16[128,2432]{1,0:T(8,128)(2,1)} %get-tuple-element.81), channel_id=1, source_target_pairs={{0,24},{8,0},{16,8},{24,16},{1,25},{9,1},{17,9},{25,17},{2,26},{10... | collective-permute-start | bytes 1867784 | tf_op jit(solution)/shard_map/ppermute | solution.py:73
  385.1 173.7 %reduce-scatter.5.cloned.1.call-start = ((), (), s32[]{:S(2)}) async-start(), calls=%async_computation.7 | async-start | bytes 5406720 | tf_op jit(solution)/shard_map/reduce_scatter | solution.py:762
  419.2 9.3 %collective-permute-start.32 = (bf16[128,512]{1,0:T(8,128)(2,1)S(1)}, bf16[128,512]{1,0:T(8,128)(2,1)S(1)}, u32[]{:S(2)}, u32[]{:S(2)}) collective-permute-start(bf16[128,512]{1,0:T(8,128)(2,1)S(1)} %get-tuple-element.111), channel_id=1, source_target_pairs={{0,6},{2,0},{4,2},{6,4},{1,7},{3,1},{5,3},{7,5},{8,14},{10,8},{12,... | collective-permute-start | bytes 393224 | tf_op jit(solution)/shard_map/ppermute | solution.py:73
  421.7 6.8 collective-permute-start.33
  422.2 9.1 %collective-permute-start.34 = (bf16[128,512]{1,0:T(8,128)(2,1)S(1)}, bf16[128,512]{1,0:T(8,128)(2,1)S(1)}, u32[]{:S(2)}, u32[]{:S(2)}) collective-permute-start(bf16[128,512]{1,0:T(8,128)(2,1)S(1)} %get-tuple-element.109), channel_id=1, source_target_pairs={{0,2},{2,4},{4,6},{6,0},{1,3},{3,5},{5,7},{7,1},{8,10},{10,12},{12... | collective-permute-start | bytes 393224 | tf_op jit(solution)/shard_map/ppermute | solution.py:73
  428.4 244.9 %all-gather.8.cloned.1.call-start = ((), (), s32[]{:S(2)}) async-start(), calls=%async_computation.8 | async-start | bytes 8982528 | tf_op jit(solution)/shard_map/all_gather | solution.py:765
  454.6 6.7 collective-permute-start.35
  456.0 58.8 %collective-permute-start.40 = (bf16[4,512,512]{2,1,0:T(8,128)(2,1)}, bf16[4,512,512]{2,1,0:T(8,128)(2,1)}, u32[]{:S(2)}, u32[]{:S(2)}) collective-permute-start(bf16[4,512,512]{2,1,0:T(8,128)(2,1)} %get-tuple-element.50), channel_id=1, source_target_pairs={{1,0},{3,2},{5,4},{7,6},{9,8},{11,10},{13,12},{15,14},{17,16},{19,... | collective-permute-start | bytes 6291464 | tf_op jit(solution)/shard_map/ppermute | solution.py:135
  458.6 56.1 %collective-permute-start.42 = (bf16[4,512,512]{2,1,0:T(8,128)(2,1)}, bf16[4,512,512]{2,1,0:T(8,128)(2,1)}, u32[]{:S(2)}, u32[]{:S(2)}) collective-permute-start(bf16[4,512,512]{2,1,0:T(8,128)(2,1)} %get-tuple-element.50), channel_id=1, source_target_pairs={{64,1},{96,33},{66,3},{98,35},{68,5},{100,37},{70,7},{102,39},{72,... | collective-permute-start | bytes 6291464 | tf_op jit(solution)/shard_map/ppermute | solution.py:136
  459.9 54.8 %collective-permute-start.43 = (bf16[4,512,512]{2,1,0:T(8,128)(2,1)}, bf16[4,512,512]{2,1,0:T(8,128)(2,1)}, u32[]{:S(2)}, u32[]{:S(2)}) collective-permute-start(bf16[4,512,512]{2,1,0:T(8,128)(2,1)} %get-tuple-element.47), channel_id=1, source_target_pairs={{96,1},{64,33},{98,3},{66,35},{100,5},{68,37},{102,7},{70,39},{104... | collective-permute-start | bytes 6291464 | tf_op jit(solution)/shard_map/ppermute | solution.py:136
  466.1 48.7 %collective-permute-start.41 = (bf16[4,512,512]{2,1,0:T(8,128)(2,1)}, bf16[4,512,512]{2,1,0:T(8,128)(2,1)}, u32[]{:S(2)}, u32[]{:S(2)}) collective-permute-start(bf16[4,512,512]{2,1,0:T(8,128)(2,1)} %add_convert_fusion.2), channel_id=1, source_target_pairs={{0,32},{1,33},{32,0},{33,1},{64,96},{65,97},{96,64},{97,65},{2,34}... | collective-permute-start | bytes 6291464 | tf_op jit(solution)/shard_map/ppermute | solution.py:138
  467.1 15.0 %collective-permute-start.36 = (bf16[128,2048]{1,0:T(8,128)(2,1)S(1)}, bf16[128,2048]{1,0:T(8,128)(2,1)S(1)}, u32[]{:S(2)}, u32[]{:S(2)}) collective-permute-start(bf16[128,2048]{1,0:T(8,128)(2,1)S(1)} %get-tuple-element.89), channel_id=1, source_target_pairs={{0,16},{8,24},{16,0},{24,8},{1,17},{9,25},{17,1},{25,9},{2,18},{10... | collective-permute-start | bytes 1572872 | tf_op jit(solution)/shard_map/ppermute | solution.py:73
  482.0 14.6 %collective-permute-start.37 = (bf16[128,2048]{1,0:T(8,128)(2,1)S(1)}, bf16[128,2048]{1,0:T(8,128)(2,1)S(1)}, u32[]{:S(2)}, u32[]{:S(2)}) collective-permute-start(bf16[128,2048]{1,0:T(8,128)(2,1)S(1)} %get-tuple-element.91), channel_id=1, source_target_pairs={{0,8},{8,16},{16,24},{24,0},{1,9},{9,17},{17,25},{25,1},{2,10},{10... | collective-permute-start | bytes 1572872 | tf_op jit(solution)/shard_map/ppermute | solution.py:73
  496.6 13.8 %collective-permute-start.38 = (bf16[128,2048]{1,0:T(8,128)(2,1)S(1)}, bf16[128,2048]{1,0:T(8,128)(2,1)S(1)}, u32[]{:S(2)}, u32[]{:S(2)}) collective-permute-start(bf16[128,2048]{1,0:T(8,128)(2,1)S(1)} %get-tuple-element.90), channel_id=1, source_target_pairs={{0,24},{8,0},{16,8},{24,16},{1,25},{9,1},{17,9},{25,17},{2,26},{10... | collective-permute-start | bytes 1572872 | tf_op jit(solution)/shard_map/ppermute | solution.py:73
  521.0 14.4 %collective-permute-start.44 = (bf16[512,512]{1,0:T(8,128)(2,1)S(1)}, bf16[512,512]{1,0:T(8,128)(2,1)S(1)}, u32[]{:S(2)}, u32[]{:S(2)}) collective-permute-start(bf16[512,512]{1,0:T(8,128)(2,1)S(1)} %get-tuple-element.86), channel_id=1, source_target_pairs={{0,16},{8,24},{16,0},{24,8},{1,17},{9,25},{17,1},{25,9},{2,18},{10... | collective-permute-start | bytes 1572872 | tf_op jit(solution)/shard_map/ppermute | solution.py:73
  524.0 23.6 %collective-permute-start.45 = (bf16[512,512]{1,0:T(8,128)(2,1)S(1)}, bf16[512,512]{1,0:T(8,128)(2,1)S(1)}, u32[]{:S(2)}, u32[]{:S(2)}) collective-permute-start(bf16[512,512]{1,0:T(8,128)(2,1)S(1)} %get-tuple-element.88), channel_id=1, source_target_pairs={{0,8},{8,16},{16,24},{24,0},{1,9},{9,17},{17,25},{25,1},{2,10},{10... | collective-permute-start | bytes 1572872 | tf_op jit(solution)/shard_map/ppermute | solution.py:73
  524.0 23.6 %collective-permute-start.46 = (bf16[512,512]{1,0:T(8,128)(2,1)S(1)}, bf16[512,512]{1,0:T(8,128)(2,1)S(1)}, u32[]{:S(2)}, u32[]{:S(2)}) collective-permute-start(bf16[512,512]{1,0:T(8,128)(2,1)S(1)} %get-tuple-element.87), channel_id=1, source_target_pairs={{0,24},{8,0},{16,8},{24,16},{1,25},{9,1},{17,9},{25,17},{2,26},{10... | collective-permute-start | bytes 1572872 | tf_op jit(solution)/shard_map/ppermute | solution.py:73
  582.1 7.1 collective-permute-start.47
  592.2 6.0 collective-permute-start.52
  600.0 11.5 %collective-permute-start.53 = (bf16[16,80,128]{2,1,0:T(8,128)(2,1)S(1)}, bf16[16,80,128]{2,1,0:T(8,128)(2,1)S(1)}, u32[]{:S(2)}, u32[]{:S(2)}) collective-permute-start(bf16[16,80,128]{2,1,0:T(8,128)(2,1)S(1)} %fusion.42), channel_id=1, source_target_pairs={{0,1},{1,0},{2,3},{3,2},{4,5},{5,4},{6,7},{7,6},{8,9},{9,8},{10,11... | collective-permute-start | bytes 983048 | tf_op jit(solution)/shard_map/ppermute | solution.py:69
  610.9 88.4 %collective-permute-start.39 = (bf16[64,2048]{1,0:T(8,128)(2,1)}, bf16[64,2048]{1,0:T(8,128)(2,1)}, u32[]{:S(2)}, u32[]{:S(2)}) collective-permute-start(bf16[64,2048]{1,0:T(8,128)(2,1)} %get-tuple-element.107), channel_id=1, source_target_pairs={{0,1},{1,0},{2,3},{3,2},{4,5},{5,4},{6,7},{7,6},{8,9},{9,8},{10,11... | collective-permute-start | bytes 786440 | tf_op jit(solution)/shard_map/ppermute | solution.py:69
  611.6 18.0 %collective-permute-start.54 = (bf16[4,80,128]{2,1,0:T(8,128)(2,1)S(1)}, bf16[4,80,128]{2,1,0:T(8,128)(2,1)S(1)}, u32[]{:S(2)}, u32[]{:S(2)}) collective-permute-start(bf16[4,80,128]{2,1,0:T(8,128)(2,1)S(1)} %get-tuple-element.99), channel_id=1, source_target_pairs={{0,32},{32,64},{64,96},{96,0},{1,33},{33,65},{65,97},{97,1},{2,34}... | collective-permute-start | bytes 245768 | tf_op jit(solution)/shard_map/ppermute | solution.py:73
  611.7 19.1 %collective-permute-start.55 = (bf16[4,80,128]{2,1,0:T(8,128)(2,1)S(1)}, bf16[4,80,128]{2,1,0:T(8,128)(2,1)S(1)}, u32[]{:S(2)}, u32[]{:S(2)}) collective-permute-start(bf16[4,80,128]{2,1,0:T(8,128)(2,1)S(1)} %get-tuple-element.101), channel_id=1, source_target_pairs={{0,64},{32,96},{64,0},{96,32},{1,65},{33,97},{65,1},{97,33},{2,66}... | collective-permute-start | bytes 245768 | tf_op jit(solution)/shard_map/ppermute | solution.py:73
  638.4 30.4 %collective-permute-start.66 = (bf16[128,2048]{1,0:T(8,128)(2,1)S(1)}, bf16[128,2048]{1,0:T(8,128)(2,1)S(1)}, u32[]{:S(2)}, u32[]{:S(2)}) collective-permute-start(bf16[128,2048]{1,0:T(8,128)(2,1)S(1)} %get-tuple-element.83), channel_id=1, source_target_pairs={{0,4},{2,6},{4,0},{6,2},{1,5},{3,7},{5,1},{7,3},{8,12},{10,14},{12... | collective-permute-start | bytes 1572872 | tf_op jit(solution)/shard_map/ppermute | solution.py:73
  639.4 32.2 %collective-permute-start.67 = (bf16[128,2048]{1,0:T(8,128)(2,1)S(1)}, bf16[128,2048]{1,0:T(8,128)(2,1)S(1)}, u32[]{:S(2)}, u32[]{:S(2)}) collective-permute-start(bf16[128,2048]{1,0:T(8,128)(2,1)S(1)} %get-tuple-element.85), channel_id=1, source_target_pairs={{0,2},{2,4},{4,6},{6,0},{1,3},{3,5},{5,7},{7,1},{8,10},{10,12},{12... | collective-permute-start | bytes 1572872 | tf_op jit(solution)/shard_map/ppermute | solution.py:73
  639.4 32.1 %collective-permute-start.68 = (bf16[128,2048]{1,0:T(8,128)(2,1)S(1)}, bf16[128,2048]{1,0:T(8,128)(2,1)S(1)}, u32[]{:S(2)}, u32[]{:S(2)}) collective-permute-start(bf16[128,2048]{1,0:T(8,128)(2,1)S(1)} %get-tuple-element.84), channel_id=1, source_target_pairs={{0,6},{2,0},{4,2},{6,4},{1,7},{3,1},{5,3},{7,5},{8,14},{10,8},{12,... | collective-permute-start | bytes 1572872 | tf_op jit(solution)/shard_map/ppermute | solution.py:73
  666.7 21.3 %collective-permute-start.73 = (bf16[4,4,80,128]{3,2,1,0:T(8,128)(2,1)}, bf16[4,4,80,128]{3,2,1,0:T(8,128)(2,1)}, u32[]{:S(2)}, u32[]{:S(2)}) collective-permute-start(bf16[4,4,80,128]{3,2,1,0:T(8,128)(2,1)} %bitcast_dynamic-update-slice_fusion.15), channel_id=1, source_target_pairs={{0,6},{2,0},{4,2},{6,4},{1,7},{3,1},{5,3},{7,5},{8,14},{10,8},{12,... | collective-permute-start | bytes 983048 | tf_op jit(solution)/shard_map/ppermute | solution.py:73
  668.8 20.2 %collective-permute-start.74 = (bf16[4,4,80,128]{3,2,1,0:T(8,128)(2,1)}, bf16[4,4,80,128]{3,2,1,0:T(8,128)(2,1)}, u32[]{:S(2)}, u32[]{:S(2)}) collective-permute-start(bf16[4,4,80,128]{3,2,1,0:T(8,128)(2,1)} %bitcast_dynamic-update-slice_fusion.15), channel_id=1, source_target_pairs={{0,4},{2,6},{4,0},{6,2},{1,5},{3,7},{5,1},{7,3},{8,12},{10,14},{12... | collective-permute-start | bytes 983048 | tf_op jit(solution)/shard_map/ppermute | solution.py:73
  671.5 18.6 %collective-permute-start.75 = (bf16[4,4,80,128]{3,2,1,0:T(8,128)(2,1)}, bf16[4,4,80,128]{3,2,1,0:T(8,128)(2,1)}, u32[]{:S(2)}, u32[]{:S(2)}) collective-permute-start(bf16[4,4,80,128]{3,2,1,0:T(8,128)(2,1)} %bitcast_dynamic-update-slice_fusion.15), channel_id=1, source_target_pairs={{0,2},{2,4},{4,6},{6,0},{1,3},{3,5},{5,7},{7,1},{8,10},{10,12},{12... | collective-permute-start | bytes 983048 | tf_op jit(solution)/shard_map/ppermute | solution.py:73
  691.1 11.2 %collective-permute-start.76 = (bf16[4,16,80,128]{3,2,1,0:T(8,128)(2,1)S(1)}, bf16[4,16,80,128]{3,2,1,0:T(8,128)(2,1)S(1)}, u32[]{:S(2)}, u32[]{:S(2)}) collective-permute-start(bf16[4,16,80,128]{3,2,1,0:T(8,128)(2,1)S(1)} %bitcast.277), channel_id=1, source_target_pairs={{0,1},{1,0},{2,3},{3,2},{4,5},{5,4},{6,7},{7,6},{8,9},{9,8},{10,11... | collective-permute-start | bytes 3932168 | tf_op jit(solution)/shard_map/ppermute | solution.py:69
  (101 other events, 1493.4 us)
Sparse Core Ops, SparseCore 0:
  11.1 102.6 all-gather.3
  235.5 95.8 all-gather.5
  385.2 78.4 reduce-scatter.2
  467.8 90.9 reduce-scatter.4
  567.1 102.6 all-gather.7

commit v8 on v7

--- a/solution.py
+++ b/solution.py
@@ -227,11 +227,14 @@
         allowed = allowed_mask(pos_ref[...], start_ref[...], kpos_ref[0])
         dk = jnp.zeros((GROUP, HEAD_SIZE), f32)
         dv = jnp.zeros((GROUP, HEAD_SIZE), f32)
+        both = [
+            times_transposed(q_ref[:, head * HEAD_SIZE : (head + 1) * HEAD_SIZE], tile_buf[:, :HEAD_SIZE])
+            for head in range(2)
+        ]
         for head in range(2):
             cols = slice(head * HEAD_SIZE, (head + 1) * HEAD_SIZE)
             query, dout = q_ref[:, cols], dout_ref[:, cols]
-            scores = times_transposed(query, tile_buf[:, :HEAD_SIZE])
-            weights_p = jnp.where(allowed, jnp.exp(scores - lse_ref[head]), 0.0)
+            weights_p = jnp.where(allowed, jnp.exp(both[head] - lse_ref[head]), 0.0)
             dprobs = times_transposed(dout, tile_buf[:, HEAD_SIZE:])
             dscores = (weights_p * (dprobs - delta[head])).astype(bf16)
             dq_ref[:, cols] += product(dscores, tile_buf[:, :HEAD_SIZE])

time: 722 us -> 731 us (1.012)
  starting transfers between devices: 147 us -> 169 us
    ppermute x60, starting transfers between devices: 96.4 us -> 114 us  [shift(): lax.ppermute(value, RING[ring], [(i, (i + step) % 4) for i in range(4)])]
    all_gather x1, waiting for transfers between devices: 12.8 us -> 20.1 us  [local(): lax.all_gather(ffn, OVER_X, axis=0, tiled=False).reshape(16, 2, 192, 2048)]
  transfers between devices with their start and end apart: 84 -> 84, of which waited for: 43 -> 41; matrix products, arithmetic and copies ran while one was open for 21% -> 21% of each run, Pallas kernels for 6% -> 6%
where the time goes in v8:
time: 731 us; the launch traced here: 726 us
  waiting for transfers between devices  274 us (37%)
  starting transfers between devices  169 us (23%)
  Pallas kernels  90.5 us (12%)
  local copies, waits for them, and re-layouts  76.1 us (10%)
  matrix products  49.5 us (7%)
  other arithmetic  41.9 us (6%)
  between operations  24 us (3%)
    ppermute x60, waiting for transfers between devices, shift(): lax.ppermute(value, RING[ring], [(i, (i + step) % 4) for i in range(4)])  210 us
    ppermute x60, starting transfers between devices, shift(): lax.ppermute(value, RING[ring], [(i, (i + step) % 4) for i in range(4)])  114 us
    pallas_call x1, Pallas kernels, feed_forward(): pl.pallas_call(ffn_kernel, grid_spec=pltpu.PrefetchScalarGridSpec(num_sca...  45.6 us
    dot_general x11, matrix products, product(): return jnp.dot(left, right, preferred_element_type=f32)  25.2 us
    all_gather x1, waiting for transfers between devices, local(): lax.all_gather(ffn, OVER_X, axis=0, tiled=False).reshape(16, 2, 192, 2048)  20.1 us
    ppermute x2, waiting for transfers between devices, gather_row(): ahead = [lax.ppermute(line, CORNER, pairs) for pairs in LATER]  20 us
    ppermute x1, waiting for transfers between devices, gather_row(): partner = lax.ppermute(line, CORNER, PARTNER)  18.2 us
    pallas_call x1, Pallas kernels, attend_back(): pl.pallas_call(attend_back_kernel, grid_spec=pltpu.PrefetchScalarGridSpec...  17.2 us
  transfers between devices with their start and end apart: 84, of which 41 were waited for; matrix products, arithmetic and copies ran while one was open for 21% of the time, Pallas kernels for 6%

profile of v8, /device:TPU:1, one launch (start us, length us, event | category | flops | bytes accessed | tf_op | source)
XLA Modules:
  0.0 726.0 jit_solution(2794136414749313659)
XLA Ops:
  12.7 5.0 all-to-all-start
  31.1 6.1 collective-permute-done.5
  37.9 3.5 collective-permute-done.6
  42.5 11.6 %collective-permute-done.7 = bf16[128,2048]{1,0:T(8,128)(2,1)S(1)} collective-permute-done((bf16[128,2048]{1,0:T(8,128)(2,1)S(1)}, bf16[128,2048]{1,0:T(8,128)(2,1)S(1)}, u32[]{:S(2)}, u32[]{:S(2)}) %collective-permute-start.7) | collective-permute-done | bytes 524320 | tf_op jit(solution)/shard_map/ppermute | solution.py:73
  54.4 5.9 collective-permute-start.9
  63.2 2.6 collective-permute-done.10
  65.8 7.4 %collective-permute-start.11 = (bf16[4,128,512]{2,1,0:T(8,128)(2,1)S(1)}, bf16[4,128,512]{2,1,0:T(8,128)(2,1)S(1)}, u32[]{:S(2)}, u32[]{:S(2)}) collective-permute-start(bf16[4,128,512]{2,1,0:T(8,128)(2,1)S(1)} %bitcast_dynamic-update-slice_fusion.11), channel_id=1, source_target_pairs={{0,96},{32,0},{64,32},{96,64},{1,97},{33,1},{65,33},{97,65},{2,98}... | collective-permute-start | bytes 1572872 | tf_op jit(solution)/shard_map/ppermute | solution.py:73
  76.4 4.4 collective-permute-done.11
  81.6 3.2 collective-permute-done.12
  85.6 25.4 %collective-permute-done.13 = bf16[4,128,512]{2,1,0:T(8,128)(2,1)S(1)} collective-permute-done((bf16[4,128,512]{2,1,0:T(8,128)(2,1)S(1)}, bf16[4,128,512]{2,1,0:T(8,128)(2,1)S(1)}, u32[]{:S(2)}, u32[]{:S(2)}) %collective-permute-start.13) | collective-permute-done | bytes 524320 | tf_op jit(solution)/shard_map/ppermute | solution.py:73
  115.7 3.1 fusion.2
  119.9 2.9 fusion.147
  122.8 4.2 broadcast_select_fusion
  130.1 12.0 %collective-permute-done.15 = bf16[512,512]{1,0:T(8,128)(2,1)S(1)} collective-permute-done((bf16[512,512]{1,0:T(8,128)(2,1)S(1)}, bf16[512,512]{1,0:T(8,128)(2,1)S(1)}, u32[]{:S(2)}, u32[]{:S(2)}) %collective-permute-start.15) | collective-permute-done | bytes 524320 | tf_op jit(solution)/shard_map/ppermute | solution.py:73
  143.5 11.9 %collective-permute-done.17 = bf16[512,512]{1,0:T(8,128)(2,1)S(1)} collective-permute-done((bf16[512,512]{1,0:T(8,128)(2,1)S(1)}, bf16[512,512]{1,0:T(8,128)(2,1)S(1)}, u32[]{:S(2)}, u32[]{:S(2)}) %collective-permute-start.17) | collective-permute-done | bytes 524320 | tf_op jit(solution)/shard_map/ppermute | solution.py:73
  156.9 6.1 collective-permute-start.19
  163.0 2.7 collective-permute-start.20
  179.2 6.5 all-to-all-start.1
  185.7 18.2 %collective-permute-done.18.refs_1_ = bf16[4,512,512]{2,1,0:T(8,128)(2,1)} collective-permute-done((bf16[4,512,512]{2,1,0:T(8,128)(2,1)}, bf16[4,512,512]{2,1,0:T(8,128)(2,1)}, u32[]{:S(2)}, u32[]{:S(2)}) %collective-permute-start.18) | collective-permute-done | bytes 2097184 | tf_op jit(solution)/shard_map/ppermute | solution.py:129
  205.2 20.0 %collective-permute-done.19.refs_2_ = bf16[4,512,512]{2,1,0:T(8,128)(2,1)} collective-permute-done((bf16[4,512,512]{2,1,0:T(8,128)(2,1)}, bf16[4,512,512]{2,1,0:T(8,128)(2,1)}, u32[]{:S(2)}, u32[]{:S(2)}) %collective-permute-start.19) | collective-permute-done | bytes 2097184 | tf_op jit(solution)/shard_map/ppermute | solution.py:128
  243.7 2.8 reshape.658
  250.3 11.6 %attend.1 = (f32[512,512]{1,0:T(8,128)S(1)}, f32[2,512,1]{2,1,0:T(8,128)S(1)}) custom-call(s32[64]{0:T(128)S(1)} %pad_add_fusion.2.active, bf16[512,512]{1,0:T(8,128)(2,1)S(1)} %fusion.23.q_ref, s32[512,1]{1,0:T(8,128)S(1)} %copy.137.pos_ref, s32[512,1]{1,0:T(8,128)S(1)} %copy.138.start_ref, s32[16,1,512]{2,1,0:T(1,128)S(1)} %reshape.659.kpos_ref, ...), custom_call_target="tpu_custom_call" | custom-call | flops 6442450944 | bytes 10485760 | tf_op jit(solution)/shard_map/attend/pallas_call | solution.py:287
  277.6 5.0 multiply_reduce_fusion.1
  283.7 2.7 collective-permute-start.27
  293.4 13.0 %collective-permute-done.28 = bf16[128,2048]{1,0:T(8,128)(2,1)S(1)} collective-permute-done((bf16[128,2048]{1,0:T(8,128)(2,1)S(1)}, bf16[128,2048]{1,0:T(8,128)(2,1)S(1)}, u32[]{:S(2)}, u32[]{:S(2)}) %collective-permute-start.28) | collective-permute-done | bytes 524320 | tf_op jit(solution)/shard_map/ppermute | solution.py:73
  309.6 20.1 %all-gather.6.cloned.1.call-done = bf16[32,192,2048]{2,1,0:T(8,128)(2,1)} async-done(((bf16[1,192,2048]{2,1,0:T(8,128)(2,1)}), bf16[32,192,2048]{2,1,0:T(8,128)(2,1)}) %all-gather.6.cloned.1.call-update) | async-done | bytes 25165840 | tf_op jit(solution)/shard_map/all_gather | solution.py:651
  329.7 45.6 %feed_forward.1 = (bf16[512,2048]{1,0:T(8,128)(2,1)}, bf16[512,2432]{1,0:T(8,128)(2,1)}, f32[4,4,2,192,128]{4,3,2,1,0:T(8,128)}) custom-call(s32[1]{0:T(128)} %bitcast.36.at, bf16[512,2048]{1,0:T(8,128)(2,1)} %pad_maximum_fusion.1.nm_ref, bf16[512,2048]{1,0:T(8,128)(2,1)} %copy-done.59, bf16[512,256]{1,0:T(8,128)(2,1)} %fusion.3.lgu_ref, ...), custom_call_target="tpu_custom_call" | custom-call | flops 30064771072 | bytes 41943040 | tf_op jit(solution)/shard_map/feed_forward/pallas_call | solution.py:406
  375.3 2.7 fusion.137
  378.0 2.8 collective-permute-start.29
  383.7 11.5 %collective-permute-done.29 = bf16[128,2432]{1,0:T(8,128)(2,1)} collective-permute-done((bf16[128,2432]{1,0:T(8,128)(2,1)}, bf16[128,2432]{1,0:T(8,128)(2,1)}, u32[]{:S(2)}, u32[]{:S(2)}) %collective-permute-start.29) | collective-permute-done | bytes 622624 | tf_op jit(solution)/shard_map/ppermute | solution.py:73
  395.3 13.9 %collective-permute-done.30 = bf16[128,2432]{1,0:T(8,128)(2,1)} collective-permute-done((bf16[128,2432]{1,0:T(8,128)(2,1)}, bf16[128,2432]{1,0:T(8,128)(2,1)}, u32[]{:S(2)}, u32[]{:S(2)}) %collective-permute-start.30) | collective-permute-done | bytes 622624 | tf_op jit(solution)/shard_map/ppermute | solution.py:73
  414.2 2.9 fusion.128
  417.5 2.5 collective-permute-start.32
  423.8 2.9 copy.147
  426.8 2.9 collective-permute-done.34
  433.0 17.2 %attend_back.1 = (f32[512,512]{1,0:T(8,128)S(1)}, bf16[4,512,512]{2,1,0:T(8,128)(2,1)}, bf16[4,512,512]{2,1,0:T(8,128)(2,1)}, bf16[4,512,512]{2,1,0:T(8,128)(2,1)}, bf16[4,512,512]{2,1,0:T(8,128)(2,1)}) custom-call(s32[64]{0:T(128)S(1)} %pad_add_fusion.2.active, bf16[512,512]{1,0:T(8,128)(2,1)S(1)} %fusion.23.q_ref, s32[512,1]{1,0:T(8,128)S(1)} %copy-done.4, ...), custom_call_target="tpu_custom_call" | custom-call | flops 12884901888 | bytes 20971520 | tf_op jit(solution)/shard_map/attend_back/pallas_call | solution.py:312
  450.2 3.6 collective-permute-start.35
  453.9 2.7 collective-permute-start.40
  459.2 3.6 add_convert_fusion.2
  464.0 5.9 collective-permute-start.41
  470.9 5.8 collective-permute-start.36
  476.7 11.6 %collective-permute-done.36 = bf16[128,2048]{1,0:T(8,128)(2,1)S(1)} collective-permute-done((bf16[128,2048]{1,0:T(8,128)(2,1)S(1)}, bf16[128,2048]{1,0:T(8,128)(2,1)S(1)}, u32[]{:S(2)}, u32[]{:S(2)}) %collective-permute-start.36) | collective-permute-done | bytes 524320 | tf_op jit(solution)/shard_map/ppermute | solution.py:73
  488.3 15.0 %collective-permute-start.37 = (bf16[128,2048]{1,0:T(8,128)(2,1)S(1)}, bf16[128,2048]{1,0:T(8,128)(2,1)S(1)}, u32[]{:S(2)}, u32[]{:S(2)}) collective-permute-start(bf16[128,2048]{1,0:T(8,128)(2,1)S(1)} %get-tuple-element.91), channel_id=1, source_target_pairs={{0,8},{8,16},{16,24},{24,0},{1,9},{9,17},{17,25},{25,1},{2,10},{10... | collective-permute-start | bytes 1572872 | tf_op jit(solution)/shard_map/ppermute | solution.py:73
  503.3 11.3 %collective-permute-done.37 = bf16[128,2048]{1,0:T(8,128)(2,1)S(1)} collective-permute-done((bf16[128,2048]{1,0:T(8,128)(2,1)S(1)}, bf16[128,2048]{1,0:T(8,128)(2,1)S(1)}, u32[]{:S(2)}, u32[]{:S(2)}) %collective-permute-start.37) | collective-permute-done | bytes 524320 | tf_op jit(solution)/shard_map/ppermute | solution.py:73
  516.3 11.8 %collective-permute-done.38 = bf16[128,2048]{1,0:T(8,128)(2,1)S(1)} collective-permute-done((bf16[128,2048]{1,0:T(8,128)(2,1)S(1)}, bf16[128,2048]{1,0:T(8,128)(2,1)S(1)}, u32[]{:S(2)}, u32[]{:S(2)}) %collective-permute-start.38) | collective-permute-done | bytes 524320 | tf_op jit(solution)/shard_map/ppermute | solution.py:73
  532.4 6.0 add_convert_fusion.1
  543.5 8.7 %collective-permute-done.44 = bf16[512,512]{1,0:T(8,128)(2,1)S(1)} collective-permute-done((bf16[512,512]{1,0:T(8,128)(2,1)S(1)}, bf16[512,512]{1,0:T(8,128)(2,1)S(1)}, u32[]{:S(2)}, u32[]{:S(2)}) %collective-permute-start.44) | collective-permute-done | bytes 524320 | tf_op jit(solution)/shard_map/ppermute | solution.py:73
  552.3 12.9 %collective-permute-done.45 = bf16[512,512]{1,0:T(8,128)(2,1)S(1)} collective-permute-done((bf16[512,512]{1,0:T(8,128)(2,1)S(1)}, bf16[512,512]{1,0:T(8,128)(2,1)S(1)}, u32[]{:S(2)}, u32[]{:S(2)}) %collective-permute-start.45) | collective-permute-done | bytes 524320 | tf_op jit(solution)/shard_map/ppermute | solution.py:73
  567.5 3.4 reduce-scatter.5.cloned.1.call-done
  580.9 2.8 reshape.669
  596.4 2.7 collective-permute-start.49
  612.9 7.2 collective-permute-start.53
  621.8 13.9 %collective-permute-start.55 = (bf16[4,80,128]{2,1,0:T(8,128)(2,1)S(1)}, bf16[4,80,128]{2,1,0:T(8,128)(2,1)S(1)}, u32[]{:S(2)}, u32[]{:S(2)}) collective-permute-start(bf16[4,80,128]{2,1,0:T(8,128)(2,1)S(1)} %get-tuple-element.101), channel_id=1, source_target_pairs={{0,64},{32,96},{64,0},{96,32},{1,65},{33,97},{65,1},{97,33},{2,66}... | collective-permute-start | bytes 245768 | tf_op jit(solution)/shard_map/ppermute | solution.py:73
  637.7 2.9 fusion.30
  641.4 3.3 collective-permute-start.58
  644.9 2.9 add_convert_fusion
  650.9 2.7 collective-permute-start.68
  658.7 3.8 collective-permute-done.62
  668.7 3.2 collective-permute-done.64
  674.1 3.1 collective-permute-done.65
  680.3 3.6 collective-permute-done.67
  685.7 11.4 %unpack_early.1 = (f32[128,8192]{1,0:T(8,128)}, f32[128,8192]{1,0:T(8,128)}, f32[8192,128]{1,0:T(8,128)}, f32[2048,128]{1,0:T(8,128)}, f32[128,2048]{1,0:T(8,128...) custom-call(bf16[128,272,128]{2,1,0:T(8,128)(2,1)} %all-gather.8.cloned.1.call-done.all_ref), custom_call_target="tpu_custom_call" | custom-call | flops 1048576 | bytes 28311552 | tf_op jit(solution)/shard_map/unpack_early/pallas_call | solution.py:474
  703.5 6.0 collective-permute-start.76
  714.5 4.8 unpack_late.1
  (513 shorter events, 202.5 us)
Async XLA Ops:
  7.2 224.1 %all-gather.4.cloned.1.call-start = ((), (), s32[]{:S(2)}) async-start(), calls=%async_computation.4 | async-start | bytes 8454144 | tf_op jit(solution)/shard_map/all_gather | solution.py:630
  9.1 9.4 %collective-permute-start = (bf16[64,2048]{1,0:T(8,128)(2,1)S(1)}, bf16[64,2048]{1,0:T(8,128)(2,1)S(1)}, u32[]{:S(2)}, u32[]{:S(2)}) collective-permute-start(bf16[64,2048]{1,0:T(8,128)(2,1)S(1)} %get-tuple-element.122), channel_id=1, source_target_pairs={{0,1},{1,0},{2,3},{3,2},{4,5},{5,4},{6,7},{7,6},{8,9},{9,8},{10,11... | collective-permute-start | bytes 786440 | tf_op jit(solution)/shard_map/ppermute | solution.py:69
  11.6 7.8 %collective-permute-start.1 = (bf16[64,2048]{1,0:T(8,128)(2,1)S(1)}, bf16[64,2048]{1,0:T(8,128)(2,1)}, u32[]{:S(2)}, u32[]{:S(2)}) collective-permute-start(bf16[64,2048]{1,0:T(8,128)(2,1)S(1)} %get-tuple-element.120), channel_id=1, source_target_pairs={{0,1},{1,0},{2,3},{3,2},{4,5},{5,4},{6,7},{7,6},{8,9},{9,8},{10,11... | collective-permute-start | bytes 786440 | tf_op jit(solution)/shard_map/ppermute | solution.py:69
  12.7 10.3 %all-to-all-start = ((bf16[8,16,512]{2,1,0:T(8,128)(2,1)}), bf16[8,16,512]{2,1,0:T(8,128)(2,1)S(1)}, u32[]{:S(2)}, u32[]{:S(2)}) async-start(bf16[8,16,512]{2,1,0:T(8,128)(2,1)} %bitcast.9), calls=%async_computation | async-start | bytes 262144 | tf_op jit(solution)/shard_map/all_to_all | solution.py:616
  23.0 14.2 %collective-permute-start.5 = (bf16[128,2048]{1,0:T(8,128)(2,1)S(1)}, bf16[128,2048]{1,0:T(8,128)(2,1)S(1)}, u32[]{:S(2)}, u32[]{:S(2)}) collective-permute-start(bf16[128,2048]{1,0:T(8,128)(2,1)S(1)} %pad_maximum_fusion.4), channel_id=1, source_target_pairs={{0,24},{8,0},{16,8},{24,16},{1,25},{9,1},{17,9},{25,17},{2,26},{10... | collective-permute-start | bytes 1572872 | tf_op jit(solution)/shard_map/ppermute | solution.py:73
  27.0 14.4 %collective-permute-start.6 = (bf16[128,2048]{1,0:T(8,128)(2,1)S(1)}, bf16[128,2048]{1,0:T(8,128)(2,1)}, u32[]{:S(2)}, u32[]{:S(2)}) collective-permute-start(bf16[128,2048]{1,0:T(8,128)(2,1)S(1)} %pad_maximum_fusion.4), channel_id=1, source_target_pairs={{0,16},{8,24},{16,0},{24,8},{1,17},{9,25},{17,1},{25,9},{2,18},{10... | collective-permute-start | bytes 1572872 | tf_op jit(solution)/shard_map/ppermute | solution.py:73
  28.2 25.9 %collective-permute-start.7 = (bf16[128,2048]{1,0:T(8,128)(2,1)S(1)}, bf16[128,2048]{1,0:T(8,128)(2,1)S(1)}, u32[]{:S(2)}, u32[]{:S(2)}) collective-permute-start(bf16[128,2048]{1,0:T(8,128)(2,1)S(1)} %pad_maximum_fusion.4), channel_id=1, source_target_pairs={{0,8},{8,16},{16,24},{24,0},{1,9},{9,17},{17,25},{25,1},{2,10},{10... | collective-permute-start | bytes 1572872 | tf_op jit(solution)/shard_map/ppermute | solution.py:73
  29.0 25.2 %collective-permute-start.2 = (bf16[128,2048]{1,0:T(8,128)(2,1)S(1)}, bf16[128,2048]{1,0:T(8,128)(2,1)S(1)}, u32[]{:S(2)}, u32[]{:S(2)}) collective-permute-start(bf16[128,2048]{1,0:T(8,128)(2,1)S(1)} %fusion.9), channel_id=1, source_target_pairs={{0,6},{2,0},{4,2},{6,4},{1,7},{3,1},{5,3},{7,5},{8,14},{10,8},{12,... | collective-permute-start | bytes 1572872 | tf_op jit(solution)/shard_map/ppermute | solution.py:73
  29.9 24.3 %collective-permute-start.3 = (bf16[128,2048]{1,0:T(8,128)(2,1)S(1)}, bf16[128,2048]{1,0:T(8,128)(2,1)S(1)}, u32[]{:S(2)}, u32[]{:S(2)}) collective-permute-start(bf16[128,2048]{1,0:T(8,128)(2,1)S(1)} %fusion.9), channel_id=1, source_target_pairs={{0,4},{2,6},{4,0},{6,2},{1,5},{3,7},{5,1},{7,3},{8,12},{10,14},{12... | collective-permute-start | bytes 1572872 | tf_op jit(solution)/shard_map/ppermute | solution.py:73
  37.2 17.1 %collective-permute-start.4 = (bf16[128,2048]{1,0:T(8,128)(2,1)S(1)}, bf16[128,2048]{1,0:T(8,128)(2,1)S(1)}, u32[]{:S(2)}, u32[]{:S(2)}) collective-permute-start(bf16[128,2048]{1,0:T(8,128)(2,1)S(1)} %fusion.9), channel_id=1, source_target_pairs={{0,2},{2,4},{4,6},{6,0},{1,3},{3,5},{5,7},{7,1},{8,10},{10,12},{12... | collective-permute-start | bytes 1572872 | tf_op jit(solution)/shard_map/ppermute | solution.py:73
  54.4 7.7 %collective-permute-start.8 = (bf16[128,512]{1,0:T(8,128)(2,1)S(1)}, bf16[128,512]{1,0:T(8,128)(2,1)S(1)}, u32[]{:S(2)}, u32[]{:S(2)}) collective-permute-start(bf16[128,512]{1,0:T(8,128)(2,1)S(1)} %bitcast.300), channel_id=1, source_target_pairs={{0,24},{8,0},{16,8},{24,16},{1,25},{9,1},{17,9},{25,17},{2,26},{10... | collective-permute-start | bytes 393224 | tf_op jit(solution)/shard_map/ppermute | solution.py:73
  54.4 8.8 %collective-permute-start.9 = (bf16[128,512]{1,0:T(8,128)(2,1)S(1)}, bf16[128,512]{1,0:T(8,128)(2,1)S(1)}, u32[]{:S(2)}, u32[]{:S(2)}) collective-permute-start(bf16[128,512]{1,0:T(8,128)(2,1)S(1)} %bitcast.301), channel_id=1, source_target_pairs={{0,16},{8,24},{16,0},{24,8},{1,17},{9,25},{17,1},{25,9},{2,18},{10... | collective-permute-start | bytes 393224 | tf_op jit(solution)/shard_map/ppermute | solution.py:73
  65.8 15.0 %collective-permute-start.11 = (bf16[4,128,512]{2,1,0:T(8,128)(2,1)S(1)}, bf16[4,128,512]{2,1,0:T(8,128)(2,1)S(1)}, u32[]{:S(2)}, u32[]{:S(2)}) collective-permute-start(bf16[4,128,512]{2,1,0:T(8,128)(2,1)S(1)} %bitcast_dynamic-update-slice_fusion.11), channel_id=1, source_target_pairs={{0,96},{32,0},{64,32},{96,64},{1,97},{33,1},{65,33},{97,65},{2,98}... | collective-permute-start | bytes 1572872 | tf_op jit(solution)/shard_map/ppermute | solution.py:73
  73.3 11.5 %collective-permute-start.12 = (bf16[4,128,512]{2,1,0:T(8,128)(2,1)S(1)}, bf16[4,128,512]{2,1,0:T(8,128)(2,1)S(1)}, u32[]{:S(2)}, u32[]{:S(2)}) collective-permute-start(bf16[4,128,512]{2,1,0:T(8,128)(2,1)S(1)} %bitcast_dynamic-update-slice_fusion.11), channel_id=1, source_target_pairs={{0,64},{32,96},{64,0},{96,32},{1,65},{33,97},{65,1},{97,33},{2,66}... | collective-permute-start | bytes 1572872 | tf_op jit(solution)/shard_map/ppermute | solution.py:73
  73.9 37.2 %collective-permute-start.13 = (bf16[4,128,512]{2,1,0:T(8,128)(2,1)S(1)}, bf16[4,128,512]{2,1,0:T(8,128)(2,1)S(1)}, u32[]{:S(2)}, u32[]{:S(2)}) collective-permute-start(bf16[4,128,512]{2,1,0:T(8,128)(2,1)S(1)} %bitcast_dynamic-update-slice_fusion.11), channel_id=1, source_target_pairs={{0,32},{32,64},{64,96},{96,0},{1,33},{33,65},{65,97},{97,1},{2,34}... | collective-permute-start | bytes 1572872 | tf_op jit(solution)/shard_map/ppermute | solution.py:73
  111.9 10.9 %collective-permute-start.14 = (bf16[2048,512]{1,0:T(8,128)(2,1)}, bf16[2048,512]{1,0:T(8,128)(2,1)}, u32[]{:S(2)}, u32[]{:S(2)}) collective-permute-start(bf16[2048,512]{1,0:T(8,128)(2,1)} %bitcast.19), channel_id=1, source_target_pairs={{0,1},{1,0},{2,3},{3,2},{4,5},{5,4},{6,7},{7,6},{8,9},{9,8},{10,11... | collective-permute-start | bytes 6291464 | tf_op jit(solution)/shard_map/ppermute | solution.py:69
  128.5 13.6 %collective-permute-start.15 = (bf16[512,512]{1,0:T(8,128)(2,1)S(1)}, bf16[512,512]{1,0:T(8,128)(2,1)S(1)}, u32[]{:S(2)}, u32[]{:S(2)}) collective-permute-start(bf16[512,512]{1,0:T(8,128)(2,1)S(1)} %get-tuple-element.116), channel_id=1, source_target_pairs={{0,24},{8,0},{16,8},{24,16},{1,25},{9,1},{17,9},{25,17},{2,26},{10... | collective-permute-start | bytes 1572872 | tf_op jit(solution)/shard_map/ppermute | solution.py:73
  128.7 14.7 %collective-permute-start.16 = (bf16[512,512]{1,0:T(8,128)(2,1)S(1)}, bf16[512,512]{1,0:T(8,128)(2,1)S(1)}, u32[]{:S(2)}, u32[]{:S(2)}) collective-permute-start(bf16[512,512]{1,0:T(8,128)(2,1)S(1)} %get-tuple-element.116), channel_id=1, source_target_pairs={{0,16},{8,24},{16,0},{24,8},{1,17},{9,25},{17,1},{25,9},{2,18},{10... | collective-permute-start | bytes 1572872 | tf_op jit(solution)/shard_map/ppermute | solution.py:73
  128.7 26.6 %collective-permute-start.17 = (bf16[512,512]{1,0:T(8,128)(2,1)S(1)}, bf16[512,512]{1,0:T(8,128)(2,1)S(1)}, u32[]{:S(2)}, u32[]{:S(2)}) collective-permute-start(bf16[512,512]{1,0:T(8,128)(2,1)S(1)} %get-tuple-element.116), channel_id=1, source_target_pairs={{0,8},{8,16},{16,24},{24,0},{1,9},{9,17},{17,25},{25,1},{2,10},{10... | collective-permute-start | bytes 1572872 | tf_op jit(solution)/shard_map/ppermute | solution.py:73
  156.9 47.0 %collective-permute-start.18 = (bf16[4,512,512]{2,1,0:T(8,128)(2,1)}, bf16[4,512,512]{2,1,0:T(8,128)(2,1)}, u32[]{:S(2)}, u32[]{:S(2)}) collective-permute-start(bf16[4,512,512]{2,1,0:T(8,128)(2,1)} %pad_maximum_fusion.refs_0_), channel_id=1, source_target_pairs={{0,32},{1,33},{32,0},{33,1},{64,96},{65,97},{96,64},{97,65},{2,34}... | collective-permute-start | bytes 6291464 | tf_op jit(solution)/shard_map/ppermute | solution.py:129
  156.9 68.2 %collective-permute-start.19 = (bf16[4,512,512]{2,1,0:T(8,128)(2,1)}, bf16[4,512,512]{2,1,0:T(8,128)(2,1)}, u32[]{:S(2)}, u32[]{:S(2)}) collective-permute-start(bf16[4,512,512]{2,1,0:T(8,128)(2,1)} %pad_maximum_fusion.refs_0_), channel_id=1, source_target_pairs={{1,64},{33,96},{3,66},{35,98},{5,68},{37,100},{7,70},{39,102},{9,7... | collective-permute-start | bytes 6291464 | tf_op jit(solution)/shard_map/ppermute | solution.py:128
  163.0 64.6 %collective-permute-start.20 = (bf16[4,512,512]{2,1,0:T(8,128)(2,1)}, bf16[4,512,512]{2,1,0:T(8,128)(2,1)}, u32[]{:S(2)}, u32[]{:S(2)}) collective-permute-start(bf16[4,512,512]{2,1,0:T(8,128)(2,1)} %pad_maximum_fusion.refs_0_), channel_id=1, source_target_pairs={{1,96},{33,64},{3,98},{35,66},{5,100},{37,68},{7,102},{39,70},{9,1... | collective-permute-start | bytes 6291464 | tf_op jit(solution)/shard_map/ppermute | solution.py:128
  165.7 63.8 %collective-permute-start.21 = (bf16[4,512,512]{2,1,0:T(8,128)(2,1)}, bf16[4,512,512]{2,1,0:T(8,128)(2,1)}, u32[]{:S(2)}, u32[]{:S(2)}) collective-permute-start(bf16[4,512,512]{2,1,0:T(8,128)(2,1)} %pad_maximum_fusion.refs_0_), channel_id=1, source_target_pairs={{0,1},{2,3},{4,5},{6,7},{8,9},{10,11},{12,13},{14,15},{16,17},{18,... | collective-permute-start | bytes 6291464 | tf_op jit(solution)/shard_map/ppermute | solution.py:130
  179.2 54.0 %all-to-all-start.1 = ((bf16[8,16,2048]{2,1,0:T(8,128)(2,1)}), bf16[8,16,2048]{2,1,0:T(8,128)(2,1)}, u32[]{:S(2)}, u32[]{:S(2)}) async-start(bf16[8,16,2048]{2,1,0:T(8,128)(2,1)} %maximum_add_fusion.1), calls=%async_computation.1 | async-start | bytes 1048576 | tf_op jit(solution)/shard_map/all_to_all | solution.py:648
  185.7 144.0 %all-gather.6.cloned.1.call-start = ((), (), s32[]{:S(2)}) async-start(), calls=%async_computation.5 | async-start | bytes 25952256 | tf_op jit(solution)/shard_map/all_gather | solution.py:651
  235.4 294.5 %reduce-scatter.3.cloned.1.call-start = ((), (), s32[]{:S(2)}) async-start(), calls=%async_computation.6 | async-start | bytes 3244032 | tf_op jit(solution)/shard_map/reduce_scatter | solution.py:714
  236.9 13.4 %collective-permute-start.22 = (bf16[4,512,512]{2,1,0:T(8,128)(2,1)}, bf16[4,512,512]{2,1,0:T(8,128)(2,1)}, u32[]{:S(2)}, u32[]{:S(2)}) collective-permute-start(bf16[4,512,512]{2,1,0:T(8,128)(2,1)} %collective-permute-done.18.refs_1_), channel_id=1, source_target_pairs={{0,1},{2,3},{4,5},{6,7},{8,9},{10,11},{12,13},{14,15},{16,17},{18,... | collective-permute-start | bytes 6291464 | tf_op jit(solution)/shard_map/ppermute | solution.py:130
  263.1 7.3 %collective-permute-start.23 = (bf16[128,512]{1,0:T(8,128)(2,1)S(1)}, bf16[128,512]{1,0:T(8,128)(2,1)S(1)}, u32[]{:S(2)}, u32[]{:S(2)}) collective-permute-start(bf16[128,512]{1,0:T(8,128)(2,1)S(1)} %get-tuple-element.114), channel_id=1, source_target_pairs={{0,2},{2,4},{4,6},{6,0},{1,3},{3,5},{5,7},{7,1},{8,10},{10,12},{12... | collective-permute-start | bytes 393224 | tf_op jit(solution)/shard_map/ppermute | solution.py:73
  283.4 8.5 %collective-permute-start.26 = (bf16[128,2048]{1,0:T(8,128)(2,1)S(1)}, bf16[128,2048]{1,0:T(8,128)(2,1)S(1)}, u32[]{:S(2)}, u32[]{:S(2)}) collective-permute-start(bf16[128,2048]{1,0:T(8,128)(2,1)S(1)} %multiply_convert_fusion.1), channel_id=1, source_target_pairs={{0,24},{8,0},{16,8},{24,16},{1,25},{9,1},{17,9},{25,17},{2,26},{10... | collective-permute-start | bytes 1572872 | tf_op jit(solution)/shard_map/ppermute | solution.py:73
  283.7 9.6 %collective-permute-start.27 = (bf16[128,2048]{1,0:T(8,128)(2,1)S(1)}, bf16[128,2048]{1,0:T(8,128)(2,1)S(1)}, u32[]{:S(2)}, u32[]{:S(2)}) collective-permute-start(bf16[128,2048]{1,0:T(8,128)(2,1)S(1)} %multiply_convert_fusion.1), channel_id=1, source_target_pairs={{0,16},{8,24},{16,0},{24,8},{1,17},{9,25},{17,1},{25,9},{2,18},{10... | collective-permute-start | bytes 1572872 | tf_op jit(solution)/shard_map/ppermute | solution.py:73
  286.4 19.9 %collective-permute-start.28 = (bf16[128,2048]{1,0:T(8,128)(2,1)S(1)}, bf16[128,2048]{1,0:T(8,128)(2,1)S(1)}, u32[]{:S(2)}, u32[]{:S(2)}) collective-permute-start(bf16[128,2048]{1,0:T(8,128)(2,1)S(1)} %multiply_convert_fusion.1), channel_id=1, source_target_pairs={{0,8},{8,16},{16,24},{24,0},{1,9},{9,17},{17,25},{25,1},{2,10},{10... | collective-permute-start | bytes 1572872 | tf_op jit(solution)/shard_map/ppermute | solution.py:73
  378.0 17.2 %collective-permute-start.29 = (bf16[128,2432]{1,0:T(8,128)(2,1)}, bf16[128,2432]{1,0:T(8,128)(2,1)}, u32[]{:S(2)}, u32[]{:S(2)}) collective-permute-start(bf16[128,2432]{1,0:T(8,128)(2,1)} %get-tuple-element.80), channel_id=1, source_target_pairs={{0,16},{8,24},{16,0},{24,8},{1,17},{9,25},{17,1},{25,9},{2,18},{10... | collective-permute-start | bytes 1867784 | tf_op jit(solution)/shard_map/ppermute | solution.py:73
  380.8 28.3 %collective-permute-start.30 = (bf16[128,2432]{1,0:T(8,128)(2,1)}, bf16[128,2432]{1,0:T(8,128)(2,1)}, u32[]{:S(2)}, u32[]{:S(2)}) collective-permute-start(bf16[128,2432]{1,0:T(8,128)(2,1)} %get-tuple-element.82), channel_id=1, source_target_pairs={{0,8},{8,16},{16,24},{24,0},{1,9},{9,17},{17,25},{25,1},{2,10},{10... | collective-permute-start | bytes 1867784 | tf_op jit(solution)/shard_map/ppermute | solution.py:73
  381.0 28.1 %collective-permute-start.31 = (bf16[128,2432]{1,0:T(8,128)(2,1)}, bf16[128,2432]{1,0:T(8,128)(2,1)}, u32[]{:S(2)}, u32[]{:S(2)}) collective-permute-start(bf16[128,2432]{1,0:T(8,128)(2,1)} %get-tuple-element.81), channel_id=1, source_target_pairs={{0,24},{8,0},{16,8},{24,16},{1,25},{9,1},{17,9},{25,17},{2,26},{10... | collective-permute-start | bytes 1867784 | tf_op jit(solution)/shard_map/ppermute | solution.py:73
  383.5 187.4 %reduce-scatter.5.cloned.1.call-start = ((), (), s32[]{:S(2)}) async-start(), calls=%async_computation.7 | async-start | bytes 5406720 | tf_op jit(solution)/shard_map/reduce_scatter | solution.py:765
  417.5 9.3 %collective-permute-start.32 = (bf16[128,512]{1,0:T(8,128)(2,1)S(1)}, bf16[128,512]{1,0:T(8,128)(2,1)S(1)}, u32[]{:S(2)}, u32[]{:S(2)}) collective-permute-start(bf16[128,512]{1,0:T(8,128)(2,1)S(1)} %get-tuple-element.111), channel_id=1, source_target_pairs={{0,6},{2,0},{4,2},{6,4},{1,7},{3,1},{5,3},{7,5},{8,14},{10,8},{12,... | collective-permute-start | bytes 393224 | tf_op jit(solution)/shard_map/ppermute | solution.py:73
  420.0 6.8 collective-permute-start.33
  420.6 9.2 %collective-permute-start.34 = (bf16[128,512]{1,0:T(8,128)(2,1)S(1)}, bf16[128,512]{1,0:T(8,128)(2,1)S(1)}, u32[]{:S(2)}, u32[]{:S(2)}) collective-permute-start(bf16[128,512]{1,0:T(8,128)(2,1)S(1)} %get-tuple-element.109), channel_id=1, source_target_pairs={{0,2},{2,4},{4,6},{6,0},{1,3},{3,5},{5,7},{7,1},{8,10},{10,12},{12... | collective-permute-start | bytes 393224 | tf_op jit(solution)/shard_map/ppermute | solution.py:73
  426.7 258.9 %all-gather.8.cloned.1.call-start = ((), (), s32[]{:S(2)}) async-start(), calls=%async_computation.8 | async-start | bytes 8982528 | tf_op jit(solution)/shard_map/all_gather | solution.py:768
  450.2 8.9 %collective-permute-start.35 = (bf16[4,512,512]{2,1,0:T(8,128)(2,1)}, bf16[4,512,512]{2,1,0:T(8,128)(2,1)S(1)}, u32[]{:S(2)}, u32[]{:S(2)}) collective-permute-start(bf16[4,512,512]{2,1,0:T(8,128)(2,1)} %get-tuple-element.47), channel_id=1, source_target_pairs={{1,0},{3,2},{5,4},{7,6},{9,8},{11,10},{13,12},{15,14},{17,16},{19,... | collective-permute-start | bytes 6291464 | tf_op jit(solution)/shard_map/ppermute | solution.py:135
  453.9 78.5 %collective-permute-start.40 = (bf16[4,512,512]{2,1,0:T(8,128)(2,1)}, bf16[4,512,512]{2,1,0:T(8,128)(2,1)}, u32[]{:S(2)}, u32[]{:S(2)}) collective-permute-start(bf16[4,512,512]{2,1,0:T(8,128)(2,1)} %get-tuple-element.50), channel_id=1, source_target_pairs={{1,0},{3,2},{5,4},{7,6},{9,8},{11,10},{13,12},{15,14},{17,16},{19,... | collective-permute-start | bytes 6291464 | tf_op jit(solution)/shard_map/ppermute | solution.py:135
  456.5 75.8 %collective-permute-start.42 = (bf16[4,512,512]{2,1,0:T(8,128)(2,1)}, bf16[4,512,512]{2,1,0:T(8,128)(2,1)}, u32[]{:S(2)}, u32[]{:S(2)}) collective-permute-start(bf16[4,512,512]{2,1,0:T(8,128)(2,1)} %get-tuple-element.50), channel_id=1, source_target_pairs={{64,1},{96,33},{66,3},{98,35},{68,5},{100,37},{70,7},{102,39},{72,... | collective-permute-start | bytes 6291464 | tf_op jit(solution)/shard_map/ppermute | solution.py:136
  457.8 74.6 %collective-permute-start.43 = (bf16[4,512,512]{2,1,0:T(8,128)(2,1)}, bf16[4,512,512]{2,1,0:T(8,128)(2,1)}, u32[]{:S(2)}, u32[]{:S(2)}) collective-permute-start(bf16[4,512,512]{2,1,0:T(8,128)(2,1)} %get-tuple-element.47), channel_id=1, source_target_pairs={{96,1},{64,33},{98,3},{66,35},{100,5},{68,37},{102,7},{70,39},{104... | collective-permute-start | bytes 6291464 | tf_op jit(solution)/shard_map/ppermute | solution.py:136
  464.0 68.4 %collective-permute-start.41 = (bf16[4,512,512]{2,1,0:T(8,128)(2,1)}, bf16[4,512,512]{2,1,0:T(8,128)(2,1)}, u32[]{:S(2)}, u32[]{:S(2)}) collective-permute-start(bf16[4,512,512]{2,1,0:T(8,128)(2,1)} %add_convert_fusion.2), channel_id=1, source_target_pairs={{0,32},{1,33},{32,0},{33,1},{64,96},{65,97},{96,64},{97,65},{2,34}... | collective-permute-start | bytes 6291464 | tf_op jit(solution)/shard_map/ppermute | solution.py:138
  470.9 17.4 %collective-permute-start.36 = (bf16[128,2048]{1,0:T(8,128)(2,1)S(1)}, bf16[128,2048]{1,0:T(8,128)(2,1)S(1)}, u32[]{:S(2)}, u32[]{:S(2)}) collective-permute-start(bf16[128,2048]{1,0:T(8,128)(2,1)S(1)} %get-tuple-element.89), channel_id=1, source_target_pairs={{0,16},{8,24},{16,0},{24,8},{1,17},{9,25},{17,1},{25,9},{2,18},{10... | collective-permute-start | bytes 1572872 | tf_op jit(solution)/shard_map/ppermute | solution.py:73
  488.3 26.3 %collective-permute-start.37 = (bf16[128,2048]{1,0:T(8,128)(2,1)S(1)}, bf16[128,2048]{1,0:T(8,128)(2,1)S(1)}, u32[]{:S(2)}, u32[]{:S(2)}) collective-permute-start(bf16[128,2048]{1,0:T(8,128)(2,1)S(1)} %get-tuple-element.91), channel_id=1, source_target_pairs={{0,8},{8,16},{16,24},{24,0},{1,9},{9,17},{17,25},{25,1},{2,10},{10... | collective-permute-start | bytes 1572872 | tf_op jit(solution)/shard_map/ppermute | solution.py:73
  514.6 13.5 %collective-permute-start.38 = (bf16[128,2048]{1,0:T(8,128)(2,1)S(1)}, bf16[128,2048]{1,0:T(8,128)(2,1)S(1)}, u32[]{:S(2)}, u32[]{:S(2)}) collective-permute-start(bf16[128,2048]{1,0:T(8,128)(2,1)S(1)} %get-tuple-element.90), channel_id=1, source_target_pairs={{0,24},{8,0},{16,8},{24,16},{1,25},{9,1},{17,9},{25,17},{2,26},{10... | collective-permute-start | bytes 1572872 | tf_op jit(solution)/shard_map/ppermute | solution.py:73
  538.6 13.7 %collective-permute-start.44 = (bf16[512,512]{1,0:T(8,128)(2,1)S(1)}, bf16[512,512]{1,0:T(8,128)(2,1)S(1)}, u32[]{:S(2)}, u32[]{:S(2)}) collective-permute-start(bf16[512,512]{1,0:T(8,128)(2,1)S(1)} %get-tuple-element.86), channel_id=1, source_target_pairs={{0,16},{8,24},{16,0},{24,8},{1,17},{9,25},{17,1},{25,9},{2,18},{10... | collective-permute-start | bytes 1572872 | tf_op jit(solution)/shard_map/ppermute | solution.py:73
  540.9 24.4 %collective-permute-start.45 = (bf16[512,512]{1,0:T(8,128)(2,1)S(1)}, bf16[512,512]{1,0:T(8,128)(2,1)S(1)}, u32[]{:S(2)}, u32[]{:S(2)}) collective-permute-start(bf16[512,512]{1,0:T(8,128)(2,1)S(1)} %get-tuple-element.88), channel_id=1, source_target_pairs={{0,8},{8,16},{16,24},{24,0},{1,9},{9,17},{17,25},{25,1},{2,10},{10... | collective-permute-start | bytes 1572872 | tf_op jit(solution)/shard_map/ppermute | solution.py:73
  541.3 23.9 %collective-permute-start.46 = (bf16[512,512]{1,0:T(8,128)(2,1)S(1)}, bf16[512,512]{1,0:T(8,128)(2,1)S(1)}, u32[]{:S(2)}, u32[]{:S(2)}) collective-permute-start(bf16[512,512]{1,0:T(8,128)(2,1)S(1)} %get-tuple-element.87), channel_id=1, source_target_pairs={{0,24},{8,0},{16,8},{24,16},{1,25},{9,1},{17,9},{25,17},{2,26},{10... | collective-permute-start | bytes 1572872 | tf_op jit(solution)/shard_map/ppermute | solution.py:73
  594.2 8.0 %collective-permute-start.47 = (bf16[128,384]{0,1:T(8,128)(2,1)}, bf16[128,384]{0,1:T(8,128)(2,1)}, u32[]{:S(2)}, u32[]{:S(2)}) collective-permute-start(bf16[128,384]{0,1:T(8,128)(2,1)} %get-tuple-element.123), channel_id=1, source_target_pairs={{0,4},{2,6},{4,0},{6,2},{1,5},{3,7},{5,1},{7,3},{8,12},{10,14},{12... | collective-permute-start | bytes 294920 | tf_op jit(solution)/shard_map/ppermute | solution.py:73
  612.9 8.6 %collective-permute-start.53 = (bf16[16,80,128]{2,1,0:T(8,128)(2,1)S(1)}, bf16[16,80,128]{2,1,0:T(8,128)(2,1)S(1)}, u32[]{:S(2)}, u32[]{:S(2)}) collective-permute-start(bf16[16,80,128]{2,1,0:T(8,128)(2,1)S(1)} %fusion.42), channel_id=1, source_target_pairs={{0,1},{1,0},{2,3},{3,2},{4,5},{5,4},{6,7},{7,6},{8,9},{9,8},{10,11... | collective-permute-start | bytes 983048 | tf_op jit(solution)/shard_map/ppermute | solution.py:69
  621.0 89.5 %collective-permute-start.39 = (bf16[64,2048]{1,0:T(8,128)(2,1)}, bf16[64,2048]{1,0:T(8,128)(2,1)}, u32[]{:S(2)}, u32[]{:S(2)}) collective-permute-start(bf16[64,2048]{1,0:T(8,128)(2,1)} %get-tuple-element.107), channel_id=1, source_target_pairs={{0,1},{1,0},{2,3},{3,2},{4,5},{5,4},{6,7},{7,6},{8,9},{9,8},{10,11... | collective-permute-start | bytes 786440 | tf_op jit(solution)/shard_map/ppermute | solution.py:69
  621.7 18.9 %collective-permute-start.54 = (bf16[4,80,128]{2,1,0:T(8,128)(2,1)S(1)}, bf16[4,80,128]{2,1,0:T(8,128)(2,1)S(1)}, u32[]{:S(2)}, u32[]{:S(2)}) collective-permute-start(bf16[4,80,128]{2,1,0:T(8,128)(2,1)S(1)} %get-tuple-element.99), channel_id=1, source_target_pairs={{0,32},{32,64},{64,96},{96,0},{1,33},{33,65},{65,97},{97,1},{2,34}... | collective-permute-start | bytes 245768 | tf_op jit(solution)/shard_map/ppermute | solution.py:73
  621.8 19.1 %collective-permute-start.55 = (bf16[4,80,128]{2,1,0:T(8,128)(2,1)S(1)}, bf16[4,80,128]{2,1,0:T(8,128)(2,1)S(1)}, u32[]{:S(2)}, u32[]{:S(2)}) collective-permute-start(bf16[4,80,128]{2,1,0:T(8,128)(2,1)S(1)} %get-tuple-element.101), channel_id=1, source_target_pairs={{0,64},{32,96},{64,0},{96,32},{1,65},{33,97},{65,1},{97,33},{2,66}... | collective-permute-start | bytes 245768 | tf_op jit(solution)/shard_map/ppermute | solution.py:73
  641.0 6.8 collective-permute-start.57
  641.4 6.4 collective-permute-start.58
  649.1 30.9 %collective-permute-start.66 = (bf16[128,2048]{1,0:T(8,128)(2,1)S(1)}, bf16[128,2048]{1,0:T(8,128)(2,1)S(1)}, u32[]{:S(2)}, u32[]{:S(2)}) collective-permute-start(bf16[128,2048]{1,0:T(8,128)(2,1)S(1)} %get-tuple-element.83), channel_id=1, source_target_pairs={{0,4},{2,6},{4,0},{6,2},{1,5},{3,7},{5,1},{7,3},{8,12},{10,14},{12... | collective-permute-start | bytes 1572872 | tf_op jit(solution)/shard_map/ppermute | solution.py:73
  650.9 33.0 %collective-permute-start.67 = (bf16[128,2048]{1,0:T(8,128)(2,1)S(1)}, bf16[128,2048]{1,0:T(8,128)(2,1)S(1)}, u32[]{:S(2)}, u32[]{:S(2)}) collective-permute-start(bf16[128,2048]{1,0:T(8,128)(2,1)S(1)} %get-tuple-element.85), channel_id=1, source_target_pairs={{0,2},{2,4},{4,6},{6,0},{1,3},{3,5},{5,7},{7,1},{8,10},{10,12},{12... | collective-permute-start | bytes 1572872 | tf_op jit(solution)/shard_map/ppermute | solution.py:73
  650.9 33.0 %collective-permute-start.68 = (bf16[128,2048]{1,0:T(8,128)(2,1)S(1)}, bf16[128,2048]{1,0:T(8,128)(2,1)S(1)}, u32[]{:S(2)}, u32[]{:S(2)}) collective-permute-start(bf16[128,2048]{1,0:T(8,128)(2,1)S(1)} %get-tuple-element.84), channel_id=1, source_target_pairs={{0,6},{2,0},{4,2},{6,4},{1,7},{3,1},{5,3},{7,5},{8,14},{10,8},{12,... | collective-permute-start | bytes 1572872 | tf_op jit(solution)/shard_map/ppermute | solution.py:73
  677.8 22.6 %collective-permute-start.73 = (bf16[4,4,80,128]{3,2,1,0:T(8,128)(2,1)}, bf16[4,4,80,128]{3,2,1,0:T(8,128)(2,1)}, u32[]{:S(2)}, u32[]{:S(2)}) collective-permute-start(bf16[4,4,80,128]{3,2,1,0:T(8,128)(2,1)} %bitcast_dynamic-update-slice_fusion.15), channel_id=1, source_target_pairs={{0,6},{2,0},{4,2},{6,4},{1,7},{3,1},{5,3},{7,5},{8,14},{10,8},{12,... | collective-permute-start | bytes 983048 | tf_op jit(solution)/shard_map/ppermute | solution.py:73
  680.0 21.5 %collective-permute-start.74 = (bf16[4,4,80,128]{3,2,1,0:T(8,128)(2,1)}, bf16[4,4,80,128]{3,2,1,0:T(8,128)(2,1)}, u32[]{:S(2)}, u32[]{:S(2)}) collective-permute-start(bf16[4,4,80,128]{3,2,1,0:T(8,128)(2,1)} %bitcast_dynamic-update-slice_fusion.15), channel_id=1, source_target_pairs={{0,4},{2,6},{4,0},{6,2},{1,5},{3,7},{5,1},{7,3},{8,12},{10,14},{12... | collective-permute-start | bytes 983048 | tf_op jit(solution)/shard_map/ppermute | solution.py:73
  683.9 18.6 %collective-permute-start.75 = (bf16[4,4,80,128]{3,2,1,0:T(8,128)(2,1)}, bf16[4,4,80,128]{3,2,1,0:T(8,128)(2,1)}, u32[]{:S(2)}, u32[]{:S(2)}) collective-permute-start(bf16[4,4,80,128]{3,2,1,0:T(8,128)(2,1)} %bitcast_dynamic-update-slice_fusion.15), channel_id=1, source_target_pairs={{0,2},{2,4},{4,6},{6,0},{1,3},{3,5},{5,7},{7,1},{8,10},{10,12},{12... | collective-permute-start | bytes 983048 | tf_op jit(solution)/shard_map/ppermute | solution.py:73
  703.5 9.9 %collective-permute-start.76 = (bf16[4,16,80,128]{3,2,1,0:T(8,128)(2,1)S(1)}, bf16[4,16,80,128]{3,2,1,0:T(8,128)(2,1)S(1)}, u32[]{:S(2)}, u32[]{:S(2)}) collective-permute-start(bf16[4,16,80,128]{3,2,1,0:T(8,128)(2,1)S(1)} %bitcast.277), channel_id=1, source_target_pairs={{0,1},{1,0},{2,3},{3,2},{4,5},{5,4},{6,7},{7,6},{8,9},{9,8},{10,11... | collective-permute-start | bytes 3932168 | tf_op jit(solution)/shard_map/ppermute | solution.py:69
  (101 other events, 1515.9 us)
Sparse Core Ops, SparseCore 0:
  11.1 102.6 all-gather.3
  235.5 94.1 all-gather.5
  383.6 80.3 reduce-scatter.2
  468.0 102.8 reduce-scatter.4
  579.2 103.2 all-gather.7
